TPU v7x, 32 devices: a whole 2x2x4 slice. The times are simulated.
32 devices in a mesh: seq: 8 (over z, y), mp: 4 (over x, core).
Axes of the slice: x: 2, y: 2, z: 4, core: 2. Of those that a mesh axis runs over, the one named last changes fastest.
Arguments:
- tokens: bfloat16 [9792, 2048], P(('seq', 'mp')), may hold values from -6 to 6
- cotangent: bfloat16 [9792, 2048], P(('seq', 'mp')), may hold values from -6 to 6
- present: int32 [8, 4], P('seq'), may hold values from 0 to 1, as said below
- summary_mask: int32 [8, 4, 50], P('seq'), may hold values 0 or 1
- attention_weight: float32 [4, 2048, 2048], P(None, 'seq', 'mp'), may hold values from -0.5466517 to 0.5466517
- attention_first: float32 [4, 2048, 2048], P(None, 'seq', 'mp'), may hold values from -9.1552734e-05 to 9.1552734e-05
- attention_second: float32 [4, 2048, 2048], P(None, 'seq', 'mp'), may hold values from 5.163215e-10 to 4.170289e-09
- attention_average: float32 [4, 2048, 2048], P(None, 'seq', 'mp'), may hold values from -0.125 to 0.125
- hidden_weight: float32 [2, 2048, 8192], P(None, 'seq', 'mp'), may hold values from -0.09375 to 0.09375
- hidden_first: float32 [2, 2048, 8192], P(None, 'seq', 'mp'), may hold values from -9.1552734e-05 to 9.1552734e-05
- hidden_second: float32 [2, 2048, 8192], P(None, 'seq', 'mp'), may hold values from 5.163215e-10 to 4.170289e-09
- hidden_average: float32 [2, 2048, 8192], P(None, 'seq', 'mp'), may hold values from -0.09375 to 0.09375
- norm_params: float32 [6, 2048], P(None, 'seq'), may hold values from -1.2 to 2.2
- norm_first: float32 [6, 2048], P(None, 'seq'), may hold values from -0.00024414062 to 0.00024414062
- norm_second: float32 [6, 2048], P(None, 'seq'), may hold values from 4.5674593e-09 to 3.7731184e-08
- norm_average: float32 [6, 2048], P(None, 'seq'), may hold values from -1.2 to 2.2
- head_bias: float32 [2, 2048], P(None, ('mp', 'seq')), may hold values from -1.75 to 1.75
- head_first: float32 [2, 2048], P(None, ('mp', 'seq')), may hold values from -0.00024414062 to 0.00024414062
- head_second: float32 [2, 2048], P(None, ('mp', 'seq')), may hold values from 4.5674593e-09 to 3.7731184e-08
- head_average: float32 [2, 2048], P(None, ('mp', 'seq')), may hold values from -1.75 to 1.75
- unit_bias: float32 [8192], P(('mp', 'seq')), may hold values from -1.75 to 1.75
- unit_first: float32 [8192], P(('mp', 'seq')), may hold values from -9.1552734e-05 to 9.1552734e-05
- unit_second: float32 [8192], P(('mp', 'seq')), may hold values from 5.163215e-10 to 4.170289e-09
- unit_average: float32 [8192], P(('mp', 'seq')), may hold values from -1.75 to 1.75
Outputs:
- block_output: bfloat16 [9792, 2048], P(('seq', 'mp'))
- input_grad: bfloat16 [9792, 2048], P(('seq', 'mp'))
- grad_norm: float32 [], replicated
- attention_updated: float32 [4, 2048, 2048], P(None, 'seq', 'mp')
- attention_momentum: float32 [4, 2048, 2048], P(None, 'seq', 'mp')
- attention_variance: float32 [4, 2048, 2048], P(None, 'seq', 'mp')
- attention_averaged: float32 [4, 2048, 2048], P(None, 'seq', 'mp')
- attention_copy: bfloat16 [4, 2048, 2048], P(None, 'seq', 'mp')
- hidden_updated: float32 [2, 2048, 8192], P(None, 'seq', 'mp')
- hidden_momentum: float32 [2, 2048, 8192], P(None, 'seq', 'mp')
- hidden_variance: float32 [2, 2048, 8192], P(None, 'seq', 'mp')
- hidden_averaged: float32 [2, 2048, 8192], P(None, 'seq', 'mp')
- hidden_copy: bfloat16 [2, 2048, 8192], P(None, 'seq', 'mp')
- norm_updated: float32 [6, 2048], P(None, 'seq')
- norm_momentum: float32 [6, 2048], P(None, 'seq')
- norm_variance: float32 [6, 2048], P(None, 'seq')
- norm_averaged: float32 [6, 2048], P(None, 'seq')
- norm_copy: bfloat16 [6, 2048], P(None, 'seq')
- head_updated: float32 [2, 2048], P(None, ('mp', 'seq'))
- head_momentum: float32 [2, 2048], P(None, ('mp', 'seq'))
- head_variance: float32 [2, 2048], P(None, ('mp', 'seq'))
- head_averaged: float32 [2, 2048], P(None, ('mp', 'seq'))
- head_copy: bfloat16 [2, 2048], P(None, ('mp', 'seq'))
- unit_updated: float32 [8192], P(('mp', 'seq'))
- unit_momentum: float32 [8192], P(('mp', 'seq'))
- unit_variance: float32 [8192], P(('mp', 'seq'))
- unit_averaged: float32 [8192], P(('mp', 'seq'))
- unit_copy: bfloat16 [8192], P(('mp', 'seq'))
Inputs may be any that keep to these rules, and one draw needn't show every extreme that they name: In every item the first and the last of the 4 segments are present.
All inputs are finite; a program needn't handle non-finite values. No bound on the sum of `summary_mask` on one device may be relied on, other than what follows from the above.
Results may differ from a plain program's by a relative error of at most 0.02.
Values may be sent and summed in bfloat16 or wider, within the bound.
A program may use at most 320 MiB of HBM per device.

v0:
```python
import jax
import jax.numpy as jnp
from jax import lax
from jax.sharding import PartitionSpec as P

D = 2048
HEAD_DIM = 64
FF = 8192
SUMM = 50
NSEG = 4
SEG = 256
STEP = 10


norm_eps = 1e-05
beta_first = 0.9
beta_second = 0.95
adam_eps = 1e-08
clip_limit = 1.0
weight_decay = 0.1
average_keep = 0.6
vector_rate = 0.4


def layer_norm(value, gain, shift):
    center = value - jnp.mean(value, axis=-1, keepdims=True)
    spread = jnp.mean(center * center, axis=-1, keepdims=True)
    return center * lax.rsqrt(spread + norm_eps) * gain + shift


def gelu_tanh(value):
    return jax.nn.gelu(value, approximate=True)


def item_layout(present, summary):
    period = SEG + SUMM
    places = jnp.arange(NSEG * period, dtype=jnp.int32)
    segment = places // period
    slot_place = places % period - SEG
    segment_hit = segment[:, None] == jnp.arange(NSEG, dtype=jnp.int32)[None, :]
    slot_hit = slot_place[:, None] == jnp.arange(SUMM, dtype=jnp.int32)[None, :]
    segment_on = jnp.sum(jnp.where(segment_hit, present[None, :], 0), axis=1, dtype=jnp.int32)
    both_hit = segment_hit[:, :, None] & slot_hit[:, None, :]
    slot_on = jnp.sum(jnp.where(both_hit, summary[None], 0), axis=(1, 2), dtype=jnp.int32)
    summary_row = slot_place >= 0
    row_kept = segment_on * jnp.where(summary_row, slot_on, 1)
    return (places, segment, summary_row, row_kept)


def visible(query_places, query_segment, places, segment, summary_row, row_kept):
    same_segment = (segment[None, :] == query_segment[:, None]) & (
        places[None, :] <= query_places[:, None]
    )
    earlier_summary = summary_row[None, :] & (segment[None, :] < query_segment[:, None])
    itself = places[None, :] == query_places[:, None]
    return itself | (row_kept[None, :] == 1) & (same_segment | earlier_summary)


def block_count(total_rows):
    count_best = 1
    for divisor in range(1, total_rows + 1):
        if total_rows % divisor == 0 and total_rows // divisor >= 512:
            count_best = divisor
    return count_best


def owned_part(whole, dim):
    count = whole.shape[dim] // lax.axis_size("seq")
    return lax.dynamic_slice_in_dim(whole, lax.axis_index("seq") * count, count, dim)


def adam_step(master, grad, first, second, average, factor, rate, decay):
    clipped = grad * factor
    first_new = beta_first * first + (1.0 - beta_first) * clipped
    second_new = beta_second * second + (1.0 - beta_second) * clipped * clipped
    first_hat = first_new / (1.0 - beta_first**STEP)
    second_hat = second_new / (1.0 - beta_second**STEP)
    master_new = master - rate * (first_hat / (jnp.sqrt(second_hat) + adam_eps) + decay * master)
    average_new = average_keep * average + (1.0 - average_keep) * master_new
    return (master_new, first_new, second_new, average_new, master_new.astype(jnp.bfloat16))


def per_device(
    tokens,
    cotangent,
    present,
    summary_mask,
    attention_weight,
    attention_first,
    attention_second,
    attention_average,
    hidden_weight,
    hidden_first,
    hidden_second,
    hidden_average,
    norm_params,
    norm_first,
    norm_second,
    norm_average,
    head_bias,
    head_first,
    head_second,
    head_average,
    unit_bias,
    unit_first,
    unit_second,
    unit_average,
):
    local_rows = tokens.shape[0]
    item_rows = local_rows * lax.axis_size("mp")
    first_row = lax.axis_index("mp") * local_rows
    attn_full, hidden_full, norm_full, head_full, unit_full = (
        lax.all_gather(attention_weight.astype(jnp.bfloat16), "seq", axis=1, tiled=True),
        lax.all_gather(hidden_weight.astype(jnp.bfloat16), "seq", axis=1, tiled=True),
        lax.all_gather(norm_params.astype(jnp.bfloat16), "seq", axis=1, tiled=True),
        lax.all_gather(head_bias.astype(jnp.bfloat16), "seq", axis=1, tiled=True),
        lax.all_gather(unit_bias.astype(jnp.bfloat16), "seq", axis=0, tiled=True),
    )
    norm_vals = norm_full.astype(jnp.float32)
    head_vals = head_full.astype(jnp.float32)
    unit_vals = unit_full.astype(jnp.float32)
    places, segment, summary_row, row_kept = item_layout(present[0], summary_mask[0])
    local_weight = lax.dynamic_slice_in_dim(row_kept, first_row, local_rows, 0).astype(jnp.float32)[
        :, None
    ]
    inputs = tokens.astype(jnp.float32)
    normed_local = layer_norm(inputs, norm_vals[0], norm_vals[1]).astype(jnp.bfloat16)
    normed = lax.all_gather(normed_local, "mp", axis=0, tiled=True)
    projected = jnp.einsum("td,kdh->kth", normed, attn_full[:3], preferred_element_type=jnp.float32)
    head_count = projected.shape[2] // HEAD_DIM
    query_heads = (
        (projected[0] + head_vals[0]).astype(jnp.bfloat16).reshape(item_rows, head_count, HEAD_DIM)
    )
    key_heads = projected[1].astype(jnp.bfloat16).reshape(item_rows, head_count, HEAD_DIM)
    value_heads = (
        (projected[2] + head_vals[1]).astype(jnp.bfloat16).reshape(item_rows, head_count, HEAD_DIM)
    )
    score_scale = HEAD_DIM ** (-0.5)
    blocks = block_count(item_rows)
    block_rows = item_rows // blocks

    def scores_for(start):
        query_block = lax.dynamic_slice_in_dim(query_heads, start, block_rows, 0)
        raw_scores = (
            jnp.einsum("qhd,khd->hqk", query_block, key_heads, preferred_element_type=jnp.float32)
            * score_scale
        )
        block_places = start + jnp.arange(block_rows, dtype=jnp.int32)
        block_segment = lax.dynamic_slice_in_dim(segment, start, block_rows, 0)
        allowed = visible(block_places, block_segment, places, segment, summary_row, row_kept)
        return (jnp.where(allowed[None], raw_scores, -1e30), query_block)

    def forward_block(block_index):
        scores, unused_query = scores_for(block_index * block_rows)
        peak_score = jnp.max(scores, axis=-1, keepdims=True)
        raised = jnp.exp(scores - peak_score)
        denominator = jnp.sum(raised, axis=-1, keepdims=True)
        softmaxed = (raised / denominator).astype(jnp.bfloat16)
        context_block = jnp.einsum(
            "hqk,khd->qhd", softmaxed, value_heads, preferred_element_type=jnp.float32
        )
        return (
            context_block.astype(jnp.bfloat16),
            peak_score[..., 0] + jnp.log(denominator[..., 0]),
        )

    context_blocks, log_totals = lax.map(forward_block, jnp.arange(blocks, dtype=jnp.int32))
    context = context_blocks.reshape(item_rows, head_count * HEAD_DIM)
    part_rows = lax.slice_in_dim(context, 0, local_rows * lax.axis_size("mp"), axis=0)
    attended = (
        lax.psum_scatter(
            jnp.einsum(
                "th,dh->td", part_rows, attn_full[3], preferred_element_type=jnp.float32
            ).astype(jnp.bfloat16),
            "mp",
            scatter_dimension=0,
            tiled=True,
        ).astype(jnp.float32)
        + norm_vals[4]
    )
    middle = inputs + local_weight * attended
    second_local = layer_norm(middle, norm_vals[2], norm_vals[3]).astype(jnp.bfloat16)
    second_rows = lax.all_gather(second_local, "mp", axis=0, tiled=True)
    pre_act = jnp.dot(second_rows, hidden_full[0], preferred_element_type=jnp.float32) + unit_vals
    activated = gelu_tanh(pre_act).astype(jnp.bfloat16)
    part_rows = lax.slice_in_dim(activated, 0, local_rows * lax.axis_size("mp"), axis=0)
    feed_out = lax.psum_scatter(
        jnp.einsum(
            "tf,df->td", part_rows, hidden_full[1], preferred_element_type=jnp.float32
        ).astype(jnp.bfloat16),
        "mp",
        scatter_dimension=0,
        tiled=True,
    ).astype(jnp.float32)
    block_output = (middle + local_weight * (feed_out + norm_vals[5])).astype(jnp.bfloat16)
    out_grad = cotangent.astype(jnp.float32)
    feed_grad = local_weight * out_grad
    down_bias_grad = jnp.sum(feed_grad, axis=0)
    feed_rows = lax.all_gather(feed_grad.astype(jnp.bfloat16), "mp", axis=0, tiled=True)
    grad_down = jnp.einsum("td,tf->df", feed_rows, activated, preferred_element_type=jnp.float32)
    act_grad = jnp.dot(feed_rows, hidden_full[1], preferred_element_type=jnp.float32)
    gelu_pull = jax.vjp(gelu_tanh, pre_act)[1]
    pre_grad = gelu_pull(act_grad)[0].astype(jnp.bfloat16)
    grad_unit = jnp.sum(pre_grad, axis=0, dtype=jnp.float32)
    grad_up = jnp.einsum("td,tf->df", second_rows, pre_grad, preferred_element_type=jnp.float32)
    grad_hidden = jnp.stack([grad_up, grad_down])
    part_rows = lax.slice_in_dim(pre_grad, 0, local_rows * lax.axis_size("mp"), axis=0)
    second_grad = lax.psum_scatter(
        jnp.einsum(
            "tf,df->td", part_rows, hidden_full[0], preferred_element_type=jnp.float32
        ).astype(jnp.bfloat16),
        "mp",
        scatter_dimension=0,
        tiled=True,
    ).astype(jnp.float32)
    second_pull = jax.vjp(layer_norm, middle, norm_vals[2], norm_vals[3])[1]
    middle_part, gain_two_grad, shift_two_grad = second_pull(second_grad)
    middle_grad = out_grad + middle_part
    attn_grad = local_weight * middle_grad
    out_bias_grad = jnp.sum(attn_grad, axis=0)
    attn_rows = lax.all_gather(attn_grad.astype(jnp.bfloat16), "mp", axis=0, tiled=True)
    grad_output_proj = jnp.einsum(
        "td,th->dh", attn_rows, context, preferred_element_type=jnp.float32
    )
    context_grad = jnp.dot(attn_rows, attn_full[3], preferred_element_type=jnp.float32).astype(
        jnp.bfloat16
    )
    context_heads = context_grad.reshape(item_rows, head_count, HEAD_DIM)

    def backward_block(carry, operands):
        key_grad, value_grad = carry
        block_index, log_block = operands
        start = block_index * block_rows
        scores, query_block = scores_for(start)
        softmaxed = jnp.exp(scores - log_block[..., None])
        grad_block = lax.dynamic_slice_in_dim(context_heads, start, block_rows, 0)
        value_grad = value_grad + jnp.einsum(
            "hqk,qhd->khd",
            softmaxed.astype(jnp.bfloat16),
            grad_block,
            preferred_element_type=jnp.float32,
        )
        prob_grad = jnp.einsum(
            "qhd,khd->hqk", grad_block, value_heads, preferred_element_type=jnp.float32
        )
        inner_sum = jnp.sum(softmaxed * prob_grad, axis=-1, keepdims=True)
        score_grad = (softmaxed * (prob_grad - inner_sum)).astype(jnp.bfloat16)
        query_grad = (
            jnp.einsum("hqk,khd->qhd", score_grad, key_heads, preferred_element_type=jnp.float32)
            * score_scale
        )
        key_grad = (
            key_grad
            + jnp.einsum(
                "hqk,qhd->khd", score_grad, query_block, preferred_element_type=jnp.float32
            )
            * score_scale
        )
        return ((key_grad, value_grad), query_grad)

    zero_heads = jnp.zeros((item_rows, head_count, HEAD_DIM), jnp.float32)
    (key_grad, value_grad), query_grads = lax.scan(
        backward_block, (zero_heads, zero_heads), (jnp.arange(blocks, dtype=jnp.int32), log_totals)
    )
    head_width = head_count * HEAD_DIM
    qkv_grad = jnp.stack(
        [
            query_grads.reshape(item_rows, head_width),
            key_grad.reshape(item_rows, head_width),
            value_grad.reshape(item_rows, head_width),
        ]
    ).astype(jnp.bfloat16)
    grad_heads_bias = jnp.stack(
        [
            jnp.sum(qkv_grad[0], axis=0, dtype=jnp.float32),
            jnp.sum(qkv_grad[2], axis=0, dtype=jnp.float32),
        ]
    )
    grad_qkv = jnp.einsum("td,kth->kdh", normed, qkv_grad, preferred_element_type=jnp.float32)
    grad_attention = jnp.concatenate([grad_qkv, grad_output_proj[None]], axis=0)
    part_rows = lax.slice_in_dim(qkv_grad, 0, local_rows * lax.axis_size("mp"), axis=1)
    first_grad = lax.psum_scatter(
        jnp.einsum(
            "kth,kdh->td", part_rows, attn_full[:3], preferred_element_type=jnp.float32
        ).astype(jnp.bfloat16),
        "mp",
        scatter_dimension=0,
        tiled=True,
    ).astype(jnp.float32)
    first_pull = jax.vjp(layer_norm, inputs, norm_vals[0], norm_vals[1])[1]
    input_part, gain_one_grad, shift_one_grad = first_pull(first_grad)
    input_grad = (middle_grad + input_part).astype(jnp.bfloat16)
    vector_grad = jnp.stack(
        [
            gain_one_grad,
            shift_one_grad,
            gain_two_grad,
            shift_two_grad,
            out_bias_grad,
            down_bias_grad,
        ]
    )
    summed = (
        lax.psum(grad_attention.astype(jnp.bfloat16), "seq").astype(jnp.float32),
        lax.psum(grad_hidden.astype(jnp.bfloat16), "seq").astype(jnp.float32),
        lax.psum(vector_grad.astype(jnp.bfloat16), "seq").astype(jnp.float32),
        lax.psum(grad_heads_bias.astype(jnp.bfloat16), "seq").astype(jnp.float32),
        lax.psum(grad_unit.astype(jnp.bfloat16), "seq").astype(jnp.float32),
    )
    attn_shard = owned_part(summed[0], 1)
    hidden_shard = owned_part(summed[1], 1)
    norm_shard = owned_part(summed[2], 1)
    head_shard = owned_part(summed[3], 1)
    unit_shard = owned_part(summed[4], 0)
    norm_shard = lax.psum(norm_shard, "mp")
    leader = (lax.axis_index("mp") == 0).astype(jnp.float32)
    local_squares = (
        jnp.sum(attn_shard * attn_shard)
        + jnp.sum(hidden_shard * hidden_shard)
        + jnp.sum(head_shard * head_shard)
        + jnp.sum(unit_shard * unit_shard)
        + leader * jnp.sum(norm_shard * norm_shard)
    )
    grad_norm = jnp.sqrt(lax.psum(local_squares, ("seq", "mp")))
    factor = jnp.minimum(1.0, clip_limit / (grad_norm + 1e-06))
    hidden_rate = jnp.array([D ** (-0.5), FF ** (-0.5)], jnp.float32)[:, None, None]
    attention_out = adam_step(
        attention_weight,
        attn_shard,
        attention_first,
        attention_second,
        attention_average,
        factor,
        D ** (-0.5),
        weight_decay,
    )
    hidden_out = adam_step(
        hidden_weight,
        hidden_shard,
        hidden_first,
        hidden_second,
        hidden_average,
        factor,
        hidden_rate,
        weight_decay,
    )
    norm_out = adam_step(
        norm_params, norm_shard, norm_first, norm_second, norm_average, factor, vector_rate, 0.0
    )
    head_out = adam_step(
        head_bias, head_shard, head_first, head_second, head_average, factor, vector_rate, 0.0
    )
    unit_out = adam_step(
        unit_bias, unit_shard, unit_first, unit_second, unit_average, factor, vector_rate, 0.0
    )
    return (
        block_output,
        input_grad,
        grad_norm,
        attention_out[0],
        attention_out[1],
        attention_out[2],
        attention_out[3],
        attention_out[4],
        hidden_out[0],
        hidden_out[1],
        hidden_out[2],
        hidden_out[3],
        hidden_out[4],
        norm_out[0],
        norm_out[1],
        norm_out[2],
        norm_out[3],
        norm_out[4],
        head_out[0],
        head_out[1],
        head_out[2],
        head_out[3],
        head_out[4],
        unit_out[0],
        unit_out[1],
        unit_out[2],
        unit_out[3],
        unit_out[4],
    )


def solution(mesh):
    return jax.shard_map(
        per_device,
        mesh=mesh,
        in_specs=(
            P(("seq", "mp"), None),
            P(("seq", "mp"), None),
            P("seq", None),
            P("seq", None, None),
            P(None, "seq", "mp"),
            P(None, "seq", "mp"),
            P(None, "seq", "mp"),
            P(None, "seq", "mp"),
            P(None, "seq", "mp"),
            P(None, "seq", "mp"),
            P(None, "seq", "mp"),
            P(None, "seq", "mp"),
            P(None, "seq"),
            P(None, "seq"),
            P(None, "seq"),
            P(None, "seq"),
            P(None, ("mp", "seq")),
            P(None, ("mp", "seq")),
            P(None, ("mp", "seq")),
            P(None, ("mp", "seq")),
            P(("mp", "seq")),
            P(("mp", "seq")),
            P(("mp", "seq")),
            P(("mp", "seq")),
        ),
        out_specs=(
            P(("seq", "mp"), None),
            P(("seq", "mp"), None),
            P(),
            P(None, "seq", "mp"),
            P(None, "seq", "mp"),
            P(None, "seq", "mp"),
            P(None, "seq", "mp"),
            P(None, "seq", "mp"),
            P(None, "seq", "mp"),
            P(None, "seq", "mp"),
            P(None, "seq", "mp"),
            P(None, "seq", "mp"),
            P(None, "seq", "mp"),
            P(None, "seq"),
            P(None, "seq"),
            P(None, "seq"),
            P(None, "seq"),
            P(None, "seq"),
            P(None, ("mp", "seq")),
            P(None, ("mp", "seq")),
            P(None, ("mp", "seq")),
            P(None, ("mp", "seq")),
            P(None, ("mp", "seq")),
            P(("mp", "seq")),
            P(("mp", "seq")),
            P(("mp", "seq")),
            P(("mp", "seq")),
            P(("mp", "seq")),
        ),
        check_vma=False,
    )
```

profile of v0, /device:TPU:0, one launch (start us, length us, event | category | flops | bytes accessed | tf_op | source)
XLA Modules:
  0.0 1953.2 jit_solution(7397723521839225412)
XLA Ops:
  11.0 32.2 %all_gather.27 = bf16[6,2048]{1,0:T(8,128)(2,1)S(1)} all-gather(bf16[6,256]{1,0:T(8,128)(2,1)S(1)} %convert_element_type.160), channel_id=1, replica_groups=mesh['seq'=8,'mp'=4] {'seq'}, dimensions={1}, use_global_device_ids=true | all-gather | bytes 27648 | tf_op jit(solution)/shard_map/all_gather | solution.py:115
  47.3 20.4 %all-gather.1 = bf16[8,64,2]{1,2,0:T(2,128)(2,1)S(1)} all-gather(bf16[1,64,2]{1,2,0:T(2,128)(2,1)S(1)} %convert_bitcast_fusion.3), channel_id=1, replica_groups=mesh['seq'=8,'mp'=4] {'seq'}, dimensions={0}, use_global_device_ids=true | all-gather | bytes 2304 | tf_op jit(solution)/shard_map/all_gather | solution.py:116
  70.0 16.8 all-gather.17.cloned.1.call-done
  86.8 6.0 reshape.550
  92.7 121.8 %all-gather.13.cloned.1.call-done = bf16[4,2048,512]{2,1,0:T(8,128)(2,1)} async-done(((bf16[4,256,512]{2,1,0:T(8,128)(2,1)}), bf16[4,2048,512]{2,1,0:T(8,128)(2,1)}) %all-gather.13.cloned.1.call-update) | async-done | bytes 8388624 | tf_op jit(solution)/shard_map/all_gather | solution.py:113
  214.5 12.4 fusion.74
  240.8 79.4 %while.30 = (s32[]{:T(128)}, bf16[2,612,8,64]{1,3,2,0:T(8,128)(2,1)}, f32[2,8,612]{2,1,0:T(8,128)S(1)}, s32[2]{0:T(128)S(1)}, s32[1224]{0:T(1024)S(1)}, /*index=...) while((s32[]{:T(128)}, ...), condition=%wide.region_7.8_spmd.clone.clone, body=%wide.region_4.7_spmd.clone.clone.sunk | while | flops 1613106560 | bytes 89033248 | solution.py:167
  244.2 12.1 fusion.195
  256.3 11.2 fusion.196
  267.5 12.0 fusion.197
  283.8 12.1 fusion.195
  295.9 11.2 fusion.196
  307.1 12.0 fusion.197
  320.2 4.7 copy.141
  324.9 4.4 reshape.526
  329.3 7.3 convolution_convert_fusion
  336.6 47.9 %fusion.8 = bf16[312,2048]{1,0:T(8,128)(2,1)S(1)} fusion(bf16[1224,2048]{1,0:T(8,128)(2,1)} %convolution_convert_fusion), kind=kCustom, calls=%all-reduce-scatter | all-reduce-scatter fusion | flops 2555905 | bytes 6291968
  387.0 6.3 concatenate.5
  404.0 18.3 all-gather.3
  422.3 16.6 all-gather.21.cloned.1.call-done
  438.9 6.2 reshape.545
  445.1 35.6 %all-gather.19.cloned.1.call-done = bf16[4,306,2048]{2,1,0:T(8,128)(2,1)} async-done(((bf16[1,306,2048]{2,1,0:T(8,128)(2,1)}), bf16[4,306,2048]{2,1,0:T(8,128)(2,1)}) %all-gather.19.cloned.1.call-update) | async-done | bytes 5013520 | tf_op jit(solution)/shard_map/all_gather | solution.py:183
  480.6 6.0 reshape.541
  486.6 224.2 %all-gather.15.cloned.1.call-done = bf16[2,2048,2048]{2,1,0:T(8,128)(2,1)} async-done(((bf16[2,256,2048]{2,1,0:T(8,128)(2,1)}), bf16[2,2048,2048]{2,1,0:T(8,128)(2,1)}) %all-gather.15.cloned.1.call-update) | async-done | bytes 16777232 | tf_op jit(solution)/shard_map/all_gather | solution.py:114
  710.9 17.2 fusion.69
  728.1 21.3 %fusion.149 = (bf16[2048]{0:T(1024)(128)(2,1)}, bf16[1224,2048]{1,0:T(8,128)(2,1)S(1)}) fusion(f32[1224,2048]{1,0:T(8,128)} %fusion.69, f32[2048]{0:T(1024)S(1)} %bitcast.170, bf16[1224,2048]{1,0:T(8,128)(2,1)S(1)} %copy-done.24, bf16[2,2048,2048]{2,1,0:T(8,128)(2,1)} %all-gather.15.cloned.1.call-done), kind=kOutput, calls=%fused_computation.237 | convolution fusion | flops 10322802688 | bytes 28454912 | tf_op jit(solution)/shard_map/dot_general | solution.py:201
  751.6 15.1 convolution_convert_fusion.1
  766.7 48.6 %fusion.10 = bf16[312,2048]{1,0:T(8,128)(2,1)} fusion(bf16[1224,2048]{1,0:T(8,128)(2,1)} %convolution_convert_fusion.1), kind=kCustom, calls=%all-reduce-scatter.2 | all-reduce-scatter fusion | flops 2555905 | bytes 6291968
  818.5 8.2 concatenate.7
  826.7 3.9 fusion.95
  835.2 14.8 convert_bitcast_fusion.1
  850.0 15.8 convert_bitcast_fusion
  865.8 6.8 pad_maximum_fusion
  876.4 6.0 reshape.547
  882.4 6.6 fusion.91
  889.0 5.5 convolution_convert_fusion.4
  897.1 173.1 %while.31 = (s32[]{:T(128)}, f32[1224,8,64]{0,2,1:T(8,128)}, f32[1224,8,64]{0,2,1:T(8,128)}, bf16[2,612,8,64]{1,3,2,0:T(8,128)(2,1)}, s32[2]{0:T(128)S(1)}, /*in...) while((s32[]{:T(128)}, f32[1224,8,64]{0,2,1:T(8,128)}, ...), condition=%wide.region_17.18_spmd.clone.clone, body=%wide.region_15.17_spmd.clone.clone.sunk | while | flops 3899460352 | bytes 202585840 | solution.py:262
  900.7 11.4 fusion.207
  912.2 18.3 multiply_reduce_fusion.5
  930.5 21.0 %multiply_convert_fusion.6 = bf16[8,612,1224]{1,2,0:T(8,128)(2,1)} fusion(f32[8,612,1224]{1,2,0:T(8,128)} %get-tuple-element.726, f32[8,612,1224]{1,2,0:T(8,128)} %fusion.207, f32[8,612]{1,0:T(8,128)S(1)} %get-tuple-element.727), kind=kLoop, calls=%fused_computation.34.clone.1 | loop fusion | flops 17978112 | bytes 59946624 | tf_op jit(solution)/shard_map/while/body/eval_jaxpr/convert_element_type | solution.py:247
  951.5 13.8 fusion.211
  965.3 7.5 fusion.212
  972.8 10.2 fusion.210
  986.2 11.4 fusion.207
  997.6 18.4 multiply_reduce_fusion.5
  1016.0 21.0 %multiply_convert_fusion.6 = bf16[8,612,1224]{1,2,0:T(8,128)(2,1)} fusion(f32[8,612,1224]{1,2,0:T(8,128)} %get-tuple-element.726, f32[8,612,1224]{1,2,0:T(8,128)} %fusion.207, f32[8,612]{1,0:T(8,128)S(1)} %get-tuple-element.727), kind=kLoop, calls=%fused_computation.34.clone.1 | loop fusion | flops 17978112 | bytes 59946624 | tf_op jit(solution)/shard_map/while/body/eval_jaxpr/convert_element_type | solution.py:247
  1037.1 14.5 fusion.211
  1051.6 7.5 fusion.212
  1059.1 11.0 fusion.210
  1076.4 4.5 reshape.553
  1084.6 12.1 convert_bitcast_fusion.2
  1096.6 5.6 pad_maximum_fusion.1
  1113.5 18.9 convolution_convert_fusion.2
  1133.6 12.5 bitcast_convert_fusion
  1146.1 90.4 %fusion.130 = (bf16[312,2048]{1,0:T(8,128)(2,1)S(1)}, bf16[312,2048]{1,0:T(8,128)(2,1)}) fusion(bf16[1224,2048]{1,0:T(8,128)(2,1)} %convolution_convert_fusion.2, bf16[1224,2048]{1,0:T(8,128)(2,1)} %bitcast_convert_fusion), kind=kCustom, calls=%all-reduce-scatter.4 | all-reduce-scatter fusion | flops 5111809 | bytes 12583424
  1242.5 6.6 concatenate.8
  1252.1 39.6 %all-reduce.8 = (bf16[2,512]{1,0:T(2,128)(2,1)S(1)}, bf16[2048]{0:T(1024)(128)(2,1)S(1)}, bf16[6,2048]{1,0:T(8,128)(2,1)S(1)}) all-reduce(bf16[2,512]{1,0:T(2,128)(2,1)S(1)} %pad_maximum_fusion.5, bf16[2048]{0:T(1024)(128)(2,1)S(1)} %copy-done.66, bf16[6,2048]{1,0:T(8,128)(2,1)S(1)} %stack.57), channel_id=1, replica_groups=mesh['seq'=8,'mp'=4] {'seq'}, use_global_device_ids=true, to_apply=%region_27.28 | all-reduce | flops 15360 | bytes 61440 | tf_op jit(solution)/shard_map/psum | solution.py:307
  1291.7 6.2 psum.54
  1299.2 8.3 concatenate.6
  1308.8 542.8 %all-reduce.13.cloned.1.call-done = (bf16[4,2048,512]{1,2,0:T(8,128)(2,1)}, bf16[2,2048,2048]{2,1,0:T(8,128)(2,1)}) async-done(((bf16[4,2048,512]{1,2,0:T(8,128)(2,1)}, bf16[2,2048,2048]{2,1,0:T(8,128)(2,1)}), (bf16[4,2048,512]{1,2,0:T(8,128)(2,1)}, bf16[2,2048,2048]{2,1,0:T(8,128)(2,1)})) %all-reduce.13.cloned.1.call-update) | async-done | bytes 25165840 | tf_op jit(solution)/shard_map/psum | solution.py:304
  1859.8 6.6 add_convert_fusion.2
  1866.4 39.6 %psum.55 = f32[]{:T(128)} all-reduce(f32[]{:T(128)S(6)} %add.367), channel_id=1, replica_groups=mesh['seq'=8,'mp'=4] {'seq','mp'}, use_global_device_ids=true, to_apply=%region_41.42 | all-reduce | flops 1 | bytes 8 | tf_op jit(solution)/shard_map/psum | solution.py:324
  1906.7 6.9 fusion.142
  1931.6 9.7 fusion.139
  (318 shorter events, 124.8 us)
Async XLA Ops:
  7.2 37.2 %copy-start.2 = (bf16[306,2048]{1,0:T(8,128)(2,1)S(1)}, bf16[306,2048]{1,0:T(8,128)(2,1)}, u32[]{:S(2)}) copy-start(bf16[306,2048]{1,0:T(8,128)(2,1)} %param.29) | copy-start | bytes 3760132
  7.2 3.7 copy-start.52
  7.2 79.5 %all-gather.17.cloned.1.call-start = ((), (), s32[]{:S(2)}) async-start(), calls=%async_computation.2 | async-start | bytes 6389760 | tf_op jit(solution)/shard_map/all_gather | solution.py:128
  8.9 34.9 %copy-start.45 = (f32[306]{0:T(512)}, f32[306]{0:T(512)S(1)}, u32[]{:S(2)}) copy-start(f32[306]{0:T(512)S(1)} %broadcast_multiply_fusion.1) | copy-start | bytes 3676
  8.9 37.1 %copy-start.17 = (f32[4,256,512]{2,1,0:T(8,128)S(1)}, f32[4,256,512]{2,1,0:T(8,128)}, u32[]{:S(2)}) copy-start(f32[4,256,512]{2,1,0:T(8,128)} %param.33) | copy-start | bytes 6291460
  10.9 32.9 %copy-start.56 = (f32[306]{0:T(512)}, f32[306]{0:T(512)S(1)}, u32[]{:S(2)}) copy-start(f32[306]{0:T(512)S(1)} %fusion.97) | copy-start | bytes 3676
  10.9 32.9 %copy-start.47 = (f32[306]{0:T(512)}, f32[306]{0:T(512)S(1)}, u32[]{:S(2)}) copy-start(f32[306]{0:T(512)S(1)} %fusion.117) | copy-start | bytes 3676
  46.0 22.0 %copy-start.69 = (s32[1,4,50]{2,1,0:T(4,128)S(1)}, s32[1,4,50]{2,1,0:T(4,128)}, u32[]{:S(2)}) copy-start(s32[1,4,50]{2,1,0:T(4,128)} %param.32) | copy-start | bytes 2404
  46.0 22.1 %copy-start.82 = (u32[32]{0:T(128)S(1)}, u32[32]{0:T(128)}, u32[]{:S(2)}) copy-start(u32[32]{0:T(128)} %constant.122) | copy-start | bytes 388
  46.0 23.3 %copy-start.81 = (s32[1,4]{1,0:T(1,128)S(1)}, s32[1,4]{1,0:T(1,128)}, u32[]{:S(2)}) copy-start(s32[1,4]{1,0:T(1,128)} %param.31) | copy-start | bytes 52
  46.0 168.5 %all-gather.13.cloned.1.call-start = ((), (), s32[]{:S(2)}) async-start(), calls=%async_computation | async-start | bytes 9437184 | tf_op jit(solution)/shard_map/all_gather | solution.py:113
  47.2 391.7 %all-gather.21.cloned.1.call-start = ((), (), s32[]{:S(2)}) async-start(), calls=%async_computation.4 | async-start | bytes 6389760 | tf_op jit(solution)/shard_map/all_gather | solution.py:199
  256.3 11.2 copy-start.31
  295.9 11.2 copy-start.31
  320.1 9.1 copy-start
  320.2 9.1 copy-start.5
  320.2 9.1 copy-start.27
  320.2 9.1 copy-start.38
  320.2 65.9 %copy-start.34 = (s32[1224]{0:T(1024)}, s32[1224]{0:T(1024)S(1)}, u32[]{:S(2)}) copy-start(s32[1224]{0:T(1024)S(1)} %get-tuple-element.850) | copy-start | bytes 14692
  384.5 8.9 copy-start.3
  384.5 8.9 copy-start.36
  384.5 2.5 collective-permute-start
  386.2 446.3 %copy-start.42 = (f32[306]{0:T(512)}, f32[306]{0:T(512)S(1)}, u32[]{:S(2)}) copy-start(f32[306]{0:T(512)S(1)} %dynamic-slice_convert_fusion.1) | copy-start | bytes 3676
  393.3 437.4 %copy-start.8 = (bf16[330,2048]{1,0:T(8,128)(2,1)}, bf16[330,2048]{1,0:T(8,128)(2,1)S(1)}, u32[]{:S(2)}) copy-start(bf16[330,2048]{1,0:T(8,128)(2,1)S(1)} %concatenate.5) | copy-start | bytes 4055044
  397.6 83.0 %all-gather.19.cloned.1.call-start = ((), (), s32[]{:S(2)}) async-start(), calls=%async_computation.3 | async-start | bytes 6389760 | tf_op jit(solution)/shard_map/all_gather | solution.py:183
  400.0 4.0 copy-start.72
  400.0 310.8 %all-gather.15.cloned.1.call-start = ((), (), s32[]{:S(2)}) async-start(), calls=%async_computation.1 | async-start | bytes 18874368 | tf_op jit(solution)/shard_map/all_gather | solution.py:114
  403.9 472.5 %all-gather.23.cloned.1.call-start = ((), (), s32[]{:S(2)}) async-start(), calls=%async_computation.5 | async-start | bytes 6389760 | tf_op jit(solution)/shard_map/all_gather | solution.py:221
  422.3 427.7 %copy-start.64 = (f32[8,1,256]{2,1,0:T(1,128)}, f32[8,1,256]{2,1,0:T(1,128)S(1)}, u32[]{:S(2)}) copy-start(f32[8,1,256]{2,1,0:T(1,128)S(1)} %convert_element_type.207) | copy-start | bytes 24580
  710.9 17.2 copy-start.24
  816.3 2.2 collective-permute-start.2
  826.7 4.0 copy-start.12
  835.1 1016.4 %all-reduce.13.cloned.1.call-start = ((), (), s32[]{:S(2)}) async-start(), calls=%async_computation.6 | async-start | bytes 50331648 | tf_op jit(solution)/shard_map/psum | solution.py:304
  872.6 9.8 copy-start.30
  882.4 6.6 copy-start.25
  889.0 8.0 copy-start.6
  1070.2 3.4 copy-start.22
  1076.4 4.5 copy-start.7
  1113.4 18.9 copy-start.13
  1113.4 19.3 copy-start.58
  1113.4 19.3 copy-start.60
  1113.5 19.3 copy-start.59
  1113.5 19.3 copy-start.23
  1236.5 6.0 copy-start.20
  1236.5 13.0 copy-start.4
  1236.5 13.0 copy-start.41
  1236.5 13.0 copy-start.46
  1237.7 4.8 collective-permute-start.3
  1239.0 60.1 %collective-permute-start.1 = (bf16[18,2048]{1,0:T(8,128)(2,1)S(1)}, bf16[18,2048]{1,0:T(8,128)(2,1)S(1)}, u32[]{:S(2)}, u32[]{:S(2)}) collective-permute-start(bf16[18,2048]{1,0:T(8,128)(2,1)S(1)} %slice.85), channel_id=1, source_target_pairs={{0,1},{1,2},{2,3},{4,5},{5,6},{6,7},{8,9},{9,10},{10,11},{12,13},{... | collective-permute-start | bytes 221192
  1299.1 560.7 %copy-start.9 = (bf16[330,2048]{1,0:T(8,128)(2,1)S(1)}, bf16[330,2048]{1,0:T(8,128)(2,1)}, u32[]{:S(2)}) copy-start(bf16[330,2048]{1,0:T(8,128)(2,1)} %copy-done.8) | copy-start | bytes 4055044
  1299.1 560.7 %copy-start.37 = (f32[1,2048]{1,0:T(1,128)S(1)}, f32[1,2048]{1,0:T(1,128)}, u32[]{:S(2)}) copy-start(f32[1,2048]{1,0:T(1,128)} %get-tuple-element.575) | copy-start | bytes 24580
  1299.1 560.7 %copy-start.43 = (f32[306]{0:T(512)S(1)}, f32[306]{0:T(512)}, u32[]{:S(2)}) copy-start(f32[306]{0:T(512)} %copy-done.42) | copy-start | bytes 3676
  1299.1 560.7 %copy-start.49 = (f32[1,2048]{1,0:T(1,128)S(1)}, f32[1,2048]{1,0:T(1,128)}, u32[]{:S(2)}) copy-start(f32[1,2048]{1,0:T(1,128)} %get-tuple-element.572) | copy-start | bytes 24580
  1299.1 560.7 %copy-start.55 = (f32[306]{0:T(512)S(1)}, f32[306]{0:T(512)}, u32[]{:S(2)}) copy-start(f32[306]{0:T(512)} %copy-done.54) | copy-start | bytes 3676
  1926.0 3.8 copy-start.71
  1926.0 4.3 copy-start.53
  1926.0 4.3 copy-start.61
  1926.0 4.3 copy-start.62
  1926.0 4.9 copy-start.63
  1926.0 5.5 copy-start.80
  1928.5 12.8 copy-start.67
  1929.8 11.6 copy-start.68
  1931.0 10.4 copy-start.51
  1931.6 9.8 copy-start.26
  (33 other events, 73.9 us)
Sparse Core Ops, SparseCore 0:
  46.1 40.5 all-gather.16
  89.5 124.9 all-gather.12
  397.7 41.1 all-gather.20
  440.9 39.6 all-gather.18
  483.2 227.5 all-gather.14
  835.3 41.1 all-gather.22
  1102.4 749.1 all-reduce.12
where the time goes:
time: 1960 us; the launch traced here: 1950 us
  waiting for transfers between devices  963 us (49%)
  blocking collectives  343 us (18%)
  matrix products  331 us (17%)
  other arithmetic  161 us (8%)
  local copies, waits for them, and re-layouts  121 us (6%)
  between operations  21.5 us (1%)
    psum x1, waiting for transfers between devices, per_device(): lax.psum(grad_attention.astype(jnp.bfloat16), 'seq').astype(jnp.float32)  543 us
    all_gather x1, waiting for transfers between devices, per_device(): lax.all_gather(hidden_weight.astype(jnp.bfloat16), 'seq', axis=1, tiled=T...  224 us
    unnamed x3, blocking collectives  187 us
    all_gather x1, waiting for transfers between devices, per_device(): lax.all_gather(attention_weight.astype(jnp.bfloat16), 'seq', axis=1, tile...  122 us
    unnamed x187, local copies, waits for them, and re-layouts  82.6 us
    dot_general x4, matrix products, scores_for(): jnp.einsum('qhd,khd->hqk', query_block, key_heads, preferred_element_type...  60.9 us
    convert_element_type x2, other arithmetic, backward_block(): score_grad = (softmaxed * (prob_grad - inner_sum)).astype(jnp.bfloat16)  42.1 us
    psum x1, blocking collectives, per_device(): grad_norm = jnp.sqrt(lax.psum(local_squares, ('seq', 'mp')))  39.6 us
  transfers between devices with their start and end apart: 11, of which 9 were waited for; matrix products, arithmetic and copies ran while one was open for 11% of the time, Pallas kernels for 0%

commit v1 on v0

v1 whole, which is shorter than its diff:
```python
import functools

import jax
import jax.numpy as jnp
import numpy as np
from jax import lax
from jax.experimental import pallas as pl
from jax.experimental.pallas import tpu as pltpu
from jax.sharding import PartitionSpec as P

D = 2048
HEAD_DIM = 64
FF = 8192
SUMM = 50
NSEG = 4
SEG = 256
STEP = 10
PERIOD = SEG + SUMM
SEG_PAD = 320
SLAB = 64
KEYS = SLAB * (NSEG - 1) + SEG_PAD

norm_eps = 1e-05
beta_first = 0.9
beta_second = 0.95
adam_eps = 1e-08
clip_limit = 1.0
weight_decay = 0.1
average_keep = 0.6
vector_rate = 0.4
score_scale = HEAD_DIM ** (-0.5)
query_blocks = ((0, 128), (128, 256), (256, SEG_PAD))

f32 = jnp.float32
bf16 = jnp.bfloat16


def seq_grid():
    count = lax.axis_size("seq")
    inner = count // 4
    return count // inner, inner


def shift_outer(value, step):
    outer, inner = seq_grid()
    pairs = [
        (a * inner + b, ((a + step) % outer) * inner + b) for a in range(outer) for b in range(inner)
    ]
    return lax.ppermute(value, "seq", pairs)


def shift_inner(value, step):
    outer, inner = seq_grid()
    pairs = [
        (a * inner + b, a * inner + (b + step) % inner) for a in range(outer) for b in range(inner)
    ]
    return lax.ppermute(value, "seq", pairs)


def swap(value, bits):
    return lax.ppermute(value, "mp", [(m, m ^ bits) for m in range(lax.axis_size("mp"))])


def feature_order():
    outer, inner = seq_grid()
    me = lax.axis_index("seq")
    mine_a, mine_b = me // inner, me % inner
    return jnp.stack(
        [
            ((mine_a - i + outer) % outer) * inner + (mine_b - j + inner) % inner
            for j in range(inner)
            for i in range(outer)
        ]
    ).astype(jnp.int32)


def row_codes():
    count = lax.axis_size("mp")
    return [high * 2 + low for low in range(2) for high in range(count // 2)]


def gather_weight(own):
    outer, inner = seq_grid()
    line = [own]
    for _ in range(outer - 1):
        line.append(shift_outer(line[-1], 1))
    blocks = list(line)
    for _ in range(inner - 1):
        line = [shift_inner(part, 1) for part in line]
        blocks += line
    return jnp.concatenate(blocks, axis=0)


def scatter_weight(block_grad):
    outer, inner = seq_grid()
    total = None
    for i in reversed(range(outer)):
        part = block_grad(inner - 1, i)
        for j in reversed(range(inner - 1)):
            part = block_grad(j, i) + shift_inner(part.astype(bf16), -1).astype(f32)
        if total is not None:
            part = part + shift_outer(total.astype(bf16), -1).astype(f32)
        total = part
    return total


def gather_rows(own):
    count = lax.axis_size("mp")
    high = [own]
    for bit in range(1, count.bit_length() - 1):
        high = high + [swap(part, 1 << bit) for part in high]
    low = [swap(part, 1) for part in high]
    return jnp.concatenate(high + low, axis=0)


def scatter_rows(part):
    count = lax.axis_size("mp")
    half = part.shape[0] // 2
    kept = part[:half].astype(f32) + swap(part[half:], 1).astype(f32)
    rows = half // (count // 2)
    total = kept[:rows]
    for high in range(1, count // 2):
        total = total + swap(kept[high * rows : (high + 1) * rows].astype(bf16), high * 2).astype(f32)
    return total


def to_blocks_kernel(order_ref, in_ref, out_ref):
    rows = in_ref.shape[0]
    out_ref[...] = jnp.zeros_like(out_ref)
    out_ref[:rows, :] = in_ref[...]


def to_blocks(value, order, rows_padded):
    rows, width = value.shape
    count = order.shape[0]
    wide = width // count
    return pl.pallas_call(
        to_blocks_kernel,
        out_shape=jax.ShapeDtypeStruct((rows_padded, width), value.dtype),
        grid_spec=pltpu.PrefetchScalarGridSpec(
            num_scalar_prefetch=1,
            grid=(count,),
            in_specs=[pl.BlockSpec((rows, wide), lambda n, order_ref: (0, order_ref[n]))],
            out_specs=pl.BlockSpec((rows_padded, wide), lambda n, order_ref: (0, n)),
        ),
        name="to_blocks",
    )(order, value)


def from_blocks_kernel(order_ref, in_ref, out_ref):
    rows = out_ref.shape[0]
    out_ref[...] = in_ref[:rows, :].astype(out_ref.dtype)


def from_blocks(value, order, rows):
    rows_padded, width = value.shape
    count = order.shape[0]
    wide = width // count
    return pl.pallas_call(
        from_blocks_kernel,
        out_shape=jax.ShapeDtypeStruct((rows, width), bf16),
        grid_spec=pltpu.PrefetchScalarGridSpec(
            num_scalar_prefetch=1,
            grid=(count,),
            in_specs=[pl.BlockSpec((rows_padded, wide), lambda n, order_ref: (0, n))],
            out_specs=pl.BlockSpec((rows, wide), lambda n, order_ref: (0, order_ref[n])),
        ),
        name="from_blocks",
    )(order, value)


def segment_starts(me, mp_count, rows_padded):
    group = mp_count // NSEG
    starts = []
    for s in range(NSEG):
        pieces = []
        for r in range(group):
            code = jnp.bitwise_xor(me, s * group + r)
            place = jnp.bitwise_and(code, 1) * (mp_count // 2) + lax.shift_right_logical(code, 1)
            pieces.append(pl.multiple_of(place * rows_padded, rows_padded))
        starts.append(pieces)
    return starts


def load_segment(ref, pieces, rows_padded):
    parts = [ref[pl.ds(start, rows_padded), :] for start in pieces]
    return parts[0] if len(parts) == 1 else jnp.concatenate(parts, axis=0)


def load_slab(ref, pieces, rows_padded):
    return ref[pl.ds(pl.multiple_of(pieces[-1] + (rows_padded - SLAB), 16), SLAB), :]


def store_segment(ref, pieces, rows_padded, value):
    for r, start in enumerate(pieces):
        ref[pl.ds(start, rows_padded), :] = value[r * rows_padded : (r + 1) * rows_padded]


def lane_halves(shape):
    lane = lax.broadcasted_iota(jnp.int32, shape, 1)
    return lane < HEAD_DIM


def attend_kernel(mp_count, rows_padded, me_ref, q_ref, k_ref, v_ref, bias_ref, o_ref, p_ref):
    starts = segment_starts(me_ref[0], mp_count, rows_padded)
    for s in range(NSEG):
        keys = jnp.concatenate(
            [load_slab(k_ref, starts[e], rows_padded) for e in range(s)]
            + [load_segment(k_ref, starts[s], rows_padded)],
            axis=0,
        )
        values = jnp.concatenate(
            [load_slab(v_ref, starts[e], rows_padded) for e in range(s)]
            + [load_segment(v_ref, starts[s], rows_padded)],
            axis=0,
        )
        queries = load_segment(q_ref, starts[s], rows_padded)
        first_head = lane_halves(queries.shape)
        zero = jnp.zeros_like(queries)
        head_queries = (jnp.where(first_head, queries, zero), jnp.where(first_head, zero, queries))
        outs = []
        for low, high in query_blocks:
            count = SLAB * s + high
            bias = bias_ref[s, low:high, :count]
            both = []
            for h in range(2):
                scores = (
                    lax.dot_general(
                        head_queries[h][low:high],
                        keys[:count],
                        (((1,), (1,)), ((), ())),
                        preferred_element_type=f32,
                    )
                    + bias
                )
                peak = jnp.max(scores, axis=-1, keepdims=True)
                raised = jnp.exp(scores - peak)
                share = raised * (1.0 / jnp.sum(raised, axis=-1, keepdims=True))
                share = share.astype(bf16)
                p_ref[h, s * SEG_PAD + low : s * SEG_PAD + high, :count] = share
                both.append(jnp.dot(share, values[:count], preferred_element_type=f32))
            outs.append(jnp.where(first_head[low:high], both[0], both[1]))
        out = jnp.concatenate(outs, axis=0).astype(bf16)
        store_segment(o_ref, starts[s], rows_padded, out)


def attend(qkv, bias, me, mp_count, rows_padded):
    rows, width = qkv.shape
    pairs = width // 3 // 128
    return pl.pallas_call(
        functools.partial(attend_kernel, mp_count, rows_padded),
        out_shape=(
            jax.ShapeDtypeStruct((rows, width // 3), bf16),
            jax.ShapeDtypeStruct((pairs * 2, rows, KEYS), bf16),
        ),
        grid_spec=pltpu.PrefetchScalarGridSpec(
            num_scalar_prefetch=1,
            grid=(pairs,),
            in_specs=[
                pl.BlockSpec((rows, 128), lambda n, me_ref: (0, n)),
                pl.BlockSpec((rows, 128), lambda n, me_ref: (0, pairs + n)),
                pl.BlockSpec((rows, 128), lambda n, me_ref: (0, 2 * pairs + n)),
                pl.BlockSpec(bias.shape, lambda n, me_ref: (0, 0, 0)),
            ],
            out_specs=(
                pl.BlockSpec((rows, 128), lambda n, me_ref: (0, n)),
                pl.BlockSpec((2, rows, KEYS), lambda n, me_ref: (n, 0, 0)),
            ),
        ),
        compiler_params=pltpu.CompilerParams(vmem_limit_bytes=48 * 2**20),
        name="attend",
    )(me, qkv, qkv, qkv, bias)


def attend_back_kernel(
    mp_count,
    rows_padded,
    me_ref,
    q_ref,
    k_ref,
    v_ref,
    o_ref,
    g_ref,
    p_ref,
    dq_ref,
    dk_ref,
    dv_ref,
    key_sum,
    value_sum,
):
    starts = segment_starts(me_ref[0], mp_count, rows_padded)
    key_sum[...] = jnp.zeros_like(key_sum)
    value_sum[...] = jnp.zeros_like(value_sum)
    for s in range(NSEG):
        keys = jnp.concatenate(
            [load_slab(k_ref, starts[e], rows_padded) for e in range(s)]
            + [load_segment(k_ref, starts[s], rows_padded)],
            axis=0,
        )
        values = jnp.concatenate(
            [load_slab(v_ref, starts[e], rows_padded) for e in range(s)]
            + [load_segment(v_ref, starts[s], rows_padded)],
            axis=0,
        )
        queries = load_segment(q_ref, starts[s], rows_padded)
        grads = load_segment(g_ref, starts[s], rows_padded)
        outs = load_segment(o_ref, starts[s], rows_padded)
        queries_turned = queries.astype(f32).T.astype(bf16)
        grads_turned = grads.astype(f32).T.astype(bf16)
        first_head = lane_halves(queries.shape)
        zero = jnp.zeros_like(queries)
        head_grads = (jnp.where(first_head, grads, zero), jnp.where(first_head, zero, grads))
        product = grads.astype(f32) * outs.astype(f32)
        head_deltas = (
            jnp.sum(jnp.where(first_head, product, 0.0), axis=-1, keepdims=True),
            jnp.sum(jnp.where(first_head, 0.0, product), axis=-1, keepdims=True),
        )
        query_grads = []
        for low, high in query_blocks:
            count = SLAB * s + high
            both = []
            for h in range(2):
                share = p_ref[h, s * SEG_PAD + low : s * SEG_PAD + high, :count]
                share_grad = lax.dot_general(
                    head_grads[h][low:high],
                    values[:count],
                    (((1,), (1,)), ((), ())),
                    preferred_element_type=f32,
                )
                score_grad = (
                    share.astype(f32) * (share_grad - head_deltas[h][low:high])
                ).astype(bf16)
                both.append(jnp.dot(score_grad, keys[:count], preferred_element_type=f32))
                lanes = slice(h * HEAD_DIM, (h + 1) * HEAD_DIM)
                value_part = jnp.dot(
                    grads_turned[lanes, low:high], share, preferred_element_type=f32
                )
                key_part = jnp.dot(
                    queries_turned[lanes, low:high], score_grad, preferred_element_type=f32
                )
                for e in range(s):
                    place = slice((e + 1) * SEG_PAD - SLAB, (e + 1) * SEG_PAD)
                    value_sum[lanes, place] += value_part[:, e * SLAB : (e + 1) * SLAB]
                    key_sum[lanes, place] += key_part[:, e * SLAB : (e + 1) * SLAB]
                place = slice(s * SEG_PAD, s * SEG_PAD + high)
                value_sum[lanes, place] += value_part[:, s * SLAB :]
                key_sum[lanes, place] += key_part[:, s * SLAB :]
            query_grads.append(jnp.where(first_head[low:high], both[0], both[1]))
        query_grad = (jnp.concatenate(query_grads, axis=0) * score_scale).astype(bf16)
        store_segment(dq_ref, starts[s], rows_padded, query_grad)
    key_all = key_sum[...].T.astype(bf16)
    value_all = value_sum[...].T.astype(bf16)
    for s in range(NSEG):
        place = slice(s * SEG_PAD, (s + 1) * SEG_PAD)
        store_segment(dk_ref, starts[s], rows_padded, key_all[place])
        store_segment(dv_ref, starts[s], rows_padded, value_all[place])


def attend_back(qkv, out, grad, share, me, mp_count, rows_padded):
    rows, width = qkv.shape
    pairs = width // 3 // 128
    column = pl.BlockSpec((rows, 128), lambda n, me_ref: (0, n))
    piece = jax.ShapeDtypeStruct((rows, width // 3), bf16)
    return pl.pallas_call(
        functools.partial(attend_back_kernel, mp_count, rows_padded),
        out_shape=(piece, piece, piece),
        grid_spec=pltpu.PrefetchScalarGridSpec(
            num_scalar_prefetch=1,
            grid=(pairs,),
            in_specs=[
                column,
                pl.BlockSpec((rows, 128), lambda n, me_ref: (0, pairs + n)),
                pl.BlockSpec((rows, 128), lambda n, me_ref: (0, 2 * pairs + n)),
                column,
                column,
                pl.BlockSpec((2, rows, KEYS), lambda n, me_ref: (n, 0, 0)),
            ],
            out_specs=(column, column, column),
            scratch_shapes=[pltpu.VMEM((128, rows), f32), pltpu.VMEM((128, rows), f32)],
        ),
        compiler_params=pltpu.CompilerParams(vmem_limit_bytes=48 * 2**20),
        name="attend_back",
    )(me, qkv, qkv, qkv, out, grad, share)


def item_rows(present, summary, parts, rows, rows_padded):
    kept = present[:, None] * jnp.concatenate([jnp.ones((NSEG, SEG), jnp.int32), summary], axis=1)
    group = parts // NSEG
    kept = jnp.pad(kept.reshape(NSEG, group, rows), ((0, 0), (0, 0), (0, rows_padded - rows)))
    flags = np.zeros((group, rows_padded), np.int32)
    flags[:, :rows] = (np.arange(PERIOD) >= SEG).reshape(group, rows)
    return kept.reshape(NSEG, group * rows_padded), flags.reshape(group * rows_padded)


def score_bias(kept, flags):
    slab = (kept * flags[None, :])[:, SEG_PAD - SLAB :] == 1
    causal = np.tril(np.ones((SEG_PAD, SEG_PAD), bool))
    itself = np.eye(SEG_PAD, dtype=bool)
    planes = []
    for s in range(NSEG):
        own = (kept[s][None, :] == 1) & causal | itself
        pieces = [jnp.broadcast_to(slab[e][None, :], (SEG_PAD, SLAB)) for e in range(s)] + [own]
        seen = jnp.concatenate(pieces, axis=1)
        planes.append(jnp.pad(seen, ((0, 0), (0, KEYS - seen.shape[1]))))
    return jnp.where(jnp.stack(planes), 0.0, -1e30).astype(f32)


def norm_parts(value):
    center = value - jnp.mean(value, axis=-1, keepdims=True)
    spread = jnp.mean(center * center, axis=-1, keepdims=True)
    scale = lax.rsqrt(spread + norm_eps)
    return center * scale, scale


def norm_back(normed, scale, gain, grad):
    inner = grad * gain
    return scale * (
        inner
        - jnp.mean(inner, axis=-1, keepdims=True)
        - normed * jnp.mean(inner * normed, axis=-1, keepdims=True)
    )


def gelu_both(value):
    c = 0.7978845608028654
    square = value * value
    bend = jnp.tanh(c * (value + 0.044715 * value * square))
    half = 0.5 * (1.0 + bend)
    slope = half + 0.5 * value * (1.0 - bend * bend) * c * (1.0 + 3.0 * 0.044715 * square)
    return value * half, slope


def adam_step(master, grad, first, second, average, factor, rate, decay):
    clipped = grad * factor
    first_new = beta_first * first + (1.0 - beta_first) * clipped
    second_new = beta_second * second + (1.0 - beta_second) * clipped * clipped
    first_hat = first_new / (1.0 - beta_first**STEP)
    second_hat = second_new / (1.0 - beta_second**STEP)
    master_new = master - rate * (first_hat / (jnp.sqrt(second_hat) + adam_eps) + decay * master)
    average_new = average_keep * average + (1.0 - average_keep) * master_new
    return (master_new, first_new, second_new, average_new, master_new.astype(bf16))


def dot_nn(left, right):
    return jnp.dot(left, right, preferred_element_type=f32)


def dot_nt(left, right):
    return lax.dot_general(left, right, (((1,), (1,)), ((), ())), preferred_element_type=f32)


def dot_tn(left, right):
    return lax.dot_general(left, right, (((0,), (0,)), ((), ())), preferred_element_type=f32)


def per_device(
    tokens,
    cotangent,
    present,
    summary_mask,
    attention_weight,
    attention_first,
    attention_second,
    attention_average,
    hidden_weight,
    hidden_first,
    hidden_second,
    hidden_average,
    norm_params,
    norm_first,
    norm_second,
    norm_average,
    head_bias,
    head_first,
    head_second,
    head_average,
    unit_bias,
    unit_first,
    unit_second,
    unit_average,
):
    outer, inner = seq_grid()
    seqs = outer * inner
    parts = lax.axis_size("mp")
    rows = tokens.shape[0]
    rows_padded = SEG_PAD * NSEG // parts
    head_width = attention_weight.shape[2]
    depth = attention_weight.shape[1]
    me = lax.axis_index("mp")
    me_vector = me.astype(jnp.int32)[None]
    order = feature_order()
    codes = row_codes()

    inputs_own = to_blocks(tokens, order, rows_padded)
    cotangent_own = to_blocks(cotangent, order, rows_padded)
    inputs_all = gather_rows(inputs_own)
    cotangent_all = gather_rows(cotangent_own)

    attn_own = jnp.concatenate([attention_weight[n] for n in range(4)], axis=1).astype(bf16)
    attn_full = gather_weight(attn_own)
    up_full = gather_weight(hidden_weight[0].astype(bf16))
    down_full = gather_weight(hidden_weight[1].astype(bf16))
    qkv_full = attn_full[:, : 3 * head_width]
    out_full = attn_full[:, 3 * head_width :]

    packed = jnp.concatenate(
        [norm_params.reshape(-1), head_bias.reshape(-1), unit_bias]
    ).astype(bf16)
    packed = lax.all_gather(packed, "seq", axis=0, tiled=False).astype(f32)
    norm_size, head_size = norm_params.size, head_bias.size
    norm_vals = jnp.take(packed[:, :norm_size], order, axis=0).reshape(seqs, 6, depth)
    norm_vals = norm_vals.transpose(1, 0, 2).reshape(6, D)
    head_vals = packed[:, norm_size : norm_size + head_size].reshape(seqs, 2, head_width // seqs)
    head_vals = head_vals.transpose(1, 0, 2).reshape(2, head_width)
    unit_vals = packed[:, norm_size + head_size :].reshape(-1)

    kept, flags = item_rows(present[0], summary_mask[0], parts, rows, rows_padded)
    bias = score_bias(kept, flags)
    kept_parts = kept.reshape(parts, rows_padded).astype(f32)
    kept_all = jnp.take(kept_parts, jnp.stack([me ^ code for code in codes]), axis=0).reshape(-1, 1)
    kept_own = kept_all[:rows_padded]

    normed_all = norm_parts(inputs_all.astype(f32))[0]
    first_all = (normed_all * norm_vals[0] + norm_vals[1]).astype(bf16)
    qkv_bias = jnp.concatenate([head_vals[0], jnp.zeros_like(head_vals[0]), head_vals[1]])
    qkv_scale = np.concatenate(
        [np.full(head_width, score_scale, np.float32), np.ones(2 * head_width, np.float32)]
    )
    qkv = ((dot_nn(first_all, qkv_full) + qkv_bias).astype(bf16) * qkv_scale.astype(bf16))
    context, share = attend(qkv, bias, me_vector, parts, rows_padded)
    attended = scatter_rows(dot_nt(context, out_full).astype(bf16)) + norm_vals[4]
    inputs = inputs_own.astype(f32)
    middle = inputs + kept_own * attended

    normed_two, scale_two = norm_parts(middle)
    second_own = (normed_two * norm_vals[2] + norm_vals[3]).astype(bf16)
    second_all = gather_rows(second_own)
    pre_act = dot_nn(second_all, up_full) + unit_vals
    activated, slope = gelu_both(pre_act)
    activated, slope = activated.astype(bf16), slope.astype(bf16)
    feed_out = scatter_rows(dot_nt(activated, down_full).astype(bf16)) + norm_vals[5]
    block_output = from_blocks(middle + kept_own * feed_out, order, rows)

    out_grad = cotangent_own.astype(f32)
    feed_grad = (cotangent_all.astype(f32) * kept_all).astype(bf16)
    down_bias_grad = jnp.sum(kept_own * out_grad, axis=0)

    def columns(value, j, i):
        place = j * outer + i
        return value[:, place * depth : (place + 1) * depth]

    down_grad = scatter_weight(lambda j, i: dot_tn(columns(feed_grad, j, i), activated))
    pre_grad = (dot_nn(feed_grad, down_full) * slope.astype(f32)).astype(bf16)
    unit_grad = jnp.sum(pre_grad, axis=0, dtype=f32)
    second_grad = scatter_rows(dot_nt(pre_grad, up_full).astype(bf16))
    up_grad = scatter_weight(lambda j, i: dot_tn(columns(second_all, j, i), pre_grad))
    gain_two_grad = jnp.sum(second_grad * normed_two, axis=0)
    shift_two_grad = jnp.sum(second_grad, axis=0)
    middle_grad = out_grad + norm_back(normed_two, scale_two, norm_vals[2], second_grad)

    attn_grad = kept_own * middle_grad
    out_bias_grad = jnp.sum(attn_grad, axis=0)
    attn_rows = gather_rows(attn_grad.astype(bf16))
    context_grad = dot_nn(attn_rows, out_full).astype(bf16)
    out_proj_grad = scatter_weight(lambda j, i: dot_tn(columns(attn_rows, j, i), context))
    query_grad, key_grad, value_grad = attend_back(
        qkv, context, context_grad, share, me_vector, parts, rows_padded
    )
    qkv_grad = jnp.concatenate([query_grad, key_grad, value_grad], axis=1)
    head_grad = jnp.stack(
        [jnp.sum(query_grad, axis=0, dtype=f32), jnp.sum(value_grad, axis=0, dtype=f32)]
    )
    first_grad = scatter_rows(dot_nt(qkv_grad, qkv_full).astype(bf16))
    proj_grad = scatter_weight(lambda j, i: dot_tn(columns(first_all, j, i), qkv_grad))
    normed_one, scale_one = norm_parts(inputs)
    gain_one_grad = jnp.sum(first_grad * normed_one, axis=0)
    shift_one_grad = jnp.sum(first_grad, axis=0)
    input_grad = from_blocks(
        middle_grad + norm_back(normed_one, scale_one, norm_vals[0], first_grad), order, rows
    )

    vector_grad = jnp.stack(
        [
            gain_one_grad,
            shift_one_grad,
            gain_two_grad,
            shift_two_grad,
            out_bias_grad,
            down_bias_grad,
        ]
    )
    back_order = jnp.argsort(order)
    vector_grad = jnp.take(
        vector_grad.reshape(6, seqs, depth).transpose(1, 0, 2).reshape(seqs, -1), back_order, axis=0
    )
    vectors = jnp.concatenate(
        [
            vector_grad,
            head_grad.reshape(2, seqs, -1).transpose(1, 0, 2).reshape(seqs, -1),
            unit_grad.reshape(seqs, -1),
        ],
        axis=1,
    )
    vectors = lax.psum_scatter(vectors, "seq", scatter_dimension=0, tiled=False)
    norm_shard = lax.psum(vectors[:norm_size], "mp").reshape(norm_params.shape)
    head_shard = vectors[norm_size : norm_size + head_size].reshape(head_bias.shape)
    unit_shard = vectors[norm_size + head_size :]

    proj_grad = proj_grad.reshape(depth, 3, head_width).transpose(1, 0, 2)
    attn_shard = jnp.concatenate([proj_grad, out_proj_grad[None]], axis=0)
    hidden_shard = jnp.stack([up_grad, down_grad])
    leader = (me == 0).astype(f32)
    local_squares = (
        jnp.sum(attn_shard * attn_shard)
        + jnp.sum(hidden_shard * hidden_shard)
        + jnp.sum(head_shard * head_shard)
        + jnp.sum(unit_shard * unit_shard)
        + leader * jnp.sum(norm_shard * norm_shard)
    )
    grad_norm = jnp.sqrt(lax.psum(local_squares, ("seq", "mp")))
    factor = jnp.minimum(1.0, clip_limit / (grad_norm + 1e-06))
    hidden_rate = jnp.array([D ** (-0.5), FF ** (-0.5)], f32)[:, None, None]
    attention_out = adam_step(
        attention_weight,
        attn_shard,
        attention_first,
        attention_second,
        attention_average,
        factor,
        D ** (-0.5),
        weight_decay,
    )
    hidden_out = adam_step(
        hidden_weight,
        hidden_shard,
        hidden_first,
        hidden_second,
        hidden_average,
        factor,
        hidden_rate,
        weight_decay,
    )
    norm_out = adam_step(
        norm_params, norm_shard, norm_first, norm_second, norm_average, factor, vector_rate, 0.0
    )
    head_out = adam_step(
        head_bias, head_shard, head_first, head_second, head_average, factor, vector_rate, 0.0
    )
    unit_out = adam_step(
        unit_bias, unit_shard, unit_first, unit_second, unit_average, factor, vector_rate, 0.0
    )
    return (
        block_output,
        input_grad,
        grad_norm,
        *attention_out,
        *hidden_out,
        *norm_out,
        *head_out,
        *unit_out,
    )


def solution(mesh):
    token_spec = P(("seq", "mp"), None)
    weight_spec = P(None, "seq", "mp")
    norm_spec = P(None, "seq")
    head_spec = P(None, ("mp", "seq"))
    unit_spec = P(("mp", "seq"))
    return jax.shard_map(
        per_device,
        mesh=mesh,
        in_specs=(
            token_spec,
            token_spec,
            P("seq", None),
            P("seq", None, None),
            *([weight_spec] * 8),
            *([norm_spec] * 4),
            *([head_spec] * 4),
            *([unit_spec] * 4),
        ),
        out_specs=(
            token_spec,
            token_spec,
            P(),
            *([weight_spec] * 10),
            *([norm_spec] * 5),
            *([head_spec] * 5),
            *([unit_spec] * 5),
        ),
        check_vma=False,
    )
```

time: 1960 us -> 1090 us (0.56)
  waiting for transfers between devices: 963 us -> 431 us
  blocking collectives: 343 us -> 126 us
  matrix products: 331 us -> 193 us
  Pallas kernels: 0 us -> 84.3 us
  starting transfers between devices: 7.87 us -> 56.9 us
  other arithmetic: 161 us -> 112 us
  local copies, waits for them, and re-layouts: 121 us -> 72.4 us
    psum x1 -> x0, waiting for transfers between devices: 543 us -> none  [per_device(): lax.psum(grad_attention.astype(jnp.bfloat16), 'seq').astype(jnp.float32)]
    ppermute x0 -> x69, waiting for transfers between devices: none -> 431 us  [the longest x28 225 us: shift_inner(): return lax.ppermute(value, 'seq', pairs)]
    all_gather x6 -> x0, waiting for transfers between devices: 419 us -> none  [the longest x1 224 us: per_device(): lax.all_gather(hidden_weight.astype(jnp.bfloat16), 'seq', axis=1, tiled=T...]
    unnamed x3 -> x1, blocking collectives: 187 us -> 33.9 us
    dot_general x26 -> x40, matrix products: 331 us -> 193 us  [the longest x32 81.6 us: dot_tn(): lax.dot_general(left, right, (((0,), (0,)), ((), ())), preferred_element_...]
    pallas_call x0 -> x6, Pallas kernels: none -> 84.3 us  [the longest x1 36.4 us: attend(): pl.pallas_call(functools.partial(attend_kernel, mp_count, rows_padded), o...]
    ppermute x0 -> x69, starting transfers between devices: none -> 56.9 us  [the longest x21 29.4 us: shift_outer(): return lax.ppermute(value, 'seq', pairs)]
    convert_element_type x17 -> x11, other arithmetic: 76.2 us -> 36.1 us  [the longest x5 18.1 us: adam_step(): master_new.astype(bf16)]
  transfers between devices with their start and end apart: 11 -> 69, of which waited for: 9 -> 32; matrix products, arithmetic and copies ran while one was open for 11% -> 16% of each run, Pallas kernels for 0% -> 1%
where the time goes in v1:
time: 1090 us; the launch traced here: 1080 us
  waiting for transfers between devices  431 us (40%)
  matrix products  193 us (18%)
  blocking collectives  126 us (12%)
  other arithmetic  112 us (10%)
  Pallas kernels  84.3 us (8%)
  local copies, waits for them, and re-layouts  72.4 us (7%)
  starting transfers between devices  56.9 us (5%)
    ppermute x28, waiting for transfers between devices, shift_inner(): return lax.ppermute(value, 'seq', pairs)  225 us
    ppermute x21, waiting for transfers between devices, shift_outer(): return lax.ppermute(value, 'seq', pairs)  170 us
    dot_general x32, matrix products, dot_tn(): lax.dot_general(left, right, (((0,), (0,)), ((), ())), preferred_element_...  81.6 us
    dot_general x4, matrix products, dot_nn(): return jnp.dot(left, right, preferred_element_type=f32)  61 us
    unnamed x252, local copies, waits for them, and re-layouts  52.6 us
    dot_general x4, matrix products, dot_nt(): lax.dot_general(left, right, (((1,), (1,)), ((), ())), preferred_element_...  50.6 us
    all_gather x1, blocking collectives, per_device(): packed = lax.all_gather(packed, 'seq', axis=0, tiled=False).astype(f32)  49 us
    psum x1, blocking collectives, per_device(): grad_norm = jnp.sqrt(lax.psum(local_squares, ('seq', 'mp')))  37 us
  transfers between devices with their start and end apart: 69, of which 32 were waited for; matrix products, arithmetic and copies ran while one was open for 16% of the time, Pallas kernels for 1%

profile of v1, /device:TPU:0, one launch (start us, length us, event | category | flops | bytes accessed | tf_op | source)
XLA Modules:
  0.0 1083.9 jit_solution(6196330174822230938)
XLA Ops:
  1.4 6.0 to_blocks.2
  17.2 49.0 %all-gather = bf16[8,1,1920]{2,1,0:T(2,128)(2,1)S(1)} all-gather(bf16[1,1,1920]{2,1,0:T(2,128)(2,1)S(1)} %maximum_bitcast_fusion.1), channel_id=1, replica_groups=mesh['seq'=8,'mp'=4] {'seq'}, dimensions={0}, use_global_device_ids=true | all-gather | bytes 34560 | tf_op jit(solution)/shard_map/all_gather | solution.py:509
  72.2 19.0 %collective-permute-done.4 = bf16[256,2048]{1,0:T(8,128)(2,1)} collective-permute-done((bf16[256,2048]{1,0:T(8,128)(2,1)}, bf16[256,2048]{1,0:T(8,128)(2,1)}, u32[]{:S(2)}, u32[]{:S(2)}) %collective-permute-start.4) | collective-permute-done | bytes 1048608 | tf_op jit(solution)/shard_map/ppermute | solution.py:49
  97.6 5.5 fusion.2
  103.1 9.2 collective-permute-done.5
  112.2 5.2 fusion.5
  120.5 20.1 %collective-permute-done.9 = bf16[256,2048]{1,0:T(8,128)(2,1)S(1)} collective-permute-done((bf16[256,2048]{1,0:T(8,128)(2,1)S(1)}, bf16[256,2048]{1,0:T(8,128)(2,1)S(1)}, u32[]{:S(2)}, u32[]{:S(2)}) %collective-permute-start.9) | collective-permute-done | bytes 1048608 | tf_op jit(solution)/shard_map/ppermute | solution.py:57
  140.7 10.0 fusion.7.q_ref.k_ref.v_ref
  150.6 36.4 %attend.1 = (bf16[1280,512]{1,0:T(8,128)(2,1)S(1)}, bf16[8,1280,512]{2,1,0:T(8,128)(2,1)}) custom-call(s32[1]{0:T(128)} %bitcast.8.me_ref, bf16[1280,1536]{1,0:T(8,128)(2,1)} %fusion.7.q_ref.k_ref.v_ref, bf16[1280,1536]{1,0:T(8,128)(2,1)} %fusion.7.q_ref.k_ref.v_ref, bf16[1280,1536]{1,0:T(8,128)(2,1)} %fusion.7.q_ref.k_ref.v_ref, ...), custom_call_target="tpu_custom_call" | custom-call | tf_op jit(solution)/shard_map/attend/pallas_call | solution.py:250
  187.0 5.2 convolution_convert_fusion
  202.6 6.0 to_blocks.3
  212.6 14.6 %collective-permute-done.15 = bf16[256,2048]{1,0:T(8,128)(2,1)} collective-permute-done((bf16[256,2048]{1,0:T(8,128)(2,1)}, bf16[256,2048]{1,0:T(8,128)(2,1)}, u32[]{:S(2)}, u32[]{:S(2)}) %collective-permute-start.15) | collective-permute-done | bytes 1048608 | tf_op jit(solution)/shard_map/ppermute | solution.py:49
  227.2 22.5 %collective-permute-done.22 = bf16[256,2048]{1,0:T(8,128)(2,1)} collective-permute-done((bf16[256,2048]{1,0:T(8,128)(2,1)}, bf16[256,2048]{1,0:T(8,128)(2,1)}, u32[]{:S(2)}, u32[]{:S(2)}) %collective-permute-start.22) | collective-permute-done | bytes 1048608 | tf_op jit(solution)/shard_map/ppermute | solution.py:49
  255.9 16.1 %collective-permute-done.16 = bf16[256,2048]{1,0:T(8,128)(2,1)S(1)} collective-permute-done((bf16[256,2048]{1,0:T(8,128)(2,1)}, bf16[256,2048]{1,0:T(8,128)(2,1)S(1)}, u32[]{:S(2)}, u32[]{:S(2)}) %collective-permute-start.16) | collective-permute-done | bytes 1048608 | tf_op jit(solution)/shard_map/ppermute | solution.py:49
  272.5 18.8 %collective-permute-done.23 = bf16[256,2048]{1,0:T(8,128)(2,1)S(1)} collective-permute-done((bf16[256,2048]{1,0:T(8,128)(2,1)}, bf16[256,2048]{1,0:T(8,128)(2,1)S(1)}, u32[]{:S(2)}, u32[]{:S(2)}) %collective-permute-start.23) | collective-permute-done | bytes 1048608 | tf_op jit(solution)/shard_map/ppermute | solution.py:49
  298.0 21.2 %collective-permute-done.17 = bf16[256,2048]{1,0:T(8,128)(2,1)S(1)} collective-permute-done((bf16[256,2048]{1,0:T(8,128)(2,1)S(1)}, bf16[256,2048]{1,0:T(8,128)(2,1)S(1)}, u32[]{:S(2)}, u32[]{:S(2)}) %collective-permute-start.17) | collective-permute-done | bytes 1048608 | tf_op jit(solution)/shard_map/ppermute | solution.py:49
  319.8 10.8 multiply_convert_fusion.1
  336.6 4.8 collective-permute-done.24
  343.6 21.9 %collective-permute-done.20 = bf16[256,2048]{1,0:T(8,128)(2,1)S(1)} collective-permute-done((bf16[256,2048]{1,0:T(8,128)(2,1)S(1)}, bf16[256,2048]{1,0:T(8,128)(2,1)S(1)}, u32[]{:S(2)}, u32[]{:S(2)}) %collective-permute-start.20) | collective-permute-done | bytes 1048608 | tf_op jit(solution)/shard_map/ppermute | solution.py:57
  367.3 20.7 %collective-permute-done.27 = bf16[256,2048]{1,0:T(8,128)(2,1)S(1)} collective-permute-done((bf16[256,2048]{1,0:T(8,128)(2,1)S(1)}, bf16[256,2048]{1,0:T(8,128)(2,1)S(1)}, u32[]{:S(2)}, u32[]{:S(2)}) %collective-permute-start.27) | collective-permute-done | bytes 1048608 | tf_op jit(solution)/shard_map/ppermute | solution.py:57
  388.1 22.4 %collective-permute-done.21 = bf16[256,2048]{1,0:T(8,128)(2,1)S(1)} collective-permute-done((bf16[256,2048]{1,0:T(8,128)(2,1)S(1)}, bf16[256,2048]{1,0:T(8,128)(2,1)S(1)}, u32[]{:S(2)}, u32[]{:S(2)}) %collective-permute-start.21) | collective-permute-done | bytes 1048608 | tf_op jit(solution)/shard_map/ppermute | solution.py:57
  411.6 21.0 %collective-permute-done.28 = bf16[256,2048]{1,0:T(8,128)(2,1)S(1)} collective-permute-done((bf16[256,2048]{1,0:T(8,128)(2,1)S(1)}, bf16[256,2048]{1,0:T(8,128)(2,1)S(1)}, u32[]{:S(2)}, u32[]{:S(2)}) %collective-permute-start.28) | collective-permute-done | bytes 1048608 | tf_op jit(solution)/shard_map/ppermute | solution.py:57
  437.5 21.2 %multiply_convert_fusion.2 = (bf16[1280,2048]{1,0:T(8,128)(2,1)S(1)}, f32[1280,2048]{1,0:T(8,128)}) fusion(f32[2048]{0:T(1024)S(1)} %bitcast.181, bf16[2048,2048]{1,0:T(8,128)(2,1)} %constant_dynamic-update-slice_fusion.8, bf16[320,2048]{1,0:T(8,128)(2,1)} %copy-done.39, bf16[320,2048]{1,0:T(8,128)(2,1)} %copy-done.37, bf16[320,2048]{1,0:T(8,128)(2,1)} %copy-done.35, ...), kind=kOutput, calls=%fused_computation.15 | convolution fusion | flops 10784604160 | bytes 29368320 | tf_op jit(solution)/shard_map/dot_general | solution.py:445
  458.7 22.5 %convert_reduce_fusion.1 = (f32[2048]{0:T(1024)S(1)}, bf16[1280,2048]{1,0:T(8,128)(2,1)S(1)}) fusion(f32[1280,2048]{1,0:T(8,128)} %get-tuple-element.164, f32[2048]{0:T(1024)S(1)} %bitcast.182, bf16[1280,2048]{1,0:T(8,128)(2,1)S(1)} %multiply_convert_fusion.1, bf16[2048,2048]{1,0:T(8,128)(2,1)} %copy-done.46), kind=kOutput, calls=%fused_computation.11 | convolution fusion | flops 10797709312 | bytes 29376512 | tf_op jit(solution)/shard_map/dot_general | solution.py:445
  481.2 17.3 %convolution_convert_fusion.2 = bf16[1280,2048]{1,0:T(8,128)(2,1)} fusion(bf16[1280,2048]{1,0:T(8,128)(2,1)S(1)} %get-tuple-element.166, bf16[2048,2048]{1,0:T(8,128)(2,1)} %constant_dynamic-update-slice_fusion.8), kind=kOutput, calls=%fused_computation.23 | convolution fusion | flops 10740039680 | bytes 18874368 | tf_op jit(solution)/shard_map/dot_general | solution.py:449
  498.6 10.4 pad_maximum_fusion.1
  519.3 15.4 %convolution_convert_fusion.3 = bf16[1280,2048]{1,0:T(8,128)(2,1)} fusion(bf16[1280,2048]{1,0:T(8,128)(2,1)S(1)} %get-tuple-element.163, bf16[2048,2048]{1,0:T(8,128)(2,1)} %copy-done.46), kind=kOutput, calls=%fused_computation.24 | convolution fusion | flops 10740039680 | bytes 18874368 | tf_op jit(solution)/shard_map/dot_general | solution.py:449
  550.5 14.2 %collective-permute-done.58 = bf16[256,2048]{1,0:T(8,128)(2,1)S(1)} collective-permute-done((bf16[256,2048]{1,0:T(8,128)(2,1)}, bf16[256,2048]{1,0:T(8,128)(2,1)S(1)}, u32[]{:S(2)}, u32[]{:S(2)}) %collective-permute-start.58) | collective-permute-done | bytes 1048608 | tf_op jit(solution)/shard_map/ppermute | solution.py:57
  567.8 19.4 %collective-permute-done.65 = bf16[256,2048]{1,0:T(8,128)(2,1)S(1)} collective-permute-done((bf16[256,2048]{1,0:T(8,128)(2,1)S(1)}, bf16[256,2048]{1,0:T(8,128)(2,1)S(1)}, u32[]{:S(2)}, u32[]{:S(2)}) %collective-permute-start.65) | collective-permute-done | bytes 1048608 | tf_op jit(solution)/shard_map/ppermute | solution.py:57
  587.2 3.5 collective-permute-start.59
  599.2 33.0 %collective-permute-done.57 = bf16[256,2048]{1,0:T(8,128)(2,1)} collective-permute-done((bf16[256,2048]{1,0:T(8,128)(2,1)}, bf16[256,2048]{1,0:T(8,128)(2,1)}, u32[]{:S(2)}, u32[]{:S(2)}) %collective-permute-start.57) | collective-permute-done | bytes 1048608 | tf_op jit(solution)/shard_map/ppermute | solution.py:57
  632.2 3.7 collective-permute-start.66
  636.4 4.2 fusion.34
  644.2 10.5 collective-permute-done.64
  658.6 4.2 add_convert_fusion.3
  662.8 5.1 collective-permute-done.35
  670.7 23.2 %collective-permute-done.30 = bf16[320,2048]{1,0:T(8,128)(2,1)S(1)} collective-permute-done((bf16[320,2048]{1,0:T(8,128)(2,1)S(1)}, bf16[320,2048]{1,0:T(8,128)(2,1)S(1)}, u32[]{:S(2)}, u32[]{:S(2)}) %collective-permute-start.30) | collective-permute-done | bytes 1310752 | tf_op jit(solution)/shard_map/ppermute | solution.py:61
  695.0 5.5 fusion.22
  703.0 4.2 fusion.33
  707.6 12.8 %collective-permute-done.67 = bf16[256,2048]{1,0:T(8,128)(2,1)} collective-permute-done((bf16[256,2048]{1,0:T(8,128)(2,1)}, bf16[256,2048]{1,0:T(8,128)(2,1)}, u32[]{:S(2)}, u32[]{:S(2)}) %collective-permute-start.67) | collective-permute-done | bytes 1048608 | tf_op jit(solution)/shard_map/ppermute | solution.py:49
  720.3 4.2 add_convert_fusion.2
  737.7 5.1 collective-permute-done.61
  742.8 4.8 fusion.31
  747.7 14.7 %collective-permute-done.68 = bf16[256,2048]{1,0:T(8,128)(2,1)S(1)} collective-permute-done((bf16[256,2048]{1,0:T(8,128)(2,1)}, bf16[256,2048]{1,0:T(8,128)(2,1)S(1)}, u32[]{:S(2)}, u32[]{:S(2)}) %collective-permute-start.68) | collective-permute-done | bytes 1048608 | tf_op jit(solution)/shard_map/ppermute | solution.py:49
  770.2 7.3 convolution_convert_fusion.4.g_ref
  777.5 23.3 %attend_back.1 = (bf16[1280,512]{1,0:T(8,128)(2,1)S(1)}, bf16[1280,512]{1,0:T(8,128)(2,1)S(1)}, bf16[1280,512]{1,0:T(8,128)(2,1)S(1)}) custom-call(s32[1]{0:T(128)} %bitcast.8.me_ref, bf16[1280,1536]{1,0:T(8,128)(2,1)} %fusion.7.q_ref.k_ref.v_ref, bf16[1280,1536]{1,0:T(8,128)(2,1)} %fusion.7.q_ref.k_ref.v_ref, bf16[1280,1536]{1,0:T(8,128)(2,1)} %fusion.7.q_ref.k_ref.v_ref, ...), custom_call_target="tpu_custom_call" | custom-call | tf_op jit(solution)/shard_map/attend_back/pallas_call | solution.py:364
  801.2 12.6 %convolution_convert_fusion.1 = bf16[1280,2048]{1,0:T(8,128)(2,1)S(1)} fusion(bf16[1280,1536]{1,0:T(8,128)(2,1)S(1)} %constant_dynamic-update-slice_fusion.24, bf16[2048,2048]{1,0:T(8,128)(2,1)} %copy-done.45), kind=kOutput, calls=%fused_computation.22 | convolution fusion | flops 8055685120 | bytes 15466496 | tf_op jit(solution)/shard_map/dot_general | solution.py:449
  826.6 10.9 %collective-permute-done.44 = bf16[256,1536]{1,0:T(8,128)(2,1)S(1)} collective-permute-done((bf16[256,1536]{1,0:T(8,128)(2,1)S(1)}, bf16[256,1536]{1,0:T(8,128)(2,1)S(1)}, u32[]{:S(2)}, u32[]{:S(2)}) %collective-permute-start.44) | collective-permute-done | bytes 786464 | tf_op jit(solution)/shard_map/ppermute | solution.py:57
  846.1 4.6 convolution_convert_fusion.8
  850.6 3.9 collective-permute-done.43
  860.4 18.3 %collective-permute-done.51 = bf16[256,512]{1,0:T(8,128)(2,1)S(1)} collective-permute-done((bf16[256,512]{1,0:T(8,128)(2,1)S(1)}, bf16[256,512]{1,0:T(8,128)(2,1)S(1)}, u32[]{:S(2)}, u32[]{:S(2)}) %collective-permute-start.51) | collective-permute-done | bytes 262176 | tf_op jit(solution)/shard_map/ppermute | solution.py:57
  888.7 4.4 collective-permute-start.53
  902.7 7.3 collective-permute-done.49
  911.9 5.8 collective-permute-done.54
  919.6 5.3 convert_add_fusion.6
  929.3 7.2 collective-permute-done.40
  940.8 33.9 %all-reduce.5 = f32[8,1920]{1,0:T(8,128)S(1)} all-reduce(f32[8,1920]{1,0:T(8,128)S(1)} %pad_maximum_fusion.6), channel_id=2, replica_groups=mesh['seq'=8,'mp'=4] {'seq'}, use_global_device_ids=true, to_apply=%region_22.24.clone | all-reduce | flops 15360 | bytes 122880
  975.4 6.0 psum.14
  986.6 6.2 from_blocks.2
  992.9 37.0 %psum.15 = f32[]{:T(128)} all-reduce(f32[]{:T(128)S(6)} %add.538), channel_id=1, replica_groups=mesh['seq'=8,'mp'=4] {'seq','mp'}, use_global_device_ids=true, to_apply=%region_27.29 | all-reduce | flops 1 | bytes 8 | tf_op jit(solution)/shard_map/psum | solution.py:620
  1032.2 7.0 fusion.118
  1054.4 5.5 fusion.19.in_ref
  1059.9 6.4 from_blocks.3
  1069.8 9.3 fusion.116
  (517 shorter events, 228.3 us)
Async XLA Ops:
  7.5 60.9 %collective-permute-start = (bf16[320,2048]{1,0:T(8,128)(2,1)}, bf16[320,2048]{1,0:T(8,128)(2,1)S(1)}, u32[]{:S(2)}, u32[]{:S(2)}) collective-permute-start(bf16[320,2048]{1,0:T(8,128)(2,1)} %to_blocks.2), channel_id=1, source_target_pairs={{0,2},{1,3},{2,0},{3,1},{4,6},{5,7},{6,4},{7,5},{8,10},{9,11},{10,... | collective-permute-start | bytes 3932168 | tf_op jit(solution)/shard_map/ppermute | solution.py:61
  10.5 83.6 %collective-permute-start.1 = (bf16[320,2048]{1,0:T(8,128)(2,1)}, bf16[320,2048]{1,0:T(8,128)(2,1)}, u32[]{:S(2)}, u32[]{:S(2)}) collective-permute-start(bf16[320,2048]{1,0:T(8,128)(2,1)} %to_blocks.2), channel_id=1, source_target_pairs={{0,1},{1,0},{2,3},{3,2},{4,5},{5,4},{6,7},{7,6},{8,9},{9,8},{10,11... | collective-permute-start | bytes 3932168 | tf_op jit(solution)/shard_map/ppermute | solution.py:61
  13.9 54.4 %collective-permute-start.3 = (bf16[256,2048]{1,0:T(8,128)(2,1)}, bf16[256,2048]{1,0:T(8,128)(2,1)}, u32[]{:S(2)}, u32[]{:S(2)}) collective-permute-start(bf16[256,2048]{1,0:T(8,128)(2,1)} %get-tuple-element.142), channel_id=1, source_target_pairs={{0,8},{4,12},{8,16},{12,20},{16,24},{20,28},{24,0},{28,4},{1,9},{5... | collective-permute-start | bytes 3145736 | tf_op jit(solution)/shard_map/ppermute | solution.py:49
  15.5 102.1 %collective-permute-start.6 = (bf16[256,2048]{1,0:T(8,128)(2,1)}, bf16[256,2048]{1,0:T(8,128)(2,1)}, u32[]{:S(2)}, u32[]{:S(2)}) collective-permute-start(bf16[256,2048]{1,0:T(8,128)(2,1)} %get-tuple-element.142), channel_id=1, source_target_pairs={{0,4},{4,0},{8,12},{12,8},{16,20},{20,16},{24,28},{28,24},{1,5},{5... | collective-permute-start | bytes 3145736 | tf_op jit(solution)/shard_map/ppermute | solution.py:57
  68.3 22.9 %collective-permute-start.4 = (bf16[256,2048]{1,0:T(8,128)(2,1)}, bf16[256,2048]{1,0:T(8,128)(2,1)}, u32[]{:S(2)}, u32[]{:S(2)}) collective-permute-start(bf16[256,2048]{1,0:T(8,128)(2,1)} %collective-permute-done.3), channel_id=1, source_target_pairs={{0,8},{4,12},{8,16},{12,20},{16,24},{20,28},{24,0},{28,4},{1,9},{5... | collective-permute-start | bytes 3145736 | tf_op jit(solution)/shard_map/ppermute | solution.py:49
  68.4 25.7 %collective-permute-start.2 = (bf16[320,2048]{1,0:T(8,128)(2,1)S(1)}, bf16[320,2048]{1,0:T(8,128)(2,1)}, u32[]{:S(2)}, u32[]{:S(2)}) collective-permute-start(bf16[320,2048]{1,0:T(8,128)(2,1)S(1)} %collective-permute-done), channel_id=1, source_target_pairs={{0,1},{1,0},{2,3},{3,2},{4,5},{5,4},{6,7},{7,6},{8,9},{9,8},{10,11... | collective-permute-start | bytes 3932168 | tf_op jit(solution)/shard_map/ppermute | solution.py:61
  69.8 49.9 %collective-permute-start.7 = (bf16[256,2048]{1,0:T(8,128)(2,1)}, bf16[256,2048]{1,0:T(8,128)(2,1)S(1)}, u32[]{:S(2)}, u32[]{:S(2)}) collective-permute-start(bf16[256,2048]{1,0:T(8,128)(2,1)} %collective-permute-done.3), channel_id=1, source_target_pairs={{0,4},{4,0},{8,12},{12,8},{16,20},{20,16},{24,28},{28,24},{1,5},{5... | collective-permute-start | bytes 3145736 | tf_op jit(solution)/shard_map/ppermute | solution.py:57
  91.2 21.0 %collective-permute-start.5 = (bf16[256,2048]{1,0:T(8,128)(2,1)}, bf16[256,2048]{1,0:T(8,128)(2,1)S(1)}, u32[]{:S(2)}, u32[]{:S(2)}) collective-permute-start(bf16[256,2048]{1,0:T(8,128)(2,1)} %collective-permute-done.4), channel_id=1, source_target_pairs={{0,8},{4,12},{8,16},{12,20},{16,24},{20,28},{24,0},{28,4},{1,9},{5... | collective-permute-start | bytes 3145736 | tf_op jit(solution)/shard_map/ppermute | solution.py:49
  94.1 26.3 %collective-permute-start.8 = (bf16[256,2048]{1,0:T(8,128)(2,1)}, bf16[256,2048]{1,0:T(8,128)(2,1)S(1)}, u32[]{:S(2)}, u32[]{:S(2)}) collective-permute-start(bf16[256,2048]{1,0:T(8,128)(2,1)} %collective-permute-done.4), channel_id=1, source_target_pairs={{0,4},{4,0},{8,12},{12,8},{16,20},{20,16},{24,28},{28,24},{1,5},{5... | collective-permute-start | bytes 3145736 | tf_op jit(solution)/shard_map/ppermute | solution.py:57
  112.2 28.4 %collective-permute-start.9 = (bf16[256,2048]{1,0:T(8,128)(2,1)S(1)}, bf16[256,2048]{1,0:T(8,128)(2,1)S(1)}, u32[]{:S(2)}, u32[]{:S(2)}) collective-permute-start(bf16[256,2048]{1,0:T(8,128)(2,1)S(1)} %collective-permute-done.5), channel_id=1, source_target_pairs={{0,4},{4,0},{8,12},{12,8},{16,20},{20,16},{24,28},{28,24},{1,5},{5... | collective-permute-start | bytes 3145736 | tf_op jit(solution)/shard_map/ppermute | solution.py:57
  193.9 55.8 %collective-permute-start.10 = (bf16[640,2048]{1,0:T(8,128)(2,1)}, bf16[640,2048]{1,0:T(8,128)(2,1)}, u32[]{:S(2)}, u32[]{:S(2)}) collective-permute-start(bf16[640,2048]{1,0:T(8,128)(2,1)} %slice.372), channel_id=1, source_target_pairs={{0,1},{1,0},{2,3},{3,2},{4,5},{5,4},{6,7},{7,6},{8,9},{9,8},{10,11... | collective-permute-start | bytes 7864328 | tf_op jit(solution)/shard_map/ppermute | solution.py:61
  199.0 28.2 %collective-permute-start.15 = (bf16[256,2048]{1,0:T(8,128)(2,1)}, bf16[256,2048]{1,0:T(8,128)(2,1)}, u32[]{:S(2)}, u32[]{:S(2)}) collective-permute-start(bf16[256,2048]{1,0:T(8,128)(2,1)} %get-tuple-element.138), channel_id=1, source_target_pairs={{0,8},{4,12},{8,16},{12,20},{16,24},{20,28},{24,0},{28,4},{1,9},{5... | collective-permute-start | bytes 3145736 | tf_op jit(solution)/shard_map/ppermute | solution.py:49
  199.0 95.4 %collective-permute-start.18 = (bf16[256,2048]{1,0:T(8,128)(2,1)}, bf16[256,2048]{1,0:T(8,128)(2,1)}, u32[]{:S(2)}, u32[]{:S(2)}) collective-permute-start(bf16[256,2048]{1,0:T(8,128)(2,1)} %get-tuple-element.138), channel_id=1, source_target_pairs={{0,4},{4,0},{8,12},{12,8},{16,20},{20,16},{24,28},{28,24},{1,5},{5... | collective-permute-start | bytes 3145736 | tf_op jit(solution)/shard_map/ppermute | solution.py:57
  199.3 50.4 %collective-permute-start.22 = (bf16[256,2048]{1,0:T(8,128)(2,1)}, bf16[256,2048]{1,0:T(8,128)(2,1)}, u32[]{:S(2)}, u32[]{:S(2)}) collective-permute-start(bf16[256,2048]{1,0:T(8,128)(2,1)} %get-tuple-element.137), channel_id=1, source_target_pairs={{0,8},{4,12},{8,16},{12,20},{16,24},{20,28},{24,0},{28,4},{1,9},{5... | collective-permute-start | bytes 3145736 | tf_op jit(solution)/shard_map/ppermute | solution.py:49
  208.6 63.9 %collective-permute-start.31 = (bf16[320,2048]{1,0:T(8,128)(2,1)}, bf16[320,2048]{1,0:T(8,128)(2,1)}, u32[]{:S(2)}, u32[]{:S(2)}) collective-permute-start(bf16[320,2048]{1,0:T(8,128)(2,1)} %to_blocks.3), channel_id=1, source_target_pairs={{0,2},{1,3},{2,0},{3,1},{4,6},{5,7},{6,4},{7,5},{8,10},{9,11},{10,... | collective-permute-start | bytes 3932168 | tf_op jit(solution)/shard_map/ppermute | solution.py:61
  227.2 44.8 %collective-permute-start.16 = (bf16[256,2048]{1,0:T(8,128)(2,1)}, bf16[256,2048]{1,0:T(8,128)(2,1)S(1)}, u32[]{:S(2)}, u32[]{:S(2)}) collective-permute-start(bf16[256,2048]{1,0:T(8,128)(2,1)} %collective-permute-done.15), channel_id=1, source_target_pairs={{0,8},{4,12},{8,16},{12,20},{16,24},{20,28},{24,0},{28,4},{1,9},{5... | collective-permute-start | bytes 3145736 | tf_op jit(solution)/shard_map/ppermute | solution.py:49
  249.7 41.7 %collective-permute-start.23 = (bf16[256,2048]{1,0:T(8,128)(2,1)}, bf16[256,2048]{1,0:T(8,128)(2,1)S(1)}, u32[]{:S(2)}, u32[]{:S(2)}) collective-permute-start(bf16[256,2048]{1,0:T(8,128)(2,1)} %collective-permute-done.22), channel_id=1, source_target_pairs={{0,8},{4,12},{8,16},{12,20},{16,24},{20,28},{24,0},{28,4},{1,9},{5... | collective-permute-start | bytes 3145736 | tf_op jit(solution)/shard_map/ppermute | solution.py:49
  252.6 38.8 %collective-permute-start.11 = (bf16[320,2048]{1,0:T(8,128)(2,1)S(1)}, bf16[320,2048]{1,0:T(8,128)(2,1)S(1)}, u32[]{:S(2)}, u32[]{:S(2)}) collective-permute-start(bf16[320,2048]{1,0:T(8,128)(2,1)S(1)} %slice.599), channel_id=1, source_target_pairs={{0,2},{1,3},{2,0},{3,1},{4,6},{5,7},{6,4},{7,5},{8,10},{9,11},{10,... | collective-permute-start | bytes 3932168 | tf_op jit(solution)/shard_map/ppermute | solution.py:61
  272.0 23.0 %collective-permute-start.25 = (bf16[256,2048]{1,0:T(8,128)(2,1)}, bf16[256,2048]{1,0:T(8,128)(2,1)S(1)}, u32[]{:S(2)}, u32[]{:S(2)}) collective-permute-start(bf16[256,2048]{1,0:T(8,128)(2,1)} %get-tuple-element.137), channel_id=1, source_target_pairs={{0,4},{4,0},{8,12},{12,8},{16,20},{20,16},{24,28},{28,24},{1,5},{5... | collective-permute-start | bytes 3145736 | tf_op jit(solution)/shard_map/ppermute | solution.py:57
  272.4 24.0 %collective-permute-start.32 = (bf16[320,2048]{1,0:T(8,128)(2,1)S(1)}, bf16[320,2048]{1,0:T(8,128)(2,1)S(1)}, u32[]{:S(2)}, u32[]{:S(2)}) collective-permute-start(bf16[320,2048]{1,0:T(8,128)(2,1)S(1)} %copy-done.20), channel_id=1, source_target_pairs={{0,1},{1,0},{2,3},{3,2},{4,5},{5,4},{6,7},{7,6},{8,9},{9,8},{10,11... | collective-permute-start | bytes 3932168 | tf_op jit(solution)/shard_map/ppermute | solution.py:61
  291.5 27.8 %collective-permute-start.17 = (bf16[256,2048]{1,0:T(8,128)(2,1)S(1)}, bf16[256,2048]{1,0:T(8,128)(2,1)S(1)}, u32[]{:S(2)}, u32[]{:S(2)}) collective-permute-start(bf16[256,2048]{1,0:T(8,128)(2,1)S(1)} %collective-permute-done.16), channel_id=1, source_target_pairs={{0,8},{4,12},{8,16},{12,20},{16,24},{20,28},{24,0},{28,4},{1,9},{5... | collective-permute-start | bytes 3145736 | tf_op jit(solution)/shard_map/ppermute | solution.py:49
  294.4 40.6 %collective-permute-start.19 = (bf16[256,2048]{1,0:T(8,128)(2,1)}, bf16[256,2048]{1,0:T(8,128)(2,1)S(1)}, u32[]{:S(2)}, u32[]{:S(2)}) collective-permute-start(bf16[256,2048]{1,0:T(8,128)(2,1)} %collective-permute-done.15), channel_id=1, source_target_pairs={{0,4},{4,0},{8,12},{12,8},{16,20},{20,16},{24,28},{28,24},{1,5},{5... | collective-permute-start | bytes 3145736 | tf_op jit(solution)/shard_map/ppermute | solution.py:57
  295.0 48.1 %collective-permute-start.26 = (bf16[256,2048]{1,0:T(8,128)(2,1)}, bf16[256,2048]{1,0:T(8,128)(2,1)S(1)}, u32[]{:S(2)}, u32[]{:S(2)}) collective-permute-start(bf16[256,2048]{1,0:T(8,128)(2,1)} %collective-permute-done.22), channel_id=1, source_target_pairs={{0,4},{4,0},{8,12},{12,8},{16,20},{20,16},{24,28},{28,24},{1,5},{5... | collective-permute-start | bytes 3145736 | tf_op jit(solution)/shard_map/ppermute | solution.py:57
  296.5 69.1 %collective-permute-start.20 = (bf16[256,2048]{1,0:T(8,128)(2,1)S(1)}, bf16[256,2048]{1,0:T(8,128)(2,1)S(1)}, u32[]{:S(2)}, u32[]{:S(2)}) collective-permute-start(bf16[256,2048]{1,0:T(8,128)(2,1)S(1)} %collective-permute-done.16), channel_id=1, source_target_pairs={{0,4},{4,0},{8,12},{12,8},{16,20},{20,16},{24,28},{28,24},{1,5},{5... | collective-permute-start | bytes 3145736 | tf_op jit(solution)/shard_map/ppermute | solution.py:57
  297.0 44.3 %collective-permute-start.24 = (bf16[256,2048]{1,0:T(8,128)(2,1)S(1)}, bf16[256,2048]{1,0:T(8,128)(2,1)S(1)}, u32[]{:S(2)}, u32[]{:S(2)}) collective-permute-start(bf16[256,2048]{1,0:T(8,128)(2,1)S(1)} %collective-permute-done.23), channel_id=1, source_target_pairs={{0,8},{4,12},{8,16},{12,20},{16,24},{20,28},{24,0},{28,4},{1,9},{5... | collective-permute-start | bytes 3145736 | tf_op jit(solution)/shard_map/ppermute | solution.py:49
  319.3 46.3 %collective-permute-start.12 = (bf16[320,2048]{1,0:T(8,128)(2,1)S(1)}, bf16[320,2048]{1,0:T(8,128)(2,1)S(1)}, u32[]{:S(2)}, u32[]{:S(2)}) collective-permute-start(bf16[320,2048]{1,0:T(8,128)(2,1)S(1)} %add_convert_fusion.1), channel_id=1, source_target_pairs={{0,2},{1,3},{2,0},{3,1},{4,6},{5,7},{6,4},{7,5},{8,10},{9,11},{10,... | collective-permute-start | bytes 3932168 | tf_op jit(solution)/shard_map/ppermute | solution.py:61
  335.0 53.0 %collective-permute-start.27 = (bf16[256,2048]{1,0:T(8,128)(2,1)S(1)}, bf16[256,2048]{1,0:T(8,128)(2,1)S(1)}, u32[]{:S(2)}, u32[]{:S(2)}) collective-permute-start(bf16[256,2048]{1,0:T(8,128)(2,1)S(1)} %collective-permute-done.23), channel_id=1, source_target_pairs={{0,4},{4,0},{8,12},{12,8},{16,20},{20,16},{24,28},{28,24},{1,5},{5... | collective-permute-start | bytes 3145736 | tf_op jit(solution)/shard_map/ppermute | solution.py:57
  341.4 69.1 %collective-permute-start.21 = (bf16[256,2048]{1,0:T(8,128)(2,1)S(1)}, bf16[256,2048]{1,0:T(8,128)(2,1)S(1)}, u32[]{:S(2)}, u32[]{:S(2)}) collective-permute-start(bf16[256,2048]{1,0:T(8,128)(2,1)S(1)} %collective-permute-done.17), channel_id=1, source_target_pairs={{0,4},{4,0},{8,12},{12,8},{16,20},{20,16},{24,28},{28,24},{1,5},{5... | collective-permute-start | bytes 3145736 | tf_op jit(solution)/shard_map/ppermute | solution.py:57
  343.1 89.5 %collective-permute-start.28 = (bf16[256,2048]{1,0:T(8,128)(2,1)S(1)}, bf16[256,2048]{1,0:T(8,128)(2,1)S(1)}, u32[]{:S(2)}, u32[]{:S(2)}) collective-permute-start(bf16[256,2048]{1,0:T(8,128)(2,1)S(1)} %collective-permute-done.24), channel_id=1, source_target_pairs={{0,4},{4,0},{8,12},{12,8},{16,20},{20,16},{24,28},{28,24},{1,5},{5... | collective-permute-start | bytes 3145736 | tf_op jit(solution)/shard_map/ppermute | solution.py:57
  365.5 67.1 %collective-permute-start.13 = (bf16[320,2048]{1,0:T(8,128)(2,1)S(1)}, bf16[320,2048]{1,0:T(8,128)(2,1)S(1)}, u32[]{:S(2)}, u32[]{:S(2)}) collective-permute-start(bf16[320,2048]{1,0:T(8,128)(2,1)S(1)} %add_convert_fusion.1), channel_id=1, source_target_pairs={{0,1},{1,0},{2,3},{3,2},{4,5},{5,4},{6,7},{7,6},{8,9},{9,8},{10,11... | collective-permute-start | bytes 3932168 | tf_op jit(solution)/shard_map/ppermute | solution.py:61
  365.6 67.1 %collective-permute-start.14 = (bf16[320,2048]{1,0:T(8,128)(2,1)S(1)}, bf16[320,2048]{1,0:T(8,128)(2,1)S(1)}, u32[]{:S(2)}, u32[]{:S(2)}) collective-permute-start(bf16[320,2048]{1,0:T(8,128)(2,1)S(1)} %collective-permute-done.12), channel_id=1, source_target_pairs={{0,1},{1,0},{2,3},{3,2},{4,5},{5,4},{6,7},{7,6},{8,9},{9,8},{10,11... | collective-permute-start | bytes 3932168 | tf_op jit(solution)/shard_map/ppermute | solution.py:61
  536.8 56.4 %collective-permute-start.34 = (bf16[640,2048]{1,0:T(8,128)(2,1)S(1)}, bf16[640,2048]{1,0:T(8,128)(2,1)S(1)}, u32[]{:S(2)}, u32[]{:S(2)}) collective-permute-start(bf16[640,2048]{1,0:T(8,128)(2,1)S(1)} %slice.387), channel_id=1, source_target_pairs={{0,1},{1,0},{2,3},{3,2},{4,5},{5,4},{6,7},{7,6},{8,9},{9,8},{10,11... | collective-permute-start | bytes 7864328 | tf_op jit(solution)/shard_map/ppermute | solution.py:61
  538.5 26.2 %collective-permute-start.58 = (bf16[256,2048]{1,0:T(8,128)(2,1)}, bf16[256,2048]{1,0:T(8,128)(2,1)S(1)}, u32[]{:S(2)}, u32[]{:S(2)}) collective-permute-start(bf16[256,2048]{1,0:T(8,128)(2,1)} %convolution_convert_fusion.13), channel_id=1, source_target_pairs={{0,4},{4,0},{8,12},{12,8},{16,20},{20,16},{24,28},{28,24},{1,5},{5... | collective-permute-start | bytes 3145736 | tf_op jit(solution)/shard_map/ppermute | solution.py:57
  541.6 45.6 %collective-permute-start.65 = (bf16[256,2048]{1,0:T(8,128)(2,1)S(1)}, bf16[256,2048]{1,0:T(8,128)(2,1)S(1)}, u32[]{:S(2)}, u32[]{:S(2)}) collective-permute-start(bf16[256,2048]{1,0:T(8,128)(2,1)S(1)} %convolution_convert_fusion.9), channel_id=1, source_target_pairs={{0,4},{4,0},{8,12},{12,8},{16,20},{20,16},{24,28},{28,24},{1,5},{5... | collective-permute-start | bytes 3145736 | tf_op jit(solution)/shard_map/ppermute | solution.py:57
  547.4 93.2 %collective-permute-start.29 = (bf16[640,2048]{1,0:T(8,128)(2,1)}, bf16[640,2048]{1,0:T(8,128)(2,1)S(1)}, u32[]{:S(2)}, u32[]{:S(2)}) collective-permute-start(bf16[640,2048]{1,0:T(8,128)(2,1)} %slice.382), channel_id=1, source_target_pairs={{0,1},{1,0},{2,3},{3,2},{4,5},{5,4},{6,7},{7,6},{8,9},{9,8},{10,11... | collective-permute-start | bytes 7864328 | tf_op jit(solution)/shard_map/ppermute | solution.py:61
  549.9 187.1 %collective-permute-start.55 = (bf16[256,2048]{1,0:T(8,128)(2,1)}, bf16[256,2048]{1,0:T(8,128)(2,1)}, u32[]{:S(2)}, u32[]{:S(2)}) collective-permute-start(bf16[256,2048]{1,0:T(8,128)(2,1)} %convolution_convert_fusion.16), channel_id=1, source_target_pairs={{0,4},{4,0},{8,12},{12,8},{16,20},{20,16},{24,28},{28,24},{1,5},{5... | collective-permute-start | bytes 3145736 | tf_op jit(solution)/shard_map/ppermute | solution.py:57
  564.7 67.5 %collective-permute-start.57 = (bf16[256,2048]{1,0:T(8,128)(2,1)}, bf16[256,2048]{1,0:T(8,128)(2,1)}, u32[]{:S(2)}, u32[]{:S(2)}) collective-permute-start(bf16[256,2048]{1,0:T(8,128)(2,1)} %convolution_convert_fusion.14), channel_id=1, source_target_pairs={{0,4},{4,0},{8,12},{12,8},{16,20},{20,16},{24,28},{28,24},{1,5},{5... | collective-permute-start | bytes 3145736 | tf_op jit(solution)/shard_map/ppermute | solution.py:57
  587.2 48.7 %collective-permute-start.59 = (bf16[256,2048]{1,0:T(8,128)(2,1)}, bf16[256,2048]{1,0:T(8,128)(2,1)}, u32[]{:S(2)}, u32[]{:S(2)}) collective-permute-start(bf16[256,2048]{1,0:T(8,128)(2,1)} %fusion.32), channel_id=1, source_target_pairs={{0,24},{4,28},{8,0},{12,4},{16,8},{20,12},{24,16},{28,20},{1,25},{... | collective-permute-start | bytes 3145736 | tf_op jit(solution)/shard_map/ppermute | solution.py:49
  594.7 60.0 %collective-permute-start.64 = (bf16[256,2048]{1,0:T(8,128)(2,1)}, bf16[256,2048]{1,0:T(8,128)(2,1)}, u32[]{:S(2)}, u32[]{:S(2)}) collective-permute-start(bf16[256,2048]{1,0:T(8,128)(2,1)} %convolution_convert_fusion.10), channel_id=1, source_target_pairs={{0,4},{4,0},{8,12},{12,8},{16,20},{20,16},{24,28},{28,24},{1,5},{5... | collective-permute-start | bytes 3145736 | tf_op jit(solution)/shard_map/ppermute | solution.py:57
  632.2 25.9 %collective-permute-start.66 = (bf16[256,2048]{1,0:T(8,128)(2,1)}, bf16[256,2048]{1,0:T(8,128)(2,1)}, u32[]{:S(2)}, u32[]{:S(2)}) collective-permute-start(bf16[256,2048]{1,0:T(8,128)(2,1)} %add_convert_fusion.4), channel_id=1, source_target_pairs={{0,24},{4,28},{8,0},{12,4},{16,8},{20,12},{24,16},{28,20},{1,25},{... | collective-permute-start | bytes 3145736 | tf_op jit(solution)/shard_map/ppermute | solution.py:49
  635.9 32.0 %collective-permute-start.35 = (bf16[320,2048]{1,0:T(8,128)(2,1)}, bf16[320,2048]{1,0:T(8,128)(2,1)}, u32[]{:S(2)}, u32[]{:S(2)}) collective-permute-start(bf16[320,2048]{1,0:T(8,128)(2,1)} %slice.597), channel_id=1, source_target_pairs={{0,2},{1,3},{2,0},{3,1},{4,6},{5,7},{6,4},{7,5},{8,10},{9,11},{10,... | collective-permute-start | bytes 3932168 | tf_op jit(solution)/shard_map/ppermute | solution.py:61
  640.6 61.3 %collective-permute-start.56 = (bf16[256,2048]{1,0:T(8,128)(2,1)}, bf16[256,2048]{1,0:T(8,128)(2,1)}, u32[]{:S(2)}, u32[]{:S(2)}) collective-permute-start(bf16[256,2048]{1,0:T(8,128)(2,1)} %convolution_convert_fusion.15), channel_id=1, source_target_pairs={{0,4},{4,0},{8,12},{12,8},{16,20},{20,16},{24,28},{28,24},{1,5},{5... | collective-permute-start | bytes 3145736 | tf_op jit(solution)/shard_map/ppermute | solution.py:57
  654.7 52.5 %collective-permute-start.63 = (bf16[256,2048]{1,0:T(8,128)(2,1)}, bf16[256,2048]{1,0:T(8,128)(2,1)}, u32[]{:S(2)}, u32[]{:S(2)}) collective-permute-start(bf16[256,2048]{1,0:T(8,128)(2,1)} %convolution_convert_fusion.11), channel_id=1, source_target_pairs={{0,4},{4,0},{8,12},{12,8},{16,20},{20,16},{24,28},{28,24},{1,5},{5... | collective-permute-start | bytes 3145736 | tf_op jit(solution)/shard_map/ppermute | solution.py:57
  658.1 35.8 %collective-permute-start.30 = (bf16[320,2048]{1,0:T(8,128)(2,1)S(1)}, bf16[320,2048]{1,0:T(8,128)(2,1)S(1)}, u32[]{:S(2)}, u32[]{:S(2)}) collective-permute-start(bf16[320,2048]{1,0:T(8,128)(2,1)S(1)} %slice.598), channel_id=1, source_target_pairs={{0,2},{1,3},{2,0},{3,1},{4,6},{5,7},{6,4},{7,5},{8,10},{9,11},{10,... | collective-permute-start | bytes 3932168 | tf_op jit(solution)/shard_map/ppermute | solution.py:61
  667.9 34.5 %collective-permute-start.60 = (bf16[256,2048]{1,0:T(8,128)(2,1)}, bf16[256,2048]{1,0:T(8,128)(2,1)}, u32[]{:S(2)}, u32[]{:S(2)}) collective-permute-start(bf16[256,2048]{1,0:T(8,128)(2,1)} %fusion.34), channel_id=1, source_target_pairs={{0,24},{4,28},{8,0},{12,4},{16,8},{20,12},{24,16},{28,20},{1,25},{... | collective-permute-start | bytes 3145736 | tf_op jit(solution)/shard_map/ppermute | solution.py:49
  693.9 26.4 %collective-permute-start.67 = (bf16[256,2048]{1,0:T(8,128)(2,1)}, bf16[256,2048]{1,0:T(8,128)(2,1)}, u32[]{:S(2)}, u32[]{:S(2)}) collective-permute-start(bf16[256,2048]{1,0:T(8,128)(2,1)} %add_convert_fusion.3), channel_id=1, source_target_pairs={{0,24},{4,28},{8,0},{12,4},{16,8},{20,12},{24,16},{28,20},{1,25},{... | collective-permute-start | bytes 3145736 | tf_op jit(solution)/shard_map/ppermute | solution.py:49
  701.9 45.8 %collective-permute-start.62 = (bf16[256,2048]{1,0:T(8,128)(2,1)}, bf16[256,2048]{1,0:T(8,128)(2,1)}, u32[]{:S(2)}, u32[]{:S(2)}) collective-permute-start(bf16[256,2048]{1,0:T(8,128)(2,1)} %convolution_convert_fusion.12), channel_id=1, source_target_pairs={{0,4},{4,0},{8,12},{12,8},{16,20},{20,16},{24,28},{28,24},{1,5},{5... | collective-permute-start | bytes 3145736 | tf_op jit(solution)/shard_map/ppermute | solution.py:57
  702.4 34.7 %collective-permute-start.36 = (bf16[320,2048]{1,0:T(8,128)(2,1)}, bf16[320,2048]{1,0:T(8,128)(2,1)}, u32[]{:S(2)}, u32[]{:S(2)}) collective-permute-start(bf16[320,2048]{1,0:T(8,128)(2,1)} %multiply_convert_fusion.3), channel_id=1, source_target_pairs={{0,2},{1,3},{2,0},{3,1},{4,6},{5,7},{6,4},{7,5},{8,10},{9,11},{10,... | collective-permute-start | bytes 3932168 | tf_op jit(solution)/shard_map/ppermute | solution.py:61
  707.2 35.6 %collective-permute-start.61 = (bf16[256,2048]{1,0:T(8,128)(2,1)}, bf16[256,2048]{1,0:T(8,128)(2,1)}, u32[]{:S(2)}, u32[]{:S(2)}) collective-permute-start(bf16[256,2048]{1,0:T(8,128)(2,1)} %fusion.33), channel_id=1, source_target_pairs={{0,24},{4,28},{8,0},{12,4},{16,8},{20,12},{24,16},{28,20},{1,25},{... | collective-permute-start | bytes 3145736 | tf_op jit(solution)/shard_map/ppermute | solution.py:49
  724.5 37.8 %collective-permute-start.68 = (bf16[256,2048]{1,0:T(8,128)(2,1)}, bf16[256,2048]{1,0:T(8,128)(2,1)S(1)}, u32[]{:S(2)}, u32[]{:S(2)}) collective-permute-start(bf16[256,2048]{1,0:T(8,128)(2,1)} %add_convert_fusion.2), channel_id=1, source_target_pairs={{0,24},{4,28},{8,0},{12,4},{16,8},{20,12},{24,16},{28,20},{1,25},{... | collective-permute-start | bytes 3145736 | tf_op jit(solution)/shard_map/ppermute | solution.py:49
  737.0 30.0 %collective-permute-start.37 = (bf16[320,2048]{1,0:T(8,128)(2,1)}, bf16[320,2048]{1,0:T(8,128)(2,1)S(1)}, u32[]{:S(2)}, u32[]{:S(2)}) collective-permute-start(bf16[320,2048]{1,0:T(8,128)(2,1)} %multiply_convert_fusion.3), channel_id=1, source_target_pairs={{0,1},{1,0},{2,3},{3,2},{4,5},{5,4},{6,7},{7,6},{8,9},{9,8},{10,11... | collective-permute-start | bytes 3932168 | tf_op jit(solution)/shard_map/ppermute | solution.py:61
  737.1 30.0 %collective-permute-start.38 = (bf16[320,2048]{1,0:T(8,128)(2,1)}, bf16[320,2048]{1,0:T(8,128)(2,1)}, u32[]{:S(2)}, u32[]{:S(2)}) collective-permute-start(bf16[320,2048]{1,0:T(8,128)(2,1)} %collective-permute-done.36), channel_id=1, source_target_pairs={{0,1},{1,0},{2,3},{3,2},{4,5},{5,4},{6,7},{7,6},{8,9},{9,8},{10,11... | collective-permute-start | bytes 3932168 | tf_op jit(solution)/shard_map/ppermute | solution.py:61
  821.7 74.7 %collective-permute-start.39 = (bf16[640,2048]{1,0:T(8,128)(2,1)}, bf16[640,2048]{1,0:T(8,128)(2,1)}, u32[]{:S(2)}, u32[]{:S(2)}) collective-permute-start(bf16[640,2048]{1,0:T(8,128)(2,1)} %slice.391), channel_id=1, source_target_pairs={{0,1},{1,0},{2,3},{3,2},{4,5},{5,4},{6,7},{7,6},{8,9},{9,8},{10,11... | collective-permute-start | bytes 7864328 | tf_op jit(solution)/shard_map/ppermute | solution.py:61
  821.7 32.9 %collective-permute-start.43 = (bf16[256,1536]{1,0:T(8,128)(2,1)}, bf16[256,1536]{1,0:T(8,128)(2,1)}, u32[]{:S(2)}, u32[]{:S(2)}) collective-permute-start(bf16[256,1536]{1,0:T(8,128)(2,1)} %convolution_convert_fusion.6), channel_id=1, source_target_pairs={{0,4},{4,0},{8,12},{12,8},{16,20},{20,16},{24,28},{28,24},{1,5},{5... | collective-permute-start | bytes 2359304 | tf_op jit(solution)/shard_map/ppermute | solution.py:57
  842.4 44.7 %collective-permute-start.42 = (bf16[256,1536]{1,0:T(8,128)(2,1)S(1)}, bf16[256,1536]{1,0:T(8,128)(2,1)S(1)}, u32[]{:S(2)}, u32[]{:S(2)}) collective-permute-start(bf16[256,1536]{1,0:T(8,128)(2,1)S(1)} %convolution_convert_fusion.7), channel_id=1, source_target_pairs={{0,4},{4,0},{8,12},{12,8},{16,20},{20,16},{24,28},{28,24},{1,5},{5... | collective-permute-start | bytes 2359304 | tf_op jit(solution)/shard_map/ppermute | solution.py:57
  843.0 39.7 %collective-permute-start.50 = (bf16[256,512]{1,0:T(8,128)(2,1)}, bf16[256,512]{1,0:T(8,128)(2,1)S(1)}, u32[]{:S(2)}, u32[]{:S(2)}) collective-permute-start(bf16[256,512]{1,0:T(8,128)(2,1)} %convolution_convert_fusion.18), channel_id=1, source_target_pairs={{0,4},{4,0},{8,12},{12,8},{16,20},{20,16},{24,28},{28,24},{1,5},{5... | collective-permute-start | bytes 786440 | tf_op jit(solution)/shard_map/ppermute | solution.py:57
  854.5 24.2 %collective-permute-start.51 = (bf16[256,512]{1,0:T(8,128)(2,1)S(1)}, bf16[256,512]{1,0:T(8,128)(2,1)S(1)}, u32[]{:S(2)}, u32[]{:S(2)}) collective-permute-start(bf16[256,512]{1,0:T(8,128)(2,1)S(1)} %convolution_convert_fusion.17), channel_id=1, source_target_pairs={{0,4},{4,0},{8,12},{12,8},{16,20},{20,16},{24,28},{28,24},{1,5},{5... | collective-permute-start | bytes 786440 | tf_op jit(solution)/shard_map/ppermute | solution.py:57
  857.9 30.7 %collective-permute-start.46 = (bf16[256,1536]{1,0:T(8,128)(2,1)S(1)}, bf16[256,1536]{1,0:T(8,128)(2,1)S(1)}, u32[]{:S(2)}, u32[]{:S(2)}) collective-permute-start(bf16[256,1536]{1,0:T(8,128)(2,1)S(1)} %add_convert_fusion.6), channel_id=1, source_target_pairs={{0,24},{4,28},{8,0},{12,4},{16,8},{20,12},{24,16},{28,20},{1,25},{... | collective-permute-start | bytes 2359304 | tf_op jit(solution)/shard_map/ppermute | solution.py:49
  882.7 36.9 %collective-permute-start.41 = (bf16[256,1536]{1,0:T(8,128)(2,1)}, bf16[256,1536]{1,0:T(8,128)(2,1)}, u32[]{:S(2)}, u32[]{:S(2)}) collective-permute-start(bf16[256,1536]{1,0:T(8,128)(2,1)} %convolution_convert_fusion.8), channel_id=1, source_target_pairs={{0,4},{4,0},{8,12},{12,8},{16,20},{20,16},{24,28},{28,24},{1,5},{5... | collective-permute-start | bytes 2359304 | tf_op jit(solution)/shard_map/ppermute | solution.py:57
  886.0 25.9 %collective-permute-start.48 = (bf16[256,512]{1,0:T(8,128)(2,1)}, bf16[256,512]{1,0:T(8,128)(2,1)}, u32[]{:S(2)}, u32[]{:S(2)}) collective-permute-start(bf16[256,512]{1,0:T(8,128)(2,1)} %convolution_convert_fusion.20), channel_id=1, source_target_pairs={{0,4},{4,0},{8,12},{12,8},{16,20},{20,16},{24,28},{28,24},{1,5},{5... | collective-permute-start | bytes 786440 | tf_op jit(solution)/shard_map/ppermute | solution.py:57
  887.2 22.8 %collective-permute-start.49 = (bf16[256,512]{1,0:T(8,128)(2,1)S(1)}, bf16[256,512]{1,0:T(8,128)(2,1)S(1)}, u32[]{:S(2)}, u32[]{:S(2)}) collective-permute-start(bf16[256,512]{1,0:T(8,128)(2,1)S(1)} %convolution_convert_fusion.19), channel_id=1, source_target_pairs={{0,4},{4,0},{8,12},{12,8},{16,20},{20,16},{24,28},{28,24},{1,5},{5... | collective-permute-start | bytes 786440 | tf_op jit(solution)/shard_map/ppermute | solution.py:57
  888.7 21.8 %collective-permute-start.53 = (bf16[256,512]{1,0:T(8,128)(2,1)S(1)}, bf16[256,512]{1,0:T(8,128)(2,1)S(1)}, u32[]{:S(2)}, u32[]{:S(2)}) collective-permute-start(bf16[256,512]{1,0:T(8,128)(2,1)S(1)} %fusion.43), channel_id=1, source_target_pairs={{0,24},{4,28},{8,0},{12,4},{16,8},{20,12},{24,16},{28,20},{1,25},{... | collective-permute-start | bytes 786440 | tf_op jit(solution)/shard_map/ppermute | solution.py:49
  896.3 23.3 %collective-permute-start.47 = (bf16[256,1536]{1,0:T(8,128)(2,1)}, bf16[256,1536]{1,0:T(8,128)(2,1)}, u32[]{:S(2)}, u32[]{:S(2)}) collective-permute-start(bf16[256,1536]{1,0:T(8,128)(2,1)} %add_convert_fusion.5), channel_id=1, source_target_pairs={{0,24},{4,28},{8,0},{12,4},{16,8},{20,12},{24,16},{28,20},{1,25},{... | collective-permute-start | bytes 2359304 | tf_op jit(solution)/shard_map/ppermute | solution.py:49
  910.0 26.5 %collective-permute-start.40 = (bf16[320,2048]{1,0:T(8,128)(2,1)}, bf16[320,2048]{1,0:T(8,128)(2,1)}, u32[]{:S(2)}, u32[]{:S(2)}) collective-permute-start(bf16[320,2048]{1,0:T(8,128)(2,1)} %slice.596), channel_id=1, source_target_pairs={{0,2},{1,3},{2,0},{3,1},{4,6},{5,7},{6,4},{7,5},{8,10},{9,11},{10,... | collective-permute-start | bytes 3932168 | tf_op jit(solution)/shard_map/ppermute | solution.py:61
  (108 other events, 2844.4 us)

commit v2 on v1

--- a/solution.py
+++ b/solution.py
@@ -31,6 +31,8 @@
 score_scale = HEAD_DIM ** (-0.5)
 query_blocks = ((0, 128), (128, 256), (256, SEG_PAD))
 
+RATE = 0.59e9
+
 f32 = jnp.float32
 bf16 = jnp.bfloat16
 
@@ -59,6 +61,19 @@
 
 def swap(value, bits):
     return lax.ppermute(value, "mp", [(m, m ^ bits) for m in range(lax.axis_size("mp"))])
+
+
+def block_order():
+    outer, inner = seq_grid()
+    me = lax.axis_index("seq")
+    mine_a, mine_b = me // inner, me % inner
+    return jnp.stack(
+        [
+            ((mine_b - b + inner) % inner) * outer + (mine_a - a + outer) % outer
+            for a in range(outer)
+            for b in range(inner)
+        ]
+    ).astype(jnp.int32)
 
 
 def feature_order():
@@ -74,97 +89,588 @@
     ).astype(jnp.int32)
 
 
+def after(value, *others):
+    return lax.optimization_barrier((value, *others))[0]
+
+
 def row_codes():
     count = lax.axis_size("mp")
     return [high * 2 + low for low in range(2) for high in range(count // 2)]
 
 
-def gather_weight(own):
+def outer_groups():
     outer, inner = seq_grid()
+    return [[a * inner + b for a in range(outer)] for b in range(inner)]
+
+
+def block_spots():
+    outer, inner = seq_grid()
+    place = lax.axis_index("seq") // inner
+    return jnp.stack([(place - i + outer) % outer for i in range(outer)]).astype(jnp.int32)
+
+
+def ring_line(own):
     line = [own]
-    for _ in range(outer - 1):
+    for _ in range(seq_grid()[0] - 1):
         line.append(shift_outer(line[-1], 1))
-    blocks = list(line)
-    for _ in range(inner - 1):
-        line = [shift_inner(part, 1) for part in line]
-        blocks += line
-    return jnp.concatenate(blocks, axis=0)
-
-
-def scatter_weight(block_grad):
-    outer, inner = seq_grid()
+    return line
+
+
+def ring_rest(part):
+    rest = []
+    for _ in range(seq_grid()[1] - 1):
+        part = shift_inner(part, 1)
+        rest.append(part)
+    return rest
+
+
+def ring_scatter(parts, received):
     total = None
-    for i in reversed(range(outer)):
-        part = block_grad(inner - 1, i)
-        for j in reversed(range(inner - 1)):
-            part = block_grad(j, i) + shift_inner(part.astype(bf16), -1).astype(f32)
+    for i in reversed(range(len(parts))):
+        part = parts[i].astype(f32) + received[i].astype(f32)
         if total is not None:
             part = part + shift_outer(total.astype(bf16), -1).astype(f32)
         total = part
     return total
 
 
-def gather_rows(own):
-    count = lax.axis_size("mp")
+def inner_sum(parts):
+    inner = seq_grid()[1]
+    part = shift_inner(parts[inner - 1], -1)
+    for j in reversed(range(1, inner - 1)):
+        part = shift_inner((parts[j].astype(f32) + part.astype(f32)).astype(bf16), -1)
+    return part
+
+
+def greet(peers):
+    barrier = pltpu.get_barrier_semaphore()
+    for peer in peers:
+        pl.semaphore_signal(barrier, inc=1, device_id=peer, device_id_type=pl.DeviceIdType.MESH)
+    pl.semaphore_wait(barrier, len(peers))
+
+
+def others(axis, count):
+    me = lax.axis_index(axis)
+    return [lax.rem(me + step, count) for step in range(1, count)]
+
+
+def exchange(axis, count, pieces, slots, send_sems, recv_sems):
+    copies = []
+    for step, peer in enumerate(others(axis, count)):
+        copy = pltpu.make_async_remote_copy(
+            src_ref=pieces(peer),
+            dst_ref=slots.at[step],
+            send_sem=send_sems.at[step],
+            recv_sem=recv_sems.at[step],
+            device_id={axis: peer},
+            device_id_type=pl.DeviceIdType.MESH,
+        )
+        copy.start()
+        copies.append(copy)
+    return copies
+
+
+def reduce_vector_kernel(
+    seqs, parts, shared, in_ref, out_ref, slots, sums, send_sems, recv_sems, send_two, recv_two
+):
+    greet(
+        [{"seq": peer} for peer in others("seq", seqs)]
+        + [{"mp": peer} for peer in others("mp", parts)]
+    )
+    copies = exchange("seq", seqs, lambda peer: in_ref.at[peer], slots, send_sems, recv_sems)
+    total = in_ref[lax.axis_index("seq")]
+    for step, copy in enumerate(copies):
+        copy.wait()
+        total = total + slots[step]
+    out_ref[...] = total
+    copies = exchange(
+        "mp", parts, lambda peer: out_ref.at[:shared], sums, send_two, recv_two
+    )
+    for copy in copies:
+        copy.wait()
+    head = total[:shared]
+    for step in range(parts - 1):
+        head = head + sums[step]
+    out_ref[:shared] = head
+
+
+def reduce_vector(value, shared):
+    seqs, parts = lax.axis_size("seq"), lax.axis_size("mp")
+    vmem = pl.BlockSpec(memory_space=pltpu.VMEM)
+    block = value.shape[1:]
+    return pl.pallas_call(
+        functools.partial(reduce_vector_kernel, seqs, parts, shared),
+        out_shape=jax.ShapeDtypeStruct(block, value.dtype),
+        in_specs=[vmem],
+        out_specs=vmem,
+        scratch_shapes=[
+            pltpu.VMEM((seqs - 1, *block), value.dtype),
+            pltpu.VMEM((parts - 1, shared, *block[1:]), value.dtype),
+            pltpu.SemaphoreType.DMA((seqs - 1,)),
+            pltpu.SemaphoreType.DMA((seqs - 1,)),
+            pltpu.SemaphoreType.DMA((parts - 1,)),
+            pltpu.SemaphoreType.DMA((parts - 1,)),
+        ],
+        compiler_params=pltpu.CompilerParams(collective_id=1, has_side_effects=True),
+        name="reduce_vector",
+    )(value)
+
+
+def reduce_scalar_kernel(
+    seqs, parts, in_ref, out_ref, slots, sums, send_sems, recv_sems, send_two, recv_two
+):
+    greet(
+        [{"seq": peer} for peer in others("seq", seqs)]
+        + [{"mp": peer} for peer in others("mp", parts)]
+    )
+    copies = exchange("mp", parts, lambda peer: in_ref, sums, send_two, recv_two)
+    for copy in copies:
+        copy.wait()
+    me = lax.axis_index("mp")
+    total = jnp.zeros_like(in_ref)
+    for part in range(parts):
+        step = lax.rem(me + parts - part - 1 + parts, parts)
+        mine = part == me
+        other = sums[jnp.minimum(step, parts - 2)]
+        total = total + jnp.where(mine, in_ref[...], other)
+    out_ref[...] = total
+    copies = exchange("seq", seqs, lambda peer: out_ref, slots, send_sems, recv_sems)
+    for copy in copies:
+        copy.wait()
+    me = lax.axis_index("seq")
+    final = jnp.zeros_like(in_ref)
+    for place in range(seqs):
+        step = lax.rem(me + seqs - place - 1 + seqs, seqs)
+        mine = place == me
+        other = slots[jnp.minimum(step, seqs - 2)]
+        final = final + jnp.where(mine, total, other)
+    out_ref[...] = final
+
+
+def reduce_scalar(value):
+    seqs, parts = lax.axis_size("seq"), lax.axis_size("mp")
+    vmem = pl.BlockSpec(memory_space=pltpu.VMEM)
+    return pl.pallas_call(
+        functools.partial(reduce_scalar_kernel, seqs, parts),
+        out_shape=jax.ShapeDtypeStruct(value.shape, value.dtype),
+        in_specs=[vmem],
+        out_specs=vmem,
+        scratch_shapes=[
+            pltpu.VMEM((seqs - 1, *value.shape), value.dtype),
+            pltpu.VMEM((parts - 1, *value.shape), value.dtype),
+            pltpu.SemaphoreType.DMA((seqs - 1,)),
+            pltpu.SemaphoreType.DMA((seqs - 1,)),
+            pltpu.SemaphoreType.DMA((parts - 1,)),
+            pltpu.SemaphoreType.DMA((parts - 1,)),
+        ],
+        compiler_params=pltpu.CompilerParams(collective_id=0, has_side_effects=True),
+        name="reduce_scalar",
+    )(value)
+
+
+def gather_chips(own):
     high = [own]
-    for bit in range(1, count.bit_length() - 1):
+    for bit in range(1, lax.axis_size("mp").bit_length() - 1):
         high = high + [swap(part, 1 << bit) for part in high]
-    low = [swap(part, 1) for part in high]
-    return jnp.concatenate(high + low, axis=0)
-
-
-def scatter_rows(part):
-    count = lax.axis_size("mp")
-    half = part.shape[0] // 2
-    kept = part[:half].astype(f32) + swap(part[half:], 1).astype(f32)
-    rows = half // (count // 2)
-    total = kept[:rows]
-    for high in range(1, count // 2):
-        total = total + swap(kept[high * rows : (high + 1) * rows].astype(bf16), high * 2).astype(f32)
+    return high
+
+
+def scatter_chips(first, second):
+    count = lax.axis_size("mp") // 2
+    rows = 2 * first.shape[0] // count
+    total = first[:rows]
+    for n in range(1, count):
+        at = n * rows
+        if at < first.shape[0]:
+            part = first[at : at + rows].astype(bf16)
+        else:
+            part = second[at - first.shape[0] : at - first.shape[0] + rows]
+        total = total + swap(part, n * 2).astype(f32)
     return total
 
 
-def to_blocks_kernel(order_ref, in_ref, out_ref):
-    rows = in_ref.shape[0]
-    out_ref[...] = jnp.zeros_like(out_ref)
-    out_ref[:rows, :] = in_ref[...]
-
-
-def to_blocks(value, order, rows_padded):
-    rows, width = value.shape
-    count = order.shape[0]
-    wide = width // count
+def other_core():
+    me = lax.axis_index("mp")
+    return {"mp": me + 1 - 2 * lax.rem(me, 2)}
+
+
+def core_copy(src, dst, send_sem, recv_sem):
+    return pltpu.make_async_remote_copy(
+        src_ref=src,
+        dst_ref=dst,
+        send_sem=send_sem,
+        recv_sem=recv_sem,
+        device_id=other_core(),
+        device_id_type=pl.DeviceIdType.MESH,
+    )
+
+
+def kernel_params(number):
+    return pltpu.CompilerParams(
+        vmem_limit_bytes=56 * 2**20, collective_id=number, has_side_effects=True
+    )
+
+
+def expected(microseconds):
+    return pl.CostEstimate(
+        flops=int(microseconds * RATE), bytes_accessed=0, transcendentals=0
+    )
+
+
+def estimate(rows, depth, columns):
+    return expected(1.5 + rows * depth * columns * 2 / 7.2e8)
+
+
+def resident(shape):
+    return pl.BlockSpec(shape, lambda *place: (0,) * len(shape))
+
+
+def arrange_kernel(lefts, blocks, grid, normed, *refs):
+    pieces, rest = refs[:lefts], refs[lefts:-3]
+    got, send_sem, recv_sem = refs[-3:]
+    out_ref, own_ref = rest[-2:]
+    step = pl.program_id(0)
+    rows, width = pieces[0].shape
+    wide = width // blocks
+    outer, inner = grid
+    me = lax.axis_index("seq")
+    mine_a, mine_b = me // inner, lax.rem(me, inner)
+
+    def copy(n):
+        return core_copy(pieces[n], got.at[n], send_sem.at[n], recv_sem.at[n])
+
+    @pl.when(step == 0)
+    def _():
+        greet([other_core()])
+        for n in range(lefts):
+            copy(n).start()
+
+    def fill(p, load):
+        if normed:
+            value = load(slice(None)).astype(f32)
+            mean = jnp.mean(value, axis=-1, keepdims=True)
+            center = value - mean
+            scale = lax.rsqrt(jnp.mean(center * center, axis=-1, keepdims=True) + norm_eps)
+        for b in range(blocks):
+            place = lax.rem(mine_a - b % outer + outer, outer) * inner
+            place = place + lax.rem(mine_b - b // outer + inner, inner)
+            here = slice(b * wide, (b + 1) * wide)
+            part = load(pl.ds(pl.multiple_of(place * wide, wide), wide))
+            if p == 0:
+                own_ref[:, here] = part
+            part = part.astype(f32)
+            if normed:
+                part = (part - mean) * scale * rest[0][:, here] + rest[1][:, here]
+            else:
+                part = part * rest[0][...]
+            out_ref[:, here] = part.astype(bf16)
+
+    for n in range(lefts):
+
+        @pl.when(step == n)
+        def _(n=n):
+            fill(n, lambda columns: pieces[n][:, columns])
+
+        @pl.when(step == lefts + n)
+        def _(n=n):
+            copy(n).wait()
+            fill(lefts + n, lambda columns: got[n, :, columns])
+
+
+def arrange(pieces, extras, extra_specs, normed, number, name):
+    rows, width = pieces[0].shape
+    lefts = len(pieces)
     return pl.pallas_call(
-        to_blocks_kernel,
-        out_shape=jax.ShapeDtypeStruct((rows_padded, width), value.dtype),
+        functools.partial(arrange_kernel, lefts, lax.axis_size("seq"), seq_grid(), normed),
+        out_shape=[
+            jax.ShapeDtypeStruct((2 * lefts * rows, width), bf16),
+            jax.ShapeDtypeStruct((rows, width), bf16),
+        ],
+        grid=(2 * lefts,),
+        in_specs=[resident((rows, width))] * lefts + extra_specs,
+        out_specs=[pl.BlockSpec((rows, width), lambda n: (n, 0)), resident((rows, width))],
+        scratch_shapes=[
+            pltpu.VMEM((lefts, rows, width), bf16),
+            pltpu.SemaphoreType.DMA((lefts,)),
+            pltpu.SemaphoreType.DMA((lefts,)),
+        ],
+        compiler_params=kernel_params(number),
+        cost_estimate=expected(9.0),
+        name=name,
+    )(*pieces, *extras)
+
+
+def tall_kernel(epilogue, exchanged, lefts, blocks, extras, *refs):
+    weight = jnp.concatenate([ref[...] for ref in refs[lefts : lefts + blocks]], axis=0)
+    rest = refs[lefts + blocks :]
+    step = pl.program_id(0)
+    rows = refs[0].shape[0]
+    if exchanged:
+        others_ref, got, send_sem, recv_sem = rest[-4:]
+        rest = rest[:-4]
+
+        def copy(n):
+            return core_copy(refs[n], got.at[n], send_sem.at[n], recv_sem.at[n])
+
+        @pl.when(step == 0)
+        def _():
+            greet([other_core()])
+            for n in range(lefts):
+                copy(n).start()
+
+    def fill(left, at):
+        result = jnp.dot(left, weight, preferred_element_type=f32)
+        epilogue(result, slice(at, at + rows), rest[:extras], rest[extras:])
+
+    for n in range(lefts):
+        fill(refs[n][...], n * rows)
+    if exchanged:
+
+        @pl.when(step == 0)
+        def _():
+            for n in range(lefts):
+                copy(n).wait()
+
+        for n in range(lefts):
+            fill(got[n], (lefts + n) * rows)
+
+        @pl.when(step == pl.num_programs(0) - 1)
+        def _():
+            for n in range(lefts):
+                others_ref[n * rows : (n + 1) * rows, :] = got[n]
+
+
+def tall_dot(lefts, blocks, start, width, epilogue, extras, outs, name, number=None):
+    rows, depth = lefts[0].shape
+    exchanged = number is not None
+    count = len(lefts) * (2 if exchanged else 1)
+    tile = max(size for size in (128, 256, 512) if width % size == 0 and start % size == 0)
+    first = start // tile
+    block_depth = depth // lax.axis_size("seq")
+    specs = []
+    for block in blocks:
+        high = block_depth if block.shape[0] // block_depth < 2 else block.shape[0]
+        specs.append(pl.BlockSpec((high, tile), lambda n: (0, first + n)))
+    out_shape = [jax.ShapeDtypeStruct((height, width), dtype) for height, dtype in outs]
+    out_specs = [pl.BlockSpec((height, tile), lambda n: (0, n)) for height, _ in outs]
+    scratch = []
+    params = pltpu.CompilerParams(vmem_limit_bytes=56 * 2**20)
+    if exchanged:
+        out_shape.append(jax.ShapeDtypeStruct((len(lefts) * rows, depth), bf16))
+        out_specs.append(resident((len(lefts) * rows, depth)))
+        scratch = [
+            pltpu.VMEM((len(lefts), rows, depth), bf16),
+            pltpu.SemaphoreType.DMA((len(lefts),)),
+            pltpu.SemaphoreType.DMA((len(lefts),)),
+        ]
+        params = kernel_params(number)
+    return pl.pallas_call(
+        functools.partial(
+            tall_kernel, epilogue, exchanged, len(lefts), len(blocks), len(extras)
+        ),
+        out_shape=out_shape,
+        grid=(width // tile,),
+        in_specs=[resident(left.shape) for left in lefts]
+        + specs
+        + [pl.BlockSpec((extra.shape[0], tile), lambda n: (0, n)) for extra in extras],
+        out_specs=out_specs,
+        scratch_shapes=scratch,
+        compiler_params=params,
+        cost_estimate=estimate(rows * count, depth, width),
+        name=name,
+    )(*lefts, *blocks, *extras)
+
+
+def plain_epilogue(result, here, extras, outs):
+    outs[0][here, :] = result.astype(bf16)
+
+
+def project_epilogue(result, here, extras, outs):
+    bias, scale = extras
+    outs[0][here, :] = ((result + bias[...]).astype(bf16).astype(f32) * scale[...]).astype(bf16)
+
+
+def up_epilogue(result, here, extras, outs):
+    value, slope = gelu_both(result + extras[0][...])
+    outs[0][here, :] = value.astype(bf16)
+    outs[1][here, :] = slope.astype(bf16)
+
+
+def slope_epilogue(result, here, extras, outs):
+    grad = (result * extras[0][here, :].astype(f32)).astype(bf16)
+    outs[0][here, :] = grad
+    sums = jnp.sum(grad.astype(f32), axis=0, keepdims=True)
+    outs[1][...] = jnp.broadcast_to(sums, outs[1].shape)
+
+
+def wide_kernel(blocks, start, left_ref, *refs):
+    first_ref, second_ref, sent, got, send_sem, recv_sem = refs[blocks:]
+    step = pl.program_id(0)
+    columns = slice(start, start + left_ref.shape[1])
+
+    def copy(n):
+        return core_copy(sent.at[n], got.at[n], send_sem.at[n], recv_sem.at[n])
+
+    @pl.when(step == 0)
+    def _():
+        greet([other_core()])
+
+    result = lax.dot_general(
+        left_ref[...],
+        jnp.concatenate([ref[:, columns] for ref in refs[:blocks]], axis=0),
+        (((1,), (1,)), ((), ())),
+        preferred_element_type=f32,
+    )
+    for n in range(2):
+
+        @pl.when(step == n)
+        def _(n=n):
+            sent[n] = result.astype(bf16)
+            copy(n).start()
+
+    @pl.when(step == 2)
+    def _():
+        copy(0).wait()
+        second_ref[...] = (result + got[0].astype(f32)).astype(bf16)
+
+    @pl.when(step == 3)
+    def _():
+        copy(1).wait()
+        first_ref[...] = result + got[1].astype(f32)
+
+
+def wide_dot(left, blocks, start, features, number, name):
+    rows, width = left.shape
+    tile = rows // 4
+    block_depth = features // lax.axis_size("seq")
+    specs = []
+    for block in blocks:
+        high = block_depth if block.shape[0] // block_depth < 2 else block.shape[0]
+        specs.append(resident((high, block.shape[1])))
+    return pl.pallas_call(
+        functools.partial(wide_kernel, len(blocks), start),
+        out_shape=[
+            jax.ShapeDtypeStruct((tile, features), f32),
+            jax.ShapeDtypeStruct((tile, features), bf16),
+        ],
+        grid=(4,),
+        in_specs=[pl.BlockSpec((tile, width), lambda n: (3 - n, 0))] + specs,
+        out_specs=[resident((tile, features)), resident((tile, features))],
+        scratch_shapes=[
+            pltpu.VMEM((2, tile, features), bf16),
+            pltpu.VMEM((2, tile, features), bf16),
+            pltpu.SemaphoreType.DMA((2,)),
+            pltpu.SemaphoreType.DMA((2,)),
+        ],
+        compiler_params=kernel_params(number),
+        cost_estimate=estimate(rows, width, features),
+        name=name,
+    )(left, *blocks)
+
+
+def turned_kernel(shapes, split, added, spots_ref, *refs):
+    refs = list(refs)
+    groups = [[refs.pop(0) for _ in range(count)] for count in shapes]
+    rights = [refs.pop(0) for _ in shapes]
+    add_ref = refs.pop(0) if added else None
+
+    def fill(out_ref):
+        at = 0
+        for lefts, right_ref in zip(groups, rights):
+            width = right_ref.shape[1]
+            left = jnp.concatenate([ref[...] for ref in lefts], axis=0)
+            result = lax.dot_general(
+                left, right_ref[...], (((0,), (0,)), ((), ())), preferred_element_type=f32
+            )
+            if added:
+                result = result + add_ref[:, at : at + width].astype(f32)
+            out_ref[:, at : at + width] = result.astype(bf16)
+            at += width
+
+    if split:
+        for n, out_ref in enumerate(refs):
+            pl.when(pl.program_id(0) == n)(functools.partial(fill, out_ref))
+    else:
+        fill(refs[0])
+
+
+def turned_dot(pairs, first, spots, depth, name, split=False, add=None):
+    count = spots.shape[0]
+    width = sum(right.shape[1] for _, right in pairs)
+    rows = pairs[0][1].shape[0]
+    block = jax.ShapeDtypeStruct((depth, width), bf16)
+    if split:
+        out_shape, out_specs = [block] * count, [resident((depth, width))] * count
+    else:
+        out_shape = [jax.ShapeDtypeStruct((count * depth, width), bf16)]
+        if add is None:
+            out_specs = [pl.BlockSpec((depth, width), lambda n, spots_ref: (n, 0))]
+        else:
+            out_specs = [pl.BlockSpec((depth, width), lambda n, spots_ref: (spots_ref[n], 0))]
+    adds = [] if add is None else [add]
+    return pl.pallas_call(
+        functools.partial(
+            turned_kernel, [len(lefts) for lefts, _ in pairs], split, add is not None
+        ),
+        out_shape=out_shape,
         grid_spec=pltpu.PrefetchScalarGridSpec(
             num_scalar_prefetch=1,
             grid=(count,),
-            in_specs=[pl.BlockSpec((rows, wide), lambda n, order_ref: (0, order_ref[n]))],
-            out_specs=pl.BlockSpec((rows_padded, wide), lambda n, order_ref: (0, n)),
+            in_specs=[
+                pl.BlockSpec((left.shape[0], depth), lambda n, spots_ref: (0, first + n))
+                for lefts, _ in pairs
+                for left in lefts
+            ]
+            + [resident(right.shape) for _, right in pairs]
+            + [pl.BlockSpec((depth, width), lambda n, spots_ref: (n, 0))] * len(adds),
+            out_specs=out_specs,
         ),
-        name="to_blocks",
-    )(order, value)
-
-
-def from_blocks_kernel(order_ref, in_ref, out_ref):
-    rows = out_ref.shape[0]
-    out_ref[...] = in_ref[:rows, :].astype(out_ref.dtype)
+        compiler_params=pltpu.CompilerParams(vmem_limit_bytes=56 * 2**20),
+        cost_estimate=estimate(rows, count * depth, width),
+        name=name,
+    )(
+        spots,
+        *[left for lefts, _ in pairs for left in lefts],
+        *[right for _, right in pairs],
+        *adds,
+    )
+
+
+def far_grads(pairs, spots, depth, name, split=False):
+    outer, inner = seq_grid()
+    return [None] + [
+        turned_dot(pairs, j * outer, spots, depth, name + "_far", split=split)
+        for j in range(1, inner)
+    ]
+
+
+def line_scatter(pairs, received, spots, depth, name):
+    near = turned_dot(pairs, 0, spots, depth, name + "_near", add=received)[0]
+    return lax.psum_scatter(
+        near, "seq", scatter_dimension=0, tiled=True, axis_index_groups=outer_groups()
+    )
+
+
+def from_blocks_kernel(blocks, order_ref, in_ref, out_ref):
+    rows, width = out_ref.shape
+    wide = width // blocks
+    for b in range(blocks):
+        there = pl.ds(pl.multiple_of(order_ref[b] * wide, wide), wide)
+        out_ref[:, there] = in_ref[:rows, b * wide : (b + 1) * wide].astype(out_ref.dtype)
 
 
 def from_blocks(value, order, rows):
     rows_padded, width = value.shape
-    count = order.shape[0]
-    wide = width // count
     return pl.pallas_call(
-        from_blocks_kernel,
+        functools.partial(from_blocks_kernel, order.shape[0]),
         out_shape=jax.ShapeDtypeStruct((rows, width), bf16),
-        grid_spec=pltpu.PrefetchScalarGridSpec(
-            num_scalar_prefetch=1,
-            grid=(count,),
-            in_specs=[pl.BlockSpec((rows_padded, wide), lambda n, order_ref: (0, n))],
-            out_specs=pl.BlockSpec((rows, wide), lambda n, order_ref: (0, order_ref[n])),
-        ),
+        in_specs=[
+            pl.BlockSpec(memory_space=pltpu.SMEM),
+            pl.BlockSpec(memory_space=pltpu.VMEM),
+        ],
+        out_specs=pl.BlockSpec(memory_space=pltpu.VMEM),
+        compiler_params=pltpu.CompilerParams(vmem_limit_bytes=40 * 2**20),
+        cost_estimate=expected(3.0),
         name="from_blocks",
     )(order, value)
 
@@ -268,6 +774,7 @@
             ),
         ),
         compiler_params=pltpu.CompilerParams(vmem_limit_bytes=48 * 2**20),
+        cost_estimate=expected(36.0),
         name="attend",
     )(me, qkv, qkv, qkv, bias)
 
@@ -379,6 +886,7 @@
             scratch_shapes=[pltpu.VMEM((128, rows), f32), pltpu.VMEM((128, rows), f32)],
         ),
         compiler_params=pltpu.CompilerParams(vmem_limit_bytes=48 * 2**20),
+        cost_estimate=expected(23.0),
         name="attend_back",
     )(me, qkv, qkv, qkv, out, grad, share)
 
@@ -439,18 +947,6 @@
     master_new = master - rate * (first_hat / (jnp.sqrt(second_hat) + adam_eps) + decay * master)
     average_new = average_keep * average + (1.0 - average_keep) * master_new
     return (master_new, first_new, second_new, average_new, master_new.astype(bf16))
-
-
-def dot_nn(left, right):
-    return jnp.dot(left, right, preferred_element_type=f32)
-
-
-def dot_nt(left, right):
-    return lax.dot_general(left, right, (((1,), (1,)), ((), ())), preferred_element_type=f32)
-
-
-def dot_tn(left, right):
-    return lax.dot_general(left, right, (((0,), (0,)), ((), ())), preferred_element_type=f32)
 
 
 def per_device(
@@ -489,30 +985,44 @@
     me = lax.axis_index("mp")
     me_vector = me.astype(jnp.int32)[None]
     order = feature_order()
+    back_order = block_order()
+    spots = block_spots()
     codes = row_codes()
-
-    inputs_own = to_blocks(tokens, order, rows_padded)
-    cotangent_own = to_blocks(cotangent, order, rows_padded)
-    inputs_all = gather_rows(inputs_own)
-    cotangent_all = gather_rows(cotangent_own)
-
-    attn_own = jnp.concatenate([attention_weight[n] for n in range(4)], axis=1).astype(bf16)
-    attn_full = gather_weight(attn_own)
-    up_full = gather_weight(hidden_weight[0].astype(bf16))
-    down_full = gather_weight(hidden_weight[1].astype(bf16))
-    qkv_full = attn_full[:, : 3 * head_width]
-    out_full = attn_full[:, 3 * head_width :]
-
-    packed = jnp.concatenate(
-        [norm_params.reshape(-1), head_bias.reshape(-1), unit_bias]
+    units = hidden_weight.shape[2]
+    total_rows = parts * rows_padded
+
+    norm_size, head_size = norm_params.size, head_bias.size
+    packed = jnp.concatenate([norm_params.reshape(-1), head_bias.reshape(-1), unit_bias])
+    packed_size = packed.size
+    packed_width = 4 * head_width
+    packed = jnp.pad(packed, (0, 16 * packed_width - packed_size)).reshape(16, packed_width)
+    attn_own = jnp.concatenate(
+        [jnp.concatenate([attention_weight[n] for n in range(4)], axis=1), packed], axis=0
     ).astype(bf16)
-    packed = lax.all_gather(packed, "seq", axis=0, tiled=False).astype(f32)
-    norm_size, head_size = norm_params.size, head_bias.size
-    norm_vals = jnp.take(packed[:, :norm_size], order, axis=0).reshape(seqs, 6, depth)
-    norm_vals = norm_vals.transpose(1, 0, 2).reshape(6, D)
-    head_vals = packed[:, norm_size : norm_size + head_size].reshape(seqs, 2, head_width // seqs)
+    attn_line = ring_line(attn_own)
+    row_pad = ((0, rows_padded - rows), (0, 0))
+    tokens_all = gather_chips(jnp.pad(tokens, row_pad))
+    attn_rest = [ring_rest(part) for part in attn_line]
+    attn_blocks = attn_line + [rest[j] for j in range(inner - 1) for rest in attn_rest]
+    cotangent_pieces = gather_chips(after(jnp.pad(cotangent, row_pad), *tokens_all))
+    up_line = ring_line(after(hidden_weight[0].astype(bf16), attn_line[-1]))
+    down_line = ring_line(after(hidden_weight[1].astype(bf16), up_line[-1]))
+    up_first = ring_rest(after(up_line[0], attn_rest[-2][-1]))
+    down_first = ring_rest(after(down_line[0], attn_rest[-1][-1]))
+    up_rest = ring_rest(jnp.concatenate(after(up_line[1:], up_first[-1]), axis=0))
+    down_rest = ring_rest(
+        jnp.concatenate(after(down_line[1:], down_first[-1], up_rest[-1]), axis=0)
+    )
+    up_blocks = up_line + [part for pair in zip(up_first, up_rest) for part in pair]
+    down_blocks = down_line + [part for pair in zip(down_first, down_rest) for part in pair]
+
+    vectors = jnp.concatenate([block[depth : depth + 1] for block in attn_blocks], axis=0)
+    vectors = vectors[:, :packed_size].astype(f32)
+    norm_vals = vectors[:, :norm_size].reshape(seqs, 6, depth).transpose(1, 0, 2).reshape(6, D)
+    vectors = jnp.take(vectors[:, norm_size:], back_order, axis=0)
+    head_vals = vectors[:, :head_size].reshape(seqs, 2, head_width // seqs)
     head_vals = head_vals.transpose(1, 0, 2).reshape(2, head_width)
-    unit_vals = packed[:, norm_size + head_size :].reshape(-1)
+    unit_vals = vectors[:, head_size:].reshape(-1)
 
     kept, flags = item_rows(present[0], summary_mask[0], parts, rows, rows_padded)
     bias = score_bias(kept, flags)
@@ -520,49 +1030,105 @@
     kept_all = jnp.take(kept_parts, jnp.stack([me ^ code for code in codes]), axis=0).reshape(-1, 1)
     kept_own = kept_all[:rows_padded]
 
-    normed_all = norm_parts(inputs_all.astype(f32))[0]
-    first_all = (normed_all * norm_vals[0] + norm_vals[1]).astype(bf16)
+    first_all, inputs_own = arrange(
+        tokens_all,
+        [norm_vals[0:1], norm_vals[1:2]],
+        [resident((1, D))] * 2,
+        True,
+        2,
+        "first_norm",
+    )
     qkv_bias = jnp.concatenate([head_vals[0], jnp.zeros_like(head_vals[0]), head_vals[1]])
     qkv_scale = np.concatenate(
         [np.full(head_width, score_scale, np.float32), np.ones(2 * head_width, np.float32)]
     )
-    qkv = ((dot_nn(first_all, qkv_full) + qkv_bias).astype(bf16) * qkv_scale.astype(bf16))
+    qkv = tall_dot(
+        [first_all],
+        attn_blocks,
+        0,
+        3 * head_width,
+        project_epilogue,
+        [qkv_bias[None], qkv_scale[None]],
+        [(total_rows, bf16)],
+        "project",
+    )[0]
     context, share = attend(qkv, bias, me_vector, parts, rows_padded)
-    attended = scatter_rows(dot_nt(context, out_full).astype(bf16)) + norm_vals[4]
+    join_parts = wide_dot(context, attn_blocks, 3 * head_width, D, 4, "join")
+    attended = scatter_chips(*join_parts) + norm_vals[4]
+    feed_grad, cotangent_own = arrange(
+        cotangent_pieces,
+        [kept_all],
+        [pl.BlockSpec((rows_padded, 1), lambda n: (n, 0))],
+        False,
+        3,
+        "feed_grad",
+    )
     inputs = inputs_own.astype(f32)
     middle = inputs + kept_own * attended
 
     normed_two, scale_two = norm_parts(middle)
     second_own = (normed_two * norm_vals[2] + norm_vals[3]).astype(bf16)
-    second_all = gather_rows(second_own)
-    pre_act = dot_nn(second_all, up_full) + unit_vals
-    activated, slope = gelu_both(pre_act)
-    activated, slope = activated.astype(bf16), slope.astype(bf16)
-    feed_out = scatter_rows(dot_nt(activated, down_full).astype(bf16)) + norm_vals[5]
-    block_output = from_blocks(middle + kept_own * feed_out, order, rows)
+    second_all = gather_chips(second_own)
+    activated, slope, second_others = tall_dot(
+        second_all,
+        up_blocks,
+        0,
+        units,
+        up_epilogue,
+        [unit_vals[None]],
+        [(total_rows, bf16), (total_rows, bf16)],
+        "up",
+        5,
+    )
+    second_all = second_all + [second_others]
 
     out_grad = cotangent_own.astype(f32)
-    feed_grad = (cotangent_all.astype(f32) * kept_all).astype(bf16)
     down_bias_grad = jnp.sum(kept_own * out_grad, axis=0)
 
-    def columns(value, j, i):
-        place = j * outer + i
-        return value[:, place * depth : (place + 1) * depth]
-
-    down_grad = scatter_weight(lambda j, i: dot_tn(columns(feed_grad, j, i), activated))
-    pre_grad = (dot_nn(feed_grad, down_full) * slope.astype(f32)).astype(bf16)
-    unit_grad = jnp.sum(pre_grad, axis=0, dtype=f32)
-    second_grad = scatter_rows(dot_nt(pre_grad, up_full).astype(bf16))
-    up_grad = scatter_weight(lambda j, i: dot_tn(columns(second_all, j, i), pre_grad))
+    down_pairs = [([feed_grad], activated)]
+    down_far = far_grads(down_pairs, spots, depth, "down_grad")
+    down_received = inner_sum([far and far[0] for far in down_far])
+    pre_grad, unit_grad = tall_dot(
+        [feed_grad],
+        down_blocks,
+        0,
+        units,
+        slope_epilogue,
+        [slope],
+        [(total_rows, bf16), (8, f32)],
+        "down_back",
+    )
+    unit_grad = unit_grad[0]
+    second_parts = wide_dot(pre_grad, up_blocks, 0, D, 6, "up_back")
+    up_pairs = [(second_all, pre_grad)]
+    up_far = far_grads(up_pairs, spots, depth, "up_grad")
+    up_received = inner_sum(
+        [far and after(far[0], down_received) for far in up_far]
+    )
+    second_grad = scatter_chips(*second_parts)
     gain_two_grad = jnp.sum(second_grad * normed_two, axis=0)
     shift_two_grad = jnp.sum(second_grad, axis=0)
     middle_grad = out_grad + norm_back(normed_two, scale_two, norm_vals[2], second_grad)
 
     attn_grad = kept_own * middle_grad
     out_bias_grad = jnp.sum(attn_grad, axis=0)
-    attn_rows = gather_rows(attn_grad.astype(bf16))
-    context_grad = dot_nn(attn_rows, out_full).astype(bf16)
-    out_proj_grad = scatter_weight(lambda j, i: dot_tn(columns(attn_rows, j, i), context))
+    attn_rows = gather_chips(attn_grad.astype(bf16))
+    context_grad, attn_others = tall_dot(
+        attn_rows,
+        attn_blocks,
+        3 * head_width,
+        head_width,
+        plain_epilogue,
+        [],
+        [(total_rows, bf16)],
+        "join_back",
+        7,
+    )
+    attn_rows = attn_rows + [attn_others]
+    down_grad = line_scatter(down_pairs, down_received, spots, depth, "down_grad")
+    feed_parts = wide_dot(after(activated, second_grad), down_blocks, 0, D, 8, "down")
+    feed_out = scatter_chips(*after(feed_parts, *attn_rows)) + norm_vals[5]
+    block_output = from_blocks(middle + kept_own * feed_out, order, rows)
     query_grad, key_grad, value_grad = attend_back(
         qkv, context, context_grad, share, me_vector, parts, rows_padded
     )
@@ -570,8 +1136,18 @@
     head_grad = jnp.stack(
         [jnp.sum(query_grad, axis=0, dtype=f32), jnp.sum(value_grad, axis=0, dtype=f32)]
     )
-    first_grad = scatter_rows(dot_nt(qkv_grad, qkv_full).astype(bf16))
-    proj_grad = scatter_weight(lambda j, i: dot_tn(columns(first_all, j, i), qkv_grad))
+    attn_pairs = [([first_all], qkv_grad), (attn_rows, context)]
+    attn_far = far_grads(attn_pairs, spots, depth, "attn_grad", split=True)
+    attn_received = [None] * outer
+    last = up_received
+    for i in reversed(range(outer)):
+        last = attn_received[i] = inner_sum([far and after(far[i], last) for far in attn_far])
+    up_grad = line_scatter(up_pairs, up_received, spots, depth, "up_grad")
+    near = turned_dot(attn_pairs, 0, spots, depth, "attn_grad_near")[0]
+    attn_shard = ring_scatter(
+        [near[i * depth : (i + 1) * depth] for i in range(outer)], attn_received
+    )
+    first_grad = scatter_chips(*wide_dot(qkv_grad, attn_blocks, 0, D, 9, "project_back"))
     normed_one, scale_one = norm_parts(inputs)
     gain_one_grad = jnp.sum(first_grad * normed_one, axis=0)
     shift_one_grad = jnp.sum(first_grad, axis=0)
@@ -589,26 +1165,31 @@
             down_bias_grad,
         ]
     )
-    back_order = jnp.argsort(order)
     vector_grad = jnp.take(
         vector_grad.reshape(6, seqs, depth).transpose(1, 0, 2).reshape(seqs, -1), back_order, axis=0
     )
+    norm_room = -(-norm_size // 1024) * 1024
+    room = norm_room + -(-(packed_size - norm_size) // 1024) * 1024
     vectors = jnp.concatenate(
         [
             vector_grad,
+            jnp.zeros((seqs, norm_room - norm_size), f32),
             head_grad.reshape(2, seqs, -1).transpose(1, 0, 2).reshape(seqs, -1),
             unit_grad.reshape(seqs, -1),
+            jnp.zeros((seqs, room - norm_room - packed_size + norm_size), f32),
         ],
         axis=1,
     )
-    vectors = lax.psum_scatter(vectors, "seq", scatter_dimension=0, tiled=False)
-    norm_shard = lax.psum(vectors[:norm_size], "mp").reshape(norm_params.shape)
-    head_shard = vectors[norm_size : norm_size + head_size].reshape(head_bias.shape)
-    unit_shard = vectors[norm_size + head_size :]
-
-    proj_grad = proj_grad.reshape(depth, 3, head_width).transpose(1, 0, 2)
-    attn_shard = jnp.concatenate([proj_grad, out_proj_grad[None]], axis=0)
-    hidden_shard = jnp.stack([up_grad, down_grad])
+    vectors = reduce_vector(vectors.reshape(seqs, room // 128, 128), norm_room // 128)
+    vectors = vectors.reshape(-1)
+    norm_shard = vectors[:norm_size].reshape(norm_params.shape)
+    head_shard = vectors[norm_room : norm_room + head_size].reshape(head_bias.shape)
+    unit_shard = vectors[norm_room + head_size : norm_room + packed_size - norm_size]
+
+    attn_shard = jnp.stack(
+        [attn_shard[:, n * head_width : (n + 1) * head_width] for n in range(4)]
+    )
+    hidden_shard = jnp.stack([up_grad, down_grad]).astype(f32)
     leader = (me == 0).astype(f32)
     local_squares = (
         jnp.sum(attn_shard * attn_shard)
@@ -617,7 +1198,7 @@
         + jnp.sum(unit_shard * unit_shard)
         + leader * jnp.sum(norm_shard * norm_shard)
     )
-    grad_norm = jnp.sqrt(lax.psum(local_squares, ("seq", "mp")))
+    grad_norm = jnp.sqrt(reduce_scalar(jnp.full((8, 128), local_squares))[0, 0])
     factor = jnp.minimum(1.0, clip_limit / (grad_norm + 1e-06))
     hidden_rate = jnp.array([D ** (-0.5), FF ** (-0.5)], f32)[:, None, None]
     attention_out = adam_step(

time: 1090 us -> 848 us (0.78)
  Pallas kernels: 84.3 us -> 345 us
  matrix products: 193 us -> 0 us
  blocking collectives: 126 us -> 0 us
  waiting for transfers between devices: 431 us -> 322 us
  other arithmetic: 112 us -> 71.7 us
  local copies, waits for them, and re-layouts: 72.4 us -> 39.4 us
  starting transfers between devices: 56.9 us -> 39.4 us
  between operations: 8.01 us -> 20.5 us
    pallas_call x4 -> x20, Pallas kernels: 24.6 us -> 285 us  [the longest x4 68.8 us: tall_dot(): pl.pallas_call(functools.partial(tall_kernel, epilogue, exchanged, len(le...]
    dot_general x40 -> x0, matrix products: 193 us -> none  [the longest x32 81.6 us: dot_tn(): lax.dot_general(left, right, (((0,), (0,)), ((), ())), preferred_element_...]
    ppermute x21 -> x12, waiting for transfers between devices: 170 us -> 117 us  [shift_outer(): return lax.ppermute(value, 'seq', pairs)]
    all_gather x1 -> x0, blocking collectives: 49 us -> none  [per_device(): packed = lax.all_gather(packed, 'seq', axis=0, tiled=False).astype(f32)]
    psum x2 -> x0, blocking collectives: 43.1 us -> none  [the longest x1 37 us: per_device(): grad_norm = jnp.sqrt(lax.psum(local_squares, ('seq', 'mp')))]
    unnamed x252 -> x145, local copies, waits for them, and re-layouts: 52.6 us -> 18.2 us
    unnamed x1 -> x0, blocking collectives: 33.9 us -> none
    ppermute x20 -> x8, waiting for transfers between devices: 35.6 us -> 3.56 us  [swap(): lax.ppermute(value, 'mp', [(m, m ^ bits) for m in range(lax.axis_size('mp...]
  transfers between devices with their start and end apart: 69 -> 36, of which waited for: 32 -> 18; matrix products, arithmetic and copies ran while one was open for 16% -> 8% of each run, Pallas kernels for 1% -> 40%
where the time goes in v2:
time: 848 us; the launch traced here: 838 us
  Pallas kernels  345 us (41%)
  waiting for transfers between devices  322 us (38%)
  other arithmetic  71.7 us (8%)
  starting transfers between devices  39.4 us (5%)
  local copies, waits for them, and re-layouts  39.4 us (5%)
  between operations  20.5 us (2%)
    ppermute x14, waiting for transfers between devices, shift_inner(): return lax.ppermute(value, 'seq', pairs)  202 us
    ppermute x12, waiting for transfers between devices, shift_outer(): return lax.ppermute(value, 'seq', pairs)  117 us
    pallas_call x4, Pallas kernels, tall_dot(): pl.pallas_call(functools.partial(tall_kernel, epilogue, exchanged, len(le...  68.8 us
    pallas_call x6, Pallas kernels, turned_dot(): pl.pallas_call(functools.partial(turned_kernel, [len(lefts) for lefts, _...  68.1 us
    pallas_call x4, Pallas kernels, wide_dot(): pl.pallas_call(functools.partial(wide_kernel, len(blocks), start), out_sh...  64.2 us
    pallas_call x1, Pallas kernels, reduce_vector(): pl.pallas_call(functools.partial(reduce_vector_kernel, seqs, parts, share...  50.4 us
    pallas_call x1, Pallas kernels, attend(): pl.pallas_call(functools.partial(attend_kernel, mp_count, rows_padded), o...  36.2 us
    pallas_call x1, Pallas kernels, attend_back(): pl.pallas_call(functools.partial(attend_back_kernel, mp_count, rows_padde...  23.4 us
  transfers between devices with their start and end apart: 36, of which 18 were waited for; matrix products, arithmetic and copies ran while one was open for 8% of the time, Pallas kernels for 40%

profile of v2, /device:TPU:0, one launch (start us, length us, event | category | flops | bytes accessed | tf_op | source)
XLA Modules:
  0.0 838.0 jit_solution(9464811801956968152)
XLA Ops:
  9.5 1.7 convert.37
  11.5 3.1 collective-permute-start.1
  14.5 26.7 %collective-permute-done.1.refs_2_.refs_1_.refs_3_ = bf16[272,2048]{1,0:T(8,128)(2,1)} collective-permute-done((bf16[272,2048]{1,0:T(8,128)(2,1)S(1)}, bf16[272,2048]{1,0:T(8,128)(2,1)}, u32[]{:S(2)}, u32[]{:S(2)}) %collective-permute-start.1) | collective-permute-done | bytes 1114144 | tf_op jit(solution)/shard_map/ppermute | solution.py:51
  44.3 24.8 %collective-permute-done.2.refs_3_.refs_2_.refs_4_ = bf16[272,2048]{1,0:T(8,128)(2,1)} collective-permute-done((bf16[272,2048]{1,0:T(8,128)(2,1)}, bf16[272,2048]{1,0:T(8,128)(2,1)}, u32[]{:S(2)}, u32[]{:S(2)}) %collective-permute-start.2) | collective-permute-done | bytes 1114144 | tf_op jit(solution)/shard_map/ppermute | solution.py:51
  75.0 21.1 %collective-permute-done.3.refs_4_.refs_3_.refs_5_ = bf16[272,2048]{1,0:T(8,128)(2,1)} collective-permute-done((bf16[272,2048]{1,0:T(8,128)(2,1)}, bf16[272,2048]{1,0:T(8,128)(2,1)}, u32[]{:S(2)}, u32[]{:S(2)}) %collective-permute-start.3) | collective-permute-done | bytes 1114144 | tf_op jit(solution)/shard_map/ppermute | solution.py:51
  109.7 15.0 %collective-permute-done.6.refs_7_.refs_6_.refs_8_ = bf16[272,2048]{1,0:T(8,128)(2,1)} collective-permute-done((bf16[272,2048]{1,0:T(8,128)(2,1)}, bf16[272,2048]{1,0:T(8,128)(2,1)}, u32[]{:S(2)}, u32[]{:S(2)}) %collective-permute-start.6) | collective-permute-done | bytes 1114144 | tf_op jit(solution)/shard_map/ppermute | solution.py:59
  127.5 21.0 %collective-permute-done.7.refs_8_.refs_7_.refs_9_ = bf16[272,2048]{1,0:T(8,128)(2,1)} collective-permute-done((bf16[272,2048]{1,0:T(8,128)(2,1)}, bf16[272,2048]{1,0:T(8,128)(2,1)}, u32[]{:S(2)}, u32[]{:S(2)}) %collective-permute-start.7) | collective-permute-done | bytes 1114144 | tf_op jit(solution)/shard_map/ppermute | solution.py:59
  152.3 9.2 %first_norm.1 = (bf16[1280,2048]{1,0:T(8,128)(2,1)}, bf16[320,2048]{1,0:T(8,128)(2,1)}) custom-call(bf16[320,2048]{1,0:T(8,128)(2,1)} %pad.29.refs_0_, bf16[320,2048]{1,0:T(8,128)(2,1)} %collective-permute-done.refs_1_, f32[1,2048]{1,0:T(1,128)} %bitcast.149, f32[1,2048]{1,0:T(1,128)} %bitcast.148), custom_call_target="tpu_custom_call" | custom-call | flops 5310000128 | tf_op jit(solution)/shard_map/first_norm/pallas_call | solution.py:383
  161.5 13.5 %project.1.q_ref.k_ref.v_ref = bf16[1280,1536]{1,0:T(8,128)(2,1)} custom-call(bf16[1280,2048]{1,0:T(8,128)(2,1)} %get-tuple-element.76.refs_0_, bf16[272,2048]{1,0:T(8,128)(2,1)} %copy-done.23, bf16[272,2048]{1,0:T(8,128)(2,1)} %collective-permute-done.1.refs_2_.refs_1_.refs_3_, bf16[272,2048]{1,0:T(8,128)(2,1)} %collective-permute-done.2.refs_3_.refs_2_.refs_4_, ...), custom_call_target="tpu_custom_call" | custom-call | flops 7484038144 | tf_op jit(solution)/shard_map/project/pallas_call | solution.py:467
  175.3 36.2 %attend.1 = (bf16[1280,512]{1,0:T(8,128)(2,1)S(1)}, bf16[8,1280,512]{2,1,0:T(8,128)(2,1)}) custom-call(s32[1]{0:T(128)} %bitcast.15.me_ref, bf16[1280,1536]{1,0:T(8,128)(2,1)} %project.1.q_ref.k_ref.v_ref, bf16[1280,1536]{1,0:T(8,128)(2,1)} %project.1.q_ref.k_ref.v_ref, bf16[1280,1536]{1,0:T(8,128)(2,1)} %project.1.q_ref.k_ref.v_ref, ...), custom_call_target="tpu_custom_call" | custom-call | flops 21240000512 | tf_op jit(solution)/shard_map/attend/pallas_call | solution.py:756
  212.6 11.6 %join.1 = (f32[320,2048]{1,0:T(8,128)}, bf16[320,2048]{1,0:T(8,128)(2,1)}) custom-call(bf16[1280,512]{1,0:T(8,128)(2,1)} %copy-done, bf16[272,2048]{1,0:T(8,128)(2,1)} %copy-done.23, bf16[272,2048]{1,0:T(8,128)(2,1)} %collective-permute-done.1.refs_2_.refs_1_.refs_3_, bf16[272,2048]{1,0:T(8,128)(2,1)} %collective-permute-done.2.refs_3_.refs_2_.refs_4_, ...), custom_call_target="tpu_custom_call" | custom-call | flops 3084679424 | tf_op jit(solution)/shard_map/join/pallas_call | solution.py:550
  228.6 3.3 pad_maximum_fusion
  234.3 18.5 %collective-permute-done.16.refs_2_.refs_1_ = bf16[256,2048]{1,0:T(8,128)(2,1)} collective-permute-done((bf16[256,2048]{1,0:T(8,128)(2,1)}, bf16[256,2048]{1,0:T(8,128)(2,1)}, u32[]{:S(2)}, u32[]{:S(2)}) %collective-permute-start.16) | collective-permute-done | bytes 1048608 | tf_op jit(solution)/shard_map/ppermute | solution.py:51
  253.2 2.9 collective-permute-done.8
  257.2 2.5 fusion.43
  261.5 17.9 %collective-permute-done.17.refs_3_.refs_2_ = bf16[256,2048]{1,0:T(8,128)(2,1)} collective-permute-done((bf16[256,2048]{1,0:T(8,128)(2,1)}, bf16[256,2048]{1,0:T(8,128)(2,1)}, u32[]{:S(2)}, u32[]{:S(2)}) %collective-permute-start.17) | collective-permute-done | bytes 1048608 | tf_op jit(solution)/shard_map/ppermute | solution.py:51
  279.4 1.6 add_convert_fusion.refs_0_
  284.3 9.0 %feed_grad.1 = (bf16[1280,2048]{1,0:T(8,128)(2,1)}, bf16[320,2048]{1,0:T(8,128)(2,1)}) custom-call(bf16[320,2048]{1,0:T(8,128)(2,1)} %pad.35.refs_0_, bf16[320,2048]{1,0:T(8,128)(2,1)} %collective-permute-done.15.refs_1_, f32[1280,1]{1,0:T(8,128)} %select_n.176.refs_2_), custom_call_target="tpu_custom_call" | custom-call | flops 5310000128 | tf_op jit(solution)/shard_map/feed_grad/pallas_call | solution.py:383
  294.0 30.3 %collective-permute-done.19.refs_5_.refs_4_ = bf16[256,2048]{1,0:T(8,128)(2,1)} collective-permute-done((bf16[256,2048]{1,0:T(8,128)(2,1)}, bf16[256,2048]{1,0:T(8,128)(2,1)}, u32[]{:S(2)}, u32[]{:S(2)}) %collective-permute-start.19) | collective-permute-done | bytes 1048608 | tf_op jit(solution)/shard_map/ppermute | solution.py:59
  324.3 2.0 pad_maximum_fusion.1
  326.3 1.6 collective-permute-start.20
  327.9 26.6 %up.1 = (bf16[1280,2048]{1,0:T(8,128)(2,1)}, bf16[1280,2048]{1,0:T(8,128)(2,1)}, bf16[640,2048]{1,0:T(8,128)(2,1)}) custom-call(bf16[320,2048]{1,0:T(8,128)(2,1)} %add_convert_fusion.refs_0_, bf16[320,2048]{1,0:T(8,128)(2,1)} %collective-permute-done.9.refs_1_, bf16[256,2048]{1,0:T(8,128)(2,1)} %get-tuple-element.81.refs_2_.refs_0_, ...), custom_call_target="tpu_custom_call" | custom-call | flops 9683718144 | tf_op jit(solution)/shard_map/up/pallas_call | solution.py:467
  354.5 10.6 %down_grad_far.1 = bf16[1024,2048]{1,0:T(8,128)(2,1)} custom-call(s32[4]{0:T(128)} %pad_add_fusion.2.spots_ref, bf16[1280,2048]{1,0:T(8,128)(2,1)} %get-tuple-element.87.refs_0_, bf16[1280,2048]{1,0:T(8,128)(2,1)} %get-tuple-element.97.left_ref.refs_1_), custom_call_target="tpu_custom_call" | custom-call | flops 5284358656 | tf_op jit(solution)/shard_map/down_grad_far/pallas_call | solution.py:611
  365.6 31.9 %collective-permute-done.20.refs_6_.refs_5_ = bf16[768,2048]{1,0:T(8,128)(2,1)} collective-permute-done((bf16[768,2048]{1,0:T(8,128)(2,1)S(1)}, bf16[768,2048]{1,0:T(8,128)(2,1)}, u32[]{:S(2)}, u32[]{:S(2)}) %collective-permute-start.20) | collective-permute-done | bytes 3145760 | tf_op jit(solution)/shard_map/ppermute | solution.py:59
  397.5 17.5 %down_back.1 = (bf16[1280,2048]{1,0:T(8,128)(2,1)}, f32[8,2048]{1,0:T(8,128)}) custom-call(bf16[1280,2048]{1,0:T(8,128)(2,1)} %get-tuple-element.87.refs_0_, bf16[256,2048]{1,0:T(8,128)(2,1)} %get-tuple-element.89.refs_1_.refs_0_, bf16[256,2048]{1,0:T(8,128)(2,1)} %collective-permute-done.16.refs_2_.refs_1_, ...), custom_call_target="tpu_custom_call" | custom-call | flops 9683718144 | tf_op jit(solution)/shard_map/down_back/pallas_call | solution.py:467
  415.0 18.1 %up_back.1 = (f32[320,2048]{1,0:T(8,128)}, bf16[320,2048]{1,0:T(8,128)(2,1)}) custom-call(bf16[1280,2048]{1,0:T(8,128)(2,1)} %get-tuple-element.94.left_ref.refs_3_, bf16[256,2048]{1,0:T(8,128)(2,1)} %get-tuple-element.81.refs_2_.refs_0_, bf16[256,2048]{1,0:T(8,128)(2,1)} %collective-permute-done.10.refs_3_.refs_1_, ...), custom_call_target="tpu_custom_call" | custom-call | flops 9683718144 | tf_op jit(solution)/shard_map/up_back/pallas_call | solution.py:550
  433.7 51.3 %collective-permute-done.25.refs_2_ = bf16[1024,2048]{1,0:T(8,128)(2,1)} collective-permute-done((bf16[1024,2048]{1,0:T(8,128)(2,1)}, bf16[1024,2048]{1,0:T(8,128)(2,1)}, u32[]{:S(2)}, u32[]{:S(2)}) %collective-permute-start.25) | collective-permute-done | bytes 4194336 | tf_op jit(solution)/shard_map/ppermute | solution.py:59
  485.0 11.5 %down_grad_near.1 = bf16[1024,2048]{1,0:T(8,128)(2,1)} custom-call(s32[4]{0:T(128)} %pad_add_fusion.2.spots_ref, bf16[1280,2048]{1,0:T(8,128)(2,1)} %get-tuple-element.87.refs_0_, bf16[1280,2048]{1,0:T(8,128)(2,1)} %get-tuple-element.97.left_ref.refs_1_, bf16[1024,2048]{1,0:T(8,128)(2,1)} %collective-permute-done.25.refs_2_), custom_call_target="tpu_custom_call" | custom-call | flops 5284358656 | tf_op jit(solution)/shard_map/down_grad_near/pallas_call | solution.py:611
  496.7 3.6 multiply_reduce_fusion
  500.3 1.8 fusion.15
  504.5 10.8 %up_grad_far.1 = bf16[1024,2048]{1,0:T(8,128)(2,1)} custom-call(s32[4]{0:T(128)} %pad_add_fusion.2.spots_ref, bf16[320,2048]{1,0:T(8,128)(2,1)} %add_convert_fusion.refs_0_, bf16[320,2048]{1,0:T(8,128)(2,1)} %collective-permute-done.9.refs_1_, bf16[640,2048]{1,0:T(8,128)(2,1)} %get-tuple-element.115.refs_2_, ...), custom_call_target="tpu_custom_call" | custom-call | flops 5284358656 | tf_op jit(solution)/shard_map/up_grad_far/pallas_call | solution.py:611
  517.7 18.2 %down.1 = (f32[320,2048]{1,0:T(8,128)}, bf16[320,2048]{1,0:T(8,128)(2,1)}) custom-call(bf16[1280,2048]{1,0:T(8,128)(2,1)} %get-tuple-element.97.left_ref.refs_1_, bf16[256,2048]{1,0:T(8,128)(2,1)} %get-tuple-element.89.refs_1_.refs_0_, bf16[256,2048]{1,0:T(8,128)(2,1)} %collective-permute-done.16.refs_2_.refs_1_, ...), custom_call_target="tpu_custom_call" | custom-call | flops 9683718144 | tf_op jit(solution)/shard_map/down/pallas_call | solution.py:550
  537.0 11.1 %join_back.1 = (bf16[1280,512]{1,0:T(8,128)(2,1)}, bf16[640,2048]{1,0:T(8,128)(2,1)}) custom-call(bf16[320,2048]{1,0:T(8,128)(2,1)} %copy-done.13, bf16[320,2048]{1,0:T(8,128)(2,1)} %copy-done.20, bf16[272,2048]{1,0:T(8,128)(2,1)} %copy-done.23, bf16[272,2048]{1,0:T(8,128)(2,1)} %collective-permute-done.1.refs_2_.refs_1_.refs_3_, ...), custom_call_target="tpu_custom_call" | custom-call | flops 3084679424 | tf_op jit(solution)/shard_map/join_back/pallas_call | solution.py:467
  548.2 23.4 %attend_back.1 = (bf16[1280,512]{1,0:T(8,128)(2,1)S(1)}, bf16[1280,512]{1,0:T(8,128)(2,1)S(1)}, bf16[1280,512]{1,0:T(8,128)(2,1)S(1)}) custom-call(s32[1]{0:T(128)} %bitcast.15.me_ref, bf16[1280,1536]{1,0:T(8,128)(2,1)} %project.1.q_ref.k_ref.v_ref, bf16[1280,1536]{1,0:T(8,128)(2,1)} %project.1.q_ref.k_ref.v_ref, ...), custom_call_target="tpu_custom_call" | custom-call | flops 13569999872 | tf_op jit(solution)/shard_map/attend_back/pallas_call | solution.py:871
  574.5 1.9 copy-done.17
  576.4 16.2 %project_back.1 = (f32[320,2048]{1,0:T(8,128)}, bf16[320,2048]{1,0:T(8,128)(2,1)}) custom-call(bf16[1280,1536]{1,0:T(8,128)(2,1)} %copy-done.17, bf16[272,2048]{1,0:T(8,128)(2,1)} %copy-done.23, bf16[272,2048]{1,0:T(8,128)(2,1)} %collective-permute-done.1.refs_2_.refs_1_.refs_3_, bf16[272,2048]{1,0:T(8,128)(2,1)} %collective-permute-done.2.refs_3_.refs_2_.refs_4_, ...), custom_call_target="tpu_custom_call" | custom-call | flops 7484038144 | tf_op jit(solution)/shard_map/project_back/pallas_call | solution.py:550
  594.2 12.1 %collective-permute-done.26.refs_4_ = bf16[1024,2048]{1,0:T(8,128)(2,1)} collective-permute-done((bf16[1024,2048]{1,0:T(8,128)(2,1)}, bf16[1024,2048]{1,0:T(8,128)(2,1)}, u32[]{:S(2)}, u32[]{:S(2)}) %collective-permute-start.26) | collective-permute-done | bytes 4194336 | tf_op jit(solution)/shard_map/ppermute | solution.py:59
  606.3 11.4 %up_grad_near.1 = bf16[1024,2048]{1,0:T(8,128)(2,1)} custom-call(s32[4]{0:T(128)} %pad_add_fusion.2.spots_ref, bf16[320,2048]{1,0:T(8,128)(2,1)} %add_convert_fusion.refs_0_, bf16[320,2048]{1,0:T(8,128)(2,1)} %collective-permute-done.9.refs_1_, bf16[640,2048]{1,0:T(8,128)(2,1)} %get-tuple-element.115.refs_2_, ...), custom_call_target="tpu_custom_call" | custom-call | flops 5284358656 | tf_op jit(solution)/shard_map/up_grad_near/pallas_call | solution.py:611
  619.7 11.2 %attn_grad_near.1 = bf16[1024,2048]{1,0:T(8,128)(2,1)} custom-call(s32[4]{0:T(128)} %pad_add_fusion.2.spots_ref, bf16[1280,2048]{1,0:T(8,128)(2,1)} %get-tuple-element.76.refs_0_, bf16[320,2048]{1,0:T(8,128)(2,1)} %copy-done.13, bf16[320,2048]{1,0:T(8,128)(2,1)} %copy-done.20, bf16[640,2048]{1,0:T(8,128)(2,1)} %get-tuple-element.101.refs_3_, ...), custom_call_target="tpu_custom_call" | custom-call | flops 5284358656 | tf_op jit(solution)/shard_map/attn_grad_near/pallas_call | solution.py:611
  630.9 12.6 %attn_grad_far.1 = (bf16[256,2048]{1,0:T(8,128)(2,1)}, bf16[256,2048]{1,0:T(8,128)(2,1)}, bf16[256,2048]{1,0:T(8,128)(2,1)}, bf16[256,2048]{1,0:T(8,128)(2,1)}) custom-call(s32[4]{0:T(128)} %pad_add_fusion.2.spots_ref, bf16[1280,2048]{1,0:T(8,128)(2,1)} %get-tuple-element.76.refs_0_, bf16[320,2048]{1,0:T(8,128)(2,1)} %copy-done.13, ...), custom_call_target="tpu_custom_call" | custom-call | flops 5284358656 | tf_op jit(solution)/shard_map/attn_grad_far/pallas_call | solution.py:611
  643.5 1.6 collective-permute-start.27
  647.3 18.4 %collective-permute-done.27 = bf16[256,2048]{1,0:T(8,128)(2,1)} collective-permute-done((bf16[256,2048]{1,0:T(8,128)(2,1)}, bf16[256,2048]{1,0:T(8,128)(2,1)}, u32[]{:S(2)}, u32[]{:S(2)}) %collective-permute-start.27) | collective-permute-done | bytes 1048608 | tf_op jit(solution)/shard_map/ppermute | solution.py:59
  665.7 1.9 add_convert_fusion.3
  667.6 4.4 collective-permute-start.31
  674.2 50.4 %reduce_vector.1 = f32[24,128]{1,0:T(8,128)} custom-call(f32[8,24,128]{2,1,0:T(8,128)} %bitcast.135), custom_call_target="tpu_custom_call" | custom-call | tf_op jit(solution)/shard_map/reduce_vector/pallas_call | solution.py:201
  725.4 2.4 add_convert_fusion.2
  731.7 3.6 multiply_add_fusion.1.in_ref
  735.2 14.9 %collective-permute-done.29 = bf16[256,2048]{1,0:T(8,128)(2,1)S(1)} collective-permute-done((bf16[256,2048]{1,0:T(8,128)(2,1)}, bf16[256,2048]{1,0:T(8,128)(2,1)S(1)}, u32[]{:S(2)}, u32[]{:S(2)}) %collective-permute-start.29) | collective-permute-done | bytes 1048608 | tf_op jit(solution)/shard_map/ppermute | solution.py:59
  750.8 2.0 collective-permute-done.32
  752.8 2.8 add_convert_fusion.1
  755.6 3.3 collective-permute-start.33
  760.2 1.8 from_blocks.2
  763.1 2.8 fusion.12.in_ref
  765.9 1.8 from_blocks.3
  767.7 7.0 collective-permute-done.30
  774.8 6.0 collective-permute-done.33
  780.7 2.4 convert_add_fusion.4
  785.5 3.2 fusion.2
  791.9 11.7 %reduce_scalar.1 = f32[8,128]{1,0:T(8,128)} custom-call(f32[8,128]{1,0:T(8,128)} %broadcast_in_dim.112.in_ref), custom_call_target="tpu_custom_call" | custom-call | tf_op jit(solution)/shard_map/reduce_scalar/pallas_call | solution.py:253
  809.2 5.3 fusion.41
  814.5 1.9 multiply_add_fusion.2
  816.6 1.8 copy-done.12
  818.9 7.5 fusion.38
  826.5 3.4 multiply_add_fusion
  (307 shorter events, 79.9 us)
Async XLA Ops:
  7.2 778.2 %reduce-scatter.5.cloned.1.call-start = ((), (), s32[]{:S(2)}) async-start(), calls=%async_computation.3 | async-start | bytes 5242880 | tf_op jit(solution)/shard_map/reduce_scatter | solution.py:649
  11.2 32.2 %copy-start.11 = (f32[2,256,2048]{2,1,0:T(8,128)S(1)}, f32[2,256,2048]{2,1,0:T(8,128)}, u32[]{:S(2)}) copy-start(f32[2,256,2048]{2,1,0:T(8,128)} %param.37) | copy-start | bytes 12582916
  11.5 32.3 %copy-start.23 = (bf16[272,2048]{1,0:T(8,128)(2,1)}, bf16[272,2048]{1,0:T(8,128)(2,1)S(1)}, u32[]{:S(2)}) copy-start(bf16[272,2048]{1,0:T(8,128)(2,1)S(1)} %pad_maximum_fusion.4.refs_1_.refs_0_.refs_2_) | copy-start | bytes 3342340
  11.5 29.8 %collective-permute-start.1 = (bf16[272,2048]{1,0:T(8,128)(2,1)S(1)}, bf16[272,2048]{1,0:T(8,128)(2,1)}, u32[]{:S(2)}, u32[]{:S(2)}) collective-permute-start(bf16[272,2048]{1,0:T(8,128)(2,1)S(1)} %pad_maximum_fusion.4.refs_1_.refs_0_.refs_2_), channel_id=1, source_target_pairs={{0,8},{4,12},{8,16},{12,20},{16,24},{20,28},{24,0},{28,4},{1,9},{5... | collective-permute-start | bytes 3342344 | tf_op jit(solution)/shard_map/ppermute | solution.py:51
  41.2 27.9 %collective-permute-start.2 = (bf16[272,2048]{1,0:T(8,128)(2,1)}, bf16[272,2048]{1,0:T(8,128)(2,1)}, u32[]{:S(2)}, u32[]{:S(2)}) collective-permute-start(bf16[272,2048]{1,0:T(8,128)(2,1)} %collective-permute-done.1.refs_2_.refs_1_.refs_3_), channel_id=1, source_target_pairs={{0,8},{4,12},{8,16},{12,20},{16,24},{20,28},{24,0},{28,4},{1,9},{5... | collective-permute-start | bytes 3342344 | tf_op jit(solution)/shard_map/ppermute | solution.py:51
  41.2 61.1 %collective-permute-start.4 = (bf16[272,2048]{1,0:T(8,128)(2,1)S(1)}, bf16[272,2048]{1,0:T(8,128)(2,1)S(1)}, u32[]{:S(2)}, u32[]{:S(2)}) collective-permute-start(bf16[272,2048]{1,0:T(8,128)(2,1)S(1)} %pad_maximum_fusion.4.refs_1_.refs_0_.refs_2_), channel_id=1, source_target_pairs={{0,4},{4,0},{8,12},{12,8},{16,20},{20,16},{24,28},{28,24},{1,5},{5... | collective-permute-start | bytes 3342344 | tf_op jit(solution)/shard_map/ppermute | solution.py:59
  43.5 26.2 %copy-start.39 = (pred[320,320]{1,0:T(32,128)(4,1)S(1)}, pred[320,320]{1,0:T(32,128)(4,1)}, u32[]{:S(2)}) copy-start(pred[320,320]{1,0:T(32,128)(4,1)} %constant.299.clone) | copy-start | bytes 307204
  43.5 26.2 %copy-start.40 = (pred[320,320]{1,0:T(32,128)(4,1)S(1)}, pred[320,320]{1,0:T(32,128)(4,1)}, u32[]{:S(2)}) copy-start(pred[320,320]{1,0:T(32,128)(4,1)} %constant.298.clone) | copy-start | bytes 307204
  69.1 26.9 %collective-permute-start.3 = (bf16[272,2048]{1,0:T(8,128)(2,1)}, bf16[272,2048]{1,0:T(8,128)(2,1)}, u32[]{:S(2)}, u32[]{:S(2)}) collective-permute-start(bf16[272,2048]{1,0:T(8,128)(2,1)} %collective-permute-done.2.refs_3_.refs_2_.refs_4_), channel_id=1, source_target_pairs={{0,8},{4,12},{8,16},{12,20},{16,24},{20,28},{24,0},{28,4},{1,9},{5... | collective-permute-start | bytes 3342344 | tf_op jit(solution)/shard_map/ppermute | solution.py:51
  70.6 28.4 %copy-start.33 = (bf16[306,2048]{1,0:T(8,128)(2,1)S(1)}, bf16[306,2048]{1,0:T(8,128)(2,1)}, u32[]{:S(2)}) copy-start(bf16[306,2048]{1,0:T(8,128)(2,1)} %param.29) | copy-start | bytes 3760132
  72.9 35.9 %collective-permute-start.5 = (bf16[272,2048]{1,0:T(8,128)(2,1)}, bf16[272,2048]{1,0:T(8,128)(2,1)}, u32[]{:S(2)}, u32[]{:S(2)}) collective-permute-start(bf16[272,2048]{1,0:T(8,128)(2,1)} %collective-permute-done.1.refs_2_.refs_1_.refs_3_), channel_id=1, source_target_pairs={{0,4},{4,0},{8,12},{12,8},{16,20},{20,16},{24,28},{28,24},{1,5},{5... | collective-permute-start | bytes 3342344 | tf_op jit(solution)/shard_map/ppermute | solution.py:59
  74.2 50.4 %collective-permute-start.6 = (bf16[272,2048]{1,0:T(8,128)(2,1)}, bf16[272,2048]{1,0:T(8,128)(2,1)}, u32[]{:S(2)}, u32[]{:S(2)}) collective-permute-start(bf16[272,2048]{1,0:T(8,128)(2,1)} %collective-permute-done.2.refs_3_.refs_2_.refs_4_), channel_id=1, source_target_pairs={{0,4},{4,0},{8,12},{12,8},{16,20},{20,16},{24,28},{28,24},{1,5},{5... | collective-permute-start | bytes 3342344 | tf_op jit(solution)/shard_map/ppermute | solution.py:59
  96.0 52.5 %collective-permute-start.7 = (bf16[272,2048]{1,0:T(8,128)(2,1)}, bf16[272,2048]{1,0:T(8,128)(2,1)}, u32[]{:S(2)}, u32[]{:S(2)}) collective-permute-start(bf16[272,2048]{1,0:T(8,128)(2,1)} %collective-permute-done.3.refs_4_.refs_3_.refs_5_), channel_id=1, source_target_pairs={{0,4},{4,0},{8,12},{12,8},{16,20},{20,16},{24,28},{28,24},{1,5},{5... | collective-permute-start | bytes 3342344 | tf_op jit(solution)/shard_map/ppermute | solution.py:59
  100.4 27.1 %collective-permute-start.10 = (bf16[256,2048]{1,0:T(8,128)(2,1)}, bf16[256,2048]{1,0:T(8,128)(2,1)}, u32[]{:S(2)}, u32[]{:S(2)}) collective-permute-start(bf16[256,2048]{1,0:T(8,128)(2,1)} %get-tuple-element.81.refs_2_.refs_0_), channel_id=1, source_target_pairs={{0,8},{4,12},{8,16},{12,20},{16,24},{20,28},{24,0},{28,4},{1,9},{5... | collective-permute-start | bytes 3145736 | tf_op jit(solution)/shard_map/ppermute | solution.py:51
  102.3 50.0 %collective-permute-start = (bf16[320,2048]{1,0:T(8,128)(2,1)}, bf16[320,2048]{1,0:T(8,128)(2,1)}, u32[]{:S(2)}, u32[]{:S(2)}) collective-permute-start(bf16[320,2048]{1,0:T(8,128)(2,1)} %pad.29.refs_0_), channel_id=1, source_target_pairs={{0,2},{1,3},{2,0},{3,1},{4,6},{5,7},{6,4},{7,5},{8,10},{9,11},{10,... | collective-permute-start | bytes 3932168 | tf_op jit(solution)/shard_map/ppermute | solution.py:63
  105.2 44.9 %copy-start.49 = (pred[8]{0:T(512)(128)(4,1)S(1)}, pred[8]{0:T(512)(128)(4,1)}, u32[]{:S(2)}) copy-start(pred[8]{0:T(512)(128)(4,1)} %compare_and_fusion) | copy-start | bytes 28
  124.6 103.9 %collective-permute-start.13 = (bf16[256,2048]{1,0:T(8,128)(2,1)}, bf16[256,2048]{1,0:T(8,128)(2,1)}, u32[]{:S(2)}, u32[]{:S(2)}) collective-permute-start(bf16[256,2048]{1,0:T(8,128)(2,1)} %get-tuple-element.81.refs_2_.refs_0_), channel_id=1, source_target_pairs={{0,4},{4,0},{8,12},{12,8},{16,20},{20,16},{24,28},{28,24},{1,5},{5... | collective-permute-start | bytes 3145736 | tf_op jit(solution)/shard_map/ppermute | solution.py:59
  127.4 47.6 %collective-permute-start.11 = (bf16[256,2048]{1,0:T(8,128)(2,1)}, bf16[256,2048]{1,0:T(8,128)(2,1)}, u32[]{:S(2)}, u32[]{:S(2)}) collective-permute-start(bf16[256,2048]{1,0:T(8,128)(2,1)} %collective-permute-done.10.refs_3_.refs_1_), channel_id=1, source_target_pairs={{0,8},{4,12},{8,16},{12,20},{16,24},{20,28},{24,0},{28,4},{1,9},{5... | collective-permute-start | bytes 3145736 | tf_op jit(solution)/shard_map/ppermute | solution.py:51
  175.0 50.5 %collective-permute-start.12 = (bf16[256,2048]{1,0:T(8,128)(2,1)}, bf16[256,2048]{1,0:T(8,128)(2,1)S(1)}, u32[]{:S(2)}, u32[]{:S(2)}) collective-permute-start(bf16[256,2048]{1,0:T(8,128)(2,1)} %collective-permute-done.11.refs_4_.refs_2_), channel_id=1, source_target_pairs={{0,8},{4,12},{8,16},{12,20},{16,24},{20,28},{24,0},{28,4},{1,9},{5... | collective-permute-start | bytes 3145736 | tf_op jit(solution)/shard_map/ppermute | solution.py:51
  212.6 14.0 %copy-start.34 = (bf16[306,2048]{1,0:T(8,128)(2,1)S(1)}, bf16[306,2048]{1,0:T(8,128)(2,1)}, u32[]{:S(2)}) copy-start(bf16[306,2048]{1,0:T(8,128)(2,1)} %param.30) | copy-start | bytes 3760132
  224.2 31.9 %collective-permute-start.8 = (bf16[320,2048]{1,0:T(8,128)(2,1)}, bf16[320,2048]{1,0:T(8,128)(2,1)S(1)}, u32[]{:S(2)}, u32[]{:S(2)}) collective-permute-start(bf16[320,2048]{1,0:T(8,128)(2,1)} %get-tuple-element.79), channel_id=1, source_target_pairs={{0,2},{1,3},{2,0},{3,1},{4,6},{5,7},{6,4},{7,5},{8,10},{9,11},{10,... | collective-permute-start | bytes 3932168 | tf_op jit(solution)/shard_map/ppermute | solution.py:63
  225.6 27.3 %collective-permute-start.16 = (bf16[256,2048]{1,0:T(8,128)(2,1)}, bf16[256,2048]{1,0:T(8,128)(2,1)}, u32[]{:S(2)}, u32[]{:S(2)}) collective-permute-start(bf16[256,2048]{1,0:T(8,128)(2,1)} %get-tuple-element.89.refs_1_.refs_0_), channel_id=1, source_target_pairs={{0,8},{4,12},{8,16},{12,20},{16,24},{20,28},{24,0},{28,4},{1,9},{5... | collective-permute-start | bytes 3145736 | tf_op jit(solution)/shard_map/ppermute | solution.py:51
  228.6 28.6 %copy-start.28 = (f32[320,2048]{1,0:T(8,128)S(1)}, f32[320,2048]{1,0:T(8,128)}, u32[]{:S(2)}) copy-start(f32[320,2048]{1,0:T(8,128)} %get-tuple-element.78) | copy-start | bytes 7864324
  231.9 92.4 %collective-permute-start.14 = (bf16[768,2048]{1,0:T(8,128)(2,1)}, bf16[768,2048]{1,0:T(8,128)(2,1)}, u32[]{:S(2)}, u32[]{:S(2)}) collective-permute-start(bf16[768,2048]{1,0:T(8,128)(2,1)} %pad_maximum_fusion), channel_id=1, source_target_pairs={{0,4},{4,0},{8,12},{12,8},{16,20},{20,16},{24,28},{28,24},{1,5},{5... | collective-permute-start | bytes 9437192 | tf_op jit(solution)/shard_map/ppermute | solution.py:59
  233.4 50.9 %collective-permute-start.15 = (bf16[320,2048]{1,0:T(8,128)(2,1)}, bf16[320,2048]{1,0:T(8,128)(2,1)}, u32[]{:S(2)}, u32[]{:S(2)}) collective-permute-start(bf16[320,2048]{1,0:T(8,128)(2,1)} %pad.35.refs_0_), channel_id=1, source_target_pairs={{0,2},{1,3},{2,0},{3,1},{4,6},{5,7},{6,4},{7,5},{8,10},{9,11},{10,... | collective-permute-start | bytes 3932168 | tf_op jit(solution)/shard_map/ppermute | solution.py:63
  252.9 26.5 %collective-permute-start.17 = (bf16[256,2048]{1,0:T(8,128)(2,1)}, bf16[256,2048]{1,0:T(8,128)(2,1)}, u32[]{:S(2)}, u32[]{:S(2)}) collective-permute-start(bf16[256,2048]{1,0:T(8,128)(2,1)} %collective-permute-done.16.refs_2_.refs_1_), channel_id=1, source_target_pairs={{0,8},{4,12},{8,16},{12,20},{16,24},{20,28},{24,0},{28,4},{1,9},{5... | collective-permute-start | bytes 3145736 | tf_op jit(solution)/shard_map/ppermute | solution.py:51
  259.7 240.6 %copy-start.4 = (f32[320,2048]{1,0:T(8,128)}, f32[320,2048]{1,0:T(8,128)S(1)}, u32[]{:S(2)}) copy-start(f32[320,2048]{1,0:T(8,128)S(1)} %get-tuple-element.161) | copy-start | bytes 7864324
  260.2 64.1 %collective-permute-start.19 = (bf16[256,2048]{1,0:T(8,128)(2,1)}, bf16[256,2048]{1,0:T(8,128)(2,1)}, u32[]{:S(2)}, u32[]{:S(2)}) collective-permute-start(bf16[256,2048]{1,0:T(8,128)(2,1)} %get-tuple-element.89.refs_1_.refs_0_), channel_id=1, source_target_pairs={{0,4},{4,0},{8,12},{12,8},{16,20},{20,16},{24,28},{28,24},{1,5},{5... | collective-permute-start | bytes 3145736 | tf_op jit(solution)/shard_map/ppermute | solution.py:59
  279.4 44.9 %collective-permute-start.18 = (bf16[256,2048]{1,0:T(8,128)(2,1)}, bf16[256,2048]{1,0:T(8,128)(2,1)}, u32[]{:S(2)}, u32[]{:S(2)}) collective-permute-start(bf16[256,2048]{1,0:T(8,128)(2,1)} %collective-permute-done.17.refs_3_.refs_2_), channel_id=1, source_target_pairs={{0,8},{4,12},{8,16},{12,20},{16,24},{20,28},{24,0},{28,4},{1,9},{5... | collective-permute-start | bytes 3145736 | tf_op jit(solution)/shard_map/ppermute | solution.py:51
  281.0 46.9 %collective-permute-start.9 = (bf16[320,2048]{1,0:T(8,128)(2,1)}, bf16[320,2048]{1,0:T(8,128)(2,1)}, u32[]{:S(2)}, u32[]{:S(2)}) collective-permute-start(bf16[320,2048]{1,0:T(8,128)(2,1)} %add_convert_fusion.refs_0_), channel_id=1, source_target_pairs={{0,2},{1,3},{2,0},{3,1},{4,6},{5,7},{6,4},{7,5},{8,10},{9,11},{10,... | collective-permute-start | bytes 3932168 | tf_op jit(solution)/shard_map/ppermute | solution.py:63
  326.3 71.2 %collective-permute-start.20 = (bf16[768,2048]{1,0:T(8,128)(2,1)S(1)}, bf16[768,2048]{1,0:T(8,128)(2,1)}, u32[]{:S(2)}, u32[]{:S(2)}) collective-permute-start(bf16[768,2048]{1,0:T(8,128)(2,1)S(1)} %pad_maximum_fusion.1), channel_id=1, source_target_pairs={{0,4},{4,0},{8,12},{12,8},{16,20},{20,16},{24,28},{28,24},{1,5},{5... | collective-permute-start | bytes 9437192 | tf_op jit(solution)/shard_map/ppermute | solution.py:59
  365.1 119.9 %collective-permute-start.25 = (bf16[1024,2048]{1,0:T(8,128)(2,1)}, bf16[1024,2048]{1,0:T(8,128)(2,1)}, u32[]{:S(2)}, u32[]{:S(2)}) collective-permute-start(bf16[1024,2048]{1,0:T(8,128)(2,1)} %down_grad_far.1), channel_id=1, source_target_pairs={{0,4},{4,0},{8,12},{12,8},{16,20},{20,16},{24,28},{28,24},{1,5},{5... | collective-permute-start | bytes 12582920 | tf_op jit(solution)/shard_map/ppermute | solution.py:59
  433.1 63.5 %collective-permute-start.21 = (bf16[320,2048]{1,0:T(8,128)(2,1)}, bf16[320,2048]{1,0:T(8,128)(2,1)}, u32[]{:S(2)}, u32[]{:S(2)}) collective-permute-start(bf16[320,2048]{1,0:T(8,128)(2,1)} %get-tuple-element.96), channel_id=1, source_target_pairs={{0,2},{1,3},{2,0},{3,1},{4,6},{5,7},{6,4},{7,5},{8,10},{9,11},{10,... | collective-permute-start | bytes 3932168 | tf_op jit(solution)/shard_map/ppermute | solution.py:63
  496.5 289.0 %reduce-scatter.3.cloned.1.call-start = ((), (), s32[]{:S(2)}) async-start(), calls=%async_computation.2 | async-start | bytes 5242880 | tf_op jit(solution)/shard_map/reduce_scatter | solution.py:649
  503.9 11.4 %copy-start.13 = (bf16[320,2048]{1,0:T(8,128)(2,1)}, bf16[320,2048]{1,0:T(8,128)(2,1)S(1)}, u32[]{:S(2)}) copy-start(bf16[320,2048]{1,0:T(8,128)(2,1)S(1)} %multiply_convert_fusion.refs_0_.refs_1_) | copy-start | bytes 3932164
  503.9 32.1 %collective-permute-start.22 = (bf16[320,2048]{1,0:T(8,128)(2,1)S(1)}, bf16[320,2048]{1,0:T(8,128)(2,1)S(1)}, u32[]{:S(2)}, u32[]{:S(2)}) collective-permute-start(bf16[320,2048]{1,0:T(8,128)(2,1)S(1)} %multiply_convert_fusion.refs_0_.refs_1_), channel_id=1, source_target_pairs={{0,2},{1,3},{2,0},{3,1},{4,6},{5,7},{6,4},{7,5},{8,10},{9,11},{10,... | collective-permute-start | bytes 3932168 | tf_op jit(solution)/shard_map/ppermute | solution.py:63
  515.3 91.0 %collective-permute-start.26 = (bf16[1024,2048]{1,0:T(8,128)(2,1)}, bf16[1024,2048]{1,0:T(8,128)(2,1)}, u32[]{:S(2)}, u32[]{:S(2)}) collective-permute-start(bf16[1024,2048]{1,0:T(8,128)(2,1)} %up_grad_far.1), channel_id=1, source_target_pairs={{0,4},{4,0},{8,12},{12,8},{16,20},{20,16},{24,28},{28,24},{1,5},{5... | collective-permute-start | bytes 12582920 | tf_op jit(solution)/shard_map/ppermute | solution.py:59
  536.0 12.2 %copy-start.1 = (bf16[1280,512]{1,0:T(8,128)(2,1)S(1)}, bf16[1280,512]{1,0:T(8,128)(2,1)}, u32[]{:S(2)}) copy-start(bf16[1280,512]{1,0:T(8,128)(2,1)} %copy-done) | copy-start | bytes 3932164
  592.6 52.5 %collective-permute-start.24 = (bf16[320,2048]{1,0:T(8,128)(2,1)}, bf16[320,2048]{1,0:T(8,128)(2,1)S(1)}, u32[]{:S(2)}, u32[]{:S(2)}) collective-permute-start(bf16[320,2048]{1,0:T(8,128)(2,1)} %get-tuple-element.110), channel_id=1, source_target_pairs={{0,2},{1,3},{2,0},{3,1},{4,6},{5,7},{6,4},{7,5},{8,10},{9,11},{10,... | collective-permute-start | bytes 3932168 | tf_op jit(solution)/shard_map/ppermute | solution.py:63
  618.2 112.5 %collective-permute-start.23 = (bf16[320,2048]{1,0:T(8,128)(2,1)}, bf16[320,2048]{1,0:T(8,128)(2,1)S(1)}, u32[]{:S(2)}, u32[]{:S(2)}) collective-permute-start(bf16[320,2048]{1,0:T(8,128)(2,1)} %get-tuple-element.103), channel_id=1, source_target_pairs={{0,2},{1,3},{2,0},{3,1},{4,6},{5,7},{6,4},{7,5},{8,10},{9,11},{10,... | collective-permute-start | bytes 3932168 | tf_op jit(solution)/shard_map/ppermute | solution.py:63
  630.9 14.2 %copy-start.8 = (bf16[320,2048]{1,0:T(8,128)(2,1)S(1)}, bf16[320,2048]{1,0:T(8,128)(2,1)}, u32[]{:S(2)}) copy-start(bf16[320,2048]{1,0:T(8,128)(2,1)} %get-tuple-element.75) | copy-start | bytes 3932164
  630.9 14.2 %copy-start.14 = (f32[320,2048]{1,0:T(8,128)S(1)}, f32[320,2048]{1,0:T(8,128)}, u32[]{:S(2)}) copy-start(f32[320,2048]{1,0:T(8,128)} %get-tuple-element.109) | copy-start | bytes 7864324
  643.5 22.2 %collective-permute-start.27 = (bf16[256,2048]{1,0:T(8,128)(2,1)}, bf16[256,2048]{1,0:T(8,128)(2,1)}, u32[]{:S(2)}, u32[]{:S(2)}) collective-permute-start(bf16[256,2048]{1,0:T(8,128)(2,1)} %get-tuple-element.117), channel_id=1, source_target_pairs={{0,4},{4,0},{8,12},{12,8},{16,20},{20,16},{24,28},{28,24},{1,5},{5... | collective-permute-start | bytes 3145736 | tf_op jit(solution)/shard_map/ppermute | solution.py:59
  646.5 27.0 %copy-start.50 = (pred[8]{0:T(512)(128)(4,1)S(1)}, pred[8]{0:T(512)(128)(4,1)}, u32[]{:S(2)}) copy-start(pred[8]{0:T(512)(128)(4,1)} %compare_and_fusion) | copy-start | bytes 28
  667.6 57.8 %collective-permute-start.31 = (bf16[256,2048]{1,0:T(8,128)(2,1)S(1)}, bf16[256,2048]{1,0:T(8,128)(2,1)}, u32[]{:S(2)}, u32[]{:S(2)}) collective-permute-start(bf16[256,2048]{1,0:T(8,128)(2,1)S(1)} %add_convert_fusion.3), channel_id=1, source_target_pairs={{0,24},{4,28},{8,0},{12,4},{16,8},{20,12},{24,16},{28,20},{1,25},{... | collective-permute-start | bytes 3145736 | tf_op jit(solution)/shard_map/ppermute | solution.py:51
  672.0 52.6 %collective-permute-start.28 = (bf16[256,2048]{1,0:T(8,128)(2,1)}, bf16[256,2048]{1,0:T(8,128)(2,1)}, u32[]{:S(2)}, u32[]{:S(2)}) collective-permute-start(bf16[256,2048]{1,0:T(8,128)(2,1)} %get-tuple-element.118), channel_id=1, source_target_pairs={{0,4},{4,0},{8,12},{12,8},{16,20},{20,16},{24,28},{28,24},{1,5},{5... | collective-permute-start | bytes 3145736 | tf_op jit(solution)/shard_map/ppermute | solution.py:59
  724.7 25.5 %collective-permute-start.29 = (bf16[256,2048]{1,0:T(8,128)(2,1)}, bf16[256,2048]{1,0:T(8,128)(2,1)S(1)}, u32[]{:S(2)}, u32[]{:S(2)}) collective-permute-start(bf16[256,2048]{1,0:T(8,128)(2,1)} %get-tuple-element.119), channel_id=1, source_target_pairs={{0,4},{4,0},{8,12},{12,8},{16,20},{20,16},{24,28},{28,24},{1,5},{5... | collective-permute-start | bytes 3145736 | tf_op jit(solution)/shard_map/ppermute | solution.py:59
  727.9 24.9 %collective-permute-start.32 = (bf16[256,2048]{1,0:T(8,128)(2,1)S(1)}, bf16[256,2048]{1,0:T(8,128)(2,1)S(1)}, u32[]{:S(2)}, u32[]{:S(2)}) collective-permute-start(bf16[256,2048]{1,0:T(8,128)(2,1)S(1)} %add_convert_fusion.2), channel_id=1, source_target_pairs={{0,24},{4,28},{8,0},{12,4},{16,8},{20,12},{24,16},{28,20},{1,25},{... | collective-permute-start | bytes 3145736 | tf_op jit(solution)/shard_map/ppermute | solution.py:51
  750.1 24.7 %collective-permute-start.30 = (bf16[256,2048]{1,0:T(8,128)(2,1)}, bf16[256,2048]{1,0:T(8,128)(2,1)}, u32[]{:S(2)}, u32[]{:S(2)}) collective-permute-start(bf16[256,2048]{1,0:T(8,128)(2,1)} %get-tuple-element.120), channel_id=1, source_target_pairs={{0,4},{4,0},{8,12},{12,8},{16,20},{20,16},{24,28},{28,24},{1,5},{5... | collective-permute-start | bytes 3145736 | tf_op jit(solution)/shard_map/ppermute | solution.py:59
  755.6 25.2 %collective-permute-start.33 = (bf16[256,2048]{1,0:T(8,128)(2,1)}, bf16[256,2048]{1,0:T(8,128)(2,1)}, u32[]{:S(2)}, u32[]{:S(2)}) collective-permute-start(bf16[256,2048]{1,0:T(8,128)(2,1)} %add_convert_fusion.1), channel_id=1, source_target_pairs={{0,24},{4,28},{8,0},{12,4},{16,8},{20,12},{24,16},{28,20},{1,25},{... | collective-permute-start | bytes 3145736 | tf_op jit(solution)/shard_map/ppermute | solution.py:51
  783.4 22.3 %copy-start.52 = (f32[2,64]{1,0:T(2,128)S(1)}, f32[2,64]{1,0:T(2,128)}, u32[]{:S(2)}) copy-start(f32[2,64]{1,0:T(2,128)} %param.45) | copy-start | bytes 1540
  783.4 22.2 %copy-start.53 = (f32[2,64]{1,0:T(2,128)S(1)}, f32[2,64]{1,0:T(2,128)}, u32[]{:S(2)}) copy-start(f32[2,64]{1,0:T(2,128)} %param.46) | copy-start | bytes 1540
  783.4 22.2 %copy-start.54 = (f32[2,64]{1,0:T(2,128)S(1)}, f32[2,64]{1,0:T(2,128)}, u32[]{:S(2)}) copy-start(f32[2,64]{1,0:T(2,128)} %param.47) | copy-start | bytes 1540
  783.4 22.8 %copy-start.55 = (f32[2,64]{1,0:T(2,128)S(1)}, f32[2,64]{1,0:T(2,128)}, u32[]{:S(2)}) copy-start(f32[2,64]{1,0:T(2,128)} %param.48) | copy-start | bytes 1540
  783.4 23.4 %copy-start.57 = (f32[256]{0:T(256)S(1)}, f32[256]{0:T(256)}, u32[]{:S(2)}) copy-start(f32[256]{0:T(256)} %param.49) | copy-start | bytes 3076
  783.4 23.4 %copy-start.58 = (f32[256]{0:T(256)S(1)}, f32[256]{0:T(256)}, u32[]{:S(2)}) copy-start(f32[256]{0:T(256)} %param.50) | copy-start | bytes 3076
  783.4 23.3 %copy-start.59 = (f32[256]{0:T(256)S(1)}, f32[256]{0:T(256)}, u32[]{:S(2)}) copy-start(f32[256]{0:T(256)} %param.51) | copy-start | bytes 3076
  783.5 23.9 %copy-start.56 = (f32[256]{0:T(256)S(1)}, f32[256]{0:T(256)}, u32[]{:S(2)}) copy-start(f32[256]{0:T(256)} %param.52) | copy-start | bytes 3076
  783.5 24.5 %copy-start.43 = (f32[6,256]{1,0:T(8,128)S(1)}, f32[6,256]{1,0:T(8,128)}, u32[]{:S(2)}) copy-start(f32[6,256]{1,0:T(8,128)} %param.41) | copy-start | bytes 18436
  783.5 24.5 %copy-start.44 = (f32[6,256]{1,0:T(8,128)S(1)}, f32[6,256]{1,0:T(8,128)}, u32[]{:S(2)}) copy-start(f32[6,256]{1,0:T(8,128)} %param.42) | copy-start | bytes 18436
  783.5 24.4 %copy-start.45 = (f32[6,256]{1,0:T(8,128)S(1)}, f32[6,256]{1,0:T(8,128)}, u32[]{:S(2)}) copy-start(f32[6,256]{1,0:T(8,128)} %param.43) | copy-start | bytes 18436
  783.5 25.1 %copy-start.46 = (f32[6,256]{1,0:T(8,128)S(1)}, f32[6,256]{1,0:T(8,128)}, u32[]{:S(2)}) copy-start(f32[6,256]{1,0:T(8,128)} %param.44) | copy-start | bytes 18436
  783.5 25.7 %copy-start.16 = (f32[4,256,512]{2,1,0:T(8,128)S(1)}, f32[4,256,512]{2,1,0:T(8,128)}, u32[]{:S(2)}) copy-start(f32[4,256,512]{2,1,0:T(8,128)} %param.33) | copy-start | bytes 6291460
  806.2 8.3 copy-start.47
  (34 other events, 102.1 us)
Sparse Core Ops, SparseCore 0:
  496.6 77.5 reduce-scatter.4
  617.9 100.4 reduce-scatter.2

commit v3 on v2

--- a/solution.py
+++ b/solution.py
@@ -90,30 +90,12 @@
 
 
 def after(value, *others):
-    return lax.optimization_barrier((value, *others))[0]
+    return lax.optimization_barrier((value, *others))[0] if others else value
 
 
 def row_codes():
     count = lax.axis_size("mp")
     return [high * 2 + low for low in range(2) for high in range(count // 2)]
-
-
-def outer_groups():
-    outer, inner = seq_grid()
-    return [[a * inner + b for a in range(outer)] for b in range(inner)]
-
-
-def block_spots():
-    outer, inner = seq_grid()
-    place = lax.axis_index("seq") // inner
-    return jnp.stack([(place - i + outer) % outer for i in range(outer)]).astype(jnp.int32)
-
-
-def ring_line(own):
-    line = [own]
-    for _ in range(seq_grid()[0] - 1):
-        line.append(shift_outer(line[-1], 1))
-    return line
 
 
 def ring_rest(part):
@@ -124,22 +106,17 @@
     return rest
 
 
-def ring_scatter(parts, received):
-    total = None
-    for i in reversed(range(len(parts))):
-        part = parts[i].astype(f32) + received[i].astype(f32)
-        if total is not None:
-            part = part + shift_outer(total.astype(bf16), -1).astype(f32)
-        total = part
-    return total
-
-
-def inner_sum(parts):
-    inner = seq_grid()[1]
-    part = shift_inner(parts[inner - 1], -1)
-    for j in reversed(range(1, inner - 1)):
-        part = shift_inner((parts[j].astype(f32) + part.astype(f32)).astype(bf16), -1)
-    return part
+def ring_scatter(near, received, held=(), sums=()):
+    sums = list(sums)
+    depth = received[0].shape[0]
+    for n in range(len(sums), len(received)):
+        i = len(received) - 1 - n
+        total = near[i * depth : (i + 1) * depth].astype(f32) + received[i].astype(f32)
+        if sums:
+            last = after(sums[-1], *held[n - 1 : n])
+            total = total + shift_outer(last, -1).astype(f32)
+        sums.append(total.astype(bf16) if i else total)
+    return sums
 
 
 def greet(peers):
@@ -170,102 +147,75 @@
     return copies
 
 
-def reduce_vector_kernel(
-    seqs, parts, shared, in_ref, out_ref, slots, sums, send_sems, recv_sems, send_two, recv_two
-):
+def in_order(axis, count, mine, slots):
+    me = lax.axis_index(axis)
+    total = jnp.zeros_like(mine)
+    for place in range(count):
+        step = lax.rem(me + 2 * count - place - 1, count)
+        other = slots[jnp.minimum(step, count - 2)]
+        total = total + jnp.where(place == me, mine, other)
+    return total
+
+
+def square_tile(value):
+    return jnp.sum((value * value).reshape(-1, 8, 128), axis=0)
+
+
+def reduce_kernel(seqs, parts, shared, *refs):
+    vector_ref, square_ref, out_ref, total_ref = refs[:4]
+    first, norms, tiles, last = refs[4:8]
+    sems = refs[8:]
     greet(
         [{"seq": peer} for peer in others("seq", seqs)]
         + [{"mp": peer} for peer in others("mp", parts)]
     )
-    copies = exchange("seq", seqs, lambda peer: in_ref.at[peer], slots, send_sems, recv_sems)
-    total = in_ref[lax.axis_index("seq")]
+    copies = exchange("seq", seqs, lambda peer: vector_ref.at[peer], first, sems[0], sems[1])
+    value = vector_ref[lax.axis_index("seq")]
     for step, copy in enumerate(copies):
         copy.wait()
-        total = total + slots[step]
-    out_ref[...] = total
-    copies = exchange(
-        "mp", parts, lambda peer: out_ref.at[:shared], sums, send_two, recv_two
-    )
+        value = value + first[step]
+    out_ref[...] = value
+    total_ref[...] = square_ref[...] + square_tile(value[shared:])
+    copies = exchange("mp", parts, lambda peer: out_ref.at[:shared], norms, sems[2], sems[3])
+    copies += exchange("mp", parts, lambda peer: total_ref, tiles, sems[4], sems[5])
     for copy in copies:
         copy.wait()
-    head = total[:shared]
-    for step in range(parts - 1):
-        head = head + sums[step]
-    out_ref[:shared] = head
-
-
-def reduce_vector(value, shared):
+    norm = in_order("mp", parts, value[:shared], norms)
+    tile = in_order("mp", parts, total_ref[...], tiles) + square_tile(norm)
+    out_ref[:shared] = norm
+    total_ref[...] = tile
+    copies = exchange("seq", seqs, lambda peer: total_ref, last, sems[6], sems[7])
+    for copy in copies:
+        copy.wait()
+    total_ref[...] = in_order("seq", seqs, tile, last)
+
+
+def reduce_all(vectors, squares, shared):
     seqs, parts = lax.axis_size("seq"), lax.axis_size("mp")
     vmem = pl.BlockSpec(memory_space=pltpu.VMEM)
-    block = value.shape[1:]
+    block = vectors.shape[1:]
+    counts = [seqs, seqs, parts, parts, parts, parts, seqs, seqs]
     return pl.pallas_call(
-        functools.partial(reduce_vector_kernel, seqs, parts, shared),
-        out_shape=jax.ShapeDtypeStruct(block, value.dtype),
-        in_specs=[vmem],
-        out_specs=vmem,
+        functools.partial(reduce_kernel, seqs, parts, shared),
+        out_shape=[
+            jax.ShapeDtypeStruct(block, f32),
+            jax.ShapeDtypeStruct((8, 128), f32),
+        ],
+        in_specs=[vmem, vmem],
+        out_specs=[vmem, vmem],
         scratch_shapes=[
-            pltpu.VMEM((seqs - 1, *block), value.dtype),
-            pltpu.VMEM((parts - 1, shared, *block[1:]), value.dtype),
-            pltpu.SemaphoreType.DMA((seqs - 1,)),
-            pltpu.SemaphoreType.DMA((seqs - 1,)),
-            pltpu.SemaphoreType.DMA((parts - 1,)),
-            pltpu.SemaphoreType.DMA((parts - 1,)),
-        ],
-        compiler_params=pltpu.CompilerParams(collective_id=1, has_side_effects=True),
-        name="reduce_vector",
-    )(value)
-
-
-def reduce_scalar_kernel(
-    seqs, parts, in_ref, out_ref, slots, sums, send_sems, recv_sems, send_two, recv_two
-):
-    greet(
-        [{"seq": peer} for peer in others("seq", seqs)]
-        + [{"mp": peer} for peer in others("mp", parts)]
-    )
-    copies = exchange("mp", parts, lambda peer: in_ref, sums, send_two, recv_two)
-    for copy in copies:
-        copy.wait()
-    me = lax.axis_index("mp")
-    total = jnp.zeros_like(in_ref)
-    for part in range(parts):
-        step = lax.rem(me + parts - part - 1 + parts, parts)
-        mine = part == me
-        other = sums[jnp.minimum(step, parts - 2)]
-        total = total + jnp.where(mine, in_ref[...], other)
-    out_ref[...] = total
-    copies = exchange("seq", seqs, lambda peer: out_ref, slots, send_sems, recv_sems)
-    for copy in copies:
-        copy.wait()
-    me = lax.axis_index("seq")
-    final = jnp.zeros_like(in_ref)
-    for place in range(seqs):
-        step = lax.rem(me + seqs - place - 1 + seqs, seqs)
-        mine = place == me
-        other = slots[jnp.minimum(step, seqs - 2)]
-        final = final + jnp.where(mine, total, other)
-    out_ref[...] = final
-
-
-def reduce_scalar(value):
-    seqs, parts = lax.axis_size("seq"), lax.axis_size("mp")
-    vmem = pl.BlockSpec(memory_space=pltpu.VMEM)
-    return pl.pallas_call(
-        functools.partial(reduce_scalar_kernel, seqs, parts),
-        out_shape=jax.ShapeDtypeStruct(value.shape, value.dtype),
-        in_specs=[vmem],
-        out_specs=vmem,
-        scratch_shapes=[
-            pltpu.VMEM((seqs - 1, *value.shape), value.dtype),
-            pltpu.VMEM((parts - 1, *value.shape), value.dtype),
-            pltpu.SemaphoreType.DMA((seqs - 1,)),
-            pltpu.SemaphoreType.DMA((seqs - 1,)),
-            pltpu.SemaphoreType.DMA((parts - 1,)),
-            pltpu.SemaphoreType.DMA((parts - 1,)),
-        ],
-        compiler_params=pltpu.CompilerParams(collective_id=0, has_side_effects=True),
-        name="reduce_scalar",
-    )(value)
+            pltpu.VMEM((seqs - 1, *block), f32),
+            pltpu.VMEM((parts - 1, shared, 128), f32),
+            pltpu.VMEM((parts - 1, 8, 128), f32),
+            pltpu.VMEM((seqs - 1, 8, 128), f32),
+        ]
+        + [pltpu.SemaphoreType.DMA((count - 1,)) for count in counts],
+        compiler_params=pltpu.CompilerParams(
+            vmem_limit_bytes=4 * 2**20, collective_id=0, has_side_effects=True
+        ),
+        cost_estimate=expected(12.0),
+        name="reduce_all",
+    )(vectors, squares)
 
 
 def gather_chips(own):
@@ -568,87 +518,83 @@
     )(left, *blocks)
 
 
-def turned_kernel(shapes, split, added, spots_ref, *refs):
+def turned_kernel(shapes, sizes, *refs):
     refs = list(refs)
     groups = [[refs.pop(0) for _ in range(count)] for count in shapes]
     rights = [refs.pop(0) for _ in shapes]
-    add_ref = refs.pop(0) if added else None
-
-    def fill(out_ref):
+
+    def fill(out_ref, here):
         at = 0
         for lefts, right_ref in zip(groups, rights):
             width = right_ref.shape[1]
             left = jnp.concatenate([ref[...] for ref in lefts], axis=0)
-            result = lax.dot_general(
+            out_ref[here, at : at + width] = lax.dot_general(
                 left, right_ref[...], (((0,), (0,)), ((), ())), preferred_element_type=f32
-            )
-            if added:
-                result = result + add_ref[:, at : at + width].astype(f32)
-            out_ref[:, at : at + width] = result.astype(bf16)
+            ).astype(bf16)
             at += width
 
-    if split:
-        for n, out_ref in enumerate(refs):
-            pl.when(pl.program_id(0) == n)(functools.partial(fill, out_ref))
+    if sizes is None:
+        fill(refs[0], slice(None))
     else:
-        fill(refs[0])
-
-
-def turned_dot(pairs, first, spots, depth, name, split=False, add=None):
-    count = spots.shape[0]
+        step = 0
+        for size, out_ref in zip(sizes, refs):
+            depth = out_ref.shape[0] // size
+            for n in range(size):
+                here = slice(n * depth, (n + 1) * depth)
+                pl.when(pl.program_id(0) == step)(functools.partial(fill, out_ref, here))
+                step += 1
+
+
+def turned_dot(pairs, first, count, depth, name, sizes=None):
     width = sum(right.shape[1] for _, right in pairs)
     rows = pairs[0][1].shape[0]
-    block = jax.ShapeDtypeStruct((depth, width), bf16)
-    if split:
-        out_shape, out_specs = [block] * count, [resident((depth, width))] * count
+    if sizes is None:
+        out_shape = [jax.ShapeDtypeStruct((count * depth, width), bf16)]
+        out_specs = [pl.BlockSpec((depth, width), lambda n: (n, 0))]
     else:
-        out_shape = [jax.ShapeDtypeStruct((count * depth, width), bf16)]
-        if add is None:
-            out_specs = [pl.BlockSpec((depth, width), lambda n, spots_ref: (n, 0))]
-        else:
-            out_specs = [pl.BlockSpec((depth, width), lambda n, spots_ref: (spots_ref[n], 0))]
-    adds = [] if add is None else [add]
+        out_shape = [jax.ShapeDtypeStruct((size * depth, width), bf16) for size in sizes]
+        out_specs = [resident((size * depth, width)) for size in sizes]
     return pl.pallas_call(
-        functools.partial(
-            turned_kernel, [len(lefts) for lefts, _ in pairs], split, add is not None
-        ),
+        functools.partial(turned_kernel, [len(lefts) for lefts, _ in pairs], sizes),
         out_shape=out_shape,
-        grid_spec=pltpu.PrefetchScalarGridSpec(
-            num_scalar_prefetch=1,
-            grid=(count,),
-            in_specs=[
-                pl.BlockSpec((left.shape[0], depth), lambda n, spots_ref: (0, first + n))
-                for lefts, _ in pairs
-                for left in lefts
-            ]
-            + [resident(right.shape) for _, right in pairs]
-            + [pl.BlockSpec((depth, width), lambda n, spots_ref: (n, 0))] * len(adds),
-            out_specs=out_specs,
-        ),
+        grid=(count,),
+        in_specs=[
+            pl.BlockSpec((left.shape[0], depth), lambda n: (0, first + n))
+            for lefts, _ in pairs
+            for left in lefts
+        ]
+        + [resident(right.shape) for _, right in pairs],
+        out_specs=out_specs,
         compiler_params=pltpu.CompilerParams(vmem_limit_bytes=56 * 2**20),
         cost_estimate=estimate(rows, count * depth, width),
         name=name,
-    )(
-        spots,
-        *[left for lefts, _ in pairs for left in lefts],
-        *[right for _, right in pairs],
-        *adds,
-    )
-
-
-def far_grads(pairs, spots, depth, name, split=False):
+    )(*[left for lefts, _ in pairs for left in lefts], *[right for _, right in pairs])
+
+
+def far_grads(pairs, depth, name, sizes):
     outer, inner = seq_grid()
-    return [None] + [
-        turned_dot(pairs, j * outer, spots, depth, name + "_far", split=split)
-        for j in range(1, inner)
+    return [
+        turned_dot(pairs, j * outer, outer, depth, name + "_far", sizes) for j in range(1, inner)
     ]
 
 
-def line_scatter(pairs, received, spots, depth, name):
-    near = turned_dot(pairs, 0, spots, depth, name + "_near", add=received)[0]
-    return lax.psum_scatter(
-        near, "seq", scatter_dimension=0, tiled=True, axis_index_groups=outer_groups()
-    )
+def near_grads(pairs, depth, name):
+    return turned_dot(pairs, 0, seq_grid()[0], depth, name + "_near")[0]
+
+
+def inner_sum(far, n, *ready):
+    part = shift_inner(after(far[-1][n], *ready), -1)
+    for parts in reversed(far[:-1]):
+        part = shift_inner((parts[n].astype(f32) + part.astype(f32)).astype(bf16), -1)
+    return part
+
+
+def single_blocks(groups, depth):
+    return [
+        group[n * depth : (n + 1) * depth]
+        for group in groups
+        for n in range(group.shape[0] // depth)
+    ]
 
 
 def from_blocks_kernel(blocks, order_ref, in_ref, out_ref):
@@ -669,7 +615,7 @@
             pl.BlockSpec(memory_space=pltpu.VMEM),
         ],
         out_specs=pl.BlockSpec(memory_space=pltpu.VMEM),
-        compiler_params=pltpu.CompilerParams(vmem_limit_bytes=40 * 2**20),
+        compiler_params=pltpu.CompilerParams(vmem_limit_bytes=12 * 2**20),
         cost_estimate=expected(3.0),
         name="from_blocks",
     )(order, value)
@@ -942,11 +888,68 @@
     clipped = grad * factor
     first_new = beta_first * first + (1.0 - beta_first) * clipped
     second_new = beta_second * second + (1.0 - beta_second) * clipped * clipped
-    first_hat = first_new / (1.0 - beta_first**STEP)
-    second_hat = second_new / (1.0 - beta_second**STEP)
+    first_hat = first_new * (1.0 / (1.0 - beta_first**STEP))
+    second_hat = second_new * (1.0 / (1.0 - beta_second**STEP))
     master_new = master - rate * (first_hat / (jnp.sqrt(second_hat) + adam_eps) + decay * master)
     average_new = average_keep * average + (1.0 - average_keep) * master_new
     return (master_new, first_new, second_new, average_new, master_new.astype(bf16))
+
+
+def adam_kernel(square_ref, attn_ref, up_ref, down_ref, *refs):
+    vector_refs, state, outs = refs[:3], refs[3:23], refs[23:]
+    grad_norm = jnp.sqrt(jnp.sum(square_ref[...], keepdims=True))
+    factor = jnp.minimum(1.0, clip_limit / (grad_norm + 1e-06))
+
+    def update(part, place, grad, rate, decay):
+        old = [ref[place] for ref in state[4 * part : 4 * part + 4]]
+        new = adam_step(old[0], grad, *old[1:], factor, rate, decay)
+        for ref, value in zip(outs[5 * part : 5 * part + 5], new):
+            ref[place] = value
+
+    width = attn_ref.shape[1] // 4
+    for n in range(4):
+        update(0, n, attn_ref[:, n * width : (n + 1) * width], D ** (-0.5), weight_decay)
+    update(1, 0, up_ref[...], D ** (-0.5), weight_decay)
+    update(1, 1, down_ref[...], FF ** (-0.5), weight_decay)
+
+    @pl.when(pl.program_id(0) == 0)
+    def _():
+        for n in range(3):
+            update(2 + n, slice(None), vector_refs[n][...], vector_rate, 0.0)
+
+
+def adam_all(squares, shards, vectors, state):
+    attn, hidden = state[0], state[4]
+    depth = attn.shape[1]
+    tile = 64
+
+    def rows_of(array):
+        return pl.BlockSpec((array.shape[0], tile, array.shape[2]), lambda n: (0, n, 0))
+
+    def tall(array):
+        return pl.BlockSpec((tile, array.shape[1]), lambda n: (n, 0))
+
+    state_specs = [rows_of(array) for array in state[:8]]
+    state_specs += [resident(array.shape) for array in state[8:]]
+    out_shape, out_specs = [], []
+    for n in range(5):
+        group, specs = state[4 * n : 4 * n + 4], state_specs[4 * n : 4 * n + 4]
+        out_shape += [jax.ShapeDtypeStruct(array.shape, f32) for array in group]
+        out_shape.append(jax.ShapeDtypeStruct(group[0].shape, bf16))
+        out_specs += specs + [specs[0]]
+    return pl.pallas_call(
+        adam_kernel,
+        out_shape=out_shape,
+        grid=(depth // tile,),
+        in_specs=[resident(squares.shape)]
+        + [tall(shard) for shard in shards]
+        + [resident(vector.shape) for vector in vectors]
+        + state_specs,
+        out_specs=out_specs,
+        compiler_params=pltpu.CompilerParams(vmem_limit_bytes=60 * 2**20),
+        cost_estimate=expected(20.0),
+        name="adam_all",
+    )(squares, *shards, *vectors, *state)
 
 
 def per_device(
@@ -986,7 +989,6 @@
     me_vector = me.astype(jnp.int32)[None]
     order = feature_order()
     back_order = block_order()
-    spots = block_spots()
     codes = row_codes()
     units = hidden_weight.shape[2]
     total_rows = parts * rows_padded
@@ -999,22 +1001,25 @@
     attn_own = jnp.concatenate(
         [jnp.concatenate([attention_weight[n] for n in range(4)], axis=1), packed], axis=0
     ).astype(bf16)
-    attn_line = ring_line(attn_own)
     row_pad = ((0, rows_padded - rows), (0, 0))
     tokens_all = gather_chips(jnp.pad(tokens, row_pad))
-    attn_rest = [ring_rest(part) for part in attn_line]
+    cotangent_pieces = gather_chips(after(jnp.pad(cotangent, row_pad), *tokens_all))
+    up_own, down_own = hidden_weight[0].astype(bf16), hidden_weight[1].astype(bf16)
+    attn_line, attn_rest = [attn_own], [ring_rest(attn_own)]
+    for i in range(1, outer):
+        behind = attn_rest[i - 2] if i > 1 else []
+        behind = behind + (tokens_all[1:] if i == outer - 1 else [])
+        attn_line.append(shift_outer(after(attn_line[-1], *behind), 1))
+        attn_rest.append(ring_rest(attn_line[-1]))
     attn_blocks = attn_line + [rest[j] for j in range(inner - 1) for rest in attn_rest]
-    cotangent_pieces = gather_chips(after(jnp.pad(cotangent, row_pad), *tokens_all))
-    up_line = ring_line(after(hidden_weight[0].astype(bf16), attn_line[-1]))
-    down_line = ring_line(after(hidden_weight[1].astype(bf16), up_line[-1]))
-    up_first = ring_rest(after(up_line[0], attn_rest[-2][-1]))
-    down_first = ring_rest(after(down_line[0], attn_rest[-1][-1]))
-    up_rest = ring_rest(jnp.concatenate(after(up_line[1:], up_first[-1]), axis=0))
-    down_rest = ring_rest(
-        jnp.concatenate(after(down_line[1:], down_first[-1], up_rest[-1]), axis=0)
-    )
-    up_blocks = up_line + [part for pair in zip(up_first, up_rest) for part in pair]
-    down_blocks = down_line + [part for pair in zip(down_first, down_rest) for part in pair]
+    up_line = [up_own, shift_outer(after(up_own, attn_line[-1], *attn_rest[-2]), 1)]
+    up_line.append(shift_outer(up_line[1], 1))
+    up_line.append(shift_outer(up_line[2], 1))
+    down_line = [down_own, shift_outer(after(down_own, up_line[2]), 1)]
+    down_line.append(shift_outer(down_line[1], 1))
+    down_line.append(shift_outer(down_line[2], 1))
+    up_rest = [ring_rest(after(up_own, *attn_rest[-2]))]
+    up_rest.append(ring_rest(after(up_line[1], *attn_rest[-1])))
 
     vectors = jnp.concatenate([block[depth : depth + 1] for block in attn_blocks], axis=0)
     vectors = vectors[:, :packed_size].astype(f32)
@@ -1043,7 +1048,7 @@
         [np.full(head_width, score_scale, np.float32), np.ones(2 * head_width, np.float32)]
     )
     qkv = tall_dot(
-        [first_all],
+        [after(first_all, *cotangent_pieces)],
         attn_blocks,
         0,
         3 * head_width,
@@ -1052,9 +1057,21 @@
         [(total_rows, bf16)],
         "project",
     )[0]
+    down_rest = [ring_rest(after(down_own, qkv, *up_rest[0]))]
+    qkv = after(qkv, up_line[2], *up_rest[0])
     context, share = attend(qkv, bias, me_vector, parts, rows_padded)
+    up_rest.append(ring_rest(after(up_line[2], context, *up_rest[1])))
+    up_rest.append(ring_rest(after(up_line[3], *up_rest[2])))
+    down_rest.append(ring_rest(after(down_line[1], *up_rest[3])))
+    down_rest.append(ring_rest(after(down_line[2], *up_rest[3])))
+    down_rest.append(ring_rest(after(down_line[3], *down_rest[1])))
+    up_blocks = up_line + [rest[j] for j in range(inner - 1) for rest in up_rest]
+    down_blocks = down_line + [rest[j] for j in range(inner - 1) for rest in down_rest]
+    context = after(context, *up_rest[1])
     join_parts = wide_dot(context, attn_blocks, 3 * head_width, D, 4, "join")
+    join_parts = [join_parts[0], after(join_parts[1], down_line[1], *down_rest[0])]
     attended = scatter_chips(*join_parts) + norm_vals[4]
+    attended = after(attended, down_line[2], *up_rest[3])
     feed_grad, cotangent_own = arrange(
         cotangent_pieces,
         [kept_all],
@@ -1069,6 +1086,7 @@
     normed_two, scale_two = norm_parts(middle)
     second_own = (normed_two * norm_vals[2] + norm_vals[3]).astype(bf16)
     second_all = gather_chips(second_own)
+    second_all = after(second_all, down_line[3], *down_rest[1])
     activated, slope, second_others = tall_dot(
         second_all,
         up_blocks,
@@ -1085,9 +1103,10 @@
     out_grad = cotangent_own.astype(f32)
     down_bias_grad = jnp.sum(kept_own * out_grad, axis=0)
 
+    activated = after(activated, *down_rest[2])
     down_pairs = [([feed_grad], activated)]
-    down_far = far_grads(down_pairs, spots, depth, "down_grad")
-    down_received = inner_sum([far and far[0] for far in down_far])
+    down_far = far_grads(down_pairs, depth, "down_grad", (3, 1))
+    down_last = inner_sum(down_far, 1, *down_rest[3])
     pre_grad, unit_grad = tall_dot(
         [feed_grad],
         down_blocks,
@@ -1099,20 +1118,24 @@
         "down_back",
     )
     unit_grad = unit_grad[0]
+    down_first = inner_sum(down_far, 0, pre_grad)
+    down_near = near_grads([([after(feed_grad, pre_grad)], activated)], depth, "down_grad")
+    down_totals = ring_scatter(down_near, single_blocks([down_first, down_last], depth))
+    pre_grad = after(pre_grad, down_last, down_near)
     second_parts = wide_dot(pre_grad, up_blocks, 0, D, 6, "up_back")
-    up_pairs = [(second_all, pre_grad)]
-    up_far = far_grads(up_pairs, spots, depth, "up_grad")
-    up_received = inner_sum(
-        [far and after(far[0], down_received) for far in up_far]
-    )
-    second_grad = scatter_chips(*second_parts)
+    up_pairs = [(after(second_all, *second_parts), pre_grad)]
+    up_far = far_grads(up_pairs, depth, "up_grad", (1, 2, 1))
+    up_near = near_grads(up_pairs, depth, "up_grad")
+    second_grad = after(scatter_chips(*second_parts), up_near, *[far[2] for far in up_far])
     gain_two_grad = jnp.sum(second_grad * normed_two, axis=0)
     shift_two_grad = jnp.sum(second_grad, axis=0)
     middle_grad = out_grad + norm_back(normed_two, scale_two, norm_vals[2], second_grad)
 
     attn_grad = kept_own * middle_grad
     out_bias_grad = jnp.sum(attn_grad, axis=0)
-    attn_rows = gather_chips(attn_grad.astype(bf16))
+    up_last = inner_sum(up_far, 2, second_grad)
+    feed_parts = wide_dot(after(activated, second_grad), down_blocks, 0, D, 8, "down")
+    attn_rows = after(gather_chips(attn_grad.astype(bf16)), down_first, up_last, *feed_parts)
     context_grad, attn_others = tall_dot(
         attn_rows,
         attn_blocks,
@@ -1125,9 +1148,10 @@
         7,
     )
     attn_rows = attn_rows + [attn_others]
-    down_grad = line_scatter(down_pairs, down_received, spots, depth, "down_grad")
-    feed_parts = wide_dot(after(activated, second_grad), down_blocks, 0, D, 8, "down")
-    feed_out = scatter_chips(*after(feed_parts, *attn_rows)) + norm_vals[5]
+    up_middle = inner_sum(up_far, 1, down_first)
+    context_grad = after(context_grad, down_totals[2])
+    feed_parts = after(feed_parts, context_grad)
+    feed_out = scatter_chips(*feed_parts) + norm_vals[5]
     block_output = from_blocks(middle + kept_own * feed_out, order, rows)
     query_grad, key_grad, value_grad = attend_back(
         qkv, context, context_grad, share, me_vector, parts, rows_padded
@@ -1136,18 +1160,32 @@
     head_grad = jnp.stack(
         [jnp.sum(query_grad, axis=0, dtype=f32), jnp.sum(value_grad, axis=0, dtype=f32)]
     )
-    attn_pairs = [([first_all], qkv_grad), (attn_rows, context)]
-    attn_far = far_grads(attn_pairs, spots, depth, "attn_grad", split=True)
-    attn_received = [None] * outer
-    last = up_received
-    for i in reversed(range(outer)):
-        last = attn_received[i] = inner_sum([far and after(far[i], last) for far in attn_far])
-    up_grad = line_scatter(up_pairs, up_received, spots, depth, "up_grad")
-    near = turned_dot(attn_pairs, 0, spots, depth, "attn_grad_near")[0]
-    attn_shard = ring_scatter(
-        [near[i * depth : (i + 1) * depth] for i in range(outer)], attn_received
-    )
-    first_grad = scatter_chips(*wide_dot(qkv_grad, attn_blocks, 0, D, 9, "project_back"))
+    up_first = inner_sum(up_far, 0, up_last, qkv_grad)
+    up_totals = ring_scatter(up_near, single_blocks([up_first, up_middle, up_last], depth))
+    down_grad, up_grad = down_totals[-1], up_totals[-1]
+    attn_pairs = [
+        ([after(first_all, up_totals[1])], qkv_grad),
+        (attn_rows, context),
+    ]
+    attn_far = far_grads(attn_pairs, depth, "attn_grad", (1, 1, 1, 1))
+    all_far = [part for far in attn_far for part in far]
+    attn_pairs = [
+        ([after(first_all, down_grad, up_totals[2], *all_far)], qkv_grad),
+        (attn_rows, context),
+    ]
+    attn_near = near_grads(attn_pairs, depth, "attn_grad")
+    attn_sums = [None] * outer
+    attn_sums[3] = inner_sum(attn_far, 3, up_middle)
+    attn_sums[2] = inner_sum(attn_far, 2, up_first)
+    attn_totals = [attn_near[3 * depth :].astype(f32) + attn_sums[3].astype(f32)]
+    attn_totals[0] = attn_totals[0].astype(bf16)
+    first_parts = wide_dot(
+        after(qkv_grad, up_middle, attn_totals[0]), attn_blocks, 0, D, 9, "project_back"
+    )
+    attn_sums[1] = inner_sum(attn_far, 1, attn_sums[3], first_parts[0])
+    attn_sums[0] = inner_sum(attn_far, 0, attn_sums[2])
+    attn_totals = ring_scatter(attn_near, attn_sums, [up_totals[2], up_grad], attn_totals)
+    first_grad = scatter_chips(*first_parts)
     normed_one, scale_one = norm_parts(inputs)
     gain_one_grad = jnp.sum(first_grad * normed_one, axis=0)
     shift_one_grad = jnp.sum(first_grad, axis=0)
@@ -1180,65 +1218,49 @@
         ],
         axis=1,
     )
-    vectors = reduce_vector(vectors.reshape(seqs, room // 128, 128), norm_room // 128)
+    vectors = vectors.reshape(seqs, room // 128, 128)
+    attn_shard = attn_totals[-1]
+    squares = sum(jnp.sum(shard * shard) for shard in (attn_shard, up_grad, down_grad))
+    squares = jnp.pad(squares.reshape(1, 1), ((0, 7), (0, 127)))
+    vectors, squares = reduce_all(vectors, squares, norm_room // 128)
+    grad_norm = jnp.sqrt(jnp.sum(squares))
     vectors = vectors.reshape(-1)
     norm_shard = vectors[:norm_size].reshape(norm_params.shape)
     head_shard = vectors[norm_room : norm_room + head_size].reshape(head_bias.shape)
     unit_shard = vectors[norm_room + head_size : norm_room + packed_size - norm_size]
-
-    attn_shard = jnp.stack(
-        [attn_shard[:, n * head_width : (n + 1) * head_width] for n in range(4)]
-    )
-    hidden_shard = jnp.stack([up_grad, down_grad]).astype(f32)
-    leader = (me == 0).astype(f32)
-    local_squares = (
-        jnp.sum(attn_shard * attn_shard)
-        + jnp.sum(hidden_shard * hidden_shard)
-        + jnp.sum(head_shard * head_shard)
-        + jnp.sum(unit_shard * unit_shard)
-        + leader * jnp.sum(norm_shard * norm_shard)
-    )
-    grad_norm = jnp.sqrt(reduce_scalar(jnp.full((8, 128), local_squares))[0, 0])
-    factor = jnp.minimum(1.0, clip_limit / (grad_norm + 1e-06))
-    hidden_rate = jnp.array([D ** (-0.5), FF ** (-0.5)], f32)[:, None, None]
-    attention_out = adam_step(
-        attention_weight,
-        attn_shard,
-        attention_first,
-        attention_second,
-        attention_average,
-        factor,
-        D ** (-0.5),
-        weight_decay,
-    )
-    hidden_out = adam_step(
-        hidden_weight,
-        hidden_shard,
-        hidden_first,
-        hidden_second,
-        hidden_average,
-        factor,
-        hidden_rate,
-        weight_decay,
-    )
-    norm_out = adam_step(
-        norm_params, norm_shard, norm_first, norm_second, norm_average, factor, vector_rate, 0.0
-    )
-    head_out = adam_step(
-        head_bias, head_shard, head_first, head_second, head_average, factor, vector_rate, 0.0
-    )
-    unit_out = adam_step(
-        unit_bias, unit_shard, unit_first, unit_second, unit_average, factor, vector_rate, 0.0
+    updated = adam_all(
+        squares,
+        [attn_shard, up_grad, down_grad],
+        [norm_shard, head_shard, unit_shard[None]],
+        [
+            attention_weight,
+            attention_first,
+            attention_second,
+            attention_average,
+            hidden_weight,
+            hidden_first,
+            hidden_second,
+            hidden_average,
+            norm_params,
+            norm_first,
+            norm_second,
+            norm_average,
+            head_bias,
+            head_first,
+            head_second,
+            head_average,
+            unit_bias[None],
+            unit_first[None],
+            unit_second[None],
+            unit_average[None],
+        ],
     )
     return (
         block_output,
         input_grad,
         grad_norm,
-        *attention_out,
-        *hidden_out,
-        *norm_out,
-        *head_out,
-        *unit_out,
+        *updated[:20],
+        *[value[0] for value in updated[20:]],
     )
 
 

time: 848 us -> 680 us (0.80)
  waiting for transfers between devices: 322 us -> 199 us
  Pallas kernels: 345 us -> 319 us
  starting transfers between devices: 39.4 us -> 56.2 us
  between operations: 20.5 us -> 5.69 us
  local copies, waits for them, and re-layouts: 39.4 us -> 25.9 us
    ppermute x14 -> x21, waiting for transfers between devices: 202 us -> 22.6 us  [shift_inner(): return lax.ppermute(value, 'seq', pairs)]
    ppermute x12 -> x18, waiting for transfers between devices: 117 us -> 155 us  [shift_outer(): return lax.ppermute(value, 'seq', pairs)]
    pallas_call x2, Pallas kernels: 62.1 us -> 40.1 us  [the longest x1 23.3 us: adam_all(): pl.pallas_call(adam_kernel, out_shape=out_shape, grid=(depth // tile,), i...]
    ppermute x8, waiting for transfers between devices: 3.56 us -> 21.7 us  [swap(): lax.ppermute(value, 'mp', [(m, m ^ bits) for m in range(lax.axis_size('mp...]
    unnamed x145 -> x115, local copies, waits for them, and re-layouts: 18.2 us -> 5.61 us
    ppermute x12 -> x18, starting transfers between devices: 14 us -> 25.3 us  [shift_outer(): return lax.ppermute(value, 'seq', pairs)]
    ppermute x14 -> x21, starting transfers between devices: 16.9 us -> 22.4 us  [shift_inner(): return lax.ppermute(value, 'seq', pairs)]
    convert_element_type x9 -> x10, other arithmetic: 21.9 us -> 24.9 us  [the longest x8 22 us: ring_scatter(): sums.append(total.astype(bf16) if i else total)]
  transfers between devices with their start and end apart: 36 -> 47, of which waited for: 18 -> 22; matrix products, arithmetic and copies ran while one was open for 8% -> 11% of each run, Pallas kernels for 40% -> 42%
where the time goes in v3:
time: 680 us; the launch traced here: 670 us
  Pallas kernels  319 us (47%)
  waiting for transfers between devices  199 us (29%)
  other arithmetic  64.7 us (10%)
  starting transfers between devices  56.2 us (8%)
  local copies, waits for them, and re-layouts  25.9 us (4%)
    ppermute x18, waiting for transfers between devices, shift_outer(): return lax.ppermute(value, 'seq', pairs)  155 us
    pallas_call x4, Pallas kernels, tall_dot(): pl.pallas_call(functools.partial(tall_kernel, epilogue, exchanged, len(le...  68.5 us
    pallas_call x6, Pallas kernels, turned_dot(): pl.pallas_call(functools.partial(turned_kernel, [len(lefts) for lefts, _...  64.7 us
    pallas_call x4, Pallas kernels, wide_dot(): pl.pallas_call(functools.partial(wide_kernel, len(blocks), start), out_sh...  64 us
    pallas_call x1, Pallas kernels, attend(): pl.pallas_call(functools.partial(attend_kernel, mp_count, rows_padded), o...  36.3 us
    ppermute x18, starting transfers between devices, shift_outer(): return lax.ppermute(value, 'seq', pairs)  25.3 us
    pallas_call x1, Pallas kernels, adam_all(): pl.pallas_call(adam_kernel, out_shape=out_shape, grid=(depth // tile,), i...  23.3 us
    pallas_call x1, Pallas kernels, attend_back(): pl.pallas_call(functools.partial(attend_back_kernel, mp_count, rows_padde...  23.3 us
  transfers between devices with their start and end apart: 47, of which 22 were waited for; matrix products, arithmetic and copies ran while one was open for 11% of the time, Pallas kernels for 42%

profile of v3, /device:TPU:0, one launch (start us, length us, event | category | flops | bytes accessed | tf_op | source)
XLA Modules:
  0.0 669.9 jit_solution(3739630440554064812)
XLA Ops:
  2.9 1.7 convert.37
  4.9 3.1 collective-permute-start.1
  11.3 23.3 %collective-permute-done.1.refs_2_.refs_1_.refs_3_ = bf16[272,2048]{1,0:T(8,128)(2,1)S(1)} collective-permute-done((bf16[272,2048]{1,0:T(8,128)(2,1)S(1)}, bf16[272,2048]{1,0:T(8,128)(2,1)S(1)}, u32[]{:S(2)}, u32[]{:S(2)}) %collective-permute-start.1) | collective-permute-done | bytes 1114144 | tf_op jit(solution)/shard_map/ppermute | solution.py:51
  39.7 22.5 %collective-permute-done.3.refs_3_.refs_2_.refs_4_ = bf16[272,2048]{1,0:T(8,128)(2,1)S(1)} collective-permute-done((bf16[272,2048]{1,0:T(8,128)(2,1)S(1)}, bf16[272,2048]{1,0:T(8,128)(2,1)S(1)}, u32[]{:S(2)}, u32[]{:S(2)}) %collective-permute-start.3) | collective-permute-done | bytes 1114144 | tf_op jit(solution)/shard_map/ppermute | solution.py:51
  67.0 22.0 %collective-permute-done.5.refs_4_.refs_3_.refs_5_ = bf16[272,2048]{1,0:T(8,128)(2,1)} collective-permute-done((bf16[272,2048]{1,0:T(8,128)(2,1)S(1)}, bf16[272,2048]{1,0:T(8,128)(2,1)}, u32[]{:S(2)}, u32[]{:S(2)}) %collective-permute-start.5) | collective-permute-done | bytes 1114144 | tf_op jit(solution)/shard_map/ppermute | solution.py:51
  93.9 1.6 add_bitcast_fusion
  104.5 13.5 %collective-permute-done.9.refs_3_.refs_1_ = bf16[256,2048]{1,0:T(8,128)(2,1)} collective-permute-done((bf16[256,2048]{1,0:T(8,128)(2,1)}, bf16[256,2048]{1,0:T(8,128)(2,1)}, u32[]{:S(2)}, u32[]{:S(2)}) %collective-permute-start.9) | collective-permute-done | bytes 1048608 | tf_op jit(solution)/shard_map/ppermute | solution.py:51
  120.2 9.1 %first_norm.1 = (bf16[1280,2048]{1,0:T(8,128)(2,1)}, bf16[320,2048]{1,0:T(8,128)(2,1)}) custom-call(bf16[320,2048]{1,0:T(8,128)(2,1)} %copy-done.21, bf16[320,2048]{1,0:T(8,128)(2,1)} %copy-done.41, f32[1,2048]{1,0:T(1,128)} %bitcast.132, f32[1,2048]{1,0:T(1,128)} %bitcast.133), custom_call_target="tpu_custom_call" | custom-call | flops 5310000128 | tf_op jit(solution)/shard_map/first_norm/pallas_call | solution.py:333
  132.1 13.5 %project.1.q_ref.k_ref.v_ref = bf16[1280,1536]{1,0:T(8,128)(2,1)} custom-call(bf16[1280,2048]{1,0:T(8,128)(2,1)} %get-tuple-element.202.refs_0_, bf16[272,2048]{1,0:T(8,128)(2,1)} %copy-done.13, bf16[272,2048]{1,0:T(8,128)(2,1)} %copy-done.24, bf16[272,2048]{1,0:T(8,128)(2,1)} %copy-done.26, ...), custom_call_target="tpu_custom_call" | custom-call | flops 7484038144 | tf_op jit(solution)/shard_map/project/pallas_call | solution.py:417
  146.7 36.3 %attend.1 = (bf16[1280,512]{1,0:T(8,128)(2,1)S(1)}, bf16[8,1280,512]{2,1,0:T(8,128)(2,1)}) custom-call(s32[1]{0:T(128)} %bitcast.15.me_ref, bf16[1280,1536]{1,0:T(8,128)(2,1)} %project.1.q_ref.k_ref.v_ref, bf16[1280,1536]{1,0:T(8,128)(2,1)} %project.1.q_ref.k_ref.v_ref, bf16[1280,1536]{1,0:T(8,128)(2,1)} %project.1.q_ref.k_ref.v_ref, ...), custom_call_target="tpu_custom_call" | custom-call | flops 21240000512 | tf_op jit(solution)/shard_map/attend/pallas_call | solution.py:702
  185.9 11.6 %join.1 = (f32[320,2048]{1,0:T(8,128)}, bf16[320,2048]{1,0:T(8,128)(2,1)}) custom-call(bf16[1280,512]{1,0:T(8,128)(2,1)} %copy-done, bf16[272,2048]{1,0:T(8,128)(2,1)} %copy-done.13, bf16[272,2048]{1,0:T(8,128)(2,1)} %copy-done.24, bf16[272,2048]{1,0:T(8,128)(2,1)} %copy-done.26, bf16[272,2048]{1,0:T(8,128)(2,1)} %collective-permute-done.5.refs_4_.refs_3_.refs_5_, ...), custom_call_target="tpu_custom_call" | custom-call | flops 3084679424 | tf_op jit(solution)/shard_map/join/pallas_call | solution.py:500
  199.4 4.3 collective-permute-start.16
  203.6 8.5 %collective-permute-done.17.refs_5_.refs_3_ = bf16[256,2048]{1,0:T(8,128)(2,1)} collective-permute-done((bf16[256,2048]{1,0:T(8,128)(2,1)}, bf16[256,2048]{1,0:T(8,128)(2,1)}, u32[]{:S(2)}, u32[]{:S(2)}) %collective-permute-start.17) | collective-permute-done | bytes 1048608 | tf_op jit(solution)/shard_map/ppermute | solution.py:51
  213.7 14.9 %collective-permute-done.15 = bf16[320,2048]{1,0:T(8,128)(2,1)S(1)} collective-permute-done((bf16[320,2048]{1,0:T(8,128)(2,1)}, bf16[320,2048]{1,0:T(8,128)(2,1)S(1)}, u32[]{:S(2)}, u32[]{:S(2)}) %collective-permute-start.15) | collective-permute-done | bytes 1310752 | tf_op jit(solution)/shard_map/ppermute | solution.py:63
  228.7 2.1 add_add_fusion
  230.8 2.7 collective-permute-done.16.refs_3_.refs_2_
  233.5 1.9 collective-permute-done.19.refs_9_.refs_7_
  242.7 9.0 %feed_grad.1 = (bf16[1280,2048]{1,0:T(8,128)(2,1)}, bf16[320,2048]{1,0:T(8,128)(2,1)}) custom-call(bf16[320,2048]{1,0:T(8,128)(2,1)} %pad.36.refs_0_, bf16[320,2048]{1,0:T(8,128)(2,1)} %collective-permute-done.8.refs_1_, f32[1280,1]{1,0:T(8,128)} %select_n.167.refs_2_), custom_call_target="tpu_custom_call" | custom-call | flops 5310000128 | tf_op jit(solution)/shard_map/feed_grad/pallas_call | solution.py:333
  254.0 9.4 %collective-permute-done.21.refs_4_.refs_3_ = bf16[256,2048]{1,0:T(8,128)(2,1)} collective-permute-done((bf16[256,2048]{1,0:T(8,128)(2,1)}, bf16[256,2048]{1,0:T(8,128)(2,1)}, u32[]{:S(2)}, u32[]{:S(2)}) %collective-permute-start.21) | collective-permute-done | bytes 1048608 | tf_op jit(solution)/shard_map/ppermute | solution.py:51
  263.3 3.8 collective-permute-done.22.refs_6_.refs_5_
  268.8 26.5 %up.1 = (bf16[1280,2048]{1,0:T(8,128)(2,1)}, bf16[1280,2048]{1,0:T(8,128)(2,1)}, bf16[640,2048]{1,0:T(8,128)(2,1)}) custom-call(bf16[320,2048]{1,0:T(8,128)(2,1)} %copy-done.20, bf16[320,2048]{1,0:T(8,128)(2,1)} %copy-done.42, bf16[256,2048]{1,0:T(8,128)(2,1)} %get-tuple-element.142.refs_2_.refs_0_, ...), custom_call_target="tpu_custom_call" | custom-call | flops 9683718144 | tf_op jit(solution)/shard_map/up/pallas_call | solution.py:417
  295.4 11.4 %down_grad_far.1 = (bf16[768,2048]{1,0:T(8,128)(2,1)}, bf16[256,2048]{1,0:T(8,128)(2,1)}) custom-call(bf16[1280,2048]{1,0:T(8,128)(2,1)} %get-tuple-element.167.refs_0_, bf16[1280,2048]{1,0:T(8,128)(2,1)} %get-tuple-element.177.refs_1_.left_ref), custom_call_target="tpu_custom_call" | custom-call | flops 5284358656 | tf_op jit(solution)/shard_map/down_grad_far/pallas_call | solution.py:557
  308.8 17.7 %down_back.1 = (bf16[1280,2048]{1,0:T(8,128)(2,1)}, f32[8,2048]{1,0:T(8,128)}) custom-call(bf16[1280,2048]{1,0:T(8,128)(2,1)} %get-tuple-element.167.refs_0_, bf16[256,2048]{1,0:T(8,128)(2,1)} %get-tuple-element.150.refs_1_.refs_0_, bf16[256,2048]{1,0:T(8,128)(2,1)} %collective-permute-done.13.refs_2_.refs_1_, ...), custom_call_target="tpu_custom_call" | custom-call | flops 9683718144 | tf_op jit(solution)/shard_map/down_back/pallas_call | solution.py:417
  328.4 10.0 %down_grad_near.1 = bf16[1024,2048]{1,0:T(8,128)(2,1)} custom-call(bf16[1280,2048]{1,0:T(8,128)(2,1)} %get-tuple-element.167.refs_0_, bf16[1280,2048]{1,0:T(8,128)(2,1)} %get-tuple-element.177.refs_1_.left_ref), custom_call_target="tpu_custom_call" | custom-call | flops 5284358656 | tf_op jit(solution)/shard_map/down_grad_near/pallas_call | solution.py:557
  338.4 18.3 %up_back.1 = (f32[320,2048]{1,0:T(8,128)}, bf16[320,2048]{1,0:T(8,128)(2,1)}) custom-call(bf16[1280,2048]{1,0:T(8,128)(2,1)} %get-tuple-element.168.left_ref.refs_3_, bf16[256,2048]{1,0:T(8,128)(2,1)} %get-tuple-element.142.refs_2_.refs_0_, bf16[256,2048]{1,0:T(8,128)(2,1)} %collective-permute-done.9.refs_3_.refs_1_, ...), custom_call_target="tpu_custom_call" | custom-call | flops 9683718144 | tf_op jit(solution)/shard_map/up_back/pallas_call | solution.py:500
  358.9 2.0 collective-permute-start.30
  361.0 10.1 %up_grad_near.1 = bf16[1024,2048]{1,0:T(8,128)(2,1)} custom-call(bf16[320,2048]{1,0:T(8,128)(2,1)} %copy-done.20, bf16[320,2048]{1,0:T(8,128)(2,1)} %copy-done.42, bf16[640,2048]{1,0:T(8,128)(2,1)} %get-tuple-element.174.refs_2_, bf16[1280,2048]{1,0:T(8,128)(2,1)} %get-tuple-element.168.left_ref.refs_3_), custom_call_target="tpu_custom_call" | custom-call | flops 5284358656 | tf_op jit(solution)/shard_map/up_grad_near/pallas_call | solution.py:557
  371.1 11.4 %up_grad_far.1 = (bf16[256,2048]{1,0:T(8,128)(2,1)}, bf16[512,2048]{1,0:T(8,128)(2,1)}, bf16[256,2048]{1,0:T(8,128)(2,1)}) custom-call(bf16[320,2048]{1,0:T(8,128)(2,1)} %copy-done.20, bf16[320,2048]{1,0:T(8,128)(2,1)} %copy-done.42, bf16[640,2048]{1,0:T(8,128)(2,1)} %get-tuple-element.174.refs_2_, bf16[1280,2048]{1,0:T(8,128)(2,1)} %get-tuple-element.168.left_ref.refs_3_), custom_call_target="tpu_custom_call" | custom-call | flops 5284358656 | tf_op jit(solution)/shard_map/up_grad_far/pallas_call | solution.py:557
  382.5 5.7 collective-permute-done.26
  388.3 1.7 convert_add_fusion.3
  391.3 1.8 fusion.11
  396.1 5.3 collective-permute-done.28
  401.4 3.1 add_convert_fusion.8
  404.5 2.3 collective-permute-start.31
  406.8 18.4 %down.1 = (f32[320,2048]{1,0:T(8,128)}, bf16[320,2048]{1,0:T(8,128)(2,1)}) custom-call(bf16[1280,2048]{1,0:T(8,128)(2,1)} %get-tuple-element.177.refs_1_.left_ref, bf16[256,2048]{1,0:T(8,128)(2,1)} %get-tuple-element.150.refs_1_.refs_0_, bf16[256,2048]{1,0:T(8,128)(2,1)} %collective-permute-done.13.refs_2_.refs_1_, ...), custom_call_target="tpu_custom_call" | custom-call | flops 9683718144 | tf_op jit(solution)/shard_map/down/pallas_call | solution.py:500
  426.1 1.9 add_convert_fusion.6
  428.1 10.8 %join_back.1 = (bf16[1280,512]{1,0:T(8,128)(2,1)}, bf16[640,2048]{1,0:T(8,128)(2,1)}) custom-call(bf16[320,2048]{1,0:T(8,128)(2,1)} %multiply_convert_fusion.refs_0_.refs_1_, bf16[320,2048]{1,0:T(8,128)(2,1)} %collective-permute-done.27.refs_1_.refs_2_, bf16[272,2048]{1,0:T(8,128)(2,1)} %copy-done.13, bf16[272,2048]{1,0:T(8,128)(2,1)} %copy-done.24, ...), custom_call_target="tpu_custom_call" | custom-call | flops 3084679424 | tf_op jit(solution)/shard_map/join_back/pallas_call | solution.py:417
  438.9 3.6 add_convert_fusion.7
  443.9 23.3 %attend_back.1 = (bf16[1280,512]{1,0:T(8,128)(2,1)S(1)}, bf16[1280,512]{1,0:T(8,128)(2,1)S(1)}, bf16[1280,512]{1,0:T(8,128)(2,1)S(1)}) custom-call(s32[1]{0:T(128)} %bitcast.15.me_ref, bf16[1280,1536]{1,0:T(8,128)(2,1)} %project.1.q_ref.k_ref.v_ref, bf16[1280,1536]{1,0:T(8,128)(2,1)} %project.1.q_ref.k_ref.v_ref, ...), custom_call_target="tpu_custom_call" | custom-call | flops 13569999872 | tf_op jit(solution)/shard_map/attend_back/pallas_call | solution.py:817
  468.7 5.2 collective-permute-done.33
  474.0 3.5 add_convert_fusion.5
  479.0 11.4 %attn_grad_far.1 = (bf16[256,2048]{1,0:T(8,128)(2,1)}, bf16[256,2048]{1,0:T(8,128)(2,1)}, bf16[256,2048]{1,0:T(8,128)(2,1)}, bf16[256,2048]{1,0:T(8,128)(2,1)}) custom-call(bf16[1280,2048]{1,0:T(8,128)(2,1)} %get-tuple-element.202.refs_0_, bf16[320,2048]{1,0:T(8,128)(2,1)} %multiply_convert_fusion.refs_0_.refs_1_, ...), custom_call_target="tpu_custom_call" | custom-call | flops 5284358656 | tf_op jit(solution)/shard_map/attn_grad_far/pallas_call | solution.py:557
  491.6 4.9 collective-permute-done.39
  497.3 4.3 multiply_reduce_fusion.6
  502.7 3.1 add_convert_fusion.4
  505.8 2.1 collective-permute-start.44
  507.8 10.4 %attn_grad_near.1 = bf16[1024,2048]{1,0:T(8,128)(2,1)} custom-call(bf16[1280,2048]{1,0:T(8,128)(2,1)} %get-tuple-element.202.refs_0_, bf16[320,2048]{1,0:T(8,128)(2,1)} %multiply_convert_fusion.refs_0_.refs_1_, bf16[320,2048]{1,0:T(8,128)(2,1)} %collective-permute-done.27.refs_1_.refs_2_, bf16[640,2048]{1,0:T(8,128)(2,1)} %get-tuple-element.197.refs_3_, ...), custom_call_target="tpu_custom_call" | custom-call | flops 5284358656 | tf_op jit(solution)/shard_map/attn_grad_near/pallas_call | solution.py:557
  518.9 1.6 add_convert_fusion.3
  520.5 15.7 %project_back.1 = (f32[320,2048]{1,0:T(8,128)}, bf16[320,2048]{1,0:T(8,128)(2,1)}) custom-call(bf16[1280,1536]{1,0:T(8,128)(2,1)} %copy-done.11, bf16[272,2048]{1,0:T(8,128)(2,1)} %copy-done.13, bf16[272,2048]{1,0:T(8,128)(2,1)} %copy-done.24, bf16[272,2048]{1,0:T(8,128)(2,1)} %copy-done.26, ...), custom_call_target="tpu_custom_call" | custom-call | flops 7484038144 | tf_op jit(solution)/shard_map/project_back/pallas_call | solution.py:500
  537.0 2.9 multiply_add_fusion.in_ref
  539.9 1.8 from_blocks.2
  543.7 4.3 multiply_reduce_fusion.7
  548.1 14.2 %collective-permute-done.43 = bf16[256,2048]{1,0:T(8,128)(2,1)S(1)} collective-permute-done((bf16[256,2048]{1,0:T(8,128)(2,1)S(1)}, bf16[256,2048]{1,0:T(8,128)(2,1)S(1)}, u32[]{:S(2)}, u32[]{:S(2)}) %collective-permute-start.43) | collective-permute-done | bytes 1048608 | tf_op jit(solution)/shard_map/ppermute | solution.py:51
  562.2 3.1 add_convert_fusion.2
  565.3 2.1 collective-permute-start.45
  570.0 20.2 %collective-permute-done.45 = bf16[256,2048]{1,0:T(8,128)(2,1)} collective-permute-done((bf16[256,2048]{1,0:T(8,128)(2,1)}, bf16[256,2048]{1,0:T(8,128)(2,1)}, u32[]{:S(2)}, u32[]{:S(2)}) %collective-permute-start.45) | collective-permute-done | bytes 1048608 | tf_op jit(solution)/shard_map/ppermute | solution.py:51
  590.2 2.4 add_convert_fusion.1
  592.6 4.1 collective-permute-start.46
  596.8 2.5 fusion.8.in_ref
  599.2 1.8 from_blocks.3
  601.0 17.2 %collective-permute-done.46 = bf16[256,2048]{1,0:T(8,128)(2,1)S(1)} collective-permute-done((bf16[256,2048]{1,0:T(8,128)(2,1)S(1)}, bf16[256,2048]{1,0:T(8,128)(2,1)S(1)}, u32[]{:S(2)}, u32[]{:S(2)}) %collective-permute-start.46) | collective-permute-done | bytes 1048608 | tf_op jit(solution)/shard_map/ppermute | solution.py:51
  618.2 4.0 multiply_reduce_fusion.8
  624.2 16.8 %reduce_all.1 = (f32[24,128]{1,0:T(8,128)S(1)}, f32[8,128]{1,0:T(8,128)S(1)}) custom-call(f32[8,24,128]{2,1,0:T(8,128)S(1)} %bitcast.118, f32[8,128]{1,0:T(8,128)S(1)} %pad.40.refs_1_), custom_call_target="tpu_custom_call" | custom-call | flops 7080000000 | tf_op jit(solution)/shard_map/reduce_all/pallas_call | solution.py:198
  644.2 23.3 %adam_all.1 = (f32[4,256,512]{2,1,0:T(8,128)}, f32[4,256,512]{2,1,0:T(8,128)}, f32[4,256,512]{2,1,0:T(8,128)}, f32[4,256,512]{2,1,0:T(8,128)}, bf16[4,256,512]{2...) custom-call(f32[8,128]{1,0:T(8,128)} %copy-done.2, ...), custom_call_target="tpu_custom_call" | custom-call | flops 11800000512 | tf_op jit(solution)/shard_map/adam_all/pallas_call | solution.py:940
  (290 shorter events, 81.0 us)
Async XLA Ops:
  4.7 33.1 %copy-start.37 = (s32[1,4,50]{2,1,0:T(4,128)S(1)}, s32[1,4,50]{2,1,0:T(4,128)}, u32[]{:S(2)}) copy-start(s32[1,4,50]{2,1,0:T(4,128)} %param.31) | copy-start | bytes 2404
  4.7 33.1 %copy-start.38 = (s32[1,4]{1,0:T(1,128)S(1)}, s32[1,4]{1,0:T(1,128)}, u32[]{:S(2)}) copy-start(s32[1,4]{1,0:T(1,128)} %param.30) | copy-start | bytes 52
  4.8 33.2 %copy-start.32 = (pred[320,320]{1,0:T(32,128)(4,1)S(1)}, pred[320,320]{1,0:T(32,128)(4,1)}, u32[]{:S(2)}) copy-start(pred[320,320]{1,0:T(32,128)(4,1)} %constant.213.clone) | copy-start | bytes 307204
  4.8 33.2 %copy-start.33 = (pred[320,320]{1,0:T(32,128)(4,1)S(1)}, pred[320,320]{1,0:T(32,128)(4,1)}, u32[]{:S(2)}) copy-start(pred[320,320]{1,0:T(32,128)(4,1)} %constant.212.clone) | copy-start | bytes 307204
  4.8 58.9 %copy-start.14 = (f32[2,256,2048]{2,1,0:T(8,128)S(1)}, f32[2,256,2048]{2,1,0:T(8,128)}, u32[]{:S(2)}) copy-start(f32[2,256,2048]{2,1,0:T(8,128)} %refs_7_.1) | copy-start | bytes 12582916
  4.9 58.7 %copy-start.13 = (bf16[272,2048]{1,0:T(8,128)(2,1)}, bf16[272,2048]{1,0:T(8,128)(2,1)S(1)}, u32[]{:S(2)}) copy-start(bf16[272,2048]{1,0:T(8,128)(2,1)S(1)} %pad_maximum_fusion.refs_1_.refs_0_.refs_2_) | copy-start | bytes 3342340
  4.9 29.7 %collective-permute-start.1 = (bf16[272,2048]{1,0:T(8,128)(2,1)S(1)}, bf16[272,2048]{1,0:T(8,128)(2,1)S(1)}, u32[]{:S(2)}, u32[]{:S(2)}) collective-permute-start(bf16[272,2048]{1,0:T(8,128)(2,1)S(1)} %pad_maximum_fusion.refs_1_.refs_0_.refs_2_), channel_id=1, source_target_pairs={{0,8},{4,12},{8,16},{12,20},{16,24},{20,28},{24,0},{28,4},{1,9},{5... | collective-permute-start | bytes 3342344 | tf_op jit(solution)/shard_map/ppermute | solution.py:51
  8.0 26.6 %collective-permute-start.2 = (bf16[272,2048]{1,0:T(8,128)(2,1)S(1)}, bf16[272,2048]{1,0:T(8,128)(2,1)S(1)}, u32[]{:S(2)}, u32[]{:S(2)}) collective-permute-start(bf16[272,2048]{1,0:T(8,128)(2,1)S(1)} %pad_maximum_fusion.refs_1_.refs_0_.refs_2_), channel_id=1, source_target_pairs={{0,4},{4,0},{8,12},{12,8},{16,20},{20,16},{24,28},{28,24},{1,5},{5... | collective-permute-start | bytes 3342344 | tf_op jit(solution)/shard_map/ppermute | solution.py:59
  9.7 53.9 %copy-start.21 = (bf16[320,2048]{1,0:T(8,128)(2,1)}, bf16[320,2048]{1,0:T(8,128)(2,1)S(1)}, u32[]{:S(2)}) copy-start(bf16[320,2048]{1,0:T(8,128)(2,1)S(1)} %pad.33.refs_0_) | copy-start | bytes 3932164
  9.7 30.0 %collective-permute-start = (bf16[320,2048]{1,0:T(8,128)(2,1)S(1)}, bf16[320,2048]{1,0:T(8,128)(2,1)S(1)}, u32[]{:S(2)}, u32[]{:S(2)}) collective-permute-start(bf16[320,2048]{1,0:T(8,128)(2,1)S(1)} %pad.33.refs_0_), channel_id=1, source_target_pairs={{0,2},{1,3},{2,0},{3,1},{4,6},{5,7},{6,4},{7,5},{8,10},{9,11},{10,... | collective-permute-start | bytes 3932168 | tf_op jit(solution)/shard_map/ppermute | solution.py:63
  34.6 29.0 %copy-start.24 = (bf16[272,2048]{1,0:T(8,128)(2,1)}, bf16[272,2048]{1,0:T(8,128)(2,1)S(1)}, u32[]{:S(2)}) copy-start(bf16[272,2048]{1,0:T(8,128)(2,1)S(1)} %collective-permute-done.1.refs_2_.refs_1_.refs_3_) | copy-start | bytes 3342340
  34.6 29.0 %copy-start.25 = (bf16[272,2048]{1,0:T(8,128)(2,1)}, bf16[272,2048]{1,0:T(8,128)(2,1)S(1)}, u32[]{:S(2)}) copy-start(bf16[272,2048]{1,0:T(8,128)(2,1)S(1)} %collective-permute-done.2.refs_5_.refs_4_.refs_6_) | copy-start | bytes 3342340
  34.6 27.6 %collective-permute-start.3 = (bf16[272,2048]{1,0:T(8,128)(2,1)S(1)}, bf16[272,2048]{1,0:T(8,128)(2,1)S(1)}, u32[]{:S(2)}, u32[]{:S(2)}) collective-permute-start(bf16[272,2048]{1,0:T(8,128)(2,1)S(1)} %collective-permute-done.1.refs_2_.refs_1_.refs_3_), channel_id=1, source_target_pairs={{0,8},{4,12},{8,16},{12,20},{16,24},{20,28},{24,0},{28,4},{1,9},{5... | collective-permute-start | bytes 3342344 | tf_op jit(solution)/shard_map/ppermute | solution.py:51
  35.6 26.6 %collective-permute-start.4 = (bf16[272,2048]{1,0:T(8,128)(2,1)S(1)}, bf16[272,2048]{1,0:T(8,128)(2,1)S(1)}, u32[]{:S(2)}, u32[]{:S(2)}) collective-permute-start(bf16[272,2048]{1,0:T(8,128)(2,1)S(1)} %collective-permute-done.1.refs_2_.refs_1_.refs_3_), channel_id=1, source_target_pairs={{0,4},{4,0},{8,12},{12,8},{16,20},{20,16},{24,28},{28,24},{1,5},{5... | collective-permute-start | bytes 3342344 | tf_op jit(solution)/shard_map/ppermute | solution.py:59
  39.7 23.9 %copy-start.41 = (bf16[320,2048]{1,0:T(8,128)(2,1)}, bf16[320,2048]{1,0:T(8,128)(2,1)S(1)}, u32[]{:S(2)}) copy-start(bf16[320,2048]{1,0:T(8,128)(2,1)S(1)} %collective-permute-done.refs_1_) | copy-start | bytes 3932164
  62.2 26.8 %collective-permute-start.5 = (bf16[272,2048]{1,0:T(8,128)(2,1)S(1)}, bf16[272,2048]{1,0:T(8,128)(2,1)}, u32[]{:S(2)}, u32[]{:S(2)}) collective-permute-start(bf16[272,2048]{1,0:T(8,128)(2,1)S(1)} %collective-permute-done.3.refs_3_.refs_2_.refs_4_), channel_id=1, source_target_pairs={{0,8},{4,12},{8,16},{12,20},{16,24},{20,28},{24,0},{28,4},{1,9},{5... | collective-permute-start | bytes 3342344 | tf_op jit(solution)/shard_map/ppermute | solution.py:51
  62.3 31.6 %collective-permute-start.6 = (bf16[272,2048]{1,0:T(8,128)(2,1)S(1)}, bf16[272,2048]{1,0:T(8,128)(2,1)S(1)}, u32[]{:S(2)}, u32[]{:S(2)}) collective-permute-start(bf16[272,2048]{1,0:T(8,128)(2,1)S(1)} %collective-permute-done.3.refs_3_.refs_2_.refs_4_), channel_id=1, source_target_pairs={{0,4},{4,0},{8,12},{12,8},{16,20},{20,16},{24,28},{28,24},{1,5},{5... | collective-permute-start | bytes 3342344 | tf_op jit(solution)/shard_map/ppermute | solution.py:59
  65.4 25.4 %copy-start.23 = (bf16[306,2048]{1,0:T(8,128)(2,1)S(1)}, bf16[306,2048]{1,0:T(8,128)(2,1)}, u32[]{:S(2)}) copy-start(bf16[306,2048]{1,0:T(8,128)(2,1)} %param.29) | copy-start | bytes 3760132
  89.0 29.0 %collective-permute-start.7 = (bf16[272,2048]{1,0:T(8,128)(2,1)}, bf16[272,2048]{1,0:T(8,128)(2,1)}, u32[]{:S(2)}, u32[]{:S(2)}) collective-permute-start(bf16[272,2048]{1,0:T(8,128)(2,1)} %collective-permute-done.5.refs_4_.refs_3_.refs_5_), channel_id=1, source_target_pairs={{0,4},{4,0},{8,12},{12,8},{16,20},{20,16},{24,28},{28,24},{1,5},{5... | collective-permute-start | bytes 3342344 | tf_op jit(solution)/shard_map/ppermute | solution.py:59
  93.9 24.1 %collective-permute-start.9 = (bf16[256,2048]{1,0:T(8,128)(2,1)}, bf16[256,2048]{1,0:T(8,128)(2,1)}, u32[]{:S(2)}, u32[]{:S(2)}) collective-permute-start(bf16[256,2048]{1,0:T(8,128)(2,1)} %get-tuple-element.142.refs_2_.refs_0_), channel_id=1, source_target_pairs={{0,8},{4,12},{8,16},{12,20},{16,24},{20,28},{24,0},{28,4},{1,9},{5... | collective-permute-start | bytes 3145736 | tf_op jit(solution)/shard_map/ppermute | solution.py:51
  97.0 32.9 %copy-start.35 = (pred[8]{0:T(512)(128)(4,1)}, pred[8]{0:T(512)(128)(4,1)S(1)}, u32[]{:S(2)}) copy-start(pred[8]{0:T(512)(128)(4,1)S(1)} %compare_and_fusion) | copy-start | bytes 28
  97.0 32.3 %collective-permute-start.8 = (bf16[320,2048]{1,0:T(8,128)(2,1)}, bf16[320,2048]{1,0:T(8,128)(2,1)}, u32[]{:S(2)}, u32[]{:S(2)}) collective-permute-start(bf16[320,2048]{1,0:T(8,128)(2,1)} %pad.36.refs_0_), channel_id=1, source_target_pairs={{0,2},{1,3},{2,0},{3,1},{4,6},{5,7},{6,4},{7,5},{8,10},{9,11},{10,... | collective-permute-start | bytes 3932168 | tf_op jit(solution)/shard_map/ppermute | solution.py:63
  99.4 30.0 %copy-start.34 = (s32[1024]{0:T(1024)}, s32[1024]{0:T(1024)S(1)}, u32[]{:S(2)}) copy-start(s32[1024]{0:T(1024)S(1)} %get-tuple-element.290) | copy-start | bytes 12292
  102.4 43.2 %collective-permute-start.11 = (bf16[256,2048]{1,0:T(8,128)(2,1)}, bf16[256,2048]{1,0:T(8,128)(2,1)}, u32[]{:S(2)}, u32[]{:S(2)}) collective-permute-start(bf16[256,2048]{1,0:T(8,128)(2,1)} %get-tuple-element.142.refs_2_.refs_0_), channel_id=1, source_target_pairs={{0,4},{4,0},{8,12},{12,8},{16,20},{20,16},{24,28},{28,24},{1,5},{5... | collective-permute-start | bytes 3145736 | tf_op jit(solution)/shard_map/ppermute | solution.py:59
  118.0 28.5 %collective-permute-start.10 = (bf16[256,2048]{1,0:T(8,128)(2,1)}, bf16[256,2048]{1,0:T(8,128)(2,1)}, u32[]{:S(2)}, u32[]{:S(2)}) collective-permute-start(bf16[256,2048]{1,0:T(8,128)(2,1)} %collective-permute-done.9.refs_3_.refs_1_), channel_id=1, source_target_pairs={{0,8},{4,12},{8,16},{12,20},{16,24},{20,28},{24,0},{28,4},{1,9},{5... | collective-permute-start | bytes 3145736 | tf_op jit(solution)/shard_map/ppermute | solution.py:51
  130.9 53.8 %collective-permute-start.12 = (bf16[256,2048]{1,0:T(8,128)(2,1)}, bf16[256,2048]{1,0:T(8,128)(2,1)S(1)}, u32[]{:S(2)}, u32[]{:S(2)}) collective-permute-start(bf16[256,2048]{1,0:T(8,128)(2,1)} %collective-permute-done.9.refs_3_.refs_1_), channel_id=1, source_target_pairs={{0,4},{4,0},{8,12},{12,8},{16,20},{20,16},{24,28},{28,24},{1,5},{5... | collective-permute-start | bytes 3145736 | tf_op jit(solution)/shard_map/ppermute | solution.py:59
  145.6 51.9 %collective-permute-start.14 = (bf16[256,2048]{1,0:T(8,128)(2,1)S(1)}, bf16[256,2048]{1,0:T(8,128)(2,1)S(1)}, u32[]{:S(2)}, u32[]{:S(2)}) collective-permute-start(bf16[256,2048]{1,0:T(8,128)(2,1)S(1)} %copy-done.29), channel_id=1, source_target_pairs={{0,4},{4,0},{8,12},{12,8},{16,20},{20,16},{24,28},{28,24},{1,5},{5... | collective-permute-start | bytes 3145736 | tf_op jit(solution)/shard_map/ppermute | solution.py:59
  146.5 51.1 %collective-permute-start.13 = (bf16[256,2048]{1,0:T(8,128)(2,1)S(1)}, bf16[256,2048]{1,0:T(8,128)(2,1)}, u32[]{:S(2)}, u32[]{:S(2)}) collective-permute-start(bf16[256,2048]{1,0:T(8,128)(2,1)S(1)} %copy-done.29), channel_id=1, source_target_pairs={{0,8},{4,12},{8,16},{12,20},{16,24},{20,28},{24,0},{28,4},{1,9},{5... | collective-permute-start | bytes 3145736 | tf_op jit(solution)/shard_map/ppermute | solution.py:51
  184.0 28.2 %collective-permute-start.17 = (bf16[256,2048]{1,0:T(8,128)(2,1)}, bf16[256,2048]{1,0:T(8,128)(2,1)}, u32[]{:S(2)}, u32[]{:S(2)}) collective-permute-start(bf16[256,2048]{1,0:T(8,128)(2,1)} %collective-permute-done.10.refs_4_.refs_2_), channel_id=1, source_target_pairs={{0,8},{4,12},{8,16},{12,20},{16,24},{20,28},{24,0},{28,4},{1,9},{5... | collective-permute-start | bytes 3145736 | tf_op jit(solution)/shard_map/ppermute | solution.py:51
  184.6 28.8 %copy-start.6 = (bf16[320,2048]{1,0:T(8,128)(2,1)S(1)}, bf16[320,2048]{1,0:T(8,128)(2,1)}, u32[]{:S(2)}) copy-start(bf16[320,2048]{1,0:T(8,128)(2,1)} %get-tuple-element.137) | copy-start | bytes 3932164
  184.6 27.5 %collective-permute-start.18 = (bf16[256,2048]{1,0:T(8,128)(2,1)}, bf16[256,2048]{1,0:T(8,128)(2,1)}, u32[]{:S(2)}, u32[]{:S(2)}) collective-permute-start(bf16[256,2048]{1,0:T(8,128)(2,1)} %collective-permute-done.10.refs_4_.refs_2_), channel_id=1, source_target_pairs={{0,4},{4,0},{8,12},{12,8},{16,20},{20,16},{24,28},{28,24},{1,5},{5... | collective-permute-start | bytes 3145736 | tf_op jit(solution)/shard_map/ppermute | solution.py:59
  197.6 31.1 %collective-permute-start.15 = (bf16[320,2048]{1,0:T(8,128)(2,1)}, bf16[320,2048]{1,0:T(8,128)(2,1)S(1)}, u32[]{:S(2)}, u32[]{:S(2)}) collective-permute-start(bf16[320,2048]{1,0:T(8,128)(2,1)} %get-tuple-element.151), channel_id=1, source_target_pairs={{0,2},{1,3},{2,0},{3,1},{4,6},{5,7},{6,4},{7,5},{8,10},{9,11},{10,... | collective-permute-start | bytes 3932168 | tf_op jit(solution)/shard_map/ppermute | solution.py:63
  199.4 34.1 %collective-permute-start.16 = (bf16[256,2048]{1,0:T(8,128)(2,1)}, bf16[256,2048]{1,0:T(8,128)(2,1)}, u32[]{:S(2)}, u32[]{:S(2)}) collective-permute-start(bf16[256,2048]{1,0:T(8,128)(2,1)} %collective-permute-done.13.refs_2_.refs_1_), channel_id=1, source_target_pairs={{0,8},{4,12},{8,16},{12,20},{16,24},{20,28},{24,0},{28,4},{1,9},{5... | collective-permute-start | bytes 3145736 | tf_op jit(solution)/shard_map/ppermute | solution.py:51
  212.2 23.2 %collective-permute-start.19 = (bf16[256,2048]{1,0:T(8,128)(2,1)}, bf16[256,2048]{1,0:T(8,128)(2,1)}, u32[]{:S(2)}, u32[]{:S(2)}) collective-permute-start(bf16[256,2048]{1,0:T(8,128)(2,1)} %collective-permute-done.17.refs_5_.refs_3_), channel_id=1, source_target_pairs={{0,4},{4,0},{8,12},{12,8},{16,20},{20,16},{24,28},{28,24},{1,5},{5... | collective-permute-start | bytes 3145736 | tf_op jit(solution)/shard_map/ppermute | solution.py:59
  237.8 29.9 %collective-permute-start.20 = (bf16[320,2048]{1,0:T(8,128)(2,1)S(1)}, bf16[320,2048]{1,0:T(8,128)(2,1)S(1)}, u32[]{:S(2)}, u32[]{:S(2)}) collective-permute-start(bf16[320,2048]{1,0:T(8,128)(2,1)S(1)} %add_convert_fusion.refs_0_), channel_id=1, source_target_pairs={{0,2},{1,3},{2,0},{3,1},{4,6},{5,7},{6,4},{7,5},{8,10},{9,11},{10,... | collective-permute-start | bytes 3932168 | tf_op jit(solution)/shard_map/ppermute | solution.py:63
  239.3 24.0 %collective-permute-start.21 = (bf16[256,2048]{1,0:T(8,128)(2,1)}, bf16[256,2048]{1,0:T(8,128)(2,1)}, u32[]{:S(2)}, u32[]{:S(2)}) collective-permute-start(bf16[256,2048]{1,0:T(8,128)(2,1)} %collective-permute-done.16.refs_3_.refs_2_), channel_id=1, source_target_pairs={{0,8},{4,12},{8,16},{12,20},{16,24},{20,28},{24,0},{28,4},{1,9},{5... | collective-permute-start | bytes 3145736 | tf_op jit(solution)/shard_map/ppermute | solution.py:51
  240.7 26.4 %collective-permute-start.22 = (bf16[256,2048]{1,0:T(8,128)(2,1)}, bf16[256,2048]{1,0:T(8,128)(2,1)}, u32[]{:S(2)}, u32[]{:S(2)}) collective-permute-start(bf16[256,2048]{1,0:T(8,128)(2,1)} %collective-permute-done.13.refs_2_.refs_1_), channel_id=1, source_target_pairs={{0,4},{4,0},{8,12},{12,8},{16,20},{20,16},{24,28},{28,24},{1,5},{5... | collective-permute-start | bytes 3145736 | tf_op jit(solution)/shard_map/ppermute | solution.py:59
  252.4 42.9 %collective-permute-start.23 = (bf16[256,2048]{1,0:T(8,128)(2,1)}, bf16[256,2048]{1,0:T(8,128)(2,1)S(1)}, u32[]{:S(2)}, u32[]{:S(2)}) collective-permute-start(bf16[256,2048]{1,0:T(8,128)(2,1)} %collective-permute-done.16.refs_3_.refs_2_), channel_id=1, source_target_pairs={{0,4},{4,0},{8,12},{12,8},{16,20},{20,16},{24,28},{28,24},{1,5},{5... | collective-permute-start | bytes 3145736 | tf_op jit(solution)/shard_map/ppermute | solution.py:59
  267.1 40.4 %collective-permute-start.24 = (bf16[256,2048]{1,0:T(8,128)(2,1)}, bf16[256,2048]{1,0:T(8,128)(2,1)S(1)}, u32[]{:S(2)}, u32[]{:S(2)}) collective-permute-start(bf16[256,2048]{1,0:T(8,128)(2,1)} %collective-permute-done.21.refs_4_.refs_3_), channel_id=1, source_target_pairs={{0,4},{4,0},{8,12},{12,8},{16,20},{20,16},{24,28},{28,24},{1,5},{5... | collective-permute-start | bytes 3145736 | tf_op jit(solution)/shard_map/ppermute | solution.py:59
  307.6 30.8 %collective-permute-start.25 = (bf16[256,2048]{1,0:T(8,128)(2,1)}, bf16[256,2048]{1,0:T(8,128)(2,1)S(1)}, u32[]{:S(2)}, u32[]{:S(2)}) collective-permute-start(bf16[256,2048]{1,0:T(8,128)(2,1)} %get-tuple-element.166), channel_id=1, source_target_pairs={{0,4},{4,0},{8,12},{12,8},{16,20},{20,16},{24,28},{28,24},{1,5},{5... | collective-permute-start | bytes 3145736 | tf_op jit(solution)/shard_map/ppermute | solution.py:59
  326.5 74.9 %collective-permute-start.28 = (bf16[768,2048]{1,0:T(8,128)(2,1)}, bf16[768,2048]{1,0:T(8,128)(2,1)}, u32[]{:S(2)}, u32[]{:S(2)}) collective-permute-start(bf16[768,2048]{1,0:T(8,128)(2,1)} %get-tuple-element.182), channel_id=1, source_target_pairs={{0,4},{4,0},{8,12},{12,8},{16,20},{20,16},{24,28},{28,24},{1,5},{5... | collective-permute-start | bytes 9437192 | tf_op jit(solution)/shard_map/ppermute | solution.py:59
  356.7 31.6 %collective-permute-start.26 = (bf16[320,2048]{1,0:T(8,128)(2,1)}, bf16[320,2048]{1,0:T(8,128)(2,1)}, u32[]{:S(2)}, u32[]{:S(2)}) collective-permute-start(bf16[320,2048]{1,0:T(8,128)(2,1)} %get-tuple-element.170), channel_id=1, source_target_pairs={{0,2},{1,3},{2,0},{3,1},{4,6},{5,7},{6,4},{7,5},{8,10},{9,11},{10,... | collective-permute-start | bytes 3932168 | tf_op jit(solution)/shard_map/ppermute | solution.py:63
  358.9 37.2 %collective-permute-start.30 = (bf16[256,2048]{1,0:T(8,128)(2,1)}, bf16[256,2048]{1,0:T(8,128)(2,1)}, u32[]{:S(2)}, u32[]{:S(2)}) collective-permute-start(bf16[256,2048]{1,0:T(8,128)(2,1)} %add_convert_fusion.9), channel_id=1, source_target_pairs={{0,24},{4,28},{8,0},{12,4},{16,8},{20,12},{24,16},{28,20},{1,25},{... | collective-permute-start | bytes 3145736 | tf_op jit(solution)/shard_map/ppermute | solution.py:51
  394.3 33.8 %collective-permute-start.27 = (bf16[320,2048]{1,0:T(8,128)(2,1)}, bf16[320,2048]{1,0:T(8,128)(2,1)}, u32[]{:S(2)}, u32[]{:S(2)}) collective-permute-start(bf16[320,2048]{1,0:T(8,128)(2,1)} %multiply_convert_fusion.refs_0_.refs_1_), channel_id=1, source_target_pairs={{0,2},{1,3},{2,0},{3,1},{4,6},{5,7},{6,4},{7,5},{8,10},{9,11},{10,... | collective-permute-start | bytes 3932168 | tf_op jit(solution)/shard_map/ppermute | solution.py:63
  395.1 30.9 %collective-permute-start.29 = (bf16[256,2048]{1,0:T(8,128)(2,1)}, bf16[256,2048]{1,0:T(8,128)(2,1)}, u32[]{:S(2)}, u32[]{:S(2)}) collective-permute-start(bf16[256,2048]{1,0:T(8,128)(2,1)} %get-tuple-element.183), channel_id=1, source_target_pairs={{0,4},{4,0},{8,12},{12,8},{16,20},{20,16},{24,28},{28,24},{1,5},{5... | collective-permute-start | bytes 3145736 | tf_op jit(solution)/shard_map/ppermute | solution.py:59
  404.5 34.5 %collective-permute-start.31 = (bf16[256,2048]{1,0:T(8,128)(2,1)}, bf16[256,2048]{1,0:T(8,128)(2,1)}, u32[]{:S(2)}, u32[]{:S(2)}) collective-permute-start(bf16[256,2048]{1,0:T(8,128)(2,1)} %add_convert_fusion.8), channel_id=1, source_target_pairs={{0,24},{4,28},{8,0},{12,4},{16,8},{20,12},{24,16},{28,20},{1,25},{... | collective-permute-start | bytes 3145736 | tf_op jit(solution)/shard_map/ppermute | solution.py:51
  425.3 48.7 %collective-permute-start.33 = (bf16[512,2048]{1,0:T(8,128)(2,1)}, bf16[512,2048]{1,0:T(8,128)(2,1)S(1)}, u32[]{:S(2)}, u32[]{:S(2)}) collective-permute-start(bf16[512,2048]{1,0:T(8,128)(2,1)} %get-tuple-element.195), channel_id=1, source_target_pairs={{0,4},{4,0},{8,12},{12,8},{16,20},{20,16},{24,28},{28,24},{1,5},{5... | collective-permute-start | bytes 6291464 | tf_op jit(solution)/shard_map/ppermute | solution.py:59
  428.0 40.7 %collective-permute-start.35 = (bf16[256,2048]{1,0:T(8,128)(2,1)S(1)}, bf16[256,2048]{1,0:T(8,128)(2,1)S(1)}, u32[]{:S(2)}, u32[]{:S(2)}) collective-permute-start(bf16[256,2048]{1,0:T(8,128)(2,1)S(1)} %add_convert_fusion.6), channel_id=1, source_target_pairs={{0,24},{4,28},{8,0},{12,4},{16,8},{20,12},{24,16},{28,20},{1,25},{... | collective-permute-start | bytes 3145736 | tf_op jit(solution)/shard_map/ppermute | solution.py:51
  442.5 54.7 %collective-permute-start.34 = (bf16[256,2048]{1,0:T(8,128)(2,1)}, bf16[256,2048]{1,0:T(8,128)(2,1)}, u32[]{:S(2)}, u32[]{:S(2)}) collective-permute-start(bf16[256,2048]{1,0:T(8,128)(2,1)} %add_convert_fusion.7), channel_id=1, source_target_pairs={{0,24},{4,28},{8,0},{12,4},{16,8},{20,12},{24,16},{28,20},{1,25},{... | collective-permute-start | bytes 3145736 | tf_op jit(solution)/shard_map/ppermute | solution.py:51
  467.4 29.1 %collective-permute-start.39 = (bf16[256,2048]{1,0:T(8,128)(2,1)}, bf16[256,2048]{1,0:T(8,128)(2,1)}, u32[]{:S(2)}, u32[]{:S(2)}) collective-permute-start(bf16[256,2048]{1,0:T(8,128)(2,1)} %get-tuple-element.209), channel_id=1, source_target_pairs={{0,4},{4,0},{8,12},{12,8},{16,20},{20,16},{24,28},{28,24},{1,5},{5... | collective-permute-start | bytes 3145736 | tf_op jit(solution)/shard_map/ppermute | solution.py:59
  477.5 25.2 %collective-permute-start.36 = (bf16[256,2048]{1,0:T(8,128)(2,1)}, bf16[256,2048]{1,0:T(8,128)(2,1)}, u32[]{:S(2)}, u32[]{:S(2)}) collective-permute-start(bf16[256,2048]{1,0:T(8,128)(2,1)} %add_convert_fusion.5), channel_id=1, source_target_pairs={{0,24},{4,28},{8,0},{12,4},{16,8},{20,12},{24,16},{28,20},{1,25},{... | collective-permute-start | bytes 3145736 | tf_op jit(solution)/shard_map/ppermute | solution.py:51
  478.1 58.8 %collective-permute-start.32 = (bf16[320,2048]{1,0:T(8,128)(2,1)}, bf16[320,2048]{1,0:T(8,128)(2,1)}, u32[]{:S(2)}, u32[]{:S(2)}) collective-permute-start(bf16[320,2048]{1,0:T(8,128)(2,1)} %get-tuple-element.189), channel_id=1, source_target_pairs={{0,2},{1,3},{2,0},{3,1},{4,6},{5,7},{6,4},{7,5},{8,10},{9,11},{10,... | collective-permute-start | bytes 3932168 | tf_op jit(solution)/shard_map/ppermute | solution.py:63
  490.3 28.6 %collective-permute-start.37 = (bf16[256,2048]{1,0:T(8,128)(2,1)}, bf16[256,2048]{1,0:T(8,128)(2,1)S(1)}, u32[]{:S(2)}, u32[]{:S(2)}) collective-permute-start(bf16[256,2048]{1,0:T(8,128)(2,1)} %get-tuple-element.203), channel_id=1, source_target_pairs={{0,4},{4,0},{8,12},{12,8},{16,20},{20,16},{24,28},{28,24},{1,5},{5... | collective-permute-start | bytes 3145736 | tf_op jit(solution)/shard_map/ppermute | solution.py:59
  496.5 46.4 %collective-permute-start.40 = (bf16[256,2048]{1,0:T(8,128)(2,1)}, bf16[256,2048]{1,0:T(8,128)(2,1)}, u32[]{:S(2)}, u32[]{:S(2)}) collective-permute-start(bf16[256,2048]{1,0:T(8,128)(2,1)} %get-tuple-element.210), channel_id=1, source_target_pairs={{0,4},{4,0},{8,12},{12,8},{16,20},{20,16},{24,28},{28,24},{1,5},{5... | collective-permute-start | bytes 3145736 | tf_op jit(solution)/shard_map/ppermute | solution.py:59
  505.8 38.0 %collective-permute-start.44 = (bf16[256,2048]{1,0:T(8,128)(2,1)}, bf16[256,2048]{1,0:T(8,128)(2,1)}, u32[]{:S(2)}, u32[]{:S(2)}) collective-permute-start(bf16[256,2048]{1,0:T(8,128)(2,1)} %add_convert_fusion.4), channel_id=1, source_target_pairs={{0,24},{4,28},{8,0},{12,4},{16,8},{20,12},{24,16},{28,20},{1,25},{... | collective-permute-start | bytes 3145736 | tf_op jit(solution)/shard_map/ppermute | solution.py:51
  536.2 31.5 %collective-permute-start.38 = (bf16[320,2048]{1,0:T(8,128)(2,1)}, bf16[320,2048]{1,0:T(8,128)(2,1)S(1)}, u32[]{:S(2)}, u32[]{:S(2)}) collective-permute-start(bf16[320,2048]{1,0:T(8,128)(2,1)} %get-tuple-element.206), channel_id=1, source_target_pairs={{0,2},{1,3},{2,0},{3,1},{4,6},{5,7},{6,4},{7,5},{8,10},{9,11},{10,... | collective-permute-start | bytes 3932168 | tf_op jit(solution)/shard_map/ppermute | solution.py:63
  536.8 25.4 %collective-permute-start.43 = (bf16[256,2048]{1,0:T(8,128)(2,1)S(1)}, bf16[256,2048]{1,0:T(8,128)(2,1)S(1)}, u32[]{:S(2)}, u32[]{:S(2)}) collective-permute-start(bf16[256,2048]{1,0:T(8,128)(2,1)S(1)} %add_convert_fusion.3), channel_id=1, source_target_pairs={{0,24},{4,28},{8,0},{12,4},{16,8},{20,12},{24,16},{28,20},{1,25},{... | collective-permute-start | bytes 3145736 | tf_op jit(solution)/shard_map/ppermute | solution.py:51
  541.7 28.3 %collective-permute-start.42 = (bf16[256,2048]{1,0:T(8,128)(2,1)}, bf16[256,2048]{1,0:T(8,128)(2,1)}, u32[]{:S(2)}, u32[]{:S(2)}) collective-permute-start(bf16[256,2048]{1,0:T(8,128)(2,1)} %get-tuple-element.212), channel_id=1, source_target_pairs={{0,4},{4,0},{8,12},{12,8},{16,20},{20,16},{24,28},{28,24},{1,5},{5... | collective-permute-start | bytes 3145736 | tf_op jit(solution)/shard_map/ppermute | solution.py:59
  543.0 58.0 %collective-permute-start.41 = (bf16[256,2048]{1,0:T(8,128)(2,1)}, bf16[256,2048]{1,0:T(8,128)(2,1)}, u32[]{:S(2)}, u32[]{:S(2)}) collective-permute-start(bf16[256,2048]{1,0:T(8,128)(2,1)} %get-tuple-element.211), channel_id=1, source_target_pairs={{0,4},{4,0},{8,12},{12,8},{16,20},{20,16},{24,28},{28,24},{1,5},{5... | collective-permute-start | bytes 3145736 | tf_op jit(solution)/shard_map/ppermute | solution.py:59
  548.1 19.6 %copy-start.9 = (f32[320,2048]{1,0:T(8,128)S(1)}, f32[320,2048]{1,0:T(8,128)}, u32[]{:S(2)}) copy-start(f32[320,2048]{1,0:T(8,128)} %get-tuple-element.205) | copy-start | bytes 7864324
  565.3 24.9 %collective-permute-start.45 = (bf16[256,2048]{1,0:T(8,128)(2,1)}, bf16[256,2048]{1,0:T(8,128)(2,1)}, u32[]{:S(2)}, u32[]{:S(2)}) collective-permute-start(bf16[256,2048]{1,0:T(8,128)(2,1)} %add_convert_fusion.2), channel_id=1, source_target_pairs={{0,24},{4,28},{8,0},{12,4},{16,8},{20,12},{24,16},{28,20},{1,25},{... | collective-permute-start | bytes 3145736 | tf_op jit(solution)/shard_map/ppermute | solution.py:51
  569.8 26.9 %copy-start.8 = (bf16[320,2048]{1,0:T(8,128)(2,1)S(1)}, bf16[320,2048]{1,0:T(8,128)(2,1)}, u32[]{:S(2)}) copy-start(bf16[320,2048]{1,0:T(8,128)(2,1)} %get-tuple-element.137) | copy-start | bytes 3932164
  569.8 26.9 %copy-start.10 = (f32[320,2048]{1,0:T(8,128)S(1)}, f32[320,2048]{1,0:T(8,128)}, u32[]{:S(2)}) copy-start(f32[320,2048]{1,0:T(8,128)} %get-tuple-element.205) | copy-start | bytes 7864324
  592.6 25.5 %collective-permute-start.46 = (bf16[256,2048]{1,0:T(8,128)(2,1)S(1)}, bf16[256,2048]{1,0:T(8,128)(2,1)S(1)}, u32[]{:S(2)}, u32[]{:S(2)}) collective-permute-start(bf16[256,2048]{1,0:T(8,128)(2,1)S(1)} %add_convert_fusion.1), channel_id=1, source_target_pairs={{0,24},{4,28},{8,0},{12,4},{16,8},{20,12},{24,16},{28,20},{1,25},{... | collective-permute-start | bytes 3145736 | tf_op jit(solution)/shard_map/ppermute | solution.py:51
  (30 other events, 190.7 us)

commit v4 on v3

--- a/solution.py
+++ b/solution.py
@@ -29,7 +29,7 @@
 average_keep = 0.6
 vector_rate = 0.4
 score_scale = HEAD_DIM ** (-0.5)
-query_blocks = ((0, 128), (128, 256), (256, SEG_PAD))
+query_blocks = ((0, 128), (128, SEG_PAD))
 
 RATE = 0.59e9
 
@@ -106,17 +106,36 @@
     return rest
 
 
+def halved():
+    return seq_grid()[1] == 2
+
+
+def ring_end(part, rest, ready, late=()):
+    if not halved():
+        return [[piece] for piece in ring_rest(after(part, *ready))]
+    half = part.shape[0] // 2
+    upper = shift_inner(after(part[:half], *ready), 1)
+    return [[upper, shift_outer(after(rest[0][half:], *late), 1)]]
+
+
+def stack_ring(line, rest, end):
+    pieces = list(line)
+    for j in range(seq_grid()[1] - 1):
+        pieces += [blocks[j] for blocks in rest] + end[j]
+    return [(piece, piece.shape[0]) for piece in pieces]
+
+
 def ring_scatter(near, received, held=(), sums=()):
-    sums = list(sums)
+    sums, hop = list(sums), None
     depth = received[0].shape[0]
     for n in range(len(sums), len(received)):
         i = len(received) - 1 - n
         total = near[i * depth : (i + 1) * depth].astype(f32) + received[i].astype(f32)
         if sums:
-            last = after(sums[-1], *held[n - 1 : n])
-            total = total + shift_outer(last, -1).astype(f32)
+            hop = shift_outer(after(sums[-1], *held[n - 1 : n]), -1)
+            total = total + hop.astype(f32)
         sums.append(total.astype(bf16) if i else total)
-    return sums
+    return sums, hop
 
 
 def greet(peers):
@@ -396,11 +415,8 @@
     count = len(lefts) * (2 if exchanged else 1)
     tile = max(size for size in (128, 256, 512) if width % size == 0 and start % size == 0)
     first = start // tile
-    block_depth = depth // lax.axis_size("seq")
-    specs = []
-    for block in blocks:
-        high = block_depth if block.shape[0] // block_depth < 2 else block.shape[0]
-        specs.append(pl.BlockSpec((high, tile), lambda n: (0, first + n)))
+    specs = [pl.BlockSpec((high, tile), lambda n: (0, first + n)) for _, high in blocks]
+    blocks = [block for block, _ in blocks]
     out_shape = [jax.ShapeDtypeStruct((height, width), dtype) for height, dtype in outs]
     out_specs = [pl.BlockSpec((height, tile), lambda n: (0, n)) for height, _ in outs]
     scratch = []
@@ -489,14 +505,11 @@
         first_ref[...] = result + got[1].astype(f32)
 
 
-def wide_dot(left, blocks, start, features, number, name):
+def wide_dot(left, blocks, start, features, number, name, weight=1.0):
     rows, width = left.shape
     tile = rows // 4
-    block_depth = features // lax.axis_size("seq")
-    specs = []
-    for block in blocks:
-        high = block_depth if block.shape[0] // block_depth < 2 else block.shape[0]
-        specs.append(resident((high, block.shape[1])))
+    specs = [resident((high, block.shape[1])) for block, high in blocks]
+    blocks = [block for block, _ in blocks]
     return pl.pallas_call(
         functools.partial(wide_kernel, len(blocks), start),
         out_shape=[
@@ -513,7 +526,7 @@
             pltpu.SemaphoreType.DMA((2,)),
         ],
         compiler_params=kernel_params(number),
-        cost_estimate=estimate(rows, width, features),
+        cost_estimate=estimate(rows, width * weight, features),
         name=name,
     )(left, *blocks)
 
@@ -670,28 +683,31 @@
         first_head = lane_halves(queries.shape)
         zero = jnp.zeros_like(queries)
         head_queries = (jnp.where(first_head, queries, zero), jnp.where(first_head, zero, queries))
-        outs = []
-        for low, high in query_blocks:
-            count = SLAB * s + high
-            bias = bias_ref[s, low:high, :count]
-            both = []
-            for h in range(2):
-                scores = (
-                    lax.dot_general(
-                        head_queries[h][low:high],
-                        keys[:count],
-                        (((1,), (1,)), ((), ())),
-                        preferred_element_type=f32,
-                    )
-                    + bias
-                )
-                peak = jnp.max(scores, axis=-1, keepdims=True)
-                raised = jnp.exp(scores - peak)
-                share = raised * (1.0 / jnp.sum(raised, axis=-1, keepdims=True))
-                share = share.astype(bf16)
-                p_ref[h, s * SEG_PAD + low : s * SEG_PAD + high, :count] = share
-                both.append(jnp.dot(share, values[:count], preferred_element_type=f32))
-            outs.append(jnp.where(first_head[low:high], both[0], both[1]))
+        units = [(low, high, h) for low, high in query_blocks for h in range(2)]
+        scores = [
+            lax.dot_general(
+                head_queries[h][low:high],
+                keys[: SLAB * s + high],
+                (((1,), (1,)), ((), ())),
+                preferred_element_type=f32,
+            )
+            + bias_ref[s, low:high, : SLAB * s + high]
+            for low, high, h in units
+        ]
+        shares = []
+        for (low, high, h), score in zip(units, scores):
+            raised = jnp.exp(score - jnp.max(score, axis=-1, keepdims=True))
+            share = raised * (1.0 / jnp.sum(raised, axis=-1, keepdims=True))
+            shares.append(share.astype(bf16))
+            p_ref[h, s * SEG_PAD + low : s * SEG_PAD + high, : SLAB * s + high] = shares[-1]
+        both = [
+            jnp.dot(share, values[: SLAB * s + high], preferred_element_type=f32)
+            for (low, high, h), share in zip(units, shares)
+        ]
+        outs = [
+            jnp.where(first_head[low:high], both[2 * n], both[2 * n + 1])
+            for n, (low, high) in enumerate(query_blocks)
+        ]
         out = jnp.concatenate(outs, axis=0).astype(bf16)
         store_segment(o_ref, starts[s], rows_padded, out)
 
@@ -720,7 +736,7 @@
             ),
         ),
         compiler_params=pltpu.CompilerParams(vmem_limit_bytes=48 * 2**20),
-        cost_estimate=expected(36.0),
+        cost_estimate=expected(12.0),
         name="attend",
     )(me, qkv, qkv, qkv, bias)
 
@@ -768,37 +784,45 @@
             jnp.sum(jnp.where(first_head, product, 0.0), axis=-1, keepdims=True),
             jnp.sum(jnp.where(first_head, 0.0, product), axis=-1, keepdims=True),
         )
-        query_grads = []
-        for low, high in query_blocks:
-            count = SLAB * s + high
-            both = []
-            for h in range(2):
-                share = p_ref[h, s * SEG_PAD + low : s * SEG_PAD + high, :count]
-                share_grad = lax.dot_general(
-                    head_grads[h][low:high],
-                    values[:count],
-                    (((1,), (1,)), ((), ())),
-                    preferred_element_type=f32,
-                )
-                score_grad = (
-                    share.astype(f32) * (share_grad - head_deltas[h][low:high])
-                ).astype(bf16)
-                both.append(jnp.dot(score_grad, keys[:count], preferred_element_type=f32))
-                lanes = slice(h * HEAD_DIM, (h + 1) * HEAD_DIM)
-                value_part = jnp.dot(
-                    grads_turned[lanes, low:high], share, preferred_element_type=f32
-                )
-                key_part = jnp.dot(
-                    queries_turned[lanes, low:high], score_grad, preferred_element_type=f32
-                )
-                for e in range(s):
-                    place = slice((e + 1) * SEG_PAD - SLAB, (e + 1) * SEG_PAD)
-                    value_sum[lanes, place] += value_part[:, e * SLAB : (e + 1) * SLAB]
-                    key_sum[lanes, place] += key_part[:, e * SLAB : (e + 1) * SLAB]
-                place = slice(s * SEG_PAD, s * SEG_PAD + high)
-                value_sum[lanes, place] += value_part[:, s * SLAB :]
-                key_sum[lanes, place] += key_part[:, s * SLAB :]
-            query_grads.append(jnp.where(first_head[low:high], both[0], both[1]))
+        units = [(low, high, h) for low, high in query_blocks for h in range(2)]
+        shares = [
+            p_ref[h, s * SEG_PAD + low : s * SEG_PAD + high, : SLAB * s + high]
+            for low, high, h in units
+        ]
+        share_grads = [
+            lax.dot_general(
+                head_grads[h][low:high],
+                values[: SLAB * s + high],
+                (((1,), (1,)), ((), ())),
+                preferred_element_type=f32,
+            )
+            for low, high, h in units
+        ]
+        score_grads = [
+            (share.astype(f32) * (share_grad - head_deltas[h][low:high])).astype(bf16)
+            for (low, high, h), share, share_grad in zip(units, shares, share_grads)
+        ]
+        both = [
+            jnp.dot(score_grad, keys[: SLAB * s + high], preferred_element_type=f32)
+            for (low, high, h), score_grad in zip(units, score_grads)
+        ]
+        query_grads = [
+            jnp.where(first_head[low:high], both[2 * n], both[2 * n + 1])
+            for n, (low, high) in enumerate(query_blocks)
+        ]
+        for (low, high, h), share, score_grad in zip(units, shares, score_grads):
+            lanes = slice(h * HEAD_DIM, (h + 1) * HEAD_DIM)
+            value_part = jnp.dot(grads_turned[lanes, low:high], share, preferred_element_type=f32)
+            key_part = jnp.dot(
+                queries_turned[lanes, low:high], score_grad, preferred_element_type=f32
+            )
+            for e in range(s):
+                place = slice((e + 1) * SEG_PAD - SLAB, (e + 1) * SEG_PAD)
+                value_sum[lanes, place] += value_part[:, e * SLAB : (e + 1) * SLAB]
+                key_sum[lanes, place] += key_part[:, e * SLAB : (e + 1) * SLAB]
+            place = slice(s * SEG_PAD, s * SEG_PAD + high)
+            value_sum[lanes, place] += value_part[:, s * SLAB :]
+            key_sum[lanes, place] += key_part[:, s * SLAB :]
         query_grad = (jnp.concatenate(query_grads, axis=0) * score_scale).astype(bf16)
         store_segment(dq_ref, starts[s], rows_padded, query_grad)
     key_all = key_sum[...].T.astype(bf16)
@@ -832,7 +856,7 @@
             scratch_shapes=[pltpu.VMEM((128, rows), f32), pltpu.VMEM((128, rows), f32)],
         ),
         compiler_params=pltpu.CompilerParams(vmem_limit_bytes=48 * 2**20),
-        cost_estimate=expected(23.0),
+        cost_estimate=expected(12.5),
         name="attend_back",
     )(me, qkv, qkv, qkv, out, grad, share)
 
@@ -1012,16 +1036,14 @@
         attn_line.append(shift_outer(after(attn_line[-1], *behind), 1))
         attn_rest.append(ring_rest(attn_line[-1]))
     attn_blocks = attn_line + [rest[j] for j in range(inner - 1) for rest in attn_rest]
+    attn_blocks = [(block, depth) for block in attn_blocks]
     up_line = [up_own, shift_outer(after(up_own, attn_line[-1], *attn_rest[-2]), 1)]
     up_line.append(shift_outer(up_line[1], 1))
     up_line.append(shift_outer(up_line[2], 1))
-    down_line = [down_own, shift_outer(after(down_own, up_line[2]), 1)]
-    down_line.append(shift_outer(down_line[1], 1))
-    down_line.append(shift_outer(down_line[2], 1))
     up_rest = [ring_rest(after(up_own, *attn_rest[-2]))]
     up_rest.append(ring_rest(after(up_line[1], *attn_rest[-1])))
 
-    vectors = jnp.concatenate([block[depth : depth + 1] for block in attn_blocks], axis=0)
+    vectors = jnp.concatenate([block[depth : depth + 1] for block, _ in attn_blocks], axis=0)
     vectors = vectors[:, :packed_size].astype(f32)
     norm_vals = vectors[:, :norm_size].reshape(seqs, 6, depth).transpose(1, 0, 2).reshape(6, D)
     vectors = jnp.take(vectors[:, norm_size:], back_order, axis=0)
@@ -1060,18 +1082,19 @@
     down_rest = [ring_rest(after(down_own, qkv, *up_rest[0]))]
     qkv = after(qkv, up_line[2], *up_rest[0])
     context, share = attend(qkv, bias, me_vector, parts, rows_padded)
+    down_line = [down_own, shift_outer(after(down_own, context), 1)]
     up_rest.append(ring_rest(after(up_line[2], context, *up_rest[1])))
-    up_rest.append(ring_rest(after(up_line[3], *up_rest[2])))
-    down_rest.append(ring_rest(after(down_line[1], *up_rest[3])))
-    down_rest.append(ring_rest(after(down_line[2], *up_rest[3])))
-    down_rest.append(ring_rest(after(down_line[3], *down_rest[1])))
-    up_blocks = up_line + [rest[j] for j in range(inner - 1) for rest in up_rest]
-    down_blocks = down_line + [rest[j] for j in range(inner - 1) for rest in down_rest]
+    up_end = ring_end(up_line[3], up_rest[2], up_rest[2])
+    up_ends = [part for parts in up_end for part in parts]
+    down_line.append(shift_outer(after(down_line[1], up_ends[-1]), 1))
+    down_line.append(shift_outer(down_line[2], 1))
+    down_rest.append(ring_rest(after(down_line[1], up_ends[0])))
+    up_blocks = stack_ring(up_line, up_rest, up_end)
     context = after(context, *up_rest[1])
     join_parts = wide_dot(context, attn_blocks, 3 * head_width, D, 4, "join")
-    join_parts = [join_parts[0], after(join_parts[1], down_line[1], *down_rest[0])]
+    join_parts = [join_parts[0], after(join_parts[1], up_line[3], *down_rest[0])]
     attended = scatter_chips(*join_parts) + norm_vals[4]
-    attended = after(attended, down_line[2], *up_rest[3])
+    attended = after(attended, down_line[1], *up_rest[2])
     feed_grad, cotangent_own = arrange(
         cotangent_pieces,
         [kept_all],
@@ -1086,7 +1109,8 @@
     normed_two, scale_two = norm_parts(middle)
     second_own = (normed_two * norm_vals[2] + norm_vals[3]).astype(bf16)
     second_all = gather_chips(second_own)
-    second_all = after(second_all, down_line[3], *down_rest[1])
+    down_rest.append(ring_rest(after(down_line[2], second_all[1])))
+    second_all = after(second_all, feed_grad, down_line[2], *down_rest[1])
     activated, slope, second_others = tall_dot(
         second_all,
         up_blocks,
@@ -1103,10 +1127,13 @@
     out_grad = cotangent_own.astype(f32)
     down_bias_grad = jnp.sum(kept_own * out_grad, axis=0)
 
-    activated = after(activated, *down_rest[2])
+    down_end = ring_end(down_line[3], down_rest[2], [activated, *down_rest[1]], [activated])
+    down_ends = [part for parts in down_end for part in parts]
+    down_blocks = stack_ring(down_line, down_rest, down_end)
+    activated = after(activated, down_line[3], *down_rest[2])
     down_pairs = [([feed_grad], activated)]
     down_far = far_grads(down_pairs, depth, "down_grad", (3, 1))
-    down_last = inner_sum(down_far, 1, *down_rest[3])
+    down_last = inner_sum(down_far, 1, *down_ends)
     pre_grad, unit_grad = tall_dot(
         [feed_grad],
         down_blocks,
@@ -1120,11 +1147,11 @@
     unit_grad = unit_grad[0]
     down_first = inner_sum(down_far, 0, pre_grad)
     down_near = near_grads([([after(feed_grad, pre_grad)], activated)], depth, "down_grad")
-    down_totals = ring_scatter(down_near, single_blocks([down_first, down_last], depth))
+    down_totals, _ = ring_scatter(down_near, single_blocks([down_first, down_last], depth))
     pre_grad = after(pre_grad, down_last, down_near)
     second_parts = wide_dot(pre_grad, up_blocks, 0, D, 6, "up_back")
     up_pairs = [(after(second_all, *second_parts), pre_grad)]
-    up_far = far_grads(up_pairs, depth, "up_grad", (1, 2, 1))
+    up_far = far_grads(up_pairs, depth, "up_grad", (2, 1, 1))
     up_near = near_grads(up_pairs, depth, "up_grad")
     second_grad = after(scatter_chips(*second_parts), up_near, *[far[2] for far in up_far])
     gain_two_grad = jnp.sum(second_grad * normed_two, axis=0)
@@ -1149,6 +1176,7 @@
     )
     attn_rows = attn_rows + [attn_others]
     up_middle = inner_sum(up_far, 1, down_first)
+    up_first = inner_sum(up_far, 0, up_last, context_grad)
     context_grad = after(context_grad, down_totals[2])
     feed_parts = after(feed_parts, context_grad)
     feed_out = scatter_chips(*feed_parts) + norm_vals[5]
@@ -1160,8 +1188,7 @@
     head_grad = jnp.stack(
         [jnp.sum(query_grad, axis=0, dtype=f32), jnp.sum(value_grad, axis=0, dtype=f32)]
     )
-    up_first = inner_sum(up_far, 0, up_last, qkv_grad)
-    up_totals = ring_scatter(up_near, single_blocks([up_first, up_middle, up_last], depth))
+    up_totals, up_hop = ring_scatter(up_near, single_blocks([up_first, up_middle, up_last], depth))
     down_grad, up_grad = down_totals[-1], up_totals[-1]
     attn_pairs = [
         ([after(first_all, up_totals[1])], qkv_grad),
@@ -1169,22 +1196,20 @@
     ]
     attn_far = far_grads(attn_pairs, depth, "attn_grad", (1, 1, 1, 1))
     all_far = [part for far in attn_far for part in far]
+    first_parts = wide_dot(after(qkv_grad, *all_far), attn_blocks, 0, D, 9, "project_back")
     attn_pairs = [
-        ([after(first_all, down_grad, up_totals[2], *all_far)], qkv_grad),
+        ([after(first_all, down_grad, up_totals[2], *first_parts)], qkv_grad),
         (attn_rows, context),
     ]
     attn_near = near_grads(attn_pairs, depth, "attn_grad")
     attn_sums = [None] * outer
     attn_sums[3] = inner_sum(attn_far, 3, up_middle)
     attn_sums[2] = inner_sum(attn_far, 2, up_first)
-    attn_totals = [attn_near[3 * depth :].astype(f32) + attn_sums[3].astype(f32)]
-    attn_totals[0] = attn_totals[0].astype(bf16)
-    first_parts = wide_dot(
-        after(qkv_grad, up_middle, attn_totals[0]), attn_blocks, 0, D, 9, "project_back"
-    )
-    attn_sums[1] = inner_sum(attn_far, 1, attn_sums[3], first_parts[0])
+    attn_total = attn_near[3 * depth :].astype(f32) + attn_sums[3].astype(f32)
+    attn_total = attn_total.astype(bf16)
+    attn_sums[1] = inner_sum(attn_far, 1, attn_total, up_hop)
     attn_sums[0] = inner_sum(attn_far, 0, attn_sums[2])
-    attn_totals = ring_scatter(attn_near, attn_sums, [up_totals[2], up_grad], attn_totals)
+    attn_totals, _ = ring_scatter(attn_near, attn_sums, [up_hop], [attn_total])
     first_grad = scatter_chips(*first_parts)
     normed_one, scale_one = norm_parts(inputs)
     gain_one_grad = jnp.sum(first_grad * normed_one, axis=0)

time: 680 us -> 651 us (0.957)
  Pallas kernels: 319 us -> 284 us
    ppermute x21, waiting for transfers between devices: 22.6 us -> 76.8 us  [shift_inner(): return lax.ppermute(value, 'seq', pairs)]
    ppermute x18 -> x20, waiting for transfers between devices: 155 us -> 109 us  [shift_outer(): return lax.ppermute(value, 'seq', pairs)]
    pallas_call x1, Pallas kernels: 36.3 us -> 12.3 us  [attend(): pl.pallas_call(functools.partial(attend_kernel, mp_count, rows_padded), o...]
    ppermute x8, waiting for transfers between devices: 21.7 us -> 8.56 us  [swap(): lax.ppermute(value, 'mp', [(m, m ^ bits) for m in range(lax.axis_size('mp...]
    pallas_call x1, Pallas kernels: 23.3 us -> 12.2 us  [attend_back(): pl.pallas_call(functools.partial(attend_back_kernel, mp_count, rows_padde...]
    ppermute x18 -> x20, starting transfers between devices: 25.3 us -> 25.4 us  [shift_outer(): return lax.ppermute(value, 'seq', pairs)]
  transfers between devices with their start and end apart: 47 -> 49, of which waited for: 22 -> 24; matrix products, arithmetic and copies ran while one was open for 11% -> 13% of each run, Pallas kernels for 42% -> 38%
where the time goes in v4:
time: 651 us; the launch traced here: 642 us
  Pallas kernels  284 us (44%)
  waiting for transfers between devices  194 us (30%)
  other arithmetic  66.7 us (10%)
  starting transfers between devices  60.9 us (9%)
  local copies, waits for them, and re-layouts  30.1 us (5%)
    ppermute x20, waiting for transfers between devices, shift_outer(): return lax.ppermute(value, 'seq', pairs)  109 us
    ppermute x21, waiting for transfers between devices, shift_inner(): return lax.ppermute(value, 'seq', pairs)  76.8 us
    pallas_call x4, Pallas kernels, tall_dot(): pl.pallas_call(functools.partial(tall_kernel, epilogue, exchanged, len(le...  68.5 us
    pallas_call x6, Pallas kernels, turned_dot(): pl.pallas_call(functools.partial(turned_kernel, [len(lefts) for lefts, _...  64.3 us
    pallas_call x4, Pallas kernels, wide_dot(): pl.pallas_call(functools.partial(wide_kernel, len(blocks), start), out_sh...  64 us
    ppermute x20, starting transfers between devices, shift_outer(): return lax.ppermute(value, 'seq', pairs)  25.4 us
    ppermute x21, starting transfers between devices, shift_inner(): return lax.ppermute(value, 'seq', pairs)  25 us
    pallas_call x1, Pallas kernels, adam_all(): pl.pallas_call(adam_kernel, out_shape=out_shape, grid=(depth // tile,), i...  23.3 us
  transfers between devices with their start and end apart: 49, of which 24 were waited for; matrix products, arithmetic and copies ran while one was open for 13% of the time, Pallas kernels for 38%

profile of v4, /device:TPU:0, one launch (start us, length us, event | category | flops | bytes accessed | tf_op | source)
XLA Modules:
  0.0 641.8 jit_solution(330320800539491689)
XLA Ops:
  4.9 3.0 collective-permute-start.2
  11.2 21.3 %collective-permute-done.2.refs_5_.refs_4_.refs_6_ = bf16[272,2048]{1,0:T(8,128)(2,1)S(1)} collective-permute-done((bf16[272,2048]{1,0:T(8,128)(2,1)S(1)}, bf16[272,2048]{1,0:T(8,128)(2,1)S(1)}, u32[]{:S(2)}, u32[]{:S(2)}) %collective-permute-start.2) | collective-permute-done | bytes 1114144 | tf_op jit(solution)/shard_map/ppermute | solution.py:59
  32.5 3.4 collective-permute-done.1.refs_2_.refs_1_.refs_3_
  36.6 3.1 collective-permute-done.refs_1_
  39.8 23.4 %collective-permute-done.3.refs_3_.refs_2_.refs_4_ = bf16[272,2048]{1,0:T(8,128)(2,1)} collective-permute-done((bf16[272,2048]{1,0:T(8,128)(2,1)}, bf16[272,2048]{1,0:T(8,128)(2,1)}, u32[]{:S(2)}, u32[]{:S(2)}) %collective-permute-start.3) | collective-permute-done | bytes 1114144 | tf_op jit(solution)/shard_map/ppermute | solution.py:51
  64.8 2.5 convert.38
  69.3 18.4 %collective-permute-done.6.refs_7_.refs_6_.refs_8_ = bf16[272,2048]{1,0:T(8,128)(2,1)S(1)} collective-permute-done((bf16[272,2048]{1,0:T(8,128)(2,1)}, bf16[272,2048]{1,0:T(8,128)(2,1)S(1)}, u32[]{:S(2)}, u32[]{:S(2)}) %collective-permute-start.6) | collective-permute-done | bytes 1114144 | tf_op jit(solution)/shard_map/ppermute | solution.py:59
  87.7 1.9 collective-permute-done.5.refs_4_.refs_3_.refs_5_
  106.7 6.9 %collective-permute-done.9.refs_3_.refs_1_ = bf16[256,2048]{1,0:T(8,128)(2,1)} collective-permute-done((bf16[256,2048]{1,0:T(8,128)(2,1)}, bf16[256,2048]{1,0:T(8,128)(2,1)}, u32[]{:S(2)}, u32[]{:S(2)}) %collective-permute-start.9) | collective-permute-done | bytes 1048608 | tf_op jit(solution)/shard_map/ppermute | solution.py:51
  113.7 3.7 collective-permute-done.7.refs_8_.refs_7_.refs_9_
  122.7 9.2 %first_norm.1 = (bf16[1280,2048]{1,0:T(8,128)(2,1)}, bf16[320,2048]{1,0:T(8,128)(2,1)}) custom-call(bf16[320,2048]{1,0:T(8,128)(2,1)} %copy-done.22, bf16[320,2048]{1,0:T(8,128)(2,1)} %collective-permute-done.refs_1_, f32[1,2048]{1,0:T(1,128)} %bitcast.133, f32[1,2048]{1,0:T(1,128)} %bitcast.132), custom_call_target="tpu_custom_call" | custom-call | flops 5310000128 | tf_op jit(solution)/shard_map/first_norm/pallas_call | solution.py:352
  132.0 13.6 %project.1.q_ref.k_ref.v_ref = bf16[1280,1536]{1,0:T(8,128)(2,1)} custom-call(bf16[1280,2048]{1,0:T(8,128)(2,1)} %get-tuple-element.211.refs_0_, bf16[272,2048]{1,0:T(8,128)(2,1)} %copy-done.17, bf16[272,2048]{1,0:T(8,128)(2,1)} %collective-permute-done.1.refs_2_.refs_1_.refs_3_, bf16[272,2048]{1,0:T(8,128)(2,1)} %collective-permute-done.3.refs_3_.refs_2_.refs_4_, ...), custom_call_target="tpu_custom_call" | custom-call | flops 7484038144 | tf_op jit(solution)/shard_map/project/pallas_call | solution.py:433
  147.7 12.3 %attend.1 = (bf16[1280,512]{1,0:T(8,128)(2,1)S(1)}, bf16[8,1280,512]{2,1,0:T(8,128)(2,1)}) custom-call(s32[1]{0:T(128)} %bitcast.15.me_ref, bf16[1280,1536]{1,0:T(8,128)(2,1)} %project.1.q_ref.k_ref.v_ref, bf16[1280,1536]{1,0:T(8,128)(2,1)} %project.1.q_ref.k_ref.v_ref, bf16[1280,1536]{1,0:T(8,128)(2,1)} %project.1.q_ref.k_ref.v_ref, ...), custom_call_target="tpu_custom_call" | custom-call | flops 7080000000 | tf_op jit(solution)/shard_map/attend/pallas_call | solution.py:718
  162.3 12.0 %join.1 = (f32[320,2048]{1,0:T(8,128)}, bf16[320,2048]{1,0:T(8,128)(2,1)}) custom-call(bf16[1280,512]{1,0:T(8,128)(2,1)} %copy-done, bf16[272,2048]{1,0:T(8,128)(2,1)} %copy-done.17, bf16[272,2048]{1,0:T(8,128)(2,1)} %collective-permute-done.1.refs_2_.refs_1_.refs_3_, bf16[272,2048]{1,0:T(8,128)(2,1)} %collective-permute-done.3.refs_3_.refs_2_.refs_4_, ...), custom_call_target="tpu_custom_call" | custom-call | flops 3084679424 | tf_op jit(solution)/shard_map/join/pallas_call | solution.py:513
  174.3 6.3 collective-permute-done.14.refs_5_.refs_4_
  186.1 19.3 %collective-permute-done.17.refs_8_.refs_6_ = bf16[256,2048]{1,0:T(8,128)(2,1)} collective-permute-done((bf16[256,2048]{1,0:T(8,128)(2,1)}, bf16[256,2048]{1,0:T(8,128)(2,1)}, u32[]{:S(2)}, u32[]{:S(2)}) %collective-permute-start.17) | collective-permute-done | bytes 1048608 | tf_op jit(solution)/shard_map/ppermute | solution.py:59
  212.7 2.3 collective-permute-start.18
  215.0 3.4 collective-permute-done.19.refs_10_.refs_8_
  222.0 8.6 %feed_grad.1 = (bf16[1280,2048]{1,0:T(8,128)(2,1)}, bf16[320,2048]{1,0:T(8,128)(2,1)}) custom-call(bf16[320,2048]{1,0:T(8,128)(2,1)} %copy-done.23, bf16[320,2048]{1,0:T(8,128)(2,1)} %collective-permute-done.8.refs_1_, f32[1280,1]{1,0:T(8,128)} %select_n.167.refs_2_), custom_call_target="tpu_custom_call" | custom-call | flops 5310000128 | tf_op jit(solution)/shard_map/feed_grad/pallas_call | solution.py:352
  230.6 11.1 %collective-permute-done.20.refs_3_.refs_2_ = bf16[256,2048]{1,0:T(8,128)(2,1)} collective-permute-done((bf16[256,2048]{1,0:T(8,128)(2,1)}, bf16[256,2048]{1,0:T(8,128)(2,1)}, u32[]{:S(2)}, u32[]{:S(2)}) %collective-permute-start.20) | collective-permute-done | bytes 1048608 | tf_op jit(solution)/shard_map/ppermute | solution.py:51
  243.6 26.5 %up.1 = (bf16[1280,2048]{1,0:T(8,128)(2,1)}, bf16[1280,2048]{1,0:T(8,128)(2,1)}, bf16[640,2048]{1,0:T(8,128)(2,1)}) custom-call(bf16[320,2048]{1,0:T(8,128)(2,1)} %add_convert_fusion.refs_0_, bf16[320,2048]{1,0:T(8,128)(2,1)} %collective-permute-done.18.refs_1_, bf16[256,2048]{1,0:T(8,128)(2,1)} %get-tuple-element.143.refs_2_.refs_0_, ...), custom_call_target="tpu_custom_call" | custom-call | flops 9683718144 | tf_op jit(solution)/shard_map/up/pallas_call | solution.py:433
  271.1 2.0 collective-permute-start.26
  273.1 11.1 %down_grad_far.1 = (bf16[768,2048]{1,0:T(8,128)(2,1)}, bf16[256,2048]{1,0:T(8,128)(2,1)}) custom-call(bf16[1280,2048]{1,0:T(8,128)(2,1)} %get-tuple-element.170.refs_0_, bf16[1280,2048]{1,0:T(8,128)(2,1)} %get-tuple-element.180.refs_1_.left_ref), custom_call_target="tpu_custom_call" | custom-call | flops 5284358656 | tf_op jit(solution)/shard_map/down_grad_far/pallas_call | solution.py:570
  284.3 2.9 collective-permute-done.26.refs_9_.refs_8_
  288.4 17.5 %down_back.1 = (bf16[1280,2048]{1,0:T(8,128)(2,1)}, f32[8,2048]{1,0:T(8,128)}) custom-call(bf16[1280,2048]{1,0:T(8,128)(2,1)} %get-tuple-element.170.refs_0_, bf16[256,2048]{1,0:T(8,128)(2,1)} %get-tuple-element.152.refs_1_.refs_0_, bf16[256,2048]{1,0:T(8,128)(2,1)} %collective-permute-done.16.refs_2_.refs_1_, ...), custom_call_target="tpu_custom_call" | custom-call | flops 9683718144 | tf_op jit(solution)/shard_map/down_back/pallas_call | solution.py:433
  307.6 9.9 %down_grad_near.1 = bf16[1024,2048]{1,0:T(8,128)(2,1)} custom-call(bf16[1280,2048]{1,0:T(8,128)(2,1)} %get-tuple-element.170.refs_0_, bf16[1280,2048]{1,0:T(8,128)(2,1)} %get-tuple-element.180.refs_1_.left_ref), custom_call_target="tpu_custom_call" | custom-call | flops 5284358656 | tf_op jit(solution)/shard_map/down_grad_near/pallas_call | solution.py:570
  317.6 18.3 %up_back.1 = (f32[320,2048]{1,0:T(8,128)}, bf16[320,2048]{1,0:T(8,128)(2,1)}) custom-call(bf16[1280,2048]{1,0:T(8,128)(2,1)} %get-tuple-element.171.left_ref.refs_3_, bf16[256,2048]{1,0:T(8,128)(2,1)} %get-tuple-element.143.refs_2_.refs_0_, bf16[256,2048]{1,0:T(8,128)(2,1)} %collective-permute-done.9.refs_3_.refs_1_, ...), custom_call_target="tpu_custom_call" | custom-call | flops 9683718144 | tf_op jit(solution)/shard_map/up_back/pallas_call | solution.py:513
  337.2 2.6 add_convert_fusion.9
  339.8 2.2 collective-permute-start.32
  342.0 10.2 %up_grad_near.1 = bf16[1024,2048]{1,0:T(8,128)(2,1)} custom-call(bf16[320,2048]{1,0:T(8,128)(2,1)} %add_convert_fusion.refs_0_, bf16[320,2048]{1,0:T(8,128)(2,1)} %collective-permute-done.18.refs_1_, bf16[640,2048]{1,0:T(8,128)(2,1)} %get-tuple-element.177.refs_2_, bf16[1280,2048]{1,0:T(8,128)(2,1)} %get-tuple-element.171.left_ref.refs_3_), custom_call_target="tpu_custom_call" | custom-call | flops 5284358656 | tf_op jit(solution)/shard_map/up_grad_near/pallas_call | solution.py:570
  352.2 11.2 %up_grad_far.1 = (bf16[512,2048]{1,0:T(8,128)(2,1)}, bf16[256,2048]{1,0:T(8,128)(2,1)}, bf16[256,2048]{1,0:T(8,128)(2,1)}) custom-call(bf16[320,2048]{1,0:T(8,128)(2,1)} %add_convert_fusion.refs_0_, bf16[320,2048]{1,0:T(8,128)(2,1)} %collective-permute-done.18.refs_1_, bf16[640,2048]{1,0:T(8,128)(2,1)} %get-tuple-element.177.refs_2_, ...), custom_call_target="tpu_custom_call" | custom-call | flops 5284358656 | tf_op jit(solution)/shard_map/up_grad_far/pallas_call | solution.py:570
  363.4 4.1 collective-permute-done.28
  367.5 2.4 convert_add_fusion.3
  375.3 5.7 collective-permute-done.30
  381.0 3.1 add_convert_fusion.8
  384.1 1.9 collective-permute-start.33
  386.0 18.2 %down.1 = (f32[320,2048]{1,0:T(8,128)}, bf16[320,2048]{1,0:T(8,128)(2,1)}) custom-call(bf16[1280,2048]{1,0:T(8,128)(2,1)} %get-tuple-element.180.refs_1_.left_ref, bf16[256,2048]{1,0:T(8,128)(2,1)} %get-tuple-element.152.refs_1_.refs_0_, bf16[256,2048]{1,0:T(8,128)(2,1)} %collective-permute-done.16.refs_2_.refs_1_, ...), custom_call_target="tpu_custom_call" | custom-call | flops 9683718144 | tf_op jit(solution)/shard_map/down/pallas_call | solution.py:513
  405.5 2.9 add_convert_fusion.6
  410.1 10.8 %join_back.1 = (bf16[1280,512]{1,0:T(8,128)(2,1)}, bf16[640,2048]{1,0:T(8,128)(2,1)}) custom-call(bf16[320,2048]{1,0:T(8,128)(2,1)} %copy-done.13, bf16[320,2048]{1,0:T(8,128)(2,1)} %copy-done.16, bf16[272,2048]{1,0:T(8,128)(2,1)} %copy-done.17, bf16[272,2048]{1,0:T(8,128)(2,1)} %collective-permute-done.1.refs_2_.refs_1_.refs_3_, ...), custom_call_target="tpu_custom_call" | custom-call | flops 3084679424 | tf_op jit(solution)/shard_map/join_back/pallas_call | solution.py:433
  422.5 3.4 add_convert_fusion.7
  425.9 12.2 %attend_back.1 = (bf16[1280,512]{1,0:T(8,128)(2,1)S(1)}, bf16[1280,512]{1,0:T(8,128)(2,1)S(1)}, bf16[1280,512]{1,0:T(8,128)(2,1)S(1)}) custom-call(s32[1]{0:T(128)} %bitcast.15.me_ref, bf16[1280,1536]{1,0:T(8,128)(2,1)} %project.1.q_ref.k_ref.v_ref, bf16[1280,1536]{1,0:T(8,128)(2,1)} %project.1.q_ref.k_ref.v_ref, ...), custom_call_target="tpu_custom_call" | custom-call | flops 7375000064 | tf_op jit(solution)/shard_map/attend_back/pallas_call | solution.py:841
  441.5 3.8 add_convert_fusion.5
  445.3 2.2 collective-permute-start.40
  447.6 11.4 %attn_grad_far.1 = (bf16[256,2048]{1,0:T(8,128)(2,1)}, bf16[256,2048]{1,0:T(8,128)(2,1)}, bf16[256,2048]{1,0:T(8,128)(2,1)}, bf16[256,2048]{1,0:T(8,128)(2,1)}) custom-call(bf16[1280,2048]{1,0:T(8,128)(2,1)} %get-tuple-element.211.refs_0_, bf16[320,2048]{1,0:T(8,128)(2,1)} %copy-done.13, bf16[320,2048]{1,0:T(8,128)(2,1)} %copy-done.16, ...), custom_call_target="tpu_custom_call" | custom-call | flops 5284358656 | tf_op jit(solution)/shard_map/attn_grad_far/pallas_call | solution.py:570
  460.1 15.5 %project_back.1 = (f32[320,2048]{1,0:T(8,128)}, bf16[320,2048]{1,0:T(8,128)(2,1)}) custom-call(bf16[1280,1536]{1,0:T(8,128)(2,1)} %copy-done.15, bf16[272,2048]{1,0:T(8,128)(2,1)} %copy-done.17, bf16[272,2048]{1,0:T(8,128)(2,1)} %collective-permute-done.1.refs_2_.refs_1_.refs_3_, bf16[272,2048]{1,0:T(8,128)(2,1)} %collective-permute-done.3.refs_3_.refs_2_.refs_4_, ...), custom_call_target="tpu_custom_call" | custom-call | flops 7484038144 | tf_op jit(solution)/shard_map/project_back/pallas_call | solution.py:513
  476.5 4.8 multiply_reduce_fusion.6
  481.3 2.1 multiply_add_fusion.in_ref
  483.5 3.1 add_convert_fusion.4
  491.1 10.5 %attn_grad_near.1 = bf16[1024,2048]{1,0:T(8,128)(2,1)} custom-call(bf16[1280,2048]{1,0:T(8,128)(2,1)} %get-tuple-element.211.refs_0_, bf16[320,2048]{1,0:T(8,128)(2,1)} %copy-done.13, bf16[320,2048]{1,0:T(8,128)(2,1)} %copy-done.16, bf16[640,2048]{1,0:T(8,128)(2,1)} %get-tuple-element.200.refs_3_, bf16[1280,1536]{1,0:T(8,128)(2,1)} %copy-done.15, ...), custom_call_target="tpu_custom_call" | custom-call | flops 5284358656 | tf_op jit(solution)/shard_map/attn_grad_near/pallas_call | solution.py:570
  501.7 2.7 add_convert_fusion.3
  504.4 7.5 %collective-permute-done.44 = bf16[256,2048]{1,0:T(8,128)(2,1)S(1)} collective-permute-done((bf16[256,2048]{1,0:T(8,128)(2,1)}, bf16[256,2048]{1,0:T(8,128)(2,1)S(1)}, u32[]{:S(2)}, u32[]{:S(2)}) %collective-permute-start.44) | collective-permute-done | bytes 1048608 | tf_op jit(solution)/shard_map/ppermute | solution.py:51
  511.9 3.8 collective-permute-start.46
  520.2 17.6 %collective-permute-done.46 = bf16[256,2048]{1,0:T(8,128)(2,1)} collective-permute-done((bf16[256,2048]{1,0:T(8,128)(2,1)}, bf16[256,2048]{1,0:T(8,128)(2,1)}, u32[]{:S(2)}, u32[]{:S(2)}) %collective-permute-start.46) | collective-permute-done | bytes 1048608 | tf_op jit(solution)/shard_map/ppermute | solution.py:51
  537.8 2.4 add_convert_fusion.2
  540.2 4.3 collective-permute-start.47
  544.7 1.8 collective-permute-start.42
  546.6 18.9 %collective-permute-done.47 = bf16[256,2048]{1,0:T(8,128)(2,1)S(1)} collective-permute-done((bf16[256,2048]{1,0:T(8,128)(2,1)S(1)}, bf16[256,2048]{1,0:T(8,128)(2,1)S(1)}, u32[]{:S(2)}, u32[]{:S(2)}) %collective-permute-start.47) | collective-permute-done | bytes 1048608 | tf_op jit(solution)/shard_map/ppermute | solution.py:51
  566.0 4.3 collective-permute-start.48
  570.4 2.9 fusion.8.in_ref
  575.0 4.0 multiply_reduce_fusion.7
  579.1 11.3 %collective-permute-done.48 = bf16[256,2048]{1,0:T(8,128)(2,1)S(1)} collective-permute-done((bf16[256,2048]{1,0:T(8,128)(2,1)S(1)}, bf16[256,2048]{1,0:T(8,128)(2,1)S(1)}, u32[]{:S(2)}, u32[]{:S(2)}) %collective-permute-start.48) | collective-permute-done | bytes 1048608 | tf_op jit(solution)/shard_map/ppermute | solution.py:51
  590.4 2.5 multiply_reduce_fusion.8
  594.9 17.7 %reduce_all.1 = (f32[24,128]{1,0:T(8,128)S(1)}, f32[8,128]{1,0:T(8,128)S(1)}) custom-call(f32[8,24,128]{2,1,0:T(8,128)S(1)} %bitcast.118, f32[8,128]{1,0:T(8,128)S(1)} %pad.40.refs_1_), custom_call_target="tpu_custom_call" | custom-call | flops 7080000000 | tf_op jit(solution)/shard_map/reduce_all/pallas_call | solution.py:217
  615.8 23.3 %adam_all.1 = (f32[4,256,512]{2,1,0:T(8,128)}, f32[4,256,512]{2,1,0:T(8,128)}, f32[4,256,512]{2,1,0:T(8,128)}, f32[4,256,512]{2,1,0:T(8,128)}, bf16[4,256,512]{2...) custom-call(f32[8,128]{1,0:T(8,128)} %copy-done.4, ...), custom_call_target="tpu_custom_call" | custom-call | flops 11800000512 | tf_op jit(solution)/shard_map/adam_all/pallas_call | solution.py:964
  (305 shorter events, 92.3 us)
Async XLA Ops:
  4.7 31.8 %copy-start.42 = (s32[1,4,50]{2,1,0:T(4,128)S(1)}, s32[1,4,50]{2,1,0:T(4,128)}, u32[]{:S(2)}) copy-start(s32[1,4,50]{2,1,0:T(4,128)} %param.31) | copy-start | bytes 2404
  4.7 31.8 %copy-start.43 = (s32[1,4]{1,0:T(1,128)S(1)}, s32[1,4]{1,0:T(1,128)}, u32[]{:S(2)}) copy-start(s32[1,4]{1,0:T(1,128)} %param.30) | copy-start | bytes 52
  4.9 62.4 %copy-start.17 = (bf16[272,2048]{1,0:T(8,128)(2,1)}, bf16[272,2048]{1,0:T(8,128)(2,1)S(1)}, u32[]{:S(2)}) copy-start(bf16[272,2048]{1,0:T(8,128)(2,1)S(1)} %pad_maximum_fusion.refs_1_.refs_0_.refs_2_) | copy-start | bytes 3342340
  4.9 27.6 %collective-permute-start.2 = (bf16[272,2048]{1,0:T(8,128)(2,1)S(1)}, bf16[272,2048]{1,0:T(8,128)(2,1)S(1)}, u32[]{:S(2)}, u32[]{:S(2)}) collective-permute-start(bf16[272,2048]{1,0:T(8,128)(2,1)S(1)} %pad_maximum_fusion.refs_1_.refs_0_.refs_2_), channel_id=1, source_target_pairs={{0,4},{4,0},{8,12},{12,8},{16,20},{20,16},{24,28},{28,24},{1,5},{5... | collective-permute-start | bytes 3342344 | tf_op jit(solution)/shard_map/ppermute | solution.py:59
  7.9 28.0 %collective-permute-start.1 = (bf16[272,2048]{1,0:T(8,128)(2,1)S(1)}, bf16[272,2048]{1,0:T(8,128)(2,1)}, u32[]{:S(2)}, u32[]{:S(2)}) collective-permute-start(bf16[272,2048]{1,0:T(8,128)(2,1)S(1)} %pad_maximum_fusion.refs_1_.refs_0_.refs_2_), channel_id=1, source_target_pairs={{0,8},{4,12},{8,16},{12,20},{16,24},{20,28},{24,0},{28,4},{1,9},{5... | collective-permute-start | bytes 3342344 | tf_op jit(solution)/shard_map/ppermute | solution.py:51
  9.6 57.6 %copy-start.22 = (bf16[320,2048]{1,0:T(8,128)(2,1)}, bf16[320,2048]{1,0:T(8,128)(2,1)S(1)}, u32[]{:S(2)}) copy-start(bf16[320,2048]{1,0:T(8,128)(2,1)S(1)} %pad.33.refs_0_) | copy-start | bytes 3932164
  9.7 30.1 %collective-permute-start = (bf16[320,2048]{1,0:T(8,128)(2,1)S(1)}, bf16[320,2048]{1,0:T(8,128)(2,1)}, u32[]{:S(2)}, u32[]{:S(2)}) collective-permute-start(bf16[320,2048]{1,0:T(8,128)(2,1)S(1)} %pad.33.refs_0_), channel_id=1, source_target_pairs={{0,2},{1,3},{2,0},{3,1},{4,6},{5,7},{6,4},{7,5},{8,10},{9,11},{10,... | collective-permute-start | bytes 3932168 | tf_op jit(solution)/shard_map/ppermute | solution.py:63
  32.5 67.3 %copy-start.26 = (bf16[272,2048]{1,0:T(8,128)(2,1)}, bf16[272,2048]{1,0:T(8,128)(2,1)S(1)}, u32[]{:S(2)}) copy-start(bf16[272,2048]{1,0:T(8,128)(2,1)S(1)} %collective-permute-done.2.refs_5_.refs_4_.refs_6_) | copy-start | bytes 3342340
  35.9 27.3 %collective-permute-start.3 = (bf16[272,2048]{1,0:T(8,128)(2,1)}, bf16[272,2048]{1,0:T(8,128)(2,1)}, u32[]{:S(2)}, u32[]{:S(2)}) collective-permute-start(bf16[272,2048]{1,0:T(8,128)(2,1)} %collective-permute-done.1.refs_2_.refs_1_.refs_3_), channel_id=1, source_target_pairs={{0,8},{4,12},{8,16},{12,20},{16,24},{20,28},{24,0},{28,4},{1,9},{5... | collective-permute-start | bytes 3342344 | tf_op jit(solution)/shard_map/ppermute | solution.py:51
  35.9 27.3 %collective-permute-start.4 = (bf16[272,2048]{1,0:T(8,128)(2,1)}, bf16[272,2048]{1,0:T(8,128)(2,1)}, u32[]{:S(2)}, u32[]{:S(2)}) collective-permute-start(bf16[272,2048]{1,0:T(8,128)(2,1)} %collective-permute-done.1.refs_2_.refs_1_.refs_3_), channel_id=1, source_target_pairs={{0,4},{4,0},{8,12},{12,8},{16,20},{20,16},{24,28},{28,24},{1,5},{5... | collective-permute-start | bytes 3342344 | tf_op jit(solution)/shard_map/ppermute | solution.py:59
  63.2 26.4 %collective-permute-start.5 = (bf16[272,2048]{1,0:T(8,128)(2,1)}, bf16[272,2048]{1,0:T(8,128)(2,1)}, u32[]{:S(2)}, u32[]{:S(2)}) collective-permute-start(bf16[272,2048]{1,0:T(8,128)(2,1)} %collective-permute-done.3.refs_3_.refs_2_.refs_4_), channel_id=1, source_target_pairs={{0,8},{4,12},{8,16},{12,20},{16,24},{20,28},{24,0},{28,4},{1,9},{5... | collective-permute-start | bytes 3342344 | tf_op jit(solution)/shard_map/ppermute | solution.py:51
  63.2 24.5 %collective-permute-start.6 = (bf16[272,2048]{1,0:T(8,128)(2,1)}, bf16[272,2048]{1,0:T(8,128)(2,1)S(1)}, u32[]{:S(2)}, u32[]{:S(2)}) collective-permute-start(bf16[272,2048]{1,0:T(8,128)(2,1)} %collective-permute-done.3.refs_3_.refs_2_.refs_4_), channel_id=1, source_target_pairs={{0,4},{4,0},{8,12},{12,8},{16,20},{20,16},{24,28},{28,24},{1,5},{5... | collective-permute-start | bytes 3342344 | tf_op jit(solution)/shard_map/ppermute | solution.py:59
  67.3 24.5 %copy-start.25 = (bf16[306,2048]{1,0:T(8,128)(2,1)S(1)}, bf16[306,2048]{1,0:T(8,128)(2,1)}, u32[]{:S(2)}) copy-start(bf16[306,2048]{1,0:T(8,128)(2,1)} %param.29) | copy-start | bytes 3760132
  89.6 24.0 %collective-permute-start.9 = (bf16[256,2048]{1,0:T(8,128)(2,1)}, bf16[256,2048]{1,0:T(8,128)(2,1)}, u32[]{:S(2)}, u32[]{:S(2)}) collective-permute-start(bf16[256,2048]{1,0:T(8,128)(2,1)} %get-tuple-element.143.refs_2_.refs_0_), channel_id=1, source_target_pairs={{0,8},{4,12},{8,16},{12,20},{16,24},{20,28},{24,0},{28,4},{1,9},{5... | collective-permute-start | bytes 3145736 | tf_op jit(solution)/shard_map/ppermute | solution.py:51
  89.6 27.7 %collective-permute-start.7 = (bf16[272,2048]{1,0:T(8,128)(2,1)}, bf16[272,2048]{1,0:T(8,128)(2,1)S(1)}, u32[]{:S(2)}, u32[]{:S(2)}) collective-permute-start(bf16[272,2048]{1,0:T(8,128)(2,1)} %collective-permute-done.5.refs_4_.refs_3_.refs_5_), channel_id=1, source_target_pairs={{0,4},{4,0},{8,12},{12,8},{16,20},{20,16},{24,28},{28,24},{1,5},{5... | collective-permute-start | bytes 3342344 | tf_op jit(solution)/shard_map/ppermute | solution.py:59
  91.9 39.9 %copy-start.23 = (bf16[320,2048]{1,0:T(8,128)(2,1)}, bf16[320,2048]{1,0:T(8,128)(2,1)S(1)}, u32[]{:S(2)}) copy-start(bf16[320,2048]{1,0:T(8,128)(2,1)S(1)} %pad.36.refs_0_) | copy-start | bytes 3932164
  93.2 24.2 %copy-start.40 = (bf16[1,2048]{1,0:T(2,128)(2,1)S(1)}, bf16[1,2048]{1,0:T(2,128)(2,1)}, u32[]{:S(2)}) copy-start(bf16[1,2048]{1,0:T(2,128)(2,1)} %slice.219) | copy-start | bytes 12292
  101.1 30.8 %collective-permute-start.8 = (bf16[320,2048]{1,0:T(8,128)(2,1)S(1)}, bf16[320,2048]{1,0:T(8,128)(2,1)}, u32[]{:S(2)}, u32[]{:S(2)}) collective-permute-start(bf16[320,2048]{1,0:T(8,128)(2,1)S(1)} %pad.36.refs_0_), channel_id=1, source_target_pairs={{0,2},{1,3},{2,0},{3,1},{4,6},{5,7},{6,4},{7,5},{8,10},{9,11},{10,... | collective-permute-start | bytes 3932168 | tf_op jit(solution)/shard_map/ppermute | solution.py:63
  103.7 41.9 %collective-permute-start.11 = (bf16[256,2048]{1,0:T(8,128)(2,1)}, bf16[256,2048]{1,0:T(8,128)(2,1)}, u32[]{:S(2)}, u32[]{:S(2)}) collective-permute-start(bf16[256,2048]{1,0:T(8,128)(2,1)} %get-tuple-element.143.refs_2_.refs_0_), channel_id=1, source_target_pairs={{0,4},{4,0},{8,12},{12,8},{16,20},{20,16},{24,28},{28,24},{1,5},{5... | collective-permute-start | bytes 3145736 | tf_op jit(solution)/shard_map/ppermute | solution.py:59
  113.6 33.0 %collective-permute-start.10 = (bf16[256,2048]{1,0:T(8,128)(2,1)}, bf16[256,2048]{1,0:T(8,128)(2,1)}, u32[]{:S(2)}, u32[]{:S(2)}) collective-permute-start(bf16[256,2048]{1,0:T(8,128)(2,1)} %collective-permute-done.9.refs_3_.refs_1_), channel_id=1, source_target_pairs={{0,8},{4,12},{8,16},{12,20},{16,24},{20,28},{24,0},{28,4},{1,9},{5... | collective-permute-start | bytes 3145736 | tf_op jit(solution)/shard_map/ppermute | solution.py:51
  121.7 40.6 %collective-permute-start.12 = (bf16[256,2048]{1,0:T(8,128)(2,1)}, bf16[256,2048]{1,0:T(8,128)(2,1)S(1)}, u32[]{:S(2)}, u32[]{:S(2)}) collective-permute-start(bf16[256,2048]{1,0:T(8,128)(2,1)} %collective-permute-done.9.refs_3_.refs_1_), channel_id=1, source_target_pairs={{0,4},{4,0},{8,12},{12,8},{16,20},{20,16},{24,28},{28,24},{1,5},{5... | collective-permute-start | bytes 3145736 | tf_op jit(solution)/shard_map/ppermute | solution.py:59
  145.6 35.0 %collective-permute-start.14 = (bf16[256,2048]{1,0:T(8,128)(2,1)S(1)}, bf16[256,2048]{1,0:T(8,128)(2,1)S(1)}, u32[]{:S(2)}, u32[]{:S(2)}) collective-permute-start(bf16[256,2048]{1,0:T(8,128)(2,1)S(1)} %copy-done.29), channel_id=1, source_target_pairs={{0,4},{4,0},{8,12},{12,8},{16,20},{20,16},{24,28},{28,24},{1,5},{5... | collective-permute-start | bytes 3145736 | tf_op jit(solution)/shard_map/ppermute | solution.py:59
  146.7 33.9 %collective-permute-start.13 = (bf16[256,2048]{1,0:T(8,128)(2,1)}, bf16[256,2048]{1,0:T(8,128)(2,1)S(1)}, u32[]{:S(2)}, u32[]{:S(2)}) collective-permute-start(bf16[256,2048]{1,0:T(8,128)(2,1)} %collective-permute-done.10.refs_4_.refs_2_), channel_id=1, source_target_pairs={{0,8},{4,12},{8,16},{12,20},{16,24},{20,28},{24,0},{28,4},{1,9},{5... | collective-permute-start | bytes 3145736 | tf_op jit(solution)/shard_map/ppermute | solution.py:51
  181.6 26.8 %collective-permute-start.15 = (bf16[320,2048]{1,0:T(8,128)(2,1)}, bf16[320,2048]{1,0:T(8,128)(2,1)S(1)}, u32[]{:S(2)}, u32[]{:S(2)}) collective-permute-start(bf16[320,2048]{1,0:T(8,128)(2,1)} %get-tuple-element.151), channel_id=1, source_target_pairs={{0,2},{1,3},{2,0},{3,1},{4,6},{5,7},{6,4},{7,5},{8,10},{9,11},{10,... | collective-permute-start | bytes 3932168 | tf_op jit(solution)/shard_map/ppermute | solution.py:63
  183.1 22.3 %collective-permute-start.17 = (bf16[256,2048]{1,0:T(8,128)(2,1)}, bf16[256,2048]{1,0:T(8,128)(2,1)}, u32[]{:S(2)}, u32[]{:S(2)}) collective-permute-start(bf16[256,2048]{1,0:T(8,128)(2,1)} %collective-permute-done.10.refs_4_.refs_2_), channel_id=1, source_target_pairs={{0,4},{4,0},{8,12},{12,8},{16,20},{20,16},{24,28},{28,24},{1,5},{5... | collective-permute-start | bytes 3145736 | tf_op jit(solution)/shard_map/ppermute | solution.py:59
  184.3 24.2 %copy-start.19 = (f32[320,2048]{1,0:T(8,128)S(1)}, f32[320,2048]{1,0:T(8,128)}, u32[]{:S(2)}) copy-start(f32[320,2048]{1,0:T(8,128)} %get-tuple-element.148) | copy-start | bytes 7864324
  184.4 25.0 %collective-permute-start.16 = (bf16[256,2048]{1,0:T(8,128)(2,1)}, bf16[256,2048]{1,0:T(8,128)(2,1)}, u32[]{:S(2)}, u32[]{:S(2)}) collective-permute-start(bf16[256,2048]{1,0:T(8,128)(2,1)} %get-tuple-element.152.refs_1_.refs_0_), channel_id=1, source_target_pairs={{0,8},{4,12},{8,16},{12,20},{16,24},{20,28},{24,0},{28,4},{1,9},{5... | collective-permute-start | bytes 3145736 | tf_op jit(solution)/shard_map/ppermute | solution.py:51
  206.5 11.9 %collective-permute-start.19 = (bf16[128,2048]{1,0:T(8,128)(2,1)S(1)}, bf16[128,2048]{1,0:T(8,128)(2,1)S(1)}, u32[]{:S(2)}, u32[]{:S(2)}) collective-permute-start(bf16[128,2048]{1,0:T(8,128)(2,1)S(1)} %slice.316), channel_id=1, source_target_pairs={{0,8},{4,12},{8,16},{12,20},{16,24},{20,28},{24,0},{28,4},{1,9},{5... | collective-permute-start | bytes 1572872 | tf_op jit(solution)/shard_map/ppermute | solution.py:51
  206.5 11.9 %collective-permute-start.21 = (bf16[128,2048]{1,0:T(8,128)(2,1)S(1)}, bf16[128,2048]{1,0:T(8,128)(2,1)S(1)}, u32[]{:S(2)}, u32[]{:S(2)}) collective-permute-start(bf16[128,2048]{1,0:T(8,128)(2,1)S(1)} %slice.317), channel_id=1, source_target_pairs={{0,4},{4,0},{8,12},{12,8},{16,20},{20,16},{24,28},{28,24},{1,5},{5... | collective-permute-start | bytes 1572872 | tf_op jit(solution)/shard_map/ppermute | solution.py:59
  210.6 161.8 %copy-start.5 = (f32[320,2048]{1,0:T(8,128)}, f32[320,2048]{1,0:T(8,128)S(1)}, u32[]{:S(2)}) copy-start(f32[320,2048]{1,0:T(8,128)S(1)} %get-tuple-element.268) | copy-start | bytes 7864324
  212.7 29.0 %collective-permute-start.18 = (bf16[320,2048]{1,0:T(8,128)(2,1)}, bf16[320,2048]{1,0:T(8,128)(2,1)}, u32[]{:S(2)}, u32[]{:S(2)}) collective-permute-start(bf16[320,2048]{1,0:T(8,128)(2,1)} %add_convert_fusion.refs_0_), channel_id=1, source_target_pairs={{0,2},{1,3},{2,0},{3,1},{4,6},{5,7},{6,4},{7,5},{8,10},{9,11},{10,... | collective-permute-start | bytes 3932168 | tf_op jit(solution)/shard_map/ppermute | solution.py:63
  218.4 23.3 %collective-permute-start.20 = (bf16[256,2048]{1,0:T(8,128)(2,1)}, bf16[256,2048]{1,0:T(8,128)(2,1)}, u32[]{:S(2)}, u32[]{:S(2)}) collective-permute-start(bf16[256,2048]{1,0:T(8,128)(2,1)} %collective-permute-done.16.refs_2_.refs_1_), channel_id=1, source_target_pairs={{0,8},{4,12},{8,16},{12,20},{16,24},{20,28},{24,0},{28,4},{1,9},{5... | collective-permute-start | bytes 3145736 | tf_op jit(solution)/shard_map/ppermute | solution.py:51
  219.3 24.3 %collective-permute-start.22 = (bf16[256,2048]{1,0:T(8,128)(2,1)}, bf16[256,2048]{1,0:T(8,128)(2,1)}, u32[]{:S(2)}, u32[]{:S(2)}) collective-permute-start(bf16[256,2048]{1,0:T(8,128)(2,1)} %collective-permute-done.16.refs_2_.refs_1_), channel_id=1, source_target_pairs={{0,4},{4,0},{8,12},{12,8},{16,20},{20,16},{24,28},{28,24},{1,5},{5... | collective-permute-start | bytes 3145736 | tf_op jit(solution)/shard_map/ppermute | solution.py:59
  241.7 28.4 %collective-permute-start.23 = (bf16[256,2048]{1,0:T(8,128)(2,1)}, bf16[256,2048]{1,0:T(8,128)(2,1)S(1)}, u32[]{:S(2)}, u32[]{:S(2)}) collective-permute-start(bf16[256,2048]{1,0:T(8,128)(2,1)} %collective-permute-done.20.refs_3_.refs_2_), channel_id=1, source_target_pairs={{0,8},{4,12},{8,16},{12,20},{16,24},{20,28},{24,0},{28,4},{1,9},{5... | collective-permute-start | bytes 3145736 | tf_op jit(solution)/shard_map/ppermute | solution.py:51
  241.7 29.3 %collective-permute-start.24 = (bf16[256,2048]{1,0:T(8,128)(2,1)}, bf16[256,2048]{1,0:T(8,128)(2,1)S(1)}, u32[]{:S(2)}, u32[]{:S(2)}) collective-permute-start(bf16[256,2048]{1,0:T(8,128)(2,1)} %collective-permute-done.20.refs_3_.refs_2_), channel_id=1, source_target_pairs={{0,4},{4,0},{8,12},{12,8},{16,20},{20,16},{24,28},{28,24},{1,5},{5... | collective-permute-start | bytes 3145736 | tf_op jit(solution)/shard_map/ppermute | solution.py:59
  270.2 14.0 %collective-permute-start.25 = (bf16[128,2048]{1,0:T(8,128)(2,1)S(1)}, bf16[128,2048]{1,0:T(8,128)(2,1)S(1)}, u32[]{:S(2)}, u32[]{:S(2)}) collective-permute-start(bf16[128,2048]{1,0:T(8,128)(2,1)S(1)} %slice.319), channel_id=1, source_target_pairs={{0,4},{4,0},{8,12},{12,8},{16,20},{20,16},{24,28},{28,24},{1,5},{5... | collective-permute-start | bytes 1572872 | tf_op jit(solution)/shard_map/ppermute | solution.py:59
  271.1 16.0 %collective-permute-start.26 = (bf16[128,2048]{1,0:T(8,128)(2,1)S(1)}, bf16[128,2048]{1,0:T(8,128)(2,1)S(1)}, u32[]{:S(2)}, u32[]{:S(2)}) collective-permute-start(bf16[128,2048]{1,0:T(8,128)(2,1)S(1)} %slice.320), channel_id=1, source_target_pairs={{0,8},{4,12},{8,16},{12,20},{16,24},{20,28},{24,0},{28,4},{1,9},{5... | collective-permute-start | bytes 1572872 | tf_op jit(solution)/shard_map/ppermute | solution.py:51
  287.2 30.4 %collective-permute-start.27 = (bf16[256,2048]{1,0:T(8,128)(2,1)}, bf16[256,2048]{1,0:T(8,128)(2,1)}, u32[]{:S(2)}, u32[]{:S(2)}) collective-permute-start(bf16[256,2048]{1,0:T(8,128)(2,1)} %get-tuple-element.169), channel_id=1, source_target_pairs={{0,4},{4,0},{8,12},{12,8},{16,20},{20,16},{24,28},{28,24},{1,5},{5... | collective-permute-start | bytes 3145736 | tf_op jit(solution)/shard_map/ppermute | solution.py:59
  306.8 74.2 %collective-permute-start.30 = (bf16[768,2048]{1,0:T(8,128)(2,1)}, bf16[768,2048]{1,0:T(8,128)(2,1)}, u32[]{:S(2)}, u32[]{:S(2)}) collective-permute-start(bf16[768,2048]{1,0:T(8,128)(2,1)} %get-tuple-element.185), channel_id=1, source_target_pairs={{0,4},{4,0},{8,12},{12,8},{16,20},{20,16},{24,28},{28,24},{1,5},{5... | collective-permute-start | bytes 9437192 | tf_op jit(solution)/shard_map/ppermute | solution.py:59
  335.9 31.6 %collective-permute-start.28 = (bf16[320,2048]{1,0:T(8,128)(2,1)}, bf16[320,2048]{1,0:T(8,128)(2,1)}, u32[]{:S(2)}, u32[]{:S(2)}) collective-permute-start(bf16[320,2048]{1,0:T(8,128)(2,1)} %get-tuple-element.173), channel_id=1, source_target_pairs={{0,2},{1,3},{2,0},{3,1},{4,6},{5,7},{6,4},{7,5},{8,10},{9,11},{10,... | collective-permute-start | bytes 3932168 | tf_op jit(solution)/shard_map/ppermute | solution.py:63
  339.8 35.4 %collective-permute-start.32 = (bf16[256,2048]{1,0:T(8,128)(2,1)}, bf16[256,2048]{1,0:T(8,128)(2,1)}, u32[]{:S(2)}, u32[]{:S(2)}) collective-permute-start(bf16[256,2048]{1,0:T(8,128)(2,1)} %add_convert_fusion.9), channel_id=1, source_target_pairs={{0,24},{4,28},{8,0},{12,4},{16,8},{20,12},{24,16},{28,20},{1,25},{... | collective-permute-start | bytes 3145736 | tf_op jit(solution)/shard_map/ppermute | solution.py:51
  371.1 34.4 %collective-permute-start.31 = (bf16[256,2048]{1,0:T(8,128)(2,1)}, bf16[256,2048]{1,0:T(8,128)(2,1)}, u32[]{:S(2)}, u32[]{:S(2)}) collective-permute-start(bf16[256,2048]{1,0:T(8,128)(2,1)} %get-tuple-element.186), channel_id=1, source_target_pairs={{0,4},{4,0},{8,12},{12,8},{16,20},{20,16},{24,28},{28,24},{1,5},{5... | collective-permute-start | bytes 3145736 | tf_op jit(solution)/shard_map/ppermute | solution.py:59
  374.4 29.7 %copy-start.13 = (bf16[320,2048]{1,0:T(8,128)(2,1)}, bf16[320,2048]{1,0:T(8,128)(2,1)S(1)}, u32[]{:S(2)}) copy-start(bf16[320,2048]{1,0:T(8,128)(2,1)S(1)} %multiply_convert_fusion.refs_0_.refs_1_) | copy-start | bytes 3932164
  374.4 34.7 %collective-permute-start.29 = (bf16[320,2048]{1,0:T(8,128)(2,1)S(1)}, bf16[320,2048]{1,0:T(8,128)(2,1)S(1)}, u32[]{:S(2)}, u32[]{:S(2)}) collective-permute-start(bf16[320,2048]{1,0:T(8,128)(2,1)S(1)} %multiply_convert_fusion.refs_0_.refs_1_), channel_id=1, source_target_pairs={{0,2},{1,3},{2,0},{3,1},{4,6},{5,7},{6,4},{7,5},{8,10},{9,11},{10,... | collective-permute-start | bytes 3932168 | tf_op jit(solution)/shard_map/ppermute | solution.py:63
  384.1 38.4 %collective-permute-start.33 = (bf16[256,2048]{1,0:T(8,128)(2,1)}, bf16[256,2048]{1,0:T(8,128)(2,1)}, u32[]{:S(2)}, u32[]{:S(2)}) collective-permute-start(bf16[256,2048]{1,0:T(8,128)(2,1)} %add_convert_fusion.8), channel_id=1, source_target_pairs={{0,24},{4,28},{8,0},{12,4},{16,8},{20,12},{24,16},{28,20},{1,25},{... | collective-permute-start | bytes 3145736 | tf_op jit(solution)/shard_map/ppermute | solution.py:51
  404.2 37.3 %collective-permute-start.35 = (bf16[256,2048]{1,0:T(8,128)(2,1)}, bf16[256,2048]{1,0:T(8,128)(2,1)}, u32[]{:S(2)}, u32[]{:S(2)}) collective-permute-start(bf16[256,2048]{1,0:T(8,128)(2,1)} %get-tuple-element.198), channel_id=1, source_target_pairs={{0,4},{4,0},{8,12},{12,8},{16,20},{20,16},{24,28},{28,24},{1,5},{5... | collective-permute-start | bytes 3145736 | tf_op jit(solution)/shard_map/ppermute | solution.py:59
  408.4 33.1 %collective-permute-start.36 = (bf16[256,2048]{1,0:T(8,128)(2,1)}, bf16[256,2048]{1,0:T(8,128)(2,1)}, u32[]{:S(2)}, u32[]{:S(2)}) collective-permute-start(bf16[256,2048]{1,0:T(8,128)(2,1)} %add_convert_fusion.6), channel_id=1, source_target_pairs={{0,24},{4,28},{8,0},{12,4},{16,8},{20,12},{24,16},{28,20},{1,25},{... | collective-permute-start | bytes 3145736 | tf_op jit(solution)/shard_map/ppermute | solution.py:51
  421.0 62.5 %collective-permute-start.39 = (bf16[512,2048]{1,0:T(8,128)(2,1)}, bf16[512,2048]{1,0:T(8,128)(2,1)}, u32[]{:S(2)}, u32[]{:S(2)}) collective-permute-start(bf16[512,2048]{1,0:T(8,128)(2,1)} %get-tuple-element.210), channel_id=1, source_target_pairs={{0,4},{4,0},{8,12},{12,8},{16,20},{20,16},{24,28},{28,24},{1,5},{5... | collective-permute-start | bytes 6291464 | tf_op jit(solution)/shard_map/ppermute | solution.py:59
  425.9 49.7 %collective-permute-start.38 = (bf16[256,2048]{1,0:T(8,128)(2,1)}, bf16[256,2048]{1,0:T(8,128)(2,1)}, u32[]{:S(2)}, u32[]{:S(2)}) collective-permute-start(bf16[256,2048]{1,0:T(8,128)(2,1)} %add_convert_fusion.7), channel_id=1, source_target_pairs={{0,24},{4,28},{8,0},{12,4},{16,8},{20,12},{24,16},{28,20},{1,25},{... | collective-permute-start | bytes 3145736 | tf_op jit(solution)/shard_map/ppermute | solution.py:51
  440.0 41.3 %collective-permute-start.34 = (bf16[320,2048]{1,0:T(8,128)(2,1)}, bf16[320,2048]{1,0:T(8,128)(2,1)}, u32[]{:S(2)}, u32[]{:S(2)}) collective-permute-start(bf16[320,2048]{1,0:T(8,128)(2,1)} %get-tuple-element.192), channel_id=1, source_target_pairs={{0,2},{1,3},{2,0},{3,1},{4,6},{5,7},{6,4},{7,5},{8,10},{9,11},{10,... | collective-permute-start | bytes 3932168 | tf_op jit(solution)/shard_map/ppermute | solution.py:63
  445.3 38.1 %collective-permute-start.40 = (bf16[256,2048]{1,0:T(8,128)(2,1)S(1)}, bf16[256,2048]{1,0:T(8,128)(2,1)S(1)}, u32[]{:S(2)}, u32[]{:S(2)}) collective-permute-start(bf16[256,2048]{1,0:T(8,128)(2,1)S(1)} %add_convert_fusion.5), channel_id=1, source_target_pairs={{0,24},{4,28},{8,0},{12,4},{16,8},{20,12},{24,16},{28,20},{1,25},{... | collective-permute-start | bytes 3145736 | tf_op jit(solution)/shard_map/ppermute | solution.py:51
  458.9 42.7 %collective-permute-start.43 = (bf16[256,2048]{1,0:T(8,128)(2,1)}, bf16[256,2048]{1,0:T(8,128)(2,1)S(1)}, u32[]{:S(2)}, u32[]{:S(2)}) collective-permute-start(bf16[256,2048]{1,0:T(8,128)(2,1)} %get-tuple-element.214), channel_id=1, source_target_pairs={{0,4},{4,0},{8,12},{12,8},{16,20},{20,16},{24,28},{28,24},{1,5},{5... | collective-permute-start | bytes 3145736 | tf_op jit(solution)/shard_map/ppermute | solution.py:59
  475.6 40.1 %collective-permute-start.37 = (bf16[320,2048]{1,0:T(8,128)(2,1)}, bf16[320,2048]{1,0:T(8,128)(2,1)S(1)}, u32[]{:S(2)}, u32[]{:S(2)}) collective-permute-start(bf16[320,2048]{1,0:T(8,128)(2,1)} %get-tuple-element.207), channel_id=1, source_target_pairs={{0,2},{1,3},{2,0},{3,1},{4,6},{5,7},{6,4},{7,5},{8,10},{9,11},{10,... | collective-permute-start | bytes 3932168 | tf_op jit(solution)/shard_map/ppermute | solution.py:63
  486.5 25.4 %collective-permute-start.44 = (bf16[256,2048]{1,0:T(8,128)(2,1)}, bf16[256,2048]{1,0:T(8,128)(2,1)S(1)}, u32[]{:S(2)}, u32[]{:S(2)}) collective-permute-start(bf16[256,2048]{1,0:T(8,128)(2,1)} %add_convert_fusion.4), channel_id=1, source_target_pairs={{0,24},{4,28},{8,0},{12,4},{16,8},{20,12},{24,16},{28,20},{1,25},{... | collective-permute-start | bytes 3145736 | tf_op jit(solution)/shard_map/ppermute | solution.py:51
  490.1 30.1 %collective-permute-start.41 = (bf16[256,2048]{1,0:T(8,128)(2,1)}, bf16[256,2048]{1,0:T(8,128)(2,1)}, u32[]{:S(2)}, u32[]{:S(2)}) collective-permute-start(bf16[256,2048]{1,0:T(8,128)(2,1)} %get-tuple-element.212), channel_id=1, source_target_pairs={{0,4},{4,0},{8,12},{12,8},{16,20},{20,16},{24,28},{28,24},{1,5},{5... | collective-permute-start | bytes 3145736 | tf_op jit(solution)/shard_map/ppermute | solution.py:59
  491.1 24.6 %copy-start.14 = (f32[320,2048]{1,0:T(8,128)S(1)}, f32[320,2048]{1,0:T(8,128)}, u32[]{:S(2)}) copy-start(f32[320,2048]{1,0:T(8,128)} %get-tuple-element.206) | copy-start | bytes 7864324
  511.9 25.9 %collective-permute-start.46 = (bf16[256,2048]{1,0:T(8,128)(2,1)}, bf16[256,2048]{1,0:T(8,128)(2,1)}, u32[]{:S(2)}, u32[]{:S(2)}) collective-permute-start(bf16[256,2048]{1,0:T(8,128)(2,1)} %add_convert_fusion.3), channel_id=1, source_target_pairs={{0,24},{4,28},{8,0},{12,4},{16,8},{20,12},{24,16},{28,20},{1,25},{... | collective-permute-start | bytes 3145736 | tf_op jit(solution)/shard_map/ppermute | solution.py:51
  517.0 27.5 %copy-start.41 = (pred[8]{0:T(512)(128)(4,1)S(1)}, pred[8]{0:T(512)(128)(4,1)}, u32[]{:S(2)}) copy-start(pred[8]{0:T(512)(128)(4,1)} %compare_and_fusion) | copy-start | bytes 28
  517.8 47.7 %copy-start.12 = (bf16[1024,2048]{1,0:T(8,128)(2,1)S(1)}, bf16[1024,2048]{1,0:T(8,128)(2,1)}, u32[]{:S(2)}) copy-start(bf16[1024,2048]{1,0:T(8,128)(2,1)} %attn_grad_near.1) | copy-start | bytes 12582916
  517.9 28.7 %collective-permute-start.45 = (bf16[256,2048]{1,0:T(8,128)(2,1)}, bf16[256,2048]{1,0:T(8,128)(2,1)S(1)}, u32[]{:S(2)}, u32[]{:S(2)}) collective-permute-start(bf16[256,2048]{1,0:T(8,128)(2,1)} %get-tuple-element.215), channel_id=1, source_target_pairs={{0,4},{4,0},{8,12},{12,8},{16,20},{20,16},{24,28},{28,24},{1,5},{5... | collective-permute-start | bytes 3145736 | tf_op jit(solution)/shard_map/ppermute | solution.py:59
  540.2 30.1 %copy-start.8 = (f32[320,2048]{1,0:T(8,128)S(1)}, f32[320,2048]{1,0:T(8,128)}, u32[]{:S(2)}) copy-start(f32[320,2048]{1,0:T(8,128)} %copy-done.7) | copy-start | bytes 7864324
  540.2 25.2 %collective-permute-start.47 = (bf16[256,2048]{1,0:T(8,128)(2,1)S(1)}, bf16[256,2048]{1,0:T(8,128)(2,1)S(1)}, u32[]{:S(2)}, u32[]{:S(2)}) collective-permute-start(bf16[256,2048]{1,0:T(8,128)(2,1)S(1)} %add_convert_fusion.2), channel_id=1, source_target_pairs={{0,24},{4,28},{8,0},{12,4},{16,8},{20,12},{24,16},{28,20},{1,25},{... | collective-permute-start | bytes 3145736 | tf_op jit(solution)/shard_map/ppermute | solution.py:51
  544.7 34.3 %collective-permute-start.42 = (bf16[256,2048]{1,0:T(8,128)(2,1)}, bf16[256,2048]{1,0:T(8,128)(2,1)S(1)}, u32[]{:S(2)}, u32[]{:S(2)}) collective-permute-start(bf16[256,2048]{1,0:T(8,128)(2,1)} %get-tuple-element.213), channel_id=1, source_target_pairs={{0,4},{4,0},{8,12},{12,8},{16,20},{20,16},{24,28},{28,24},{1,5},{5... | collective-permute-start | bytes 3145736 | tf_op jit(solution)/shard_map/ppermute | solution.py:59
  566.0 24.3 %collective-permute-start.48 = (bf16[256,2048]{1,0:T(8,128)(2,1)S(1)}, bf16[256,2048]{1,0:T(8,128)(2,1)S(1)}, u32[]{:S(2)}, u32[]{:S(2)}) collective-permute-start(bf16[256,2048]{1,0:T(8,128)(2,1)S(1)} %add_convert_fusion.1), channel_id=1, source_target_pairs={{0,24},{4,28},{8,0},{12,4},{16,8},{20,12},{24,16},{28,20},{1,25},{... | collective-permute-start | bytes 3145736 | tf_op jit(solution)/shard_map/ppermute | solution.py:51
  (36 other events, 292.7 us)

commit v5 on v4

--- a/solution.py
+++ b/solution.py
@@ -113,7 +113,7 @@
 def ring_end(part, rest, ready, late=()):
     if not halved():
         return [[piece] for piece in ring_rest(after(part, *ready))]
-    half = part.shape[0] // 2
+    half = (part.shape[0] + 31) // 32 * 16
     upper = shift_inner(after(part[:half], *ready), 1)
     return [[upper, shift_outer(after(rest[0][half:], *late), 1)]]
 
@@ -125,12 +125,13 @@
     return [(piece, piece.shape[0]) for piece in pieces]
 
 
-def ring_scatter(near, received, held=(), sums=()):
+def ring_scatter(near, received, held=(), sums=(), late=()):
     sums, hop = list(sums), None
     depth = received[0].shape[0]
     for n in range(len(sums), len(received)):
         i = len(received) - 1 - n
-        total = near[i * depth : (i + 1) * depth].astype(f32) + received[i].astype(f32)
+        part = received[i] if i else after(received[i], *late)
+        total = near[i * depth : (i + 1) * depth].astype(f32) + part.astype(f32)
         if sums:
             hop = shift_outer(after(sums[-1], *held[n - 1 : n]), -1)
             total = total + hop.astype(f32)
@@ -919,61 +920,33 @@
     return (master_new, first_new, second_new, average_new, master_new.astype(bf16))
 
 
-def adam_kernel(square_ref, attn_ref, up_ref, down_ref, *refs):
-    vector_refs, state, outs = refs[:3], refs[3:23], refs[23:]
+def vector_kernel(square_ref, *refs):
+    vector_refs, state, outs = refs[:3], refs[3:15], refs[15:]
     grad_norm = jnp.sqrt(jnp.sum(square_ref[...], keepdims=True))
     factor = jnp.minimum(1.0, clip_limit / (grad_norm + 1e-06))
-
-    def update(part, place, grad, rate, decay):
-        old = [ref[place] for ref in state[4 * part : 4 * part + 4]]
-        new = adam_step(old[0], grad, *old[1:], factor, rate, decay)
-        for ref, value in zip(outs[5 * part : 5 * part + 5], new):
-            ref[place] = value
-
-    width = attn_ref.shape[1] // 4
-    for n in range(4):
-        update(0, n, attn_ref[:, n * width : (n + 1) * width], D ** (-0.5), weight_decay)
-    update(1, 0, up_ref[...], D ** (-0.5), weight_decay)
-    update(1, 1, down_ref[...], FF ** (-0.5), weight_decay)
-
-    @pl.when(pl.program_id(0) == 0)
-    def _():
-        for n in range(3):
-            update(2 + n, slice(None), vector_refs[n][...], vector_rate, 0.0)
-
-
-def adam_all(squares, shards, vectors, state):
-    attn, hidden = state[0], state[4]
-    depth = attn.shape[1]
-    tile = 64
-
-    def rows_of(array):
-        return pl.BlockSpec((array.shape[0], tile, array.shape[2]), lambda n: (0, n, 0))
-
-    def tall(array):
-        return pl.BlockSpec((tile, array.shape[1]), lambda n: (n, 0))
-
-    state_specs = [rows_of(array) for array in state[:8]]
-    state_specs += [resident(array.shape) for array in state[8:]]
-    out_shape, out_specs = [], []
-    for n in range(5):
-        group, specs = state[4 * n : 4 * n + 4], state_specs[4 * n : 4 * n + 4]
+    for n in range(3):
+        old = [ref[...] for ref in state[4 * n : 4 * n + 4]]
+        new = adam_step(old[0], vector_refs[n][...], *old[1:], factor, vector_rate, 0.0)
+        for ref, value in zip(outs[5 * n : 5 * n + 5], new):
+            ref[...] = value
+
+
+def adam_vectors(squares, vectors, state):
+    vmem = pl.BlockSpec(memory_space=pltpu.VMEM)
+    out_shape = []
+    for n in range(3):
+        group = state[4 * n : 4 * n + 4]
         out_shape += [jax.ShapeDtypeStruct(array.shape, f32) for array in group]
         out_shape.append(jax.ShapeDtypeStruct(group[0].shape, bf16))
-        out_specs += specs + [specs[0]]
     return pl.pallas_call(
-        adam_kernel,
+        vector_kernel,
         out_shape=out_shape,
-        grid=(depth // tile,),
-        in_specs=[resident(squares.shape)]
-        + [tall(shard) for shard in shards]
-        + [resident(vector.shape) for vector in vectors]
-        + state_specs,
-        out_specs=out_specs,
-        compiler_params=pltpu.CompilerParams(vmem_limit_bytes=60 * 2**20),
-        cost_estimate=expected(20.0),
-        name="adam_all",
-    )(squares, *shards, *vectors, *state)
+        in_specs=[vmem] * (1 + len(vectors) + len(state)),
+        out_specs=[vmem] * len(out_shape),
+        compiler_params=pltpu.CompilerParams(vmem_limit_bytes=4 * 2**20),
+        cost_estimate=expected(3.0),
+        name="adam_vectors",
+    )(squares, *vectors, *state)
 
 
 def per_device(
@@ -1034,17 +1007,24 @@
         behind = attn_rest[i - 2] if i > 1 else []
         behind = behind + (tokens_all[1:] if i == outer - 1 else [])
         attn_line.append(shift_outer(after(attn_line[-1], *behind), 1))
-        attn_rest.append(ring_rest(attn_line[-1]))
-    attn_blocks = attn_line + [rest[j] for j in range(inner - 1) for rest in attn_rest]
-    attn_blocks = [(block, depth) for block in attn_blocks]
-    up_line = [up_own, shift_outer(after(up_own, attn_line[-1], *attn_rest[-2]), 1)]
+        if i < outer - 1:
+            attn_rest.append(ring_rest(attn_line[-1]))
+    attn_end = ring_end(attn_line[3], attn_rest[2], [])
+    attn_ends = [part for parts in attn_end for part in parts]
+    attn_blocks, vectors, at = [], [], 0
+    for piece, high in stack_ring(attn_line, attn_rest, attn_end):
+        used = min(high, depth - at % depth)
+        if high > used:
+            vectors.append(piece[used : used + 1, :packed_size])
+        attn_blocks.append((piece, used))
+        at += used
+    up_line = [up_own, shift_outer(after(up_own, attn_ends[-1]), 1)]
     up_line.append(shift_outer(up_line[1], 1))
     up_line.append(shift_outer(up_line[2], 1))
-    up_rest = [ring_rest(after(up_own, *attn_rest[-2]))]
-    up_rest.append(ring_rest(after(up_line[1], *attn_rest[-1])))
-
-    vectors = jnp.concatenate([block[depth : depth + 1] for block, _ in attn_blocks], axis=0)
-    vectors = vectors[:, :packed_size].astype(f32)
+    up_rest = [ring_rest(after(up_own, attn_ends[0]))]
+    up_rest.append(ring_rest(after(up_line[1], *up_rest[0])))
+
+    vectors = jnp.concatenate(vectors, axis=0).astype(f32)
     norm_vals = vectors[:, :norm_size].reshape(seqs, 6, depth).transpose(1, 0, 2).reshape(6, D)
     vectors = jnp.take(vectors[:, norm_size:], back_order, axis=0)
     head_vals = vectors[:, :head_size].reshape(seqs, 2, head_width // seqs)
@@ -1079,22 +1059,23 @@
         [(total_rows, bf16)],
         "project",
     )[0]
-    down_rest = [ring_rest(after(down_own, qkv, *up_rest[0]))]
-    qkv = after(qkv, up_line[2], *up_rest[0])
+    down_rest = []
+    down_line = [down_own, shift_outer(after(down_own, qkv), 1)]
+    qkv = after(qkv, up_line[1])
     context, share = attend(qkv, bias, me_vector, parts, rows_padded)
-    down_line = [down_own, shift_outer(after(down_own, context), 1)]
     up_rest.append(ring_rest(after(up_line[2], context, *up_rest[1])))
     up_end = ring_end(up_line[3], up_rest[2], up_rest[2])
     up_ends = [part for parts in up_end for part in parts]
     down_line.append(shift_outer(after(down_line[1], up_ends[-1]), 1))
     down_line.append(shift_outer(down_line[2], 1))
+    up_blocks = stack_ring(up_line, up_rest, up_end)
+    context = after(context, up_line[2], *up_rest[0])
+    join_parts = wide_dot(context, attn_blocks, 3 * head_width, D, 4, "join")
+    down_rest.append(ring_rest(after(down_own, *up_rest[2])))
     down_rest.append(ring_rest(after(down_line[1], up_ends[0])))
-    up_blocks = stack_ring(up_line, up_rest, up_end)
-    context = after(context, *up_rest[1])
-    join_parts = wide_dot(context, attn_blocks, 3 * head_width, D, 4, "join")
-    join_parts = [join_parts[0], after(join_parts[1], up_line[3], *down_rest[0])]
+    join_parts = [join_parts[0], after(join_parts[1], down_line[1], *up_rest[1])]
     attended = scatter_chips(*join_parts) + norm_vals[4]
-    attended = after(attended, down_line[1], *up_rest[2])
+    attended = after(attended, up_line[3], *down_rest[0])
     feed_grad, cotangent_own = arrange(
         cotangent_pieces,
         [kept_all],
@@ -1147,7 +1128,8 @@
     unit_grad = unit_grad[0]
     down_first = inner_sum(down_far, 0, pre_grad)
     down_near = near_grads([([after(feed_grad, pre_grad)], activated)], depth, "down_grad")
-    down_totals, _ = ring_scatter(down_near, single_blocks([down_first, down_last], depth))
+    down_blocks_in = single_blocks([down_first, down_last], depth)
+    down_totals = ring_scatter(down_near, down_blocks_in)[0][:-1]
     pre_grad = after(pre_grad, down_last, down_near)
     second_parts = wide_dot(pre_grad, up_blocks, 0, D, 6, "up_back")
     up_pairs = [(after(second_all, *second_parts), pre_grad)]
@@ -1178,9 +1160,6 @@
     up_middle = inner_sum(up_far, 1, down_first)
     up_first = inner_sum(up_far, 0, up_last, context_grad)
     context_grad = after(context_grad, down_totals[2])
-    feed_parts = after(feed_parts, context_grad)
-    feed_out = scatter_chips(*feed_parts) + norm_vals[5]
-    block_output = from_blocks(middle + kept_own * feed_out, order, rows)
     query_grad, key_grad, value_grad = attend_back(
         qkv, context, context_grad, share, me_vector, parts, rows_padded
     )
@@ -1189,7 +1168,7 @@
         [jnp.sum(query_grad, axis=0, dtype=f32), jnp.sum(value_grad, axis=0, dtype=f32)]
     )
     up_totals, up_hop = ring_scatter(up_near, single_blocks([up_first, up_middle, up_last], depth))
-    down_grad, up_grad = down_totals[-1], up_totals[-1]
+    up_grad = up_totals[-1]
     attn_pairs = [
         ([after(first_all, up_totals[1])], qkv_grad),
         (attn_rows, context),
@@ -1198,7 +1177,7 @@
     all_far = [part for far in attn_far for part in far]
     first_parts = wide_dot(after(qkv_grad, *all_far), attn_blocks, 0, D, 9, "project_back")
     attn_pairs = [
-        ([after(first_all, down_grad, up_totals[2], *first_parts)], qkv_grad),
+        ([after(first_all, up_totals[2], *first_parts)], qkv_grad),
         (attn_rows, context),
     ]
     attn_near = near_grads(attn_pairs, depth, "attn_grad")
@@ -1210,6 +1189,9 @@
     attn_sums[1] = inner_sum(attn_far, 1, attn_total, up_hop)
     attn_sums[0] = inner_sum(attn_far, 0, attn_sums[2])
     attn_totals, _ = ring_scatter(attn_near, attn_sums, [up_hop], [attn_total])
+    down_grad = ring_scatter(down_near, down_blocks_in, (), down_totals, [attn_total])[0][-1]
+    feed_out = scatter_chips(*after(feed_parts, attn_total)) + norm_vals[5]
+    block_output = from_blocks(middle + kept_own * feed_out, order, rows)
     first_grad = scatter_chips(*first_parts)
     normed_one, scale_one = norm_parts(inputs)
     gain_one_grad = jnp.sum(first_grad * normed_one, axis=0)
@@ -1253,19 +1235,35 @@
     norm_shard = vectors[:norm_size].reshape(norm_params.shape)
     head_shard = vectors[norm_room : norm_room + head_size].reshape(head_bias.shape)
     unit_shard = vectors[norm_room + head_size : norm_room + packed_size - norm_size]
-    updated = adam_all(
+    factor = jnp.minimum(1.0, clip_limit / (grad_norm + 1e-06))
+    hidden_rate = jnp.array([D ** (-0.5), FF ** (-0.5)], f32)[:, None, None]
+    attn_shard = jnp.stack(
+        [attn_shard[:, n * head_width : (n + 1) * head_width] for n in range(4)]
+    )
+    hidden_out = adam_step(
+        hidden_weight,
+        jnp.stack([up_grad, down_grad]),
+        hidden_first,
+        hidden_second,
+        hidden_average,
+        factor,
+        hidden_rate,
+        weight_decay,
+    )
+    attention_out = adam_step(
+        attention_weight,
+        attn_shard,
+        attention_first,
+        attention_second,
+        attention_average,
+        factor,
+        D ** (-0.5),
+        weight_decay,
+    )
+    updated = adam_vectors(
         squares,
-        [attn_shard, up_grad, down_grad],
         [norm_shard, head_shard, unit_shard[None]],
         [
-            attention_weight,
-            attention_first,
-            attention_second,
-            attention_average,
-            hidden_weight,
-            hidden_first,
-            hidden_second,
-            hidden_average,
             norm_params,
             norm_first,
             norm_second,
@@ -1284,8 +1282,10 @@
         block_output,
         input_grad,
         grad_norm,
-        *updated[:20],
-        *[value[0] for value in updated[20:]],
+        *attention_out,
+        *hidden_out,
+        *updated[:10],
+        *[value[0] for value in updated[10:]],
     )
 
 

time: 651 us -> 650 us (level)
  Pallas kernels: 284 us -> 259 us
  local copies, waits for them, and re-layouts: 30.1 us -> 43.3 us
  other arithmetic: 66.7 us -> 77.3 us
    ppermute x21, waiting for transfers between devices: 76.8 us -> 40.4 us  [shift_inner(): return lax.ppermute(value, 'seq', pairs)]
    ppermute x20 -> x21, waiting for transfers between devices: 109 us -> 140 us  [shift_outer(): return lax.ppermute(value, 'seq', pairs)]
    pallas_call x1, Pallas kernels: 23.3 us -> 0.83 us  [adam_vectors(): pl.pallas_call(vector_kernel, out_shape=out_shape, in_specs=[vmem] * (1 +...]
    convert_element_type x1 -> x2, other arithmetic: 0.01 us -> 11 us  [adam_step(): master_new.astype(bf16)]
    reduce_sum x3 -> x1, other arithmetic: 11.3 us -> 1.26 us  [per_device(): jnp.sum(shard * shard)]
    unnamed x121 -> x175, local copies, waits for them, and re-layouts: 7.8 us -> 17.4 us
    another operation x5 -> x7, other arithmetic: 6.29 us -> 14.6 us  [the longest x2 8.33 us: per_device(): jnp.stack([up_grad, down_grad])]
    ppermute x20 -> x21, starting transfers between devices: 25.4 us -> 32.1 us  [shift_outer(): return lax.ppermute(value, 'seq', pairs)]
  transfers between devices with their start and end apart: 49 -> 50, of which waited for: 24 -> 23; matrix products, arithmetic and copies ran while one was open for 13% -> 13% of each run, Pallas kernels for 38% -> 38%
where the time goes in v5:
time: 650 us; the launch traced here: 644 us
  Pallas kernels  259 us (40%)
  waiting for transfers between devices  195 us (30%)
  other arithmetic  77.3 us (12%)
  starting transfers between devices  63.8 us (10%)
  local copies, waits for them, and re-layouts  43.3 us (7%)
    ppermute x21, waiting for transfers between devices, shift_outer(): return lax.ppermute(value, 'seq', pairs)  140 us
    pallas_call x4, Pallas kernels, tall_dot(): pl.pallas_call(functools.partial(tall_kernel, epilogue, exchanged, len(le...  68.3 us
    pallas_call x6, Pallas kernels, turned_dot(): pl.pallas_call(functools.partial(turned_kernel, [len(lefts) for lefts, _...  64.2 us
    pallas_call x4, Pallas kernels, wide_dot(): pl.pallas_call(functools.partial(wide_kernel, len(blocks), start), out_sh...  63.5 us
    ppermute x21, waiting for transfers between devices, shift_inner(): return lax.ppermute(value, 'seq', pairs)  40.4 us
    ppermute x21, starting transfers between devices, shift_outer(): return lax.ppermute(value, 'seq', pairs)  32.1 us
    ppermute x21, starting transfers between devices, shift_inner(): return lax.ppermute(value, 'seq', pairs)  25.4 us
    convert_element_type x8, other arithmetic, ring_scatter(): sums.append(total.astype(bf16) if i else total)  20.6 us
  transfers between devices with their start and end apart: 50, of which 23 were waited for; matrix products, arithmetic and copies ran while one was open for 13% of the time, Pallas kernels for 38%

profile of v5, /device:TPU:0, one launch (start us, length us, event | category | flops | bytes accessed | tf_op | source)
XLA Modules:
  0.0 644.1 jit_solution(3241892558601903353)
XLA Ops:
  5.0 3.0 collective-permute-start.2
  11.2 21.3 %collective-permute-done.2.refs_5_.refs_4_.refs_6_ = bf16[272,2048]{1,0:T(8,128)(2,1)S(1)} collective-permute-done((bf16[272,2048]{1,0:T(8,128)(2,1)S(1)}, bf16[272,2048]{1,0:T(8,128)(2,1)S(1)}, u32[]{:S(2)}, u32[]{:S(2)}) %collective-permute-start.2) | collective-permute-done | bytes 1114144 | tf_op jit(solution)/shard_map/ppermute | solution.py:59
  32.6 3.3 collective-permute-done.1.refs_2_.refs_1_.refs_3_
  39.7 23.2 %collective-permute-done.3.refs_3_.refs_2_.refs_4_ = bf16[272,2048]{1,0:T(8,128)(2,1)} collective-permute-done((bf16[272,2048]{1,0:T(8,128)(2,1)S(1)}, bf16[272,2048]{1,0:T(8,128)(2,1)}, u32[]{:S(2)}, u32[]{:S(2)}) %collective-permute-start.3) | collective-permute-done | bytes 1114144 | tf_op jit(solution)/shard_map/ppermute | solution.py:51
  66.1 2.5 convert.38
  70.4 20.0 %collective-permute-done.5.refs_4_.refs_3_.refs_5_ = bf16[272,2048]{1,0:T(8,128)(2,1)} collective-permute-done((bf16[272,2048]{1,0:T(8,128)(2,1)}, bf16[272,2048]{1,0:T(8,128)(2,1)}, u32[]{:S(2)}, u32[]{:S(2)}) %collective-permute-start.5) | collective-permute-done | bytes 1114144 | tf_op jit(solution)/shard_map/ppermute | solution.py:51
  104.4 3.7 collective-permute-done.7.refs_9_.refs_8_.refs_10_
  112.7 9.2 %first_norm.1 = (bf16[1280,2048]{1,0:T(8,128)(2,1)}, bf16[320,2048]{1,0:T(8,128)(2,1)}) custom-call(bf16[320,2048]{1,0:T(8,128)(2,1)} %copy-done.46, bf16[320,2048]{1,0:T(8,128)(2,1)} %copy-done.69, f32[1,2048]{1,0:T(1,128)} %bitcast.150, f32[1,2048]{1,0:T(1,128)} %bitcast.149), custom_call_target="tpu_custom_call" | custom-call | flops 5310000128 | tf_op jit(solution)/shard_map/first_norm/pallas_call | solution.py:353
  121.9 2.8 collective-permute-done.8.refs_1_
  124.7 7.7 %collective-permute-done.10.refs_3_.refs_1_ = bf16[256,2048]{1,0:T(8,128)(2,1)} collective-permute-done((bf16[256,2048]{1,0:T(8,128)(2,1)}, bf16[256,2048]{1,0:T(8,128)(2,1)}, u32[]{:S(2)}, u32[]{:S(2)}) %collective-permute-start.10) | collective-permute-done | bytes 1048608 | tf_op jit(solution)/shard_map/ppermute | solution.py:51
  133.1 13.5 %project.1.q_ref.k_ref.v_ref = bf16[1280,1536]{1,0:T(8,128)(2,1)} custom-call(bf16[1280,2048]{1,0:T(8,128)(2,1)} %get-tuple-element.199.refs_0_, bf16[272,2048]{1,0:T(8,128)(2,1)} %copy-done.36, bf16[272,2048]{1,0:T(8,128)(2,1)} %copy-done.51, bf16[272,2048]{1,0:T(8,128)(2,1)} %collective-permute-done.3.refs_3_.refs_2_.refs_4_, ...), custom_call_target="tpu_custom_call" | custom-call | flops 7484038144 | tf_op jit(solution)/shard_map/project/pallas_call | solution.py:434
  147.4 12.3 %attend.1 = (bf16[1280,512]{1,0:T(8,128)(2,1)S(1)}, bf16[8,1280,512]{2,1,0:T(8,128)(2,1)}) custom-call(s32[1]{0:T(128)} %bitcast.15.me_ref, bf16[1280,1536]{1,0:T(8,128)(2,1)} %project.1.q_ref.k_ref.v_ref, bf16[1280,1536]{1,0:T(8,128)(2,1)} %project.1.q_ref.k_ref.v_ref, bf16[1280,1536]{1,0:T(8,128)(2,1)} %project.1.q_ref.k_ref.v_ref, ...), custom_call_target="tpu_custom_call" | custom-call | flops 7080000000 | tf_op jit(solution)/shard_map/attend/pallas_call | solution.py:719
  162.0 11.6 %join.1 = (f32[320,2048]{1,0:T(8,128)}, bf16[320,2048]{1,0:T(8,128)(2,1)}) custom-call(bf16[1280,512]{1,0:T(8,128)(2,1)} %copy-done, bf16[272,2048]{1,0:T(8,128)(2,1)} %copy-done.36, bf16[272,2048]{1,0:T(8,128)(2,1)} %copy-done.51, bf16[272,2048]{1,0:T(8,128)(2,1)} %collective-permute-done.3.refs_3_.refs_2_.refs_4_, ...), custom_call_target="tpu_custom_call" | custom-call | flops 3084679424 | tf_op jit(solution)/shard_map/join/pallas_call | solution.py:514
  173.6 3.4 collective-permute-done.13.refs_2_.refs_1_
  178.3 2.5 collective-permute-done.17.refs_8_.refs_6_
  180.8 2.5 collective-permute-start.18
  183.6 18.3 %collective-permute-done.16.refs_5_.refs_3_ = bf16[256,2048]{1,0:T(8,128)(2,1)} collective-permute-done((bf16[256,2048]{1,0:T(8,128)(2,1)}, bf16[256,2048]{1,0:T(8,128)(2,1)}, u32[]{:S(2)}, u32[]{:S(2)}) %collective-permute-start.16) | collective-permute-done | bytes 1048608 | tf_op jit(solution)/shard_map/ppermute | solution.py:51
  210.8 6.7 %collective-permute-done.20.refs_10_.refs_8_ = bf16[128,2048]{1,0:T(8,128)(2,1)S(1)} collective-permute-done((bf16[128,2048]{1,0:T(8,128)(2,1)S(1)}, bf16[128,2048]{1,0:T(8,128)(2,1)S(1)}, u32[]{:S(2)}, u32[]{:S(2)}) %collective-permute-start.20) | collective-permute-done | bytes 524320 | tf_op jit(solution)/shard_map/ppermute | solution.py:51
  222.0 8.7 %feed_grad.1 = (bf16[1280,2048]{1,0:T(8,128)(2,1)}, bf16[320,2048]{1,0:T(8,128)(2,1)}) custom-call(bf16[320,2048]{1,0:T(8,128)(2,1)} %copy-done.47, bf16[320,2048]{1,0:T(8,128)(2,1)} %collective-permute-done.8.refs_1_, f32[1280,1]{1,0:T(8,128)} %select_n.167.refs_2_), custom_call_target="tpu_custom_call" | custom-call | flops 5310000128 | tf_op jit(solution)/shard_map/feed_grad/pallas_call | solution.py:353
  230.7 10.9 %collective-permute-done.21.refs_3_.refs_2_ = bf16[256,2048]{1,0:T(8,128)(2,1)} collective-permute-done((bf16[256,2048]{1,0:T(8,128)(2,1)}, bf16[256,2048]{1,0:T(8,128)(2,1)}, u32[]{:S(2)}, u32[]{:S(2)}) %collective-permute-start.21) | collective-permute-done | bytes 1048608 | tf_op jit(solution)/shard_map/ppermute | solution.py:51
  243.6 26.5 %up.1 = (bf16[1280,2048]{1,0:T(8,128)(2,1)}, bf16[1280,2048]{1,0:T(8,128)(2,1)}, bf16[640,2048]{1,0:T(8,128)(2,1)}) custom-call(bf16[320,2048]{1,0:T(8,128)(2,1)} %add_convert_fusion.refs_0_, bf16[320,2048]{1,0:T(8,128)(2,1)} %collective-permute-done.19.refs_1_, bf16[256,2048]{1,0:T(8,128)(2,1)} %get-tuple-element.136.refs_2_.refs_0_, ...), custom_call_target="tpu_custom_call" | custom-call | flops 9683718144 | tf_op jit(solution)/shard_map/up/pallas_call | solution.py:434
  270.9 10.1 %collective-permute-start.27 = (bf16[128,2048]{1,0:T(8,128)(2,1)S(1)}, bf16[128,2048]{1,0:T(8,128)(2,1)S(1)}, u32[]{:S(2)}, u32[]{:S(2)}) collective-permute-start(bf16[128,2048]{1,0:T(8,128)(2,1)S(1)} %slice.337), channel_id=1, source_target_pairs={{0,8},{4,12},{8,16},{12,20},{16,24},{20,28},{24,0},{28,4},{1,9},{5... | collective-permute-start | bytes 1572872 | tf_op jit(solution)/shard_map/ppermute | solution.py:51
  281.0 11.1 %down_grad_far.1 = (bf16[768,2048]{1,0:T(8,128)(2,1)}, bf16[256,2048]{1,0:T(8,128)(2,1)}) custom-call(bf16[1280,2048]{1,0:T(8,128)(2,1)} %get-tuple-element.161.refs_0_, bf16[1280,2048]{1,0:T(8,128)(2,1)} %get-tuple-element.171.refs_1_.left_ref), custom_call_target="tpu_custom_call" | custom-call | flops 5284358656 | tf_op jit(solution)/shard_map/down_grad_far/pallas_call | solution.py:571
  292.1 3.0 collective-permute-done.27.refs_9_.refs_8_
  296.5 17.5 %down_back.1 = (bf16[1280,2048]{1,0:T(8,128)(2,1)}, f32[8,2048]{1,0:T(8,128)}) custom-call(bf16[1280,2048]{1,0:T(8,128)(2,1)} %get-tuple-element.161.refs_0_, bf16[256,2048]{1,0:T(8,128)(2,1)} %get-tuple-element.144.refs_1_.refs_0_, bf16[256,2048]{1,0:T(8,128)(2,1)} %collective-permute-done.13.refs_2_.refs_1_, ...), custom_call_target="tpu_custom_call" | custom-call | flops 9683718144 | tf_op jit(solution)/shard_map/down_back/pallas_call | solution.py:434
  315.7 10.0 %down_grad_near.1 = bf16[1024,2048]{1,0:T(8,128)(2,1)} custom-call(bf16[1280,2048]{1,0:T(8,128)(2,1)} %get-tuple-element.161.refs_0_, bf16[1280,2048]{1,0:T(8,128)(2,1)} %get-tuple-element.171.refs_1_.left_ref), custom_call_target="tpu_custom_call" | custom-call | flops 5284358656 | tf_op jit(solution)/shard_map/down_grad_near/pallas_call | solution.py:571
  325.7 18.4 %up_back.1 = (f32[320,2048]{1,0:T(8,128)}, bf16[320,2048]{1,0:T(8,128)(2,1)}) custom-call(bf16[1280,2048]{1,0:T(8,128)(2,1)} %get-tuple-element.162.left_ref.refs_3_, bf16[256,2048]{1,0:T(8,128)(2,1)} %get-tuple-element.136.refs_2_.refs_0_, bf16[256,2048]{1,0:T(8,128)(2,1)} %collective-permute-done.10.refs_3_.refs_1_, ...), custom_call_target="tpu_custom_call" | custom-call | flops 9683718144 | tf_op jit(solution)/shard_map/up_back/pallas_call | solution.py:514
  345.1 2.6 add_convert_fusion.6
  349.7 10.2 %up_grad_near.1 = bf16[1024,2048]{1,0:T(8,128)(2,1)} custom-call(bf16[320,2048]{1,0:T(8,128)(2,1)} %add_convert_fusion.refs_0_, bf16[320,2048]{1,0:T(8,128)(2,1)} %collective-permute-done.19.refs_1_, bf16[640,2048]{1,0:T(8,128)(2,1)} %get-tuple-element.168.refs_2_, bf16[1280,2048]{1,0:T(8,128)(2,1)} %get-tuple-element.162.left_ref.refs_3_), custom_call_target="tpu_custom_call" | custom-call | flops 5284358656 | tf_op jit(solution)/shard_map/up_grad_near/pallas_call | solution.py:571
  359.8 11.2 %up_grad_far.1 = (bf16[512,2048]{1,0:T(8,128)(2,1)}, bf16[256,2048]{1,0:T(8,128)(2,1)}, bf16[256,2048]{1,0:T(8,128)(2,1)}) custom-call(bf16[320,2048]{1,0:T(8,128)(2,1)} %add_convert_fusion.refs_0_, bf16[320,2048]{1,0:T(8,128)(2,1)} %collective-permute-done.19.refs_1_, bf16[640,2048]{1,0:T(8,128)(2,1)} %get-tuple-element.168.refs_2_, ...), custom_call_target="tpu_custom_call" | custom-call | flops 5284358656 | tf_op jit(solution)/shard_map/up_grad_far/pallas_call | solution.py:571
  371.0 4.6 collective-permute-done.29
  375.6 2.4 convert_add_fusion.3
  383.1 5.8 collective-permute-done.32
  388.9 3.1 add_convert_fusion.5
  392.0 2.1 collective-permute-start.38
  394.1 18.2 %down.1 = (f32[320,2048]{1,0:T(8,128)}, bf16[320,2048]{1,0:T(8,128)(2,1)}) custom-call(bf16[1280,2048]{1,0:T(8,128)(2,1)} %get-tuple-element.171.refs_1_.left_ref, bf16[256,2048]{1,0:T(8,128)(2,1)} %get-tuple-element.144.refs_1_.refs_0_, bf16[256,2048]{1,0:T(8,128)(2,1)} %collective-permute-done.13.refs_2_.refs_1_, ...), custom_call_target="tpu_custom_call" | custom-call | flops 9683718144 | tf_op jit(solution)/shard_map/down/pallas_call | solution.py:514
  413.8 2.3 slice.355
  416.2 2.9 add_convert_fusion.9
  420.2 10.8 %join_back.1 = (bf16[1280,512]{1,0:T(8,128)(2,1)}, bf16[640,2048]{1,0:T(8,128)(2,1)}) custom-call(bf16[320,2048]{1,0:T(8,128)(2,1)} %copy-done.27, bf16[320,2048]{1,0:T(8,128)(2,1)} %copy-done.34, bf16[272,2048]{1,0:T(8,128)(2,1)} %copy-done.36, bf16[272,2048]{1,0:T(8,128)(2,1)} %copy-done.51, ...), custom_call_target="tpu_custom_call" | custom-call | flops 3084679424 | tf_op jit(solution)/shard_map/join_back/pallas_call | solution.py:434
  431.8 3.5 add_convert_fusion.4
  436.0 12.2 %attend_back.1 = (bf16[1280,512]{1,0:T(8,128)(2,1)S(1)}, bf16[1280,512]{1,0:T(8,128)(2,1)S(1)}, bf16[1280,512]{1,0:T(8,128)(2,1)S(1)}) custom-call(s32[1]{0:T(128)} %bitcast.15.me_ref, bf16[1280,1536]{1,0:T(8,128)(2,1)} %project.1.q_ref.k_ref.v_ref, bf16[1280,1536]{1,0:T(8,128)(2,1)} %project.1.q_ref.k_ref.v_ref, ...), custom_call_target="tpu_custom_call" | custom-call | flops 7375000064 | tf_op jit(solution)/shard_map/attend_back/pallas_call | solution.py:842
  454.5 2.4 add_convert_fusion.8
  457.0 2.6 collective-permute-start.36
  459.6 11.4 %attn_grad_far.1 = (bf16[256,2048]{1,0:T(8,128)(2,1)}, bf16[256,2048]{1,0:T(8,128)(2,1)}, bf16[256,2048]{1,0:T(8,128)(2,1)}, bf16[256,2048]{1,0:T(8,128)(2,1)}) custom-call(bf16[1280,2048]{1,0:T(8,128)(2,1)} %get-tuple-element.199.refs_0_, bf16[320,2048]{1,0:T(8,128)(2,1)} %copy-done.27, bf16[320,2048]{1,0:T(8,128)(2,1)} %copy-done.34, ...), custom_call_target="tpu_custom_call" | custom-call | flops 5284358656 | tf_op jit(solution)/shard_map/attn_grad_far/pallas_call | solution.py:571
  472.3 15.4 %project_back.1 = (f32[320,2048]{1,0:T(8,128)}, bf16[320,2048]{1,0:T(8,128)(2,1)}) custom-call(bf16[1280,1536]{1,0:T(8,128)(2,1)} %constant_dynamic-update-slice_fusion.refs_4_.left_ref, bf16[272,2048]{1,0:T(8,128)(2,1)} %copy-done.36, bf16[272,2048]{1,0:T(8,128)(2,1)} %copy-done.51, bf16[272,2048]{1,0:T(8,128)(2,1)} %collective-permute-done.3.refs_3_.refs_2_.refs_4_, ...), custom_call_target="tpu_custom_call" | custom-call | flops 7484038144 | tf_op jit(solution)/shard_map/project_back/pallas_call | solution.py:514
  489.5 3.1 add_convert_fusion.7
  494.7 10.4 %attn_grad_near.1 = bf16[1024,2048]{1,0:T(8,128)(2,1)} custom-call(bf16[1280,2048]{1,0:T(8,128)(2,1)} %get-tuple-element.199.refs_0_, bf16[320,2048]{1,0:T(8,128)(2,1)} %copy-done.27, bf16[320,2048]{1,0:T(8,128)(2,1)} %copy-done.34, bf16[640,2048]{1,0:T(8,128)(2,1)} %get-tuple-element.191.refs_3_, ...), custom_call_target="tpu_custom_call" | custom-call | flops 5284358656 | tf_op jit(solution)/shard_map/attn_grad_near/pallas_call | solution.py:571
  505.6 2.6 add_convert_fusion.3
  510.1 4.0 fusion.15
  514.1 5.5 collective-permute-done.41
  524.4 10.2 %collective-permute-done.42 = bf16[256,2048]{1,0:T(8,128)(2,1)} collective-permute-done((bf16[256,2048]{1,0:T(8,128)(2,1)}, bf16[256,2048]{1,0:T(8,128)(2,1)}, u32[]{:S(2)}, u32[]{:S(2)}) %collective-permute-start.42) | collective-permute-done | bytes 1048608 | tf_op jit(solution)/shard_map/ppermute | solution.py:59
  534.6 11.3 %collective-permute-done.46 = bf16[256,2048]{1,0:T(8,128)(2,1)} collective-permute-done((bf16[256,2048]{1,0:T(8,128)(2,1)}, bf16[256,2048]{1,0:T(8,128)(2,1)}, u32[]{:S(2)}, u32[]{:S(2)}) %collective-permute-start.46) | collective-permute-done | bytes 1048608 | tf_op jit(solution)/shard_map/ppermute | solution.py:51
  545.9 2.4 add_convert_fusion.2
  548.3 3.8 collective-permute-start.47
  552.1 3.2 fusion.9.in_ref
  557.8 15.4 %collective-permute-done.47 = bf16[256,2048]{1,0:T(8,128)(2,1)S(1)} collective-permute-done((bf16[256,2048]{1,0:T(8,128)(2,1)S(1)}, bf16[256,2048]{1,0:T(8,128)(2,1)S(1)}, u32[]{:S(2)}, u32[]{:S(2)}) %collective-permute-start.47) | collective-permute-done | bytes 1048608 | tf_op jit(solution)/shard_map/ppermute | solution.py:51
  573.8 4.3 collective-permute-start.48
  578.1 4.4 fusion.14
  582.5 2.1 multiply_add_fusion.2.in_ref
  586.4 11.9 %collective-permute-done.48 = bf16[256,2048]{1,0:T(8,128)(2,1)S(1)} collective-permute-done((bf16[256,2048]{1,0:T(8,128)(2,1)S(1)}, bf16[256,2048]{1,0:T(8,128)(2,1)S(1)}, u32[]{:S(2)}, u32[]{:S(2)}) %collective-permute-start.48) | collective-permute-done | bytes 1048608 | tf_op jit(solution)/shard_map/ppermute | solution.py:51
  601.5 16.3 %reduce_all.1 = (f32[24,128]{1,0:T(8,128)S(1)}, f32[8,128]{1,0:T(8,128)S(1)}) custom-call(f32[8,24,128]{2,1,0:T(8,128)S(1)} %bitcast.130, f32[8,128]{1,0:T(8,128)S(1)} %pad.40.refs_1_), custom_call_target="tpu_custom_call" | custom-call | flops 7080000000 | tf_op jit(solution)/shard_map/reduce_all/pallas_call | solution.py:218
  622.4 5.4 fusion.28
  633.8 5.6 fusion.26
  639.4 3.4 multiply_add_fusion
  (366 shorter events, 105.6 us)
Async XLA Ops:
  4.7 32.4 %copy-start.66 = (s32[1,4,50]{2,1,0:T(4,128)S(1)}, s32[1,4,50]{2,1,0:T(4,128)}, u32[]{:S(2)}) copy-start(s32[1,4,50]{2,1,0:T(4,128)} %param.32) | copy-start | bytes 2404
  4.8 32.4 %copy-start.68 = (s32[1,4]{1,0:T(1,128)S(1)}, s32[1,4]{1,0:T(1,128)}, u32[]{:S(2)}) copy-start(s32[1,4]{1,0:T(1,128)} %param.31) | copy-start | bytes 52
  4.8 32.5 %copy-start.61 = (pred[320,320]{1,0:T(32,128)(4,1)S(1)}, pred[320,320]{1,0:T(32,128)(4,1)}, u32[]{:S(2)}) copy-start(pred[320,320]{1,0:T(32,128)(4,1)} %constant.248.clone) | copy-start | bytes 307204
  4.8 32.5 %copy-start.62 = (pred[320,320]{1,0:T(32,128)(4,1)S(1)}, pred[320,320]{1,0:T(32,128)(4,1)}, u32[]{:S(2)}) copy-start(pred[320,320]{1,0:T(32,128)(4,1)} %constant.247.clone) | copy-start | bytes 307204
  4.9 63.7 %copy-start.36 = (bf16[272,2048]{1,0:T(8,128)(2,1)}, bf16[272,2048]{1,0:T(8,128)(2,1)S(1)}, u32[]{:S(2)}) copy-start(bf16[272,2048]{1,0:T(8,128)(2,1)S(1)} %pad_maximum_fusion.refs_1_.refs_0_.refs_2_) | copy-start | bytes 3342340
  5.0 27.6 %collective-permute-start.2 = (bf16[272,2048]{1,0:T(8,128)(2,1)S(1)}, bf16[272,2048]{1,0:T(8,128)(2,1)S(1)}, u32[]{:S(2)}, u32[]{:S(2)}) collective-permute-start(bf16[272,2048]{1,0:T(8,128)(2,1)S(1)} %pad_maximum_fusion.refs_1_.refs_0_.refs_2_), channel_id=1, source_target_pairs={{0,4},{4,0},{8,12},{12,8},{16,20},{20,16},{24,28},{28,24},{1,5},{5... | collective-permute-start | bytes 3342344 | tf_op jit(solution)/shard_map/ppermute | solution.py:59
  8.0 27.9 %collective-permute-start.1 = (bf16[272,2048]{1,0:T(8,128)(2,1)S(1)}, bf16[272,2048]{1,0:T(8,128)(2,1)S(1)}, u32[]{:S(2)}, u32[]{:S(2)}) collective-permute-start(bf16[272,2048]{1,0:T(8,128)(2,1)S(1)} %pad_maximum_fusion.refs_1_.refs_0_.refs_2_), channel_id=1, source_target_pairs={{0,8},{4,12},{8,16},{12,20},{16,24},{20,28},{24,0},{28,4},{1,9},{5... | collective-permute-start | bytes 3342344 | tf_op jit(solution)/shard_map/ppermute | solution.py:51
  9.7 30.0 %collective-permute-start = (bf16[320,2048]{1,0:T(8,128)(2,1)S(1)}, bf16[320,2048]{1,0:T(8,128)(2,1)S(1)}, u32[]{:S(2)}, u32[]{:S(2)}) collective-permute-start(bf16[320,2048]{1,0:T(8,128)(2,1)S(1)} %pad.33.refs_0_), channel_id=1, source_target_pairs={{0,2},{1,3},{2,0},{3,1},{4,6},{5,7},{6,4},{7,5},{8,10},{9,11},{10,... | collective-permute-start | bytes 3932168 | tf_op jit(solution)/shard_map/ppermute | solution.py:63
  35.9 27.1 %copy-start.51 = (bf16[272,2048]{1,0:T(8,128)(2,1)}, bf16[272,2048]{1,0:T(8,128)(2,1)S(1)}, u32[]{:S(2)}) copy-start(bf16[272,2048]{1,0:T(8,128)(2,1)S(1)} %collective-permute-done.1.refs_2_.refs_1_.refs_3_) | copy-start | bytes 3342340
  35.9 27.1 %collective-permute-start.3 = (bf16[272,2048]{1,0:T(8,128)(2,1)S(1)}, bf16[272,2048]{1,0:T(8,128)(2,1)}, u32[]{:S(2)}, u32[]{:S(2)}) collective-permute-start(bf16[272,2048]{1,0:T(8,128)(2,1)S(1)} %collective-permute-done.1.refs_2_.refs_1_.refs_3_), channel_id=1, source_target_pairs={{0,8},{4,12},{8,16},{12,20},{16,24},{20,28},{24,0},{28,4},{1,9},{5... | collective-permute-start | bytes 3342344 | tf_op jit(solution)/shard_map/ppermute | solution.py:51
  35.9 27.1 %collective-permute-start.4 = (bf16[272,2048]{1,0:T(8,128)(2,1)S(1)}, bf16[272,2048]{1,0:T(8,128)(2,1)S(1)}, u32[]{:S(2)}, u32[]{:S(2)}) collective-permute-start(bf16[272,2048]{1,0:T(8,128)(2,1)S(1)} %collective-permute-done.1.refs_2_.refs_1_.refs_3_), channel_id=1, source_target_pairs={{0,4},{4,0},{8,12},{12,8},{16,20},{20,16},{24,28},{28,24},{1,5},{5... | collective-permute-start | bytes 3342344 | tf_op jit(solution)/shard_map/ppermute | solution.py:59
  39.7 26.4 %copy-start.69 = (bf16[320,2048]{1,0:T(8,128)(2,1)}, bf16[320,2048]{1,0:T(8,128)(2,1)S(1)}, u32[]{:S(2)}) copy-start(bf16[320,2048]{1,0:T(8,128)(2,1)S(1)} %collective-permute-done.refs_1_) | copy-start | bytes 3932164
  64.0 26.4 %collective-permute-start.5 = (bf16[272,2048]{1,0:T(8,128)(2,1)}, bf16[272,2048]{1,0:T(8,128)(2,1)}, u32[]{:S(2)}, u32[]{:S(2)}) collective-permute-start(bf16[272,2048]{1,0:T(8,128)(2,1)} %collective-permute-done.3.refs_3_.refs_2_.refs_4_), channel_id=1, source_target_pairs={{0,8},{4,12},{8,16},{12,20},{16,24},{20,28},{24,0},{28,4},{1,9},{5... | collective-permute-start | bytes 3342344 | tf_op jit(solution)/shard_map/ppermute | solution.py:51
  64.5 30.0 %collective-permute-start.6 = (bf16[272,2048]{1,0:T(8,128)(2,1)}, bf16[272,2048]{1,0:T(8,128)(2,1)}, u32[]{:S(2)}, u32[]{:S(2)}) collective-permute-start(bf16[272,2048]{1,0:T(8,128)(2,1)} %collective-permute-done.3.refs_3_.refs_2_.refs_4_), channel_id=1, source_target_pairs={{0,4},{4,0},{8,12},{12,8},{16,20},{20,16},{24,28},{28,24},{1,5},{5... | collective-permute-start | bytes 3342344 | tf_op jit(solution)/shard_map/ppermute | solution.py:59
  68.9 41.6 %copy-start.64 = (pred[8]{0:T(512)(128)(4,1)}, pred[8]{0:T(512)(128)(4,1)S(1)}, u32[]{:S(2)}) copy-start(pred[8]{0:T(512)(128)(4,1)S(1)} %compare_and_fusion) | copy-start | bytes 28
  92.3 17.4 %collective-permute-start.9 = (bf16[144,2048]{1,0:T(8,128)(2,1)}, bf16[144,2048]{1,0:T(8,128)(2,1)}, u32[]{:S(2)}, u32[]{:S(2)}) collective-permute-start(bf16[144,2048]{1,0:T(8,128)(2,1)} %slice.321), channel_id=1, source_target_pairs={{0,4},{4,0},{8,12},{12,8},{16,20},{20,16},{24,28},{28,24},{1,5},{5... | collective-permute-start | bytes 1769480 | tf_op jit(solution)/shard_map/ppermute | solution.py:59
  93.7 28.2 %copy-start.47 = (bf16[320,2048]{1,0:T(8,128)(2,1)}, bf16[320,2048]{1,0:T(8,128)(2,1)S(1)}, u32[]{:S(2)}) copy-start(bf16[320,2048]{1,0:T(8,128)(2,1)S(1)} %pad.36.refs_0_) | copy-start | bytes 3932164
  95.6 12.5 %collective-permute-start.7 = (bf16[128,2048]{1,0:T(8,128)(2,1)S(1)}, bf16[128,2048]{1,0:T(8,128)(2,1)S(1)}, u32[]{:S(2)}, u32[]{:S(2)}) collective-permute-start(bf16[128,2048]{1,0:T(8,128)(2,1)S(1)} %slice.315), channel_id=1, source_target_pairs={{0,8},{4,12},{8,16},{12,20},{16,24},{20,28},{24,0},{28,4},{1,9},{5... | collective-permute-start | bytes 1572872 | tf_op jit(solution)/shard_map/ppermute | solution.py:51
  97.0 27.7 %collective-permute-start.8 = (bf16[320,2048]{1,0:T(8,128)(2,1)S(1)}, bf16[320,2048]{1,0:T(8,128)(2,1)}, u32[]{:S(2)}, u32[]{:S(2)}) collective-permute-start(bf16[320,2048]{1,0:T(8,128)(2,1)S(1)} %pad.36.refs_0_), channel_id=1, source_target_pairs={{0,2},{1,3},{2,0},{3,1},{4,6},{5,7},{6,4},{7,5},{8,10},{9,11},{10,... | collective-permute-start | bytes 3932168 | tf_op jit(solution)/shard_map/ppermute | solution.py:63
  109.0 23.4 %collective-permute-start.10 = (bf16[256,2048]{1,0:T(8,128)(2,1)}, bf16[256,2048]{1,0:T(8,128)(2,1)}, u32[]{:S(2)}, u32[]{:S(2)}) collective-permute-start(bf16[256,2048]{1,0:T(8,128)(2,1)} %get-tuple-element.136.refs_2_.refs_0_), channel_id=1, source_target_pairs={{0,8},{4,12},{8,16},{12,20},{16,24},{20,28},{24,0},{28,4},{1,9},{5... | collective-permute-start | bytes 3145736 | tf_op jit(solution)/shard_map/ppermute | solution.py:51
  109.7 22.7 %collective-permute-start.12 = (bf16[256,2048]{1,0:T(8,128)(2,1)S(1)}, bf16[256,2048]{1,0:T(8,128)(2,1)}, u32[]{:S(2)}, u32[]{:S(2)}) collective-permute-start(bf16[256,2048]{1,0:T(8,128)(2,1)S(1)} %copy-done.54), channel_id=1, source_target_pairs={{0,4},{4,0},{8,12},{12,8},{16,20},{20,16},{24,28},{28,24},{1,5},{5... | collective-permute-start | bytes 3145736 | tf_op jit(solution)/shard_map/ppermute | solution.py:59
  132.4 28.3 %collective-permute-start.11 = (bf16[256,2048]{1,0:T(8,128)(2,1)}, bf16[256,2048]{1,0:T(8,128)(2,1)}, u32[]{:S(2)}, u32[]{:S(2)}) collective-permute-start(bf16[256,2048]{1,0:T(8,128)(2,1)} %collective-permute-done.10.refs_3_.refs_1_), channel_id=1, source_target_pairs={{0,8},{4,12},{8,16},{12,20},{16,24},{20,28},{24,0},{28,4},{1,9},{5... | collective-permute-start | bytes 3145736 | tf_op jit(solution)/shard_map/ppermute | solution.py:51
  132.4 28.3 %collective-permute-start.14 = (bf16[256,2048]{1,0:T(8,128)(2,1)}, bf16[256,2048]{1,0:T(8,128)(2,1)S(1)}, u32[]{:S(2)}, u32[]{:S(2)}) collective-permute-start(bf16[256,2048]{1,0:T(8,128)(2,1)} %collective-permute-done.10.refs_3_.refs_1_), channel_id=1, source_target_pairs={{0,4},{4,0},{8,12},{12,8},{16,20},{20,16},{24,28},{28,24},{1,5},{5... | collective-permute-start | bytes 3145736 | tf_op jit(solution)/shard_map/ppermute | solution.py:59
  146.6 30.5 %collective-permute-start.13 = (bf16[256,2048]{1,0:T(8,128)(2,1)S(1)}, bf16[256,2048]{1,0:T(8,128)(2,1)}, u32[]{:S(2)}, u32[]{:S(2)}) collective-permute-start(bf16[256,2048]{1,0:T(8,128)(2,1)S(1)} %copy-done.53), channel_id=1, source_target_pairs={{0,8},{4,12},{8,16},{12,20},{16,24},{20,28},{24,0},{28,4},{1,9},{5... | collective-permute-start | bytes 3145736 | tf_op jit(solution)/shard_map/ppermute | solution.py:51
  160.7 20.1 %collective-permute-start.17 = (bf16[256,2048]{1,0:T(8,128)(2,1)}, bf16[256,2048]{1,0:T(8,128)(2,1)}, u32[]{:S(2)}, u32[]{:S(2)}) collective-permute-start(bf16[256,2048]{1,0:T(8,128)(2,1)} %collective-permute-done.11.refs_4_.refs_2_), channel_id=1, source_target_pairs={{0,4},{4,0},{8,12},{12,8},{16,20},{20,16},{24,28},{28,24},{1,5},{5... | collective-permute-start | bytes 3145736 | tf_op jit(solution)/shard_map/ppermute | solution.py:59
  177.1 28.8 %collective-permute-start.15 = (bf16[320,2048]{1,0:T(8,128)(2,1)}, bf16[320,2048]{1,0:T(8,128)(2,1)S(1)}, u32[]{:S(2)}, u32[]{:S(2)}) collective-permute-start(bf16[320,2048]{1,0:T(8,128)(2,1)} %get-tuple-element.142), channel_id=1, source_target_pairs={{0,2},{1,3},{2,0},{3,1},{4,6},{5,7},{6,4},{7,5},{8,10},{9,11},{10,... | collective-permute-start | bytes 3932168 | tf_op jit(solution)/shard_map/ppermute | solution.py:63
  177.6 24.4 %collective-permute-start.16 = (bf16[256,2048]{1,0:T(8,128)(2,1)}, bf16[256,2048]{1,0:T(8,128)(2,1)}, u32[]{:S(2)}, u32[]{:S(2)}) collective-permute-start(bf16[256,2048]{1,0:T(8,128)(2,1)} %collective-permute-done.11.refs_4_.refs_2_), channel_id=1, source_target_pairs={{0,8},{4,12},{8,16},{12,20},{16,24},{20,28},{24,0},{28,4},{1,9},{5... | collective-permute-start | bytes 3145736 | tf_op jit(solution)/shard_map/ppermute | solution.py:51
  178.1 27.8 %copy-start.42 = (f32[320,2048]{1,0:T(8,128)S(1)}, f32[320,2048]{1,0:T(8,128)}, u32[]{:S(2)}) copy-start(f32[320,2048]{1,0:T(8,128)} %get-tuple-element.138) | copy-start | bytes 7864324
  180.8 25.6 %collective-permute-start.18 = (bf16[256,2048]{1,0:T(8,128)(2,1)}, bf16[256,2048]{1,0:T(8,128)(2,1)S(1)}, u32[]{:S(2)}, u32[]{:S(2)}) collective-permute-start(bf16[256,2048]{1,0:T(8,128)(2,1)} %get-tuple-element.144.refs_1_.refs_0_), channel_id=1, source_target_pairs={{0,4},{4,0},{8,12},{12,8},{16,20},{20,16},{24,28},{28,24},{1,5},{5... | collective-permute-start | bytes 3145736 | tf_op jit(solution)/shard_map/ppermute | solution.py:59
  204.1 13.4 %collective-permute-start.20 = (bf16[128,2048]{1,0:T(8,128)(2,1)S(1)}, bf16[128,2048]{1,0:T(8,128)(2,1)S(1)}, u32[]{:S(2)}, u32[]{:S(2)}) collective-permute-start(bf16[128,2048]{1,0:T(8,128)(2,1)S(1)} %slice.333), channel_id=1, source_target_pairs={{0,8},{4,12},{8,16},{12,20},{16,24},{20,28},{24,0},{28,4},{1,9},{5... | collective-permute-start | bytes 1572872 | tf_op jit(solution)/shard_map/ppermute | solution.py:51
  204.5 13.0 %collective-permute-start.22 = (bf16[128,2048]{1,0:T(8,128)(2,1)S(1)}, bf16[128,2048]{1,0:T(8,128)(2,1)S(1)}, u32[]{:S(2)}, u32[]{:S(2)}) collective-permute-start(bf16[128,2048]{1,0:T(8,128)(2,1)S(1)} %slice.334), channel_id=1, source_target_pairs={{0,4},{4,0},{8,12},{12,8},{16,20},{20,16},{24,28},{28,24},{1,5},{5... | collective-permute-start | bytes 1572872 | tf_op jit(solution)/shard_map/ppermute | solution.py:59
  208.2 172.2 %copy-start.16 = (f32[320,2048]{1,0:T(8,128)}, f32[320,2048]{1,0:T(8,128)S(1)}, u32[]{:S(2)}) copy-start(f32[320,2048]{1,0:T(8,128)S(1)} %get-tuple-element.254) | copy-start | bytes 7864324
  210.3 31.3 %collective-permute-start.19 = (bf16[320,2048]{1,0:T(8,128)(2,1)}, bf16[320,2048]{1,0:T(8,128)(2,1)}, u32[]{:S(2)}, u32[]{:S(2)}) collective-permute-start(bf16[320,2048]{1,0:T(8,128)(2,1)} %add_convert_fusion.refs_0_), channel_id=1, source_target_pairs={{0,2},{1,3},{2,0},{3,1},{4,6},{5,7},{6,4},{7,5},{8,10},{9,11},{10,... | collective-permute-start | bytes 3932168 | tf_op jit(solution)/shard_map/ppermute | solution.py:63
  217.5 24.0 %collective-permute-start.21 = (bf16[256,2048]{1,0:T(8,128)(2,1)}, bf16[256,2048]{1,0:T(8,128)(2,1)}, u32[]{:S(2)}, u32[]{:S(2)}) collective-permute-start(bf16[256,2048]{1,0:T(8,128)(2,1)} %collective-permute-done.13.refs_2_.refs_1_), channel_id=1, source_target_pairs={{0,8},{4,12},{8,16},{12,20},{16,24},{20,28},{24,0},{28,4},{1,9},{5... | collective-permute-start | bytes 3145736 | tf_op jit(solution)/shard_map/ppermute | solution.py:51
  219.2 24.3 %collective-permute-start.23 = (bf16[256,2048]{1,0:T(8,128)(2,1)}, bf16[256,2048]{1,0:T(8,128)(2,1)}, u32[]{:S(2)}, u32[]{:S(2)}) collective-permute-start(bf16[256,2048]{1,0:T(8,128)(2,1)} %collective-permute-done.13.refs_2_.refs_1_), channel_id=1, source_target_pairs={{0,4},{4,0},{8,12},{12,8},{16,20},{20,16},{24,28},{28,24},{1,5},{5... | collective-permute-start | bytes 3145736 | tf_op jit(solution)/shard_map/ppermute | solution.py:59
  241.6 28.5 %collective-permute-start.24 = (bf16[256,2048]{1,0:T(8,128)(2,1)}, bf16[256,2048]{1,0:T(8,128)(2,1)S(1)}, u32[]{:S(2)}, u32[]{:S(2)}) collective-permute-start(bf16[256,2048]{1,0:T(8,128)(2,1)} %collective-permute-done.21.refs_3_.refs_2_), channel_id=1, source_target_pairs={{0,8},{4,12},{8,16},{12,20},{16,24},{20,28},{24,0},{28,4},{1,9},{5... | collective-permute-start | bytes 3145736 | tf_op jit(solution)/shard_map/ppermute | solution.py:51
  241.6 29.3 %collective-permute-start.25 = (bf16[256,2048]{1,0:T(8,128)(2,1)}, bf16[256,2048]{1,0:T(8,128)(2,1)S(1)}, u32[]{:S(2)}, u32[]{:S(2)}) collective-permute-start(bf16[256,2048]{1,0:T(8,128)(2,1)} %collective-permute-done.21.refs_3_.refs_2_), channel_id=1, source_target_pairs={{0,4},{4,0},{8,12},{12,8},{16,20},{20,16},{24,28},{28,24},{1,5},{5... | collective-permute-start | bytes 3145736 | tf_op jit(solution)/shard_map/ppermute | solution.py:59
  270.1 22.0 %collective-permute-start.26 = (bf16[128,2048]{1,0:T(8,128)(2,1)S(1)}, bf16[128,2048]{1,0:T(8,128)(2,1)S(1)}, u32[]{:S(2)}, u32[]{:S(2)}) collective-permute-start(bf16[128,2048]{1,0:T(8,128)(2,1)S(1)} %slice.336), channel_id=1, source_target_pairs={{0,4},{4,0},{8,12},{12,8},{16,20},{20,16},{24,28},{28,24},{1,5},{5... | collective-permute-start | bytes 1572872 | tf_op jit(solution)/shard_map/ppermute | solution.py:59
  270.9 24.2 %collective-permute-start.27 = (bf16[128,2048]{1,0:T(8,128)(2,1)S(1)}, bf16[128,2048]{1,0:T(8,128)(2,1)S(1)}, u32[]{:S(2)}, u32[]{:S(2)}) collective-permute-start(bf16[128,2048]{1,0:T(8,128)(2,1)S(1)} %slice.337), channel_id=1, source_target_pairs={{0,8},{4,12},{8,16},{12,20},{16,24},{20,28},{24,0},{28,4},{1,9},{5... | collective-permute-start | bytes 1572872 | tf_op jit(solution)/shard_map/ppermute | solution.py:51
  295.1 30.6 %collective-permute-start.28 = (bf16[256,2048]{1,0:T(8,128)(2,1)}, bf16[256,2048]{1,0:T(8,128)(2,1)}, u32[]{:S(2)}, u32[]{:S(2)}) collective-permute-start(bf16[256,2048]{1,0:T(8,128)(2,1)} %get-tuple-element.160), channel_id=1, source_target_pairs={{0,4},{4,0},{8,12},{12,8},{16,20},{20,16},{24,28},{28,24},{1,5},{5... | collective-permute-start | bytes 3145736 | tf_op jit(solution)/shard_map/ppermute | solution.py:59
  314.8 74.1 %collective-permute-start.32 = (bf16[768,2048]{1,0:T(8,128)(2,1)}, bf16[768,2048]{1,0:T(8,128)(2,1)}, u32[]{:S(2)}, u32[]{:S(2)}) collective-permute-start(bf16[768,2048]{1,0:T(8,128)(2,1)} %get-tuple-element.178), channel_id=1, source_target_pairs={{0,4},{4,0},{8,12},{12,8},{16,20},{20,16},{24,28},{28,24},{1,5},{5... | collective-permute-start | bytes 9437192 | tf_op jit(solution)/shard_map/ppermute | solution.py:59
  344.0 31.6 %collective-permute-start.29 = (bf16[320,2048]{1,0:T(8,128)(2,1)}, bf16[320,2048]{1,0:T(8,128)(2,1)}, u32[]{:S(2)}, u32[]{:S(2)}) collective-permute-start(bf16[320,2048]{1,0:T(8,128)(2,1)} %get-tuple-element.164), channel_id=1, source_target_pairs={{0,2},{1,3},{2,0},{3,1},{4,6},{5,7},{6,4},{7,5},{8,10},{9,11},{10,... | collective-permute-start | bytes 3932168 | tf_op jit(solution)/shard_map/ppermute | solution.py:63
  347.7 35.4 %collective-permute-start.37 = (bf16[256,2048]{1,0:T(8,128)(2,1)}, bf16[256,2048]{1,0:T(8,128)(2,1)}, u32[]{:S(2)}, u32[]{:S(2)}) collective-permute-start(bf16[256,2048]{1,0:T(8,128)(2,1)} %add_convert_fusion.6), channel_id=1, source_target_pairs={{0,24},{4,28},{8,0},{12,4},{16,8},{20,12},{24,16},{28,20},{1,25},{... | collective-permute-start | bytes 3145736 | tf_op jit(solution)/shard_map/ppermute | solution.py:51
  379.2 36.9 %collective-permute-start.30 = (bf16[256,2048]{1,0:T(8,128)(2,1)}, bf16[256,2048]{1,0:T(8,128)(2,1)}, u32[]{:S(2)}, u32[]{:S(2)}) collective-permute-start(bf16[256,2048]{1,0:T(8,128)(2,1)} %get-tuple-element.175), channel_id=1, source_target_pairs={{0,4},{4,0},{8,12},{12,8},{16,20},{20,16},{24,28},{28,24},{1,5},{5... | collective-permute-start | bytes 3145736 | tf_op jit(solution)/shard_map/ppermute | solution.py:59
  382.5 29.8 %copy-start.27 = (bf16[320,2048]{1,0:T(8,128)(2,1)}, bf16[320,2048]{1,0:T(8,128)(2,1)S(1)}, u32[]{:S(2)}) copy-start(bf16[320,2048]{1,0:T(8,128)(2,1)S(1)} %multiply_convert_fusion.refs_0_.refs_1_) | copy-start | bytes 3932164
  382.5 36.6 %collective-permute-start.31 = (bf16[320,2048]{1,0:T(8,128)(2,1)S(1)}, bf16[320,2048]{1,0:T(8,128)(2,1)S(1)}, u32[]{:S(2)}, u32[]{:S(2)}) collective-permute-start(bf16[320,2048]{1,0:T(8,128)(2,1)S(1)} %multiply_convert_fusion.refs_0_.refs_1_), channel_id=1, source_target_pairs={{0,2},{1,3},{2,0},{3,1},{4,6},{5,7},{6,4},{7,5},{8,10},{9,11},{10,... | collective-permute-start | bytes 3932168 | tf_op jit(solution)/shard_map/ppermute | solution.py:63
  392.0 39.7 %collective-permute-start.38 = (bf16[256,2048]{1,0:T(8,128)(2,1)}, bf16[256,2048]{1,0:T(8,128)(2,1)}, u32[]{:S(2)}, u32[]{:S(2)}) collective-permute-start(bf16[256,2048]{1,0:T(8,128)(2,1)} %add_convert_fusion.5), channel_id=1, source_target_pairs={{0,24},{4,28},{8,0},{12,4},{16,8},{20,12},{24,16},{28,20},{1,25},{... | collective-permute-start | bytes 3145736 | tf_op jit(solution)/shard_map/ppermute | solution.py:51
  412.4 42.1 %collective-permute-start.34 = (bf16[256,2048]{1,0:T(8,128)(2,1)}, bf16[256,2048]{1,0:T(8,128)(2,1)}, u32[]{:S(2)}, u32[]{:S(2)}) collective-permute-start(bf16[256,2048]{1,0:T(8,128)(2,1)} %get-tuple-element.184), channel_id=1, source_target_pairs={{0,4},{4,0},{8,12},{12,8},{16,20},{20,16},{24,28},{28,24},{1,5},{5... | collective-permute-start | bytes 3145736 | tf_op jit(solution)/shard_map/ppermute | solution.py:59
  419.1 35.5 %collective-permute-start.35 = (bf16[256,2048]{1,0:T(8,128)(2,1)}, bf16[256,2048]{1,0:T(8,128)(2,1)}, u32[]{:S(2)}, u32[]{:S(2)}) collective-permute-start(bf16[256,2048]{1,0:T(8,128)(2,1)} %add_convert_fusion.9), channel_id=1, source_target_pairs={{0,24},{4,28},{8,0},{12,4},{16,8},{20,12},{24,16},{28,20},{1,25},{... | collective-permute-start | bytes 3145736 | tf_op jit(solution)/shard_map/ppermute | solution.py:51
  431.0 58.5 %collective-permute-start.33 = (bf16[512,2048]{1,0:T(8,128)(2,1)}, bf16[512,2048]{1,0:T(8,128)(2,1)}, u32[]{:S(2)}, u32[]{:S(2)}) collective-permute-start(bf16[512,2048]{1,0:T(8,128)(2,1)} %get-tuple-element.182), channel_id=1, source_target_pairs={{0,4},{4,0},{8,12},{12,8},{16,20},{20,16},{24,28},{28,24},{1,5},{5... | collective-permute-start | bytes 6291464 | tf_op jit(solution)/shard_map/ppermute | solution.py:59
  435.2 74.9 %collective-permute-start.49 = (bf16[256,2048]{1,0:T(8,128)(2,1)}, bf16[256,2048]{1,0:T(8,128)(2,1)}, u32[]{:S(2)}, u32[]{:S(2)}) collective-permute-start(bf16[256,2048]{1,0:T(8,128)(2,1)} %add_convert_fusion.4), channel_id=1, source_target_pairs={{0,24},{4,28},{8,0},{12,4},{16,8},{20,12},{24,16},{28,20},{1,25},{... | collective-permute-start | bytes 3145736 | tf_op jit(solution)/shard_map/ppermute | solution.py:51
  457.0 32.5 %collective-permute-start.36 = (bf16[256,2048]{1,0:T(8,128)(2,1)S(1)}, bf16[256,2048]{1,0:T(8,128)(2,1)S(1)}, u32[]{:S(2)}, u32[]{:S(2)}) collective-permute-start(bf16[256,2048]{1,0:T(8,128)(2,1)S(1)} %add_convert_fusion.8), channel_id=1, source_target_pairs={{0,24},{4,28},{8,0},{12,4},{16,8},{20,12},{24,16},{28,20},{1,25},{... | collective-permute-start | bytes 3145736 | tf_op jit(solution)/shard_map/ppermute | solution.py:51
  471.0 34.7 %collective-permute-start.39 = (bf16[256,2048]{1,0:T(8,128)(2,1)}, bf16[256,2048]{1,0:T(8,128)(2,1)S(1)}, u32[]{:S(2)}, u32[]{:S(2)}) collective-permute-start(bf16[256,2048]{1,0:T(8,128)(2,1)} %get-tuple-element.200), channel_id=1, source_target_pairs={{0,4},{4,0},{8,12},{12,8},{16,20},{20,16},{24,28},{28,24},{1,5},{5... | collective-permute-start | bytes 3145736 | tf_op jit(solution)/shard_map/ppermute | solution.py:59
  487.7 31.8 %collective-permute-start.41 = (bf16[320,2048]{1,0:T(8,128)(2,1)}, bf16[320,2048]{1,0:T(8,128)(2,1)S(1)}, u32[]{:S(2)}, u32[]{:S(2)}) collective-permute-start(bf16[320,2048]{1,0:T(8,128)(2,1)} %get-tuple-element.198), channel_id=1, source_target_pairs={{0,2},{1,3},{2,0},{3,1},{4,6},{5,7},{6,4},{7,5},{8,10},{9,11},{10,... | collective-permute-start | bytes 3932168 | tf_op jit(solution)/shard_map/ppermute | solution.py:63
  492.6 28.4 %collective-permute-start.44 = (bf16[256,2048]{1,0:T(8,128)(2,1)}, bf16[256,2048]{1,0:T(8,128)(2,1)}, u32[]{:S(2)}, u32[]{:S(2)}) collective-permute-start(bf16[256,2048]{1,0:T(8,128)(2,1)} %add_convert_fusion.7), channel_id=1, source_target_pairs={{0,24},{4,28},{8,0},{12,4},{16,8},{20,12},{24,16},{28,20},{1,25},{... | collective-permute-start | bytes 3145736 | tf_op jit(solution)/shard_map/ppermute | solution.py:51
  508.2 26.4 %collective-permute-start.42 = (bf16[256,2048]{1,0:T(8,128)(2,1)}, bf16[256,2048]{1,0:T(8,128)(2,1)}, u32[]{:S(2)}, u32[]{:S(2)}) collective-permute-start(bf16[256,2048]{1,0:T(8,128)(2,1)} %get-tuple-element.204), channel_id=1, source_target_pairs={{0,4},{4,0},{8,12},{12,8},{16,20},{20,16},{24,28},{28,24},{1,5},{5... | collective-permute-start | bytes 3145736 | tf_op jit(solution)/shard_map/ppermute | solution.py:59
  509.6 72.9 %collective-permute-start.40 = (bf16[320,2048]{1,0:T(8,128)(2,1)}, bf16[320,2048]{1,0:T(8,128)(2,1)}, u32[]{:S(2)}, u32[]{:S(2)}) collective-permute-start(bf16[320,2048]{1,0:T(8,128)(2,1)} %get-tuple-element.202), channel_id=1, source_target_pairs={{0,2},{1,3},{2,0},{3,1},{4,6},{5,7},{6,4},{7,5},{8,10},{9,11},{10,... | collective-permute-start | bytes 3932168 | tf_op jit(solution)/shard_map/ppermute | solution.py:63
  520.9 31.2 %copy-start.19 = (f32[320,2048]{1,0:T(8,128)S(1)}, f32[320,2048]{1,0:T(8,128)}, u32[]{:S(2)}) copy-start(f32[320,2048]{1,0:T(8,128)} %copy-done.18) | copy-start | bytes 7864324
  521.0 24.9 %collective-permute-start.46 = (bf16[256,2048]{1,0:T(8,128)(2,1)}, bf16[256,2048]{1,0:T(8,128)(2,1)}, u32[]{:S(2)}, u32[]{:S(2)}) collective-permute-start(bf16[256,2048]{1,0:T(8,128)(2,1)} %add_convert_fusion.3), channel_id=1, source_target_pairs={{0,24},{4,28},{8,0},{12,4},{16,8},{20,12},{24,16},{28,20},{1,25},{... | collective-permute-start | bytes 3145736 | tf_op jit(solution)/shard_map/ppermute | solution.py:51
  523.5 28.6 %copy-start.23 = (bf16[320,2048]{1,0:T(8,128)(2,1)S(1)}, bf16[320,2048]{1,0:T(8,128)(2,1)}, u32[]{:S(2)}) copy-start(bf16[320,2048]{1,0:T(8,128)(2,1)} %get-tuple-element.129) | copy-start | bytes 3932164
  523.6 34.2 %collective-permute-start.45 = (bf16[256,2048]{1,0:T(8,128)(2,1)}, bf16[256,2048]{1,0:T(8,128)(2,1)S(1)}, u32[]{:S(2)}, u32[]{:S(2)}) collective-permute-start(bf16[256,2048]{1,0:T(8,128)(2,1)} %get-tuple-element.206), channel_id=1, source_target_pairs={{0,4},{4,0},{8,12},{12,8},{16,20},{20,16},{24,28},{28,24},{1,5},{5... | collective-permute-start | bytes 3145736 | tf_op jit(solution)/shard_map/ppermute | solution.py:59
  548.3 24.9 %collective-permute-start.47 = (bf16[256,2048]{1,0:T(8,128)(2,1)S(1)}, bf16[256,2048]{1,0:T(8,128)(2,1)S(1)}, u32[]{:S(2)}, u32[]{:S(2)}) collective-permute-start(bf16[256,2048]{1,0:T(8,128)(2,1)S(1)} %add_convert_fusion.2), channel_id=1, source_target_pairs={{0,24},{4,28},{8,0},{12,4},{16,8},{20,12},{24,16},{28,20},{1,25},{... | collective-permute-start | bytes 3145736 | tf_op jit(solution)/shard_map/ppermute | solution.py:51
  557.2 29.2 %collective-permute-start.43 = (bf16[256,2048]{1,0:T(8,128)(2,1)S(1)}, bf16[256,2048]{1,0:T(8,128)(2,1)S(1)}, u32[]{:S(2)}, u32[]{:S(2)}) collective-permute-start(bf16[256,2048]{1,0:T(8,128)(2,1)S(1)} %copy-done.72), channel_id=1, source_target_pairs={{0,4},{4,0},{8,12},{12,8},{16,20},{20,16},{24,28},{28,24},{1,5},{5... | collective-permute-start | bytes 3145736 | tf_op jit(solution)/shard_map/ppermute | solution.py:59
  573.8 24.5 %collective-permute-start.48 = (bf16[256,2048]{1,0:T(8,128)(2,1)S(1)}, bf16[256,2048]{1,0:T(8,128)(2,1)S(1)}, u32[]{:S(2)}, u32[]{:S(2)}) collective-permute-start(bf16[256,2048]{1,0:T(8,128)(2,1)S(1)} %add_convert_fusion.1), channel_id=1, source_target_pairs={{0,24},{4,28},{8,0},{12,4},{16,8},{20,12},{24,16},{28,20},{1,25},{... | collective-permute-start | bytes 3145736 | tf_op jit(solution)/shard_map/ppermute | solution.py:51
  (63 other events, 439.6 us)

commit v6 on v5

--- a/solution.py
+++ b/solution.py
@@ -31,7 +31,7 @@
 score_scale = HEAD_DIM ** (-0.5)
 query_blocks = ((0, 128), (128, SEG_PAD))
 
-RATE = 0.59e9
+RATE = 0.66e9
 
 f32 = jnp.float32
 bf16 = jnp.bfloat16

time: 650 us -> 639 us (0.983)
  starting transfers between devices: 63.8 us -> 54.5 us
  local copies, waits for them, and re-layouts: 43.3 us -> 36.8 us
    ppermute x21, waiting for transfers between devices: 40.4 us -> 62.6 us  [shift_inner(): return lax.ppermute(value, 'seq', pairs)]
    ppermute x21, waiting for transfers between devices: 140 us -> 118 us  [shift_outer(): return lax.ppermute(value, 'seq', pairs)]
    unnamed x175 -> x157, local copies, waits for them, and re-layouts: 17.4 us -> 14.7 us
  transfers between devices with their start and end apart: 50 -> 50, of which waited for: 23 -> 28; matrix products, arithmetic and copies ran while one was open for 13% -> 12% of each run, Pallas kernels for 38% -> 38%
where the time goes in v6:
time: 639 us; the launch traced here: 630 us
  Pallas kernels  260 us (41%)
  waiting for transfers between devices  197 us (31%)
  other arithmetic  75.6 us (12%)
  starting transfers between devices  54.5 us (9%)
  local copies, waits for them, and re-layouts  36.8 us (6%)
    ppermute x21, waiting for transfers between devices, shift_outer(): return lax.ppermute(value, 'seq', pairs)  118 us
    pallas_call x4, Pallas kernels, tall_dot(): pl.pallas_call(functools.partial(tall_kernel, epilogue, exchanged, len(le...  68.3 us
    pallas_call x6, Pallas kernels, turned_dot(): pl.pallas_call(functools.partial(turned_kernel, [len(lefts) for lefts, _...  64.1 us
    pallas_call x4, Pallas kernels, wide_dot(): pl.pallas_call(functools.partial(wide_kernel, len(blocks), start), out_sh...  63.5 us
    ppermute x21, waiting for transfers between devices, shift_inner(): return lax.ppermute(value, 'seq', pairs)  62.6 us
    ppermute x21, starting transfers between devices, shift_outer(): return lax.ppermute(value, 'seq', pairs)  27.3 us
    ppermute x21, starting transfers between devices, shift_inner(): return lax.ppermute(value, 'seq', pairs)  21.6 us
    convert_element_type x8, other arithmetic, ring_scatter(): sums.append(total.astype(bf16) if i else total)  18.8 us
  transfers between devices with their start and end apart: 50, of which 28 were waited for; matrix products, arithmetic and copies ran while one was open for 12% of the time, Pallas kernels for 38%

profile of v6, /device:TPU:0, one launch (start us, length us, event | category | flops | bytes accessed | tf_op | source)
XLA Modules:
  0.0 629.7 jit_solution(17566236928170818811)
XLA Ops:
  5.9 3.0 collective-permute-start.2
  12.8 20.9 %collective-permute-done.2.refs_5_.refs_4_.refs_6_ = bf16[272,2048]{1,0:T(8,128)(2,1)} collective-permute-done((bf16[272,2048]{1,0:T(8,128)(2,1)}, bf16[272,2048]{1,0:T(8,128)(2,1)}, u32[]{:S(2)}, u32[]{:S(2)}) %collective-permute-start.2) | collective-permute-done | bytes 1114144 | tf_op jit(solution)/shard_map/ppermute | solution.py:59
  33.8 3.4 collective-permute-done.1.refs_2_.refs_1_.refs_3_
  38.3 2.4 collective-permute-done.refs_1_
  40.7 23.7 %collective-permute-done.3.refs_3_.refs_2_.refs_4_ = bf16[272,2048]{1,0:T(8,128)(2,1)} collective-permute-done((bf16[272,2048]{1,0:T(8,128)(2,1)}, bf16[272,2048]{1,0:T(8,128)(2,1)}, u32[]{:S(2)}, u32[]{:S(2)}) %collective-permute-start.3) | collective-permute-done | bytes 1114144 | tf_op jit(solution)/shard_map/ppermute | solution.py:51
  66.7 3.8 convert.38
  71.8 17.3 %collective-permute-done.6.refs_7_.refs_6_.refs_8_ = bf16[272,2048]{1,0:T(8,128)(2,1)} collective-permute-done((bf16[272,2048]{1,0:T(8,128)(2,1)}, bf16[272,2048]{1,0:T(8,128)(2,1)}, u32[]{:S(2)}, u32[]{:S(2)}) %collective-permute-start.6) | collective-permute-done | bytes 1114144 | tf_op jit(solution)/shard_map/ppermute | solution.py:59
  100.1 2.7 collective-permute-done.7.refs_9_.refs_8_.refs_10_
  108.3 9.3 %first_norm.1 = (bf16[1280,2048]{1,0:T(8,128)(2,1)}, bf16[320,2048]{1,0:T(8,128)(2,1)}) custom-call(bf16[320,2048]{1,0:T(8,128)(2,1)} %copy-done.44, bf16[320,2048]{1,0:T(8,128)(2,1)} %collective-permute-done.refs_1_, f32[1,2048]{1,0:T(1,128)} %bitcast.150, f32[1,2048]{1,0:T(1,128)} %bitcast.149), custom_call_target="tpu_custom_call" | custom-call | flops 5939999744 | tf_op jit(solution)/shard_map/first_norm/pallas_call | solution.py:353
  117.6 4.7 collective-permute-done.8.refs_1_
  122.3 4.8 collective-permute-done.10.refs_3_.refs_1_
  129.2 13.5 %project.1.q_ref.k_ref.v_ref = bf16[1280,1536]{1,0:T(8,128)(2,1)} custom-call(bf16[1280,2048]{1,0:T(8,128)(2,1)} %get-tuple-element.199.refs_0_, bf16[272,2048]{1,0:T(8,128)(2,1)} %pad_maximum_fusion.refs_1_.refs_0_.refs_2_, bf16[272,2048]{1,0:T(8,128)(2,1)} %collective-permute-done.1.refs_2_.refs_1_.refs_3_, ...), custom_call_target="tpu_custom_call" | custom-call | flops 8371975168 | tf_op jit(solution)/shard_map/project/pallas_call | solution.py:434
  144.4 12.3 %attend.1 = (bf16[1280,512]{1,0:T(8,128)(2,1)S(1)}, bf16[8,1280,512]{2,1,0:T(8,128)(2,1)}) custom-call(s32[1]{0:T(128)} %bitcast.15.me_ref, bf16[1280,1536]{1,0:T(8,128)(2,1)} %project.1.q_ref.k_ref.v_ref, bf16[1280,1536]{1,0:T(8,128)(2,1)} %project.1.q_ref.k_ref.v_ref, bf16[1280,1536]{1,0:T(8,128)(2,1)} %project.1.q_ref.k_ref.v_ref, ...), custom_call_target="tpu_custom_call" | custom-call | flops 7920000000 | tf_op jit(solution)/shard_map/attend/pallas_call | solution.py:719
  158.9 11.6 %join.1 = (f32[320,2048]{1,0:T(8,128)}, bf16[320,2048]{1,0:T(8,128)(2,1)}) custom-call(bf16[1280,512]{1,0:T(8,128)(2,1)} %copy-done.14, bf16[272,2048]{1,0:T(8,128)(2,1)} %pad_maximum_fusion.refs_1_.refs_0_.refs_2_, bf16[272,2048]{1,0:T(8,128)(2,1)} %collective-permute-done.1.refs_2_.refs_1_.refs_3_, ...), custom_call_target="tpu_custom_call" | custom-call | flops 3450658304 | tf_op jit(solution)/shard_map/join/pallas_call | solution.py:514
  177.4 22.0 %collective-permute-done.16.refs_5_.refs_3_ = bf16[256,2048]{1,0:T(8,128)(2,1)} collective-permute-done((bf16[256,2048]{1,0:T(8,128)(2,1)}, bf16[256,2048]{1,0:T(8,128)(2,1)}, u32[]{:S(2)}, u32[]{:S(2)}) %collective-permute-start.16) | collective-permute-done | bytes 1048608 | tf_op jit(solution)/shard_map/ppermute | solution.py:51
  208.5 6.6 %collective-permute-done.20.refs_10_.refs_8_ = bf16[128,2048]{1,0:T(8,128)(2,1)S(1)} collective-permute-done((bf16[128,2048]{1,0:T(8,128)(2,1)S(1)}, bf16[128,2048]{1,0:T(8,128)(2,1)S(1)}, u32[]{:S(2)}, u32[]{:S(2)}) %collective-permute-start.20) | collective-permute-done | bytes 524320 | tf_op jit(solution)/shard_map/ppermute | solution.py:51
  218.4 8.7 %feed_grad.1 = (bf16[1280,2048]{1,0:T(8,128)(2,1)}, bf16[320,2048]{1,0:T(8,128)(2,1)}) custom-call(bf16[320,2048]{1,0:T(8,128)(2,1)} %pad.36.refs_0_, bf16[320,2048]{1,0:T(8,128)(2,1)} %collective-permute-done.8.refs_1_, f32[1280,1]{1,0:T(8,128)} %select_n.167.refs_2_), custom_call_target="tpu_custom_call" | custom-call | flops 5939999744 | tf_op jit(solution)/shard_map/feed_grad/pallas_call | solution.py:353
  227.7 11.6 %collective-permute-done.21.refs_3_.refs_2_ = bf16[256,2048]{1,0:T(8,128)(2,1)} collective-permute-done((bf16[256,2048]{1,0:T(8,128)(2,1)}, bf16[256,2048]{1,0:T(8,128)(2,1)}, u32[]{:S(2)}, u32[]{:S(2)}) %collective-permute-start.21) | collective-permute-done | bytes 1048608 | tf_op jit(solution)/shard_map/ppermute | solution.py:51
  240.2 26.5 %up.1 = (bf16[1280,2048]{1,0:T(8,128)(2,1)}, bf16[1280,2048]{1,0:T(8,128)(2,1)}, bf16[640,2048]{1,0:T(8,128)(2,1)}) custom-call(bf16[320,2048]{1,0:T(8,128)(2,1)} %add_convert_fusion.refs_0_, bf16[320,2048]{1,0:T(8,128)(2,1)} %collective-permute-done.19.refs_1_, bf16[256,2048]{1,0:T(8,128)(2,1)} %get-tuple-element.136.refs_2_.refs_0_, ...), custom_call_target="tpu_custom_call" | custom-call | flops 10832633856 | tf_op jit(solution)/shard_map/up/pallas_call | solution.py:434
  268.8 11.0 %down_grad_far.1 = (bf16[768,2048]{1,0:T(8,128)(2,1)}, bf16[256,2048]{1,0:T(8,128)(2,1)}) custom-call(bf16[1280,2048]{1,0:T(8,128)(2,1)} %get-tuple-element.161.refs_0_, bf16[1280,2048]{1,0:T(8,128)(2,1)} %get-tuple-element.171.refs_1_.left_ref), custom_call_target="tpu_custom_call" | custom-call | flops 5911316480 | tf_op jit(solution)/shard_map/down_grad_far/pallas_call | solution.py:571
  280.8 3.2 collective-permute-done.27.refs_9_.refs_8_
  284.9 17.4 %down_back.1 = (bf16[1280,2048]{1,0:T(8,128)(2,1)}, f32[8,2048]{1,0:T(8,128)}) custom-call(bf16[1280,2048]{1,0:T(8,128)(2,1)} %get-tuple-element.161.refs_0_, bf16[256,2048]{1,0:T(8,128)(2,1)} %get-tuple-element.144.refs_1_.refs_0_, bf16[256,2048]{1,0:T(8,128)(2,1)} %collective-permute-done.13.refs_2_.refs_1_, ...), custom_call_target="tpu_custom_call" | custom-call | flops 10832633856 | tf_op jit(solution)/shard_map/down_back/pallas_call | solution.py:434
  304.4 9.9 %down_grad_near.1 = bf16[1024,2048]{1,0:T(8,128)(2,1)} custom-call(bf16[1280,2048]{1,0:T(8,128)(2,1)} %get-tuple-element.161.refs_0_, bf16[1280,2048]{1,0:T(8,128)(2,1)} %get-tuple-element.171.refs_1_.left_ref), custom_call_target="tpu_custom_call" | custom-call | flops 5911316480 | tf_op jit(solution)/shard_map/down_grad_near/pallas_call | solution.py:571
  314.4 18.4 %up_back.1 = (f32[320,2048]{1,0:T(8,128)}, bf16[320,2048]{1,0:T(8,128)(2,1)}) custom-call(bf16[1280,2048]{1,0:T(8,128)(2,1)} %get-tuple-element.162.left_ref.refs_3_, bf16[256,2048]{1,0:T(8,128)(2,1)} %get-tuple-element.136.refs_2_.refs_0_, bf16[256,2048]{1,0:T(8,128)(2,1)} %collective-permute-done.10.refs_3_.refs_1_, ...), custom_call_target="tpu_custom_call" | custom-call | flops 10832633856 | tf_op jit(solution)/shard_map/up_back/pallas_call | solution.py:514
  332.9 2.6 add_convert_fusion.6
  337.4 10.2 %up_grad_near.1 = bf16[1024,2048]{1,0:T(8,128)(2,1)} custom-call(bf16[320,2048]{1,0:T(8,128)(2,1)} %add_convert_fusion.refs_0_, bf16[320,2048]{1,0:T(8,128)(2,1)} %collective-permute-done.19.refs_1_, bf16[640,2048]{1,0:T(8,128)(2,1)} %get-tuple-element.168.refs_2_, bf16[1280,2048]{1,0:T(8,128)(2,1)} %get-tuple-element.162.left_ref.refs_3_), custom_call_target="tpu_custom_call" | custom-call | flops 5911316480 | tf_op jit(solution)/shard_map/up_grad_near/pallas_call | solution.py:571
  347.6 11.2 %up_grad_far.1 = (bf16[512,2048]{1,0:T(8,128)(2,1)}, bf16[256,2048]{1,0:T(8,128)(2,1)}, bf16[256,2048]{1,0:T(8,128)(2,1)}) custom-call(bf16[320,2048]{1,0:T(8,128)(2,1)} %add_convert_fusion.refs_0_, bf16[320,2048]{1,0:T(8,128)(2,1)} %collective-permute-done.19.refs_1_, bf16[640,2048]{1,0:T(8,128)(2,1)} %get-tuple-element.168.refs_2_, ...), custom_call_target="tpu_custom_call" | custom-call | flops 5911316480 | tf_op jit(solution)/shard_map/up_grad_far/pallas_call | solution.py:571
  358.8 5.6 collective-permute-done.29
  364.3 2.4 convert_add_fusion.3
  371.3 6.6 %collective-permute-done.32 = bf16[768,2048]{1,0:T(8,128)(2,1)} collective-permute-done((bf16[768,2048]{1,0:T(8,128)(2,1)}, bf16[768,2048]{1,0:T(8,128)(2,1)}, u32[]{:S(2)}, u32[]{:S(2)}) %collective-permute-start.32) | collective-permute-done | bytes 3145760 | tf_op jit(solution)/shard_map/ppermute | solution.py:59
  377.8 2.1 add_convert_fusion.5
  379.9 2.2 collective-permute-start.38
  382.1 18.2 %down.1 = (f32[320,2048]{1,0:T(8,128)}, bf16[320,2048]{1,0:T(8,128)(2,1)}) custom-call(bf16[1280,2048]{1,0:T(8,128)(2,1)} %get-tuple-element.171.refs_1_.left_ref, bf16[256,2048]{1,0:T(8,128)(2,1)} %get-tuple-element.144.refs_1_.refs_0_, bf16[256,2048]{1,0:T(8,128)(2,1)} %collective-permute-done.13.refs_2_.refs_1_, ...), custom_call_target="tpu_custom_call" | custom-call | flops 10832633856 | tf_op jit(solution)/shard_map/down/pallas_call | solution.py:514
  401.3 2.3 slice.355
  403.6 2.9 add_convert_fusion.9
  406.6 10.8 %join_back.1 = (bf16[1280,512]{1,0:T(8,128)(2,1)}, bf16[640,2048]{1,0:T(8,128)(2,1)}) custom-call(bf16[320,2048]{1,0:T(8,128)(2,1)} %copy-done.42, bf16[320,2048]{1,0:T(8,128)(2,1)} %collective-permute-done.31.refs_1_.refs_2_, bf16[272,2048]{1,0:T(8,128)(2,1)} %pad_maximum_fusion.refs_1_.refs_0_.refs_2_, ...), custom_call_target="tpu_custom_call" | custom-call | flops 3450658304 | tf_op jit(solution)/shard_map/join_back/pallas_call | solution.py:434
  418.6 3.0 add_convert_fusion.4
  421.7 12.3 %attend_back.1 = (bf16[1280,512]{1,0:T(8,128)(2,1)S(1)}, bf16[1280,512]{1,0:T(8,128)(2,1)S(1)}, bf16[1280,512]{1,0:T(8,128)(2,1)S(1)}) custom-call(s32[1]{0:T(128)} %bitcast.15.me_ref, bf16[1280,1536]{1,0:T(8,128)(2,1)} %project.1.q_ref.k_ref.v_ref, bf16[1280,1536]{1,0:T(8,128)(2,1)} %project.1.q_ref.k_ref.v_ref, ...), custom_call_target="tpu_custom_call" | custom-call | flops 8249999872 | tf_op jit(solution)/shard_map/attend_back/pallas_call | solution.py:842
  439.2 2.4 add_convert_fusion.8
  441.6 3.4 collective-permute-start.36
  445.0 11.4 %attn_grad_far.1 = (bf16[256,2048]{1,0:T(8,128)(2,1)}, bf16[256,2048]{1,0:T(8,128)(2,1)}, bf16[256,2048]{1,0:T(8,128)(2,1)}, bf16[256,2048]{1,0:T(8,128)(2,1)}) custom-call(bf16[1280,2048]{1,0:T(8,128)(2,1)} %get-tuple-element.199.refs_0_, bf16[320,2048]{1,0:T(8,128)(2,1)} %copy-done.42, bf16[320,2048]{1,0:T(8,128)(2,1)} %collective-permute-done.31.refs_1_.refs_2_, ...), custom_call_target="tpu_custom_call" | custom-call | flops 5911316480 | tf_op jit(solution)/shard_map/attn_grad_far/pallas_call | solution.py:571
  457.2 15.4 %project_back.1 = (f32[320,2048]{1,0:T(8,128)}, bf16[320,2048]{1,0:T(8,128)(2,1)}) custom-call(bf16[1280,1536]{1,0:T(8,128)(2,1)} %copy-done.48, bf16[272,2048]{1,0:T(8,128)(2,1)} %pad_maximum_fusion.refs_1_.refs_0_.refs_2_, bf16[272,2048]{1,0:T(8,128)(2,1)} %collective-permute-done.1.refs_2_.refs_1_.refs_3_, ...), custom_call_target="tpu_custom_call" | custom-call | flops 8371975168 | tf_op jit(solution)/shard_map/project_back/pallas_call | solution.py:514
  472.9 4.1 collective-permute-done.36
  476.9 3.1 add_convert_fusion.7
  480.0 2.1 collective-permute-start.44
  482.1 10.4 %attn_grad_near.1 = bf16[1024,2048]{1,0:T(8,128)(2,1)} custom-call(bf16[1280,2048]{1,0:T(8,128)(2,1)} %get-tuple-element.199.refs_0_, bf16[320,2048]{1,0:T(8,128)(2,1)} %copy-done.42, bf16[320,2048]{1,0:T(8,128)(2,1)} %collective-permute-done.31.refs_1_.refs_2_, bf16[640,2048]{1,0:T(8,128)(2,1)} %get-tuple-element.191.refs_3_, ...), custom_call_target="tpu_custom_call" | custom-call | flops 5911316480 | tf_op jit(solution)/shard_map/attn_grad_near/pallas_call | solution.py:571
  493.6 2.6 add_convert_fusion.3
  497.2 4.2 fusion.15
  501.4 3.1 collective-permute-done.41
  506.8 2.2 collective-permute-start.46
  510.3 12.3 %collective-permute-done.42 = bf16[256,2048]{1,0:T(8,128)(2,1)} collective-permute-done((bf16[256,2048]{1,0:T(8,128)(2,1)}, bf16[256,2048]{1,0:T(8,128)(2,1)}, u32[]{:S(2)}, u32[]{:S(2)}) %collective-permute-start.42) | collective-permute-done | bytes 1048608 | tf_op jit(solution)/shard_map/ppermute | solution.py:59
  522.6 9.0 %collective-permute-done.46 = bf16[256,2048]{1,0:T(8,128)(2,1)S(1)} collective-permute-done((bf16[256,2048]{1,0:T(8,128)(2,1)}, bf16[256,2048]{1,0:T(8,128)(2,1)S(1)}, u32[]{:S(2)}, u32[]{:S(2)}) %collective-permute-start.46) | collective-permute-done | bytes 1048608 | tf_op jit(solution)/shard_map/ppermute | solution.py:51
  531.6 2.1 add_convert_fusion.2
  533.6 3.8 collective-permute-start.47
  537.4 3.2 fusion.9.in_ref
  544.6 13.6 %collective-permute-done.47 = bf16[256,2048]{1,0:T(8,128)(2,1)S(1)} collective-permute-done((bf16[256,2048]{1,0:T(8,128)(2,1)S(1)}, bf16[256,2048]{1,0:T(8,128)(2,1)S(1)}, u32[]{:S(2)}, u32[]{:S(2)}) %collective-permute-start.47) | collective-permute-done | bytes 1048608 | tf_op jit(solution)/shard_map/ppermute | solution.py:51
  558.8 4.3 collective-permute-start.48
  563.1 4.4 fusion.14
  567.5 2.1 multiply_add_fusion.2.in_ref
  571.3 11.6 %collective-permute-done.48 = bf16[256,2048]{1,0:T(8,128)(2,1)S(1)} collective-permute-done((bf16[256,2048]{1,0:T(8,128)(2,1)S(1)}, bf16[256,2048]{1,0:T(8,128)(2,1)S(1)}, u32[]{:S(2)}, u32[]{:S(2)}) %collective-permute-start.48) | collective-permute-done | bytes 1048608 | tf_op jit(solution)/shard_map/ppermute | solution.py:51
  586.1 17.2 %reduce_all.1 = (f32[24,128]{1,0:T(8,128)S(1)}, f32[8,128]{1,0:T(8,128)S(1)}) custom-call(f32[8,24,128]{2,1,0:T(8,128)S(1)} %bitcast.130, f32[8,128]{1,0:T(8,128)S(1)} %pad.40.refs_1_), custom_call_target="tpu_custom_call" | custom-call | flops 7920000000 | tf_op jit(solution)/shard_map/reduce_all/pallas_call | solution.py:218
  607.9 5.4 fusion.28
  619.3 5.6 fusion.26
  624.9 3.4 multiply_add_fusion
  (348 shorter events, 100.4 us)
Async XLA Ops:
  4.7 32.9 %copy-start.56 = (s32[1,4,50]{2,1,0:T(4,128)S(1)}, s32[1,4,50]{2,1,0:T(4,128)}, u32[]{:S(2)}) copy-start(s32[1,4,50]{2,1,0:T(4,128)} %param.32) | copy-start | bytes 2404
  4.7 32.9 %copy-start.58 = (s32[1,4]{1,0:T(1,128)S(1)}, s32[1,4]{1,0:T(1,128)}, u32[]{:S(2)}) copy-start(s32[1,4]{1,0:T(1,128)} %param.31) | copy-start | bytes 52
  4.7 33.0 %copy-start.51 = (pred[320,320]{1,0:T(32,128)(4,1)S(1)}, pred[320,320]{1,0:T(32,128)(4,1)}, u32[]{:S(2)}) copy-start(pred[320,320]{1,0:T(32,128)(4,1)} %constant.248.clone) | copy-start | bytes 307204
  4.7 33.0 %copy-start.52 = (pred[320,320]{1,0:T(32,128)(4,1)S(1)}, pred[320,320]{1,0:T(32,128)(4,1)}, u32[]{:S(2)}) copy-start(pred[320,320]{1,0:T(32,128)(4,1)} %constant.247.clone) | copy-start | bytes 307204
  4.8 60.8 %copy-start.46 = (bf16[306,2048]{1,0:T(8,128)(2,1)S(1)}, bf16[306,2048]{1,0:T(8,128)(2,1)}, u32[]{:S(2)}) copy-start(bf16[306,2048]{1,0:T(8,128)(2,1)} %param.30) | copy-start | bytes 3760132
  5.9 27.8 %collective-permute-start.2 = (bf16[272,2048]{1,0:T(8,128)(2,1)}, bf16[272,2048]{1,0:T(8,128)(2,1)}, u32[]{:S(2)}, u32[]{:S(2)}) collective-permute-start(bf16[272,2048]{1,0:T(8,128)(2,1)} %pad_maximum_fusion.refs_1_.refs_0_.refs_2_), channel_id=1, source_target_pairs={{0,4},{4,0},{8,12},{12,8},{16,20},{20,16},{24,28},{28,24},{1,5},{5... | collective-permute-start | bytes 3342344 | tf_op jit(solution)/shard_map/ppermute | solution.py:59
  8.9 28.2 %collective-permute-start.1 = (bf16[272,2048]{1,0:T(8,128)(2,1)}, bf16[272,2048]{1,0:T(8,128)(2,1)}, u32[]{:S(2)}, u32[]{:S(2)}) collective-permute-start(bf16[272,2048]{1,0:T(8,128)(2,1)} %pad_maximum_fusion.refs_1_.refs_0_.refs_2_), channel_id=1, source_target_pairs={{0,8},{4,12},{8,16},{12,20},{16,24},{20,28},{24,0},{28,4},{1,9},{5... | collective-permute-start | bytes 3342344 | tf_op jit(solution)/shard_map/ppermute | solution.py:51
  10.6 60.0 %copy-start.44 = (bf16[320,2048]{1,0:T(8,128)(2,1)}, bf16[320,2048]{1,0:T(8,128)(2,1)S(1)}, u32[]{:S(2)}) copy-start(bf16[320,2048]{1,0:T(8,128)(2,1)S(1)} %pad.33.refs_0_) | copy-start | bytes 3932164
  10.6 30.1 %collective-permute-start = (bf16[320,2048]{1,0:T(8,128)(2,1)S(1)}, bf16[320,2048]{1,0:T(8,128)(2,1)}, u32[]{:S(2)}, u32[]{:S(2)}) collective-permute-start(bf16[320,2048]{1,0:T(8,128)(2,1)S(1)} %pad.33.refs_0_), channel_id=1, source_target_pairs={{0,2},{1,3},{2,0},{3,1},{4,6},{5,7},{6,4},{7,5},{8,10},{9,11},{10,... | collective-permute-start | bytes 3932168 | tf_op jit(solution)/shard_map/ppermute | solution.py:63
  37.1 27.3 %collective-permute-start.3 = (bf16[272,2048]{1,0:T(8,128)(2,1)}, bf16[272,2048]{1,0:T(8,128)(2,1)}, u32[]{:S(2)}, u32[]{:S(2)}) collective-permute-start(bf16[272,2048]{1,0:T(8,128)(2,1)} %collective-permute-done.1.refs_2_.refs_1_.refs_3_), channel_id=1, source_target_pairs={{0,8},{4,12},{8,16},{12,20},{16,24},{20,28},{24,0},{28,4},{1,9},{5... | collective-permute-start | bytes 3342344 | tf_op jit(solution)/shard_map/ppermute | solution.py:51
  37.1 27.3 %collective-permute-start.4 = (bf16[272,2048]{1,0:T(8,128)(2,1)}, bf16[272,2048]{1,0:T(8,128)(2,1)S(1)}, u32[]{:S(2)}, u32[]{:S(2)}) collective-permute-start(bf16[272,2048]{1,0:T(8,128)(2,1)} %collective-permute-done.1.refs_2_.refs_1_.refs_3_), channel_id=1, source_target_pairs={{0,4},{4,0},{8,12},{12,8},{16,20},{20,16},{24,28},{28,24},{1,5},{5... | collective-permute-start | bytes 3342344 | tf_op jit(solution)/shard_map/ppermute | solution.py:59
  64.4 26.4 %collective-permute-start.5 = (bf16[272,2048]{1,0:T(8,128)(2,1)}, bf16[272,2048]{1,0:T(8,128)(2,1)}, u32[]{:S(2)}, u32[]{:S(2)}) collective-permute-start(bf16[272,2048]{1,0:T(8,128)(2,1)} %collective-permute-done.3.refs_3_.refs_2_.refs_4_), channel_id=1, source_target_pairs={{0,8},{4,12},{8,16},{12,20},{16,24},{20,28},{24,0},{28,4},{1,9},{5... | collective-permute-start | bytes 3342344 | tf_op jit(solution)/shard_map/ppermute | solution.py:51
  64.5 24.7 %collective-permute-start.6 = (bf16[272,2048]{1,0:T(8,128)(2,1)}, bf16[272,2048]{1,0:T(8,128)(2,1)}, u32[]{:S(2)}, u32[]{:S(2)}) collective-permute-start(bf16[272,2048]{1,0:T(8,128)(2,1)} %collective-permute-done.3.refs_3_.refs_2_.refs_4_), channel_id=1, source_target_pairs={{0,4},{4,0},{8,12},{12,8},{16,20},{20,16},{24,28},{28,24},{1,5},{5... | collective-permute-start | bytes 3342344 | tf_op jit(solution)/shard_map/ppermute | solution.py:59
  71.4 21.6 %copy-start.31 = (bf16[2,256,2048]{2,1,0:T(8,128)(2,1)S(1)}, bf16[2,256,2048]{2,1,0:T(8,128)(2,1)}, u32[]{:S(2)}) copy-start(bf16[2,256,2048]{2,1,0:T(8,128)(2,1)} %convert.38) | copy-start | bytes 6291460
  71.8 34.3 %copy-start.54 = (pred[8]{0:T(512)(128)(4,1)}, pred[8]{0:T(512)(128)(4,1)S(1)}, u32[]{:S(2)}) copy-start(pred[8]{0:T(512)(128)(4,1)S(1)} %compare_and_fusion) | copy-start | bytes 28
  90.2 12.6 %collective-permute-start.7 = (bf16[128,2048]{1,0:T(8,128)(2,1)S(1)}, bf16[128,2048]{1,0:T(8,128)(2,1)S(1)}, u32[]{:S(2)}, u32[]{:S(2)}) collective-permute-start(bf16[128,2048]{1,0:T(8,128)(2,1)S(1)} %slice.315), channel_id=1, source_target_pairs={{0,8},{4,12},{8,16},{12,20},{16,24},{20,28},{24,0},{28,4},{1,9},{5... | collective-permute-start | bytes 1572872 | tf_op jit(solution)/shard_map/ppermute | solution.py:51
  92.0 13.2 %collective-permute-start.9 = (bf16[144,2048]{1,0:T(8,128)(2,1)S(1)}, bf16[144,2048]{1,0:T(8,128)(2,1)}, u32[]{:S(2)}, u32[]{:S(2)}) collective-permute-start(bf16[144,2048]{1,0:T(8,128)(2,1)S(1)} %slice.321), channel_id=1, source_target_pairs={{0,4},{4,0},{8,12},{12,8},{16,20},{20,16},{24,28},{28,24},{1,5},{5... | collective-permute-start | bytes 1769480 | tf_op jit(solution)/shard_map/ppermute | solution.py:59
  94.4 27.8 %collective-permute-start.8 = (bf16[320,2048]{1,0:T(8,128)(2,1)}, bf16[320,2048]{1,0:T(8,128)(2,1)}, u32[]{:S(2)}, u32[]{:S(2)}) collective-permute-start(bf16[320,2048]{1,0:T(8,128)(2,1)} %pad.36.refs_0_), channel_id=1, source_target_pairs={{0,2},{1,3},{2,0},{3,1},{4,6},{5,7},{6,4},{7,5},{8,10},{9,11},{10,... | collective-permute-start | bytes 3932168 | tf_op jit(solution)/shard_map/ppermute | solution.py:63
  95.5 22.0 %copy-start.53 = (s32[1024]{0:T(1024)}, s32[1024]{0:T(1024)S(1)}, u32[]{:S(2)}) copy-start(s32[1024]{0:T(1024)S(1)} %get-tuple-element.286) | copy-start | bytes 12292
  103.7 23.4 %collective-permute-start.10 = (bf16[256,2048]{1,0:T(8,128)(2,1)}, bf16[256,2048]{1,0:T(8,128)(2,1)}, u32[]{:S(2)}, u32[]{:S(2)}) collective-permute-start(bf16[256,2048]{1,0:T(8,128)(2,1)} %get-tuple-element.136.refs_2_.refs_0_), channel_id=1, source_target_pairs={{0,8},{4,12},{8,16},{12,20},{16,24},{20,28},{24,0},{28,4},{1,9},{5... | collective-permute-start | bytes 3145736 | tf_op jit(solution)/shard_map/ppermute | solution.py:51
  105.2 23.3 %collective-permute-start.12 = (bf16[256,2048]{1,0:T(8,128)(2,1)}, bf16[256,2048]{1,0:T(8,128)(2,1)}, u32[]{:S(2)}, u32[]{:S(2)}) collective-permute-start(bf16[256,2048]{1,0:T(8,128)(2,1)} %get-tuple-element.136.refs_2_.refs_0_), channel_id=1, source_target_pairs={{0,4},{4,0},{8,12},{12,8},{16,20},{20,16},{24,28},{28,24},{1,5},{5... | collective-permute-start | bytes 3145736 | tf_op jit(solution)/shard_map/ppermute | solution.py:59
  127.1 30.7 %collective-permute-start.11 = (bf16[256,2048]{1,0:T(8,128)(2,1)}, bf16[256,2048]{1,0:T(8,128)(2,1)}, u32[]{:S(2)}, u32[]{:S(2)}) collective-permute-start(bf16[256,2048]{1,0:T(8,128)(2,1)} %collective-permute-done.10.refs_3_.refs_1_), channel_id=1, source_target_pairs={{0,8},{4,12},{8,16},{12,20},{16,24},{20,28},{24,0},{28,4},{1,9},{5... | collective-permute-start | bytes 3145736 | tf_op jit(solution)/shard_map/ppermute | solution.py:51
  128.5 29.3 %collective-permute-start.14 = (bf16[256,2048]{1,0:T(8,128)(2,1)}, bf16[256,2048]{1,0:T(8,128)(2,1)S(1)}, u32[]{:S(2)}, u32[]{:S(2)}) collective-permute-start(bf16[256,2048]{1,0:T(8,128)(2,1)} %collective-permute-done.10.refs_3_.refs_1_), channel_id=1, source_target_pairs={{0,4},{4,0},{8,12},{12,8},{16,20},{20,16},{24,28},{28,24},{1,5},{5... | collective-permute-start | bytes 3145736 | tf_op jit(solution)/shard_map/ppermute | solution.py:59
  142.7 29.2 %collective-permute-start.13 = (bf16[256,2048]{1,0:T(8,128)(2,1)S(1)}, bf16[256,2048]{1,0:T(8,128)(2,1)}, u32[]{:S(2)}, u32[]{:S(2)}) collective-permute-start(bf16[256,2048]{1,0:T(8,128)(2,1)S(1)} %copy-done.47), channel_id=1, source_target_pairs={{0,8},{4,12},{8,16},{12,20},{16,24},{20,28},{24,0},{28,4},{1,9},{5... | collective-permute-start | bytes 3145736 | tf_op jit(solution)/shard_map/ppermute | solution.py:51
  157.8 18.4 %collective-permute-start.17 = (bf16[256,2048]{1,0:T(8,128)(2,1)}, bf16[256,2048]{1,0:T(8,128)(2,1)}, u32[]{:S(2)}, u32[]{:S(2)}) collective-permute-start(bf16[256,2048]{1,0:T(8,128)(2,1)} %collective-permute-done.11.refs_4_.refs_2_), channel_id=1, source_target_pairs={{0,4},{4,0},{8,12},{12,8},{16,20},{20,16},{24,28},{28,24},{1,5},{5... | collective-permute-start | bytes 3145736 | tf_op jit(solution)/shard_map/ppermute | solution.py:59
  171.9 31.4 %collective-permute-start.15 = (bf16[320,2048]{1,0:T(8,128)(2,1)}, bf16[320,2048]{1,0:T(8,128)(2,1)S(1)}, u32[]{:S(2)}, u32[]{:S(2)}) collective-permute-start(bf16[320,2048]{1,0:T(8,128)(2,1)} %get-tuple-element.142), channel_id=1, source_target_pairs={{0,2},{1,3},{2,0},{3,1},{4,6},{5,7},{6,4},{7,5},{8,10},{9,11},{10,... | collective-permute-start | bytes 3932168 | tf_op jit(solution)/shard_map/ppermute | solution.py:63
  173.4 26.0 %collective-permute-start.16 = (bf16[256,2048]{1,0:T(8,128)(2,1)}, bf16[256,2048]{1,0:T(8,128)(2,1)}, u32[]{:S(2)}, u32[]{:S(2)}) collective-permute-start(bf16[256,2048]{1,0:T(8,128)(2,1)} %collective-permute-done.11.refs_4_.refs_2_), channel_id=1, source_target_pairs={{0,8},{4,12},{8,16},{12,20},{16,24},{20,28},{24,0},{28,4},{1,9},{5... | collective-permute-start | bytes 3145736 | tf_op jit(solution)/shard_map/ppermute | solution.py:51
  175.7 27.6 %copy-start.39 = (f32[320,2048]{1,0:T(8,128)S(1)}, f32[320,2048]{1,0:T(8,128)}, u32[]{:S(2)}) copy-start(f32[320,2048]{1,0:T(8,128)} %get-tuple-element.138) | copy-start | bytes 7864324
  176.3 27.6 %collective-permute-start.18 = (bf16[256,2048]{1,0:T(8,128)(2,1)}, bf16[256,2048]{1,0:T(8,128)(2,1)S(1)}, u32[]{:S(2)}, u32[]{:S(2)}) collective-permute-start(bf16[256,2048]{1,0:T(8,128)(2,1)} %get-tuple-element.144.refs_1_.refs_0_), channel_id=1, source_target_pairs={{0,4},{4,0},{8,12},{12,8},{16,20},{20,16},{24,28},{28,24},{1,5},{5... | collective-permute-start | bytes 3145736 | tf_op jit(solution)/shard_map/ppermute | solution.py:59
  201.5 13.6 %collective-permute-start.20 = (bf16[128,2048]{1,0:T(8,128)(2,1)S(1)}, bf16[128,2048]{1,0:T(8,128)(2,1)S(1)}, u32[]{:S(2)}, u32[]{:S(2)}) collective-permute-start(bf16[128,2048]{1,0:T(8,128)(2,1)S(1)} %slice.333), channel_id=1, source_target_pairs={{0,8},{4,12},{8,16},{12,20},{16,24},{20,28},{24,0},{28,4},{1,9},{5... | collective-permute-start | bytes 1572872 | tf_op jit(solution)/shard_map/ppermute | solution.py:51
  202.6 12.8 %collective-permute-start.22 = (bf16[128,2048]{1,0:T(8,128)(2,1)S(1)}, bf16[128,2048]{1,0:T(8,128)(2,1)S(1)}, u32[]{:S(2)}, u32[]{:S(2)}) collective-permute-start(bf16[128,2048]{1,0:T(8,128)(2,1)S(1)} %slice.334), channel_id=1, source_target_pairs={{0,4},{4,0},{8,12},{12,8},{16,20},{20,16},{24,28},{28,24},{1,5},{5... | collective-permute-start | bytes 1572872 | tf_op jit(solution)/shard_map/ppermute | solution.py:59
  205.6 163.3 %copy-start.16 = (f32[320,2048]{1,0:T(8,128)}, f32[320,2048]{1,0:T(8,128)S(1)}, u32[]{:S(2)}) copy-start(f32[320,2048]{1,0:T(8,128)S(1)} %get-tuple-element.254) | copy-start | bytes 7864324
  207.7 31.6 %collective-permute-start.19 = (bf16[320,2048]{1,0:T(8,128)(2,1)}, bf16[320,2048]{1,0:T(8,128)(2,1)}, u32[]{:S(2)}, u32[]{:S(2)}) collective-permute-start(bf16[320,2048]{1,0:T(8,128)(2,1)} %add_convert_fusion.refs_0_), channel_id=1, source_target_pairs={{0,2},{1,3},{2,0},{3,1},{4,6},{5,7},{6,4},{7,5},{8,10},{9,11},{10,... | collective-permute-start | bytes 3932168 | tf_op jit(solution)/shard_map/ppermute | solution.py:63
  215.1 24.2 %collective-permute-start.21 = (bf16[256,2048]{1,0:T(8,128)(2,1)}, bf16[256,2048]{1,0:T(8,128)(2,1)}, u32[]{:S(2)}, u32[]{:S(2)}) collective-permute-start(bf16[256,2048]{1,0:T(8,128)(2,1)} %collective-permute-done.13.refs_2_.refs_1_), channel_id=1, source_target_pairs={{0,8},{4,12},{8,16},{12,20},{16,24},{20,28},{24,0},{28,4},{1,9},{5... | collective-permute-start | bytes 3145736 | tf_op jit(solution)/shard_map/ppermute | solution.py:51
  216.3 23.9 %collective-permute-start.23 = (bf16[256,2048]{1,0:T(8,128)(2,1)}, bf16[256,2048]{1,0:T(8,128)(2,1)}, u32[]{:S(2)}, u32[]{:S(2)}) collective-permute-start(bf16[256,2048]{1,0:T(8,128)(2,1)} %collective-permute-done.13.refs_2_.refs_1_), channel_id=1, source_target_pairs={{0,4},{4,0},{8,12},{12,8},{16,20},{20,16},{24,28},{28,24},{1,5},{5... | collective-permute-start | bytes 3145736 | tf_op jit(solution)/shard_map/ppermute | solution.py:59
  239.3 27.4 %collective-permute-start.24 = (bf16[256,2048]{1,0:T(8,128)(2,1)}, bf16[256,2048]{1,0:T(8,128)(2,1)S(1)}, u32[]{:S(2)}, u32[]{:S(2)}) collective-permute-start(bf16[256,2048]{1,0:T(8,128)(2,1)} %collective-permute-done.21.refs_3_.refs_2_), channel_id=1, source_target_pairs={{0,8},{4,12},{8,16},{12,20},{16,24},{20,28},{24,0},{28,4},{1,9},{5... | collective-permute-start | bytes 3145736 | tf_op jit(solution)/shard_map/ppermute | solution.py:51
  239.3 28.7 %collective-permute-start.25 = (bf16[256,2048]{1,0:T(8,128)(2,1)}, bf16[256,2048]{1,0:T(8,128)(2,1)S(1)}, u32[]{:S(2)}, u32[]{:S(2)}) collective-permute-start(bf16[256,2048]{1,0:T(8,128)(2,1)} %collective-permute-done.21.refs_3_.refs_2_), channel_id=1, source_target_pairs={{0,4},{4,0},{8,12},{12,8},{16,20},{20,16},{24,28},{28,24},{1,5},{5... | collective-permute-start | bytes 3145736 | tf_op jit(solution)/shard_map/ppermute | solution.py:59
  266.8 14.0 %collective-permute-start.26 = (bf16[128,2048]{1,0:T(8,128)(2,1)S(1)}, bf16[128,2048]{1,0:T(8,128)(2,1)S(1)}, u32[]{:S(2)}, u32[]{:S(2)}) collective-permute-start(bf16[128,2048]{1,0:T(8,128)(2,1)S(1)} %slice.336), channel_id=1, source_target_pairs={{0,4},{4,0},{8,12},{12,8},{16,20},{20,16},{24,28},{28,24},{1,5},{5... | collective-permute-start | bytes 1572872 | tf_op jit(solution)/shard_map/ppermute | solution.py:59
  268.0 16.0 %collective-permute-start.27 = (bf16[128,2048]{1,0:T(8,128)(2,1)S(1)}, bf16[128,2048]{1,0:T(8,128)(2,1)S(1)}, u32[]{:S(2)}, u32[]{:S(2)}) collective-permute-start(bf16[128,2048]{1,0:T(8,128)(2,1)S(1)} %slice.337), channel_id=1, source_target_pairs={{0,8},{4,12},{8,16},{12,20},{16,24},{20,28},{24,0},{28,4},{1,9},{5... | collective-permute-start | bytes 1572872 | tf_op jit(solution)/shard_map/ppermute | solution.py:51
  284.0 30.4 %collective-permute-start.28 = (bf16[256,2048]{1,0:T(8,128)(2,1)}, bf16[256,2048]{1,0:T(8,128)(2,1)}, u32[]{:S(2)}, u32[]{:S(2)}) collective-permute-start(bf16[256,2048]{1,0:T(8,128)(2,1)} %get-tuple-element.160), channel_id=1, source_target_pairs={{0,4},{4,0},{8,12},{12,8},{16,20},{20,16},{24,28},{28,24},{1,5},{5... | collective-permute-start | bytes 3145736 | tf_op jit(solution)/shard_map/ppermute | solution.py:59
  303.2 74.6 %collective-permute-start.32 = (bf16[768,2048]{1,0:T(8,128)(2,1)}, bf16[768,2048]{1,0:T(8,128)(2,1)}, u32[]{:S(2)}, u32[]{:S(2)}) collective-permute-start(bf16[768,2048]{1,0:T(8,128)(2,1)} %get-tuple-element.178), channel_id=1, source_target_pairs={{0,4},{4,0},{8,12},{12,8},{16,20},{20,16},{24,28},{28,24},{1,5},{5... | collective-permute-start | bytes 9437192 | tf_op jit(solution)/shard_map/ppermute | solution.py:59
  332.8 31.6 %collective-permute-start.29 = (bf16[320,2048]{1,0:T(8,128)(2,1)}, bf16[320,2048]{1,0:T(8,128)(2,1)}, u32[]{:S(2)}, u32[]{:S(2)}) collective-permute-start(bf16[320,2048]{1,0:T(8,128)(2,1)} %get-tuple-element.164), channel_id=1, source_target_pairs={{0,2},{1,3},{2,0},{3,1},{4,6},{5,7},{6,4},{7,5},{8,10},{9,11},{10,... | collective-permute-start | bytes 3932168 | tf_op jit(solution)/shard_map/ppermute | solution.py:63
  335.5 35.8 %collective-permute-start.37 = (bf16[256,2048]{1,0:T(8,128)(2,1)}, bf16[256,2048]{1,0:T(8,128)(2,1)}, u32[]{:S(2)}, u32[]{:S(2)}) collective-permute-start(bf16[256,2048]{1,0:T(8,128)(2,1)} %add_convert_fusion.6), channel_id=1, source_target_pairs={{0,24},{4,28},{8,0},{12,4},{16,8},{20,12},{24,16},{28,20},{1,25},{... | collective-permute-start | bytes 3145736 | tf_op jit(solution)/shard_map/ppermute | solution.py:51
  367.9 35.7 %collective-permute-start.30 = (bf16[256,2048]{1,0:T(8,128)(2,1)}, bf16[256,2048]{1,0:T(8,128)(2,1)}, u32[]{:S(2)}, u32[]{:S(2)}) collective-permute-start(bf16[256,2048]{1,0:T(8,128)(2,1)} %get-tuple-element.175), channel_id=1, source_target_pairs={{0,4},{4,0},{8,12},{12,8},{16,20},{20,16},{24,28},{28,24},{1,5},{5... | collective-permute-start | bytes 3145736 | tf_op jit(solution)/shard_map/ppermute | solution.py:59
  370.9 29.4 %copy-start.42 = (bf16[320,2048]{1,0:T(8,128)(2,1)}, bf16[320,2048]{1,0:T(8,128)(2,1)S(1)}, u32[]{:S(2)}) copy-start(bf16[320,2048]{1,0:T(8,128)(2,1)S(1)} %multiply_convert_fusion.refs_0_.refs_1_) | copy-start | bytes 3932164
  370.9 35.6 %collective-permute-start.31 = (bf16[320,2048]{1,0:T(8,128)(2,1)S(1)}, bf16[320,2048]{1,0:T(8,128)(2,1)}, u32[]{:S(2)}, u32[]{:S(2)}) collective-permute-start(bf16[320,2048]{1,0:T(8,128)(2,1)S(1)} %multiply_convert_fusion.refs_0_.refs_1_), channel_id=1, source_target_pairs={{0,2},{1,3},{2,0},{3,1},{4,6},{5,7},{6,4},{7,5},{8,10},{9,11},{10,... | collective-permute-start | bytes 3932168 | tf_op jit(solution)/shard_map/ppermute | solution.py:63
  379.9 38.7 %collective-permute-start.38 = (bf16[256,2048]{1,0:T(8,128)(2,1)S(1)}, bf16[256,2048]{1,0:T(8,128)(2,1)S(1)}, u32[]{:S(2)}, u32[]{:S(2)}) collective-permute-start(bf16[256,2048]{1,0:T(8,128)(2,1)S(1)} %add_convert_fusion.5), channel_id=1, source_target_pairs={{0,24},{4,28},{8,0},{12,4},{16,8},{20,12},{24,16},{28,20},{1,25},{... | collective-permute-start | bytes 3145736 | tf_op jit(solution)/shard_map/ppermute | solution.py:51
  400.4 36.9 %collective-permute-start.34 = (bf16[256,2048]{1,0:T(8,128)(2,1)}, bf16[256,2048]{1,0:T(8,128)(2,1)}, u32[]{:S(2)}, u32[]{:S(2)}) collective-permute-start(bf16[256,2048]{1,0:T(8,128)(2,1)} %get-tuple-element.184), channel_id=1, source_target_pairs={{0,4},{4,0},{8,12},{12,8},{16,20},{20,16},{24,28},{28,24},{1,5},{5... | collective-permute-start | bytes 3145736 | tf_op jit(solution)/shard_map/ppermute | solution.py:59
  406.5 32.7 %collective-permute-start.35 = (bf16[256,2048]{1,0:T(8,128)(2,1)}, bf16[256,2048]{1,0:T(8,128)(2,1)}, u32[]{:S(2)}, u32[]{:S(2)}) collective-permute-start(bf16[256,2048]{1,0:T(8,128)(2,1)} %add_convert_fusion.9), channel_id=1, source_target_pairs={{0,24},{4,28},{8,0},{12,4},{16,8},{20,12},{24,16},{28,20},{1,25},{... | collective-permute-start | bytes 3145736 | tf_op jit(solution)/shard_map/ppermute | solution.py:51
  417.4 59.5 %collective-permute-start.33 = (bf16[512,2048]{1,0:T(8,128)(2,1)}, bf16[512,2048]{1,0:T(8,128)(2,1)}, u32[]{:S(2)}, u32[]{:S(2)}) collective-permute-start(bf16[512,2048]{1,0:T(8,128)(2,1)} %get-tuple-element.182), channel_id=1, source_target_pairs={{0,4},{4,0},{8,12},{12,8},{16,20},{20,16},{24,28},{28,24},{1,5},{5... | collective-permute-start | bytes 6291464 | tf_op jit(solution)/shard_map/ppermute | solution.py:59
  421.7 75.5 %collective-permute-start.49 = (bf16[256,2048]{1,0:T(8,128)(2,1)}, bf16[256,2048]{1,0:T(8,128)(2,1)}, u32[]{:S(2)}, u32[]{:S(2)}) collective-permute-start(bf16[256,2048]{1,0:T(8,128)(2,1)} %add_convert_fusion.4), channel_id=1, source_target_pairs={{0,24},{4,28},{8,0},{12,4},{16,8},{20,12},{24,16},{28,20},{1,25},{... | collective-permute-start | bytes 3145736 | tf_op jit(solution)/shard_map/ppermute | solution.py:51
  441.6 35.3 %collective-permute-start.36 = (bf16[256,2048]{1,0:T(8,128)(2,1)S(1)}, bf16[256,2048]{1,0:T(8,128)(2,1)S(1)}, u32[]{:S(2)}, u32[]{:S(2)}) collective-permute-start(bf16[256,2048]{1,0:T(8,128)(2,1)S(1)} %add_convert_fusion.8), channel_id=1, source_target_pairs={{0,24},{4,28},{8,0},{12,4},{16,8},{20,12},{24,16},{28,20},{1,25},{... | collective-permute-start | bytes 3145736 | tf_op jit(solution)/shard_map/ppermute | solution.py:51
  456.4 37.3 %collective-permute-start.39 = (bf16[256,2048]{1,0:T(8,128)(2,1)}, bf16[256,2048]{1,0:T(8,128)(2,1)S(1)}, u32[]{:S(2)}, u32[]{:S(2)}) collective-permute-start(bf16[256,2048]{1,0:T(8,128)(2,1)} %get-tuple-element.200), channel_id=1, source_target_pairs={{0,4},{4,0},{8,12},{12,8},{16,20},{20,16},{24,28},{28,24},{1,5},{5... | collective-permute-start | bytes 3145736 | tf_op jit(solution)/shard_map/ppermute | solution.py:59
  472.7 31.8 %collective-permute-start.41 = (bf16[320,2048]{1,0:T(8,128)(2,1)}, bf16[320,2048]{1,0:T(8,128)(2,1)S(1)}, u32[]{:S(2)}, u32[]{:S(2)}) collective-permute-start(bf16[320,2048]{1,0:T(8,128)(2,1)} %get-tuple-element.198), channel_id=1, source_target_pairs={{0,2},{1,3},{2,0},{3,1},{4,6},{5,7},{6,4},{7,5},{8,10},{9,11},{10,... | collective-permute-start | bytes 3932168 | tf_op jit(solution)/shard_map/ppermute | solution.py:63
  480.0 26.8 %collective-permute-start.44 = (bf16[256,2048]{1,0:T(8,128)(2,1)}, bf16[256,2048]{1,0:T(8,128)(2,1)}, u32[]{:S(2)}, u32[]{:S(2)}) collective-permute-start(bf16[256,2048]{1,0:T(8,128)(2,1)} %add_convert_fusion.7), channel_id=1, source_target_pairs={{0,24},{4,28},{8,0},{12,4},{16,8},{20,12},{24,16},{28,20},{1,25},{... | collective-permute-start | bytes 3145736 | tf_op jit(solution)/shard_map/ppermute | solution.py:51
  496.2 26.4 %collective-permute-start.42 = (bf16[256,2048]{1,0:T(8,128)(2,1)}, bf16[256,2048]{1,0:T(8,128)(2,1)}, u32[]{:S(2)}, u32[]{:S(2)}) collective-permute-start(bf16[256,2048]{1,0:T(8,128)(2,1)} %get-tuple-element.204), channel_id=1, source_target_pairs={{0,4},{4,0},{8,12},{12,8},{16,20},{20,16},{24,28},{28,24},{1,5},{5... | collective-permute-start | bytes 3145736 | tf_op jit(solution)/shard_map/ppermute | solution.py:59
  497.1 70.4 %collective-permute-start.40 = (bf16[320,2048]{1,0:T(8,128)(2,1)}, bf16[320,2048]{1,0:T(8,128)(2,1)}, u32[]{:S(2)}, u32[]{:S(2)}) collective-permute-start(bf16[320,2048]{1,0:T(8,128)(2,1)} %get-tuple-element.202), channel_id=1, source_target_pairs={{0,2},{1,3},{2,0},{3,1},{4,6},{5,7},{6,4},{7,5},{8,10},{9,11},{10,... | collective-permute-start | bytes 3932168 | tf_op jit(solution)/shard_map/ppermute | solution.py:63
  505.9 31.6 %copy-start.19 = (f32[320,2048]{1,0:T(8,128)S(1)}, f32[320,2048]{1,0:T(8,128)}, u32[]{:S(2)}) copy-start(f32[320,2048]{1,0:T(8,128)} %copy-done.18) | copy-start | bytes 7864324
  506.8 30.7 %copy-start.23 = (bf16[320,2048]{1,0:T(8,128)(2,1)S(1)}, bf16[320,2048]{1,0:T(8,128)(2,1)}, u32[]{:S(2)}) copy-start(bf16[320,2048]{1,0:T(8,128)(2,1)} %get-tuple-element.129) | copy-start | bytes 3932164
  506.8 24.8 %collective-permute-start.46 = (bf16[256,2048]{1,0:T(8,128)(2,1)}, bf16[256,2048]{1,0:T(8,128)(2,1)S(1)}, u32[]{:S(2)}, u32[]{:S(2)}) collective-permute-start(bf16[256,2048]{1,0:T(8,128)(2,1)} %add_convert_fusion.3), channel_id=1, source_target_pairs={{0,24},{4,28},{8,0},{12,4},{16,8},{20,12},{24,16},{28,20},{1,25},{... | collective-permute-start | bytes 3145736 | tf_op jit(solution)/shard_map/ppermute | solution.py:51
  509.1 35.5 %collective-permute-start.45 = (bf16[256,2048]{1,0:T(8,128)(2,1)}, bf16[256,2048]{1,0:T(8,128)(2,1)S(1)}, u32[]{:S(2)}, u32[]{:S(2)}) collective-permute-start(bf16[256,2048]{1,0:T(8,128)(2,1)} %get-tuple-element.206), channel_id=1, source_target_pairs={{0,4},{4,0},{8,12},{12,8},{16,20},{20,16},{24,28},{28,24},{1,5},{5... | collective-permute-start | bytes 3145736 | tf_op jit(solution)/shard_map/ppermute | solution.py:59
  533.6 24.5 %collective-permute-start.47 = (bf16[256,2048]{1,0:T(8,128)(2,1)S(1)}, bf16[256,2048]{1,0:T(8,128)(2,1)S(1)}, u32[]{:S(2)}, u32[]{:S(2)}) collective-permute-start(bf16[256,2048]{1,0:T(8,128)(2,1)S(1)} %add_convert_fusion.2), channel_id=1, source_target_pairs={{0,24},{4,28},{8,0},{12,4},{16,8},{20,12},{24,16},{28,20},{1,25},{... | collective-permute-start | bytes 3145736 | tf_op jit(solution)/shard_map/ppermute | solution.py:51
  542.5 28.8 %collective-permute-start.43 = (bf16[256,2048]{1,0:T(8,128)(2,1)S(1)}, bf16[256,2048]{1,0:T(8,128)(2,1)S(1)}, u32[]{:S(2)}, u32[]{:S(2)}) collective-permute-start(bf16[256,2048]{1,0:T(8,128)(2,1)S(1)} %copy-done.63), channel_id=1, source_target_pairs={{0,4},{4,0},{8,12},{12,8},{16,20},{20,16},{24,28},{28,24},{1,5},{5... | collective-permute-start | bytes 3145736 | tf_op jit(solution)/shard_map/ppermute | solution.py:59
  558.8 24.1 %collective-permute-start.48 = (bf16[256,2048]{1,0:T(8,128)(2,1)S(1)}, bf16[256,2048]{1,0:T(8,128)(2,1)S(1)}, u32[]{:S(2)}, u32[]{:S(2)}) collective-permute-start(bf16[256,2048]{1,0:T(8,128)(2,1)S(1)} %add_convert_fusion.1), channel_id=1, source_target_pairs={{0,24},{4,28},{8,0},{12,4},{16,8},{20,12},{24,16},{28,20},{1,25},{... | collective-permute-start | bytes 3145736 | tf_op jit(solution)/shard_map/ppermute | solution.py:51
  (54 other events, 302.2 us)
